TPU v7x, 32 devices: a whole 2x2x4 slice. The times are simulated.
32 devices in a mesh: dp: 8 (over z, y), seq: 4 (over x, core).
Axes of the slice: x: 2, y: 2, z: 4, core: 2. Of those that a mesh axis runs over, the one named last changes fastest.
Arguments:
- tokens: bfloat16 [8, 1024, 2048], P('dp', 'seq'), may hold values from -6 to 6
- cotangent: bfloat16 [8, 1024, 2048], P('dp', 'seq'), may hold values from -6 to 6
- lengths: int32 [8], P('dp'), may hold values from 256 to 1024, as said below
- adapter_ids: int32 [8], P('dp'), may hold values from 0 to 7
- attn_gain: float32 [2048], replicated, may hold values from 0.5 to 1.5
- query_gain: float32 [64], replicated, may hold values from 0.1 to 1.9
- key_gain: float32 [64], replicated, may hold values from 0.1 to 1.9
- ffn_gain: float32 [2048], replicated, may hold values from 0.5 to 1.5
- w_query: bfloat16 [2048, 2048], P(('dp', 'seq')), may hold values from -0.125 to 0.125
- w_key: bfloat16 [2048, 512], P(('dp', 'seq')), may hold values from -0.125 to 0.125
- w_value: bfloat16 [2048, 512], P(('dp', 'seq')), may hold values from -0.125 to 0.125
- w_out: bfloat16 [2048, 2048], P(('dp', 'seq')), may hold values from -1.5 to 1.5
- gate_weight: bfloat16 [2048, 8192], P(('dp', 'seq')), may hold values from -0.125 to 0.125
- w_up: bfloat16 [2048, 8192], P(('dp', 'seq')), may hold values from -0.125 to 0.125
- w_down: bfloat16 [8192, 2048], P(('dp', 'seq')), may hold values from -0.0625 to 0.0625
- a_query: bfloat16 [8, 2048, 16], P(None, ('dp', 'seq')), may hold values from -0.125 to 0.125
- b_query: bfloat16 [8, 2048, 16], P(None, ('dp', 'seq')), may hold values from -1.5 to 1.5
- a_key: bfloat16 [8, 2048, 16], P(None, ('dp', 'seq')), may hold values from -0.125 to 0.125
- b_key: bfloat16 [8, 512, 16], P(None, ('dp', 'seq')), may hold values from -1.5 to 1.5
- a_value: bfloat16 [8, 2048, 16], P(None, ('dp', 'seq')), may hold values from -0.125 to 0.125
- b_value: bfloat16 [8, 512, 16], P(None, ('dp', 'seq')), may hold values from -1.5 to 1.5
- a_out: bfloat16 [8, 2048, 16], P(None, ('dp', 'seq')), may hold values from -1.5 to 1.5
- b_out: bfloat16 [8, 2048, 16], P(None, ('dp', 'seq')), may hold values from -1.5 to 1.5
- a_gate: bfloat16 [8, 2048, 16], P(None, ('dp', 'seq')), may hold values from -0.125 to 0.125
- b_gate: bfloat16 [8, 8192, 16], P(None, ('dp', 'seq')), may hold values from -1.5 to 1.5
- a_up: bfloat16 [8, 2048, 16], P(None, ('dp', 'seq')), may hold values from -0.125 to 0.125
- b_up: bfloat16 [8, 8192, 16], P(None, ('dp', 'seq')), may hold values from -1.5 to 1.5
- a_down: bfloat16 [8, 8192, 16], P(None, ('dp', 'seq')), may hold values from -0.0625 to 0.0625
- b_down: bfloat16 [8, 2048, 16], P(None, ('dp', 'seq')), may hold values from -1.5 to 1.5
Outputs:
- output: bfloat16 [8, 1024, 2048], P('dp', 'seq')
- grad_tokens: bfloat16 [8, 1024, 2048], P('dp', 'seq')
- grad_a_query: float32 [8, 2048, 16], P(None, ('dp', 'seq'))
- grad_b_query: float32 [8, 2048, 16], P(None, ('dp', 'seq'))
- grad_a_key: float32 [8, 2048, 16], P(None, ('dp', 'seq'))
- grad_b_key: float32 [8, 512, 16], P(None, ('dp', 'seq'))
- grad_a_value: float32 [8, 2048, 16], P(None, ('dp', 'seq'))
- grad_b_value: float32 [8, 512, 16], P(None, ('dp', 'seq'))
- grad_a_out: float32 [8, 2048, 16], P(None, ('dp', 'seq'))
- grad_b_out: float32 [8, 2048, 16], P(None, ('dp', 'seq'))
- grad_a_gate: float32 [8, 2048, 16], P(None, ('dp', 'seq'))
- grad_b_gate: float32 [8, 8192, 16], P(None, ('dp', 'seq'))
- grad_a_up: float32 [8, 2048, 16], P(None, ('dp', 'seq'))
- grad_b_up: float32 [8, 8192, 16], P(None, ('dp', 'seq'))
- grad_a_down: float32 [8, 8192, 16], P(None, ('dp', 'seq'))
- grad_b_down: float32 [8, 2048, 16], P(None, ('dp', 'seq'))
Inputs may be any that keep to these rules, and one draw needn't show every extreme that they name: `lengths`: one sequence in every draw has all 1024 tokens valid.
All inputs are finite; a program needn't handle non-finite values.
Results may differ from a plain program's by a relative error of at most 0.02.
Values may be sent and summed in bfloat16 or wider, within the bound.
No kernel may reach another device: no remote copies, remote signals or barrier semaphores. Data moves between devices by JAX's collectives and lax.ppermute only.
A program may use at most 384 MiB of HBM per device.

v0:
```python
import jax
import jax.numpy as jnp
from jax import lax
from jax.sharding import PartitionSpec as P

H = 32
KV = 8
HD = 64
ADAPT = 8


def rms_scale(operand, scaling):
    return (
        operand * lax.rsqrt(jnp.mean(operand * operand, axis=-1, keepdims=True) + 1e-05) * scaling
    )


def rotary_tables(positions, size):
    frequency = jnp.power(1000000.0, -jnp.arange(size // 2, dtype=jnp.float32) * 2.0 / size)
    angles = positions.astype(jnp.float32)[:, None] * frequency[None, :]
    return (jnp.cos(angles), jnp.sin(angles))


def rotate(operand, cosine_table, sine_table):
    half_size = operand.shape[-1] // 2
    front = operand[..., :half_size]
    second = operand[..., half_size:]
    return jnp.concatenate(
        [front * cosine_table - second * sine_table, second * cosine_table + front * sine_table],
        axis=-1,
    )


def prepare(linear, scaling, cosine_table, sine_table, head_count):
    shaped = linear.reshape(linear.shape[:-1] + (head_count, linear.shape[-1] // head_count))
    return rotate(rms_scale(shaped, scaling), cosine_table[:, None, :], sine_table[:, None, :])


def adapted(operand, matrix, lower, adapter_expand):
    adapter_inner = jnp.einsum(
        "sli,sir->slr", operand, lower, preferred_element_type=jnp.float32
    ).astype(jnp.bfloat16)
    straight_path = jnp.einsum("sli,io->slo", operand, matrix, preferred_element_type=jnp.float32)
    return (
        straight_path
        + jnp.einsum(
            "avb,ahb->avh", adapter_inner, adapter_expand, preferred_element_type=jnp.float32
        ),
        adapter_inner,
    )


def adapted_back(arriving_gradient, operand, adapter_inner, matrix, lower, adapter_expand):
    d_narrow = jnp.einsum(
        "vfz,vzj->vfj", arriving_gradient, adapter_expand, preferred_element_type=jnp.float32
    ).astype(jnp.bfloat16)
    d_operand = jnp.einsum(
        "slo,io->sli", arriving_gradient, matrix, preferred_element_type=jnp.float32
    )
    d_operand = d_operand + jnp.einsum(
        "slr,sir->sli", d_narrow, lower, preferred_element_type=jnp.float32
    )
    expand_gradient = jnp.einsum(
        "azn,azg->ang", arriving_gradient, adapter_inner, preferred_element_type=jnp.float32
    )
    lower_grad = jnp.einsum("sli,slr->sir", operand, d_narrow, preferred_element_type=jnp.float32)
    return (d_operand, lower_grad, expand_gradient)


def shards(
    tokens,
    cotangent,
    lengths,
    adapter_ids,
    attn_gain,
    query_gain,
    key_gain,
    ffn_gain,
    w_query,
    w_key,
    w_value,
    w_out,
    gate_weight,
    w_up,
    w_down,
    a_query,
    b_query,
    a_key,
    b_key,
    a_value,
    b_value,
    a_out,
    b_out,
    a_gate,
    b_gate,
    a_up,
    b_up,
    a_down,
    b_down,
):
    gathered = (
        lax.all_gather(w_query, ("dp", "seq"), axis=0, tiled=True),
        lax.all_gather(w_key, ("dp", "seq"), axis=0, tiled=True),
        lax.all_gather(w_value, ("dp", "seq"), axis=0, tiled=True),
        lax.all_gather(w_out, ("dp", "seq"), axis=0, tiled=True),
        lax.all_gather(gate_weight, ("dp", "seq"), axis=0, tiled=True),
        lax.all_gather(w_up, ("dp", "seq"), axis=0, tiled=True),
        lax.all_gather(w_down, ("dp", "seq"), axis=0, tiled=True),
        lax.all_gather(a_query, ("dp", "seq"), axis=1, tiled=True),
        lax.all_gather(b_query, ("dp", "seq"), axis=1, tiled=True),
        lax.all_gather(a_key, ("dp", "seq"), axis=1, tiled=True),
        lax.all_gather(b_key, ("dp", "seq"), axis=1, tiled=True),
        lax.all_gather(a_value, ("dp", "seq"), axis=1, tiled=True),
        lax.all_gather(b_value, ("dp", "seq"), axis=1, tiled=True),
        lax.all_gather(a_out, ("dp", "seq"), axis=1, tiled=True),
        lax.all_gather(b_out, ("dp", "seq"), axis=1, tiled=True),
        lax.all_gather(a_gate, ("dp", "seq"), axis=1, tiled=True),
        lax.all_gather(b_gate, ("dp", "seq"), axis=1, tiled=True),
        lax.all_gather(a_up, ("dp", "seq"), axis=1, tiled=True),
        lax.all_gather(b_up, ("dp", "seq"), axis=1, tiled=True),
        lax.all_gather(a_down, ("dp", "seq"), axis=1, tiled=True),
        lax.all_gather(b_down, ("dp", "seq"), axis=1, tiled=True),
    )
    seqs_here = tokens.shape[0]
    block_len = tokens.shape[1]
    groups = H // KV
    scale_factor = HD ** (-0.5)
    positions = lax.axis_index("seq") * block_len + jnp.arange(block_len)
    full_length = block_len * lax.axis_size("seq")
    key_places = jnp.arange(full_length)
    cosine_table, sine_table = rotary_tables(positions, HD)
    valid_rows = (positions[None, :] < lengths[:, None]).astype(jnp.float32)[:, :, None]
    allowed = (key_places[None, None, :] <= positions[None, :, None]) & (
        key_places[None, None, :] < lengths[:, None, None]
    )
    picked = [jnp.take(stack, adapter_ids, axis=0) for stack in gathered[7:]]
    inputs = tokens.astype(jnp.float32)
    normed_one = rms_scale(inputs, attn_gain).astype(jnp.bfloat16)
    query_lin, narrow_query = adapted(normed_one, gathered[0], picked[0], picked[1])
    key_lin, narrow_key = adapted(normed_one, gathered[1], picked[2], picked[3])
    value_lin, narrow_value = adapted(normed_one, gathered[2], picked[4], picked[5])
    queries = prepare(query_lin, query_gain, cosine_table, sine_table, H).astype(jnp.bfloat16)
    keys_here = (
        prepare(key_lin, key_gain, cosine_table, sine_table, KV)
        .astype(jnp.bfloat16)
        .reshape(seqs_here, block_len, KV * HD)
    )
    values_here = value_lin.astype(jnp.bfloat16)
    keys_all, values_all = (
        lax.all_gather(keys_here, "seq", axis=1, tiled=True),
        lax.all_gather(values_here, "seq", axis=1, tiled=True),
    )
    query_heads = queries.reshape(seqs_here, block_len, KV, groups, HD).transpose(2, 0, 3, 1, 4)
    key_heads = keys_all.reshape(seqs_here, full_length, KV, HD).transpose(2, 0, 1, 3)
    value_heads = values_all.reshape(seqs_here, full_length, KV, HD).transpose(2, 0, 1, 3)

    def head_forward(member):
        query_part, key_part, value_slice = member
        scores = (
            jnp.einsum("sgqd,skd->sgqk", query_part, key_part, preferred_element_type=jnp.float32)
            * scale_factor
        )
        scores = jnp.where(allowed[:, None], scores, -1e30)
        row_max = jnp.max(scores, axis=-1, keepdims=True)
        exponent = jnp.exp(scores - row_max)
        row_total = jnp.sum(exponent, axis=-1, keepdims=True)
        weights_low = (exponent / row_total).astype(jnp.bfloat16)
        result = jnp.einsum(
            "sgqk,skd->sgqd", weights_low, value_slice, preferred_element_type=jnp.float32
        )
        return (result, (row_max + jnp.log(row_total))[..., 0])

    attended_heads, log_totals = lax.map(head_forward, (query_heads, key_heads, value_heads))
    attended = (
        attended_heads.transpose(1, 3, 0, 2, 4)
        .reshape(seqs_here, block_len, H * HD)
        .astype(jnp.bfloat16)
    )
    update, narrow_out = adapted(attended, gathered[3], picked[6], picked[7])
    hidden = inputs + valid_rows * update
    normed_two = rms_scale(hidden, ffn_gain).astype(jnp.bfloat16)
    gate_lin, narrow_gate = adapted(normed_two, gathered[4], picked[8], picked[9])
    upward, narrow_up = adapted(normed_two, gathered[5], picked[10], picked[11])
    active = (jax.nn.silu(gate_lin) * upward).astype(jnp.bfloat16)
    lowered, narrow_down = adapted(active, gathered[6], picked[12], picked[13])
    output = (hidden + valid_rows * lowered).astype(jnp.bfloat16)
    gathered_back = (
        lax.all_gather(w_query, ("dp", "seq"), axis=0, tiled=True),
        lax.all_gather(w_key, ("dp", "seq"), axis=0, tiled=True),
        lax.all_gather(w_value, ("dp", "seq"), axis=0, tiled=True),
        lax.all_gather(w_out, ("dp", "seq"), axis=0, tiled=True),
        lax.all_gather(gate_weight, ("dp", "seq"), axis=0, tiled=True),
        lax.all_gather(w_up, ("dp", "seq"), axis=0, tiled=True),
        lax.all_gather(w_down, ("dp", "seq"), axis=0, tiled=True),
        lax.all_gather(a_query, ("dp", "seq"), axis=1, tiled=True),
        lax.all_gather(b_query, ("dp", "seq"), axis=1, tiled=True),
        lax.all_gather(a_key, ("dp", "seq"), axis=1, tiled=True),
        lax.all_gather(b_key, ("dp", "seq"), axis=1, tiled=True),
        lax.all_gather(a_value, ("dp", "seq"), axis=1, tiled=True),
        lax.all_gather(b_value, ("dp", "seq"), axis=1, tiled=True),
        lax.all_gather(a_out, ("dp", "seq"), axis=1, tiled=True),
        lax.all_gather(b_out, ("dp", "seq"), axis=1, tiled=True),
        lax.all_gather(a_gate, ("dp", "seq"), axis=1, tiled=True),
        lax.all_gather(b_gate, ("dp", "seq"), axis=1, tiled=True),
        lax.all_gather(a_up, ("dp", "seq"), axis=1, tiled=True),
        lax.all_gather(b_up, ("dp", "seq"), axis=1, tiled=True),
        lax.all_gather(a_down, ("dp", "seq"), axis=1, tiled=True),
        lax.all_gather(b_down, ("dp", "seq"), axis=1, tiled=True),
    )
    picked_back = [jnp.take(stack, adapter_ids, axis=0) for stack in gathered_back[7:]]
    arriving_gradient = cotangent.astype(jnp.float32)
    grad_lowered = (valid_rows * arriving_gradient).astype(jnp.bfloat16)
    d_active, lower_down, upper_down = adapted_back(
        grad_lowered, active, narrow_down, gathered_back[6], picked_back[12], picked_back[13]
    )
    sigmoid_gate = jax.nn.sigmoid(gate_lin)
    d_gate = (d_active * upward * sigmoid_gate * (1.0 + gate_lin * (1.0 - sigmoid_gate))).astype(
        jnp.bfloat16
    )
    d_upward = (d_active * gate_lin * sigmoid_gate).astype(jnp.bfloat16)
    from_gate, lower_gate, upper_gate = adapted_back(
        d_gate, normed_two, narrow_gate, gathered_back[4], picked_back[8], picked_back[9]
    )
    from_up, lower_up, upper_up = adapted_back(
        d_upward, normed_two, narrow_up, gathered_back[5], picked_back[10], picked_back[11]
    )
    ffn_pull = jax.vjp(lambda operand: rms_scale(operand, ffn_gain), hidden)[1]
    d_hidden = arriving_gradient + ffn_pull(from_gate + from_up)[0]
    grad_update = (valid_rows * d_hidden).astype(jnp.bfloat16)
    d_attended, lower_out, upper_out = adapted_back(
        grad_update, attended, narrow_out, gathered_back[3], picked_back[6], picked_back[7]
    )
    d_attended_heads = (
        d_attended.astype(jnp.bfloat16)
        .reshape(seqs_here, block_len, KV, groups, HD)
        .transpose(2, 0, 3, 1, 4)
    )

    def head_backward(member):
        query_part, key_part, value_slice, d_part, log_part = member
        scores = (
            jnp.einsum("sgqd,skd->sgqk", query_part, key_part, preferred_element_type=jnp.float32)
            * scale_factor
        )
        probs_exact = jnp.where(allowed[:, None], jnp.exp(scores - log_part[..., None]), 0.0)
        weights_low = probs_exact.astype(jnp.bfloat16)
        d_probs = jnp.einsum(
            "sgqd,skd->sgqk", d_part, value_slice, preferred_element_type=jnp.float32
        )
        row_dot = jnp.sum(probs_exact * d_probs, axis=-1, keepdims=True)
        d_scores = (probs_exact * (d_probs - row_dot)).astype(jnp.bfloat16)
        query_gradient_rows = (
            jnp.einsum("sgqk,skd->sgqd", d_scores, key_part, preferred_element_type=jnp.float32)
            * scale_factor
        )
        d_key = (
            jnp.einsum("sgqk,sgqd->skd", d_scores, query_part, preferred_element_type=jnp.float32)
            * scale_factor
        )
        d_value = jnp.einsum(
            "sgqk,sgqd->skd", weights_low, d_part, preferred_element_type=jnp.float32
        )
        return (query_gradient_rows, d_key, d_value)

    dq_heads, dk_heads, dv_heads = lax.map(
        head_backward, (query_heads, key_heads, value_heads, d_attended_heads, log_totals)
    )
    d_queries = dq_heads.transpose(1, 3, 0, 2, 4).reshape(seqs_here, block_len, H, HD)
    dk_full = dk_heads.transpose(1, 2, 0, 3).reshape(seqs_here, full_length, KV * HD)
    dv_full = dv_heads.transpose(1, 2, 0, 3).reshape(seqs_here, full_length, KV * HD)
    dk_here, dv_here = (
        lax.psum_scatter(
            dk_full.astype(jnp.bfloat16), "seq", scatter_dimension=1, tiled=True
        ).astype(jnp.float32),
        lax.psum_scatter(
            dv_full.astype(jnp.bfloat16), "seq", scatter_dimension=1, tiled=True
        ).astype(jnp.float32),
    )
    query_pull = jax.vjp(
        lambda operand: prepare(operand, query_gain, cosine_table, sine_table, H), query_lin
    )[1]
    key_pull = jax.vjp(
        lambda operand: prepare(operand, key_gain, cosine_table, sine_table, KV), key_lin
    )[1]
    d_query_lin = query_pull(d_queries)[0].astype(jnp.bfloat16)
    d_key_lin = key_pull(dk_here.reshape(seqs_here, block_len, KV, HD))[0].astype(jnp.bfloat16)
    d_value_lin = dv_here.astype(jnp.bfloat16)
    from_query, lower_query, upper_query = adapted_back(
        d_query_lin, normed_one, narrow_query, gathered_back[0], picked_back[0], picked_back[1]
    )
    from_key, lower_key, upper_key = adapted_back(
        d_key_lin, normed_one, narrow_key, gathered_back[1], picked_back[2], picked_back[3]
    )
    from_value, lower_value, upper_value = adapted_back(
        d_value_lin, normed_one, narrow_value, gathered_back[2], picked_back[4], picked_back[5]
    )
    attn_pull = jax.vjp(lambda operand: rms_scale(operand, attn_gain), inputs)[1]
    d_inputs = d_hidden + attn_pull(from_query + from_key + from_value)[0]
    one_hot = (adapter_ids[:, None] == jnp.arange(ADAPT)[None, :]).astype(jnp.float32)
    per_sequence = (
        lower_query,
        upper_query,
        lower_key,
        upper_key,
        lower_value,
        upper_value,
        lower_out,
        upper_out,
        lower_gate,
        upper_gate,
        lower_up,
        upper_up,
        lower_down,
        upper_down,
    )
    spread = [jnp.einsum("sa,sir->air", one_hot, member) for member in per_sequence]
    summed = (
        lax.psum_scatter(spread[0], ("dp", "seq"), scatter_dimension=1, tiled=True),
        lax.psum_scatter(spread[1], ("dp", "seq"), scatter_dimension=1, tiled=True),
        lax.psum_scatter(spread[2], ("dp", "seq"), scatter_dimension=1, tiled=True),
        lax.psum_scatter(spread[3], ("dp", "seq"), scatter_dimension=1, tiled=True),
        lax.psum_scatter(spread[4], ("dp", "seq"), scatter_dimension=1, tiled=True),
        lax.psum_scatter(spread[5], ("dp", "seq"), scatter_dimension=1, tiled=True),
        lax.psum_scatter(spread[6], ("dp", "seq"), scatter_dimension=1, tiled=True),
        lax.psum_scatter(spread[7], ("dp", "seq"), scatter_dimension=1, tiled=True),
        lax.psum_scatter(spread[8], ("dp", "seq"), scatter_dimension=1, tiled=True),
        lax.psum_scatter(spread[9], ("dp", "seq"), scatter_dimension=1, tiled=True),
        lax.psum_scatter(spread[10], ("dp", "seq"), scatter_dimension=1, tiled=True),
        lax.psum_scatter(spread[11], ("dp", "seq"), scatter_dimension=1, tiled=True),
        lax.psum_scatter(spread[12], ("dp", "seq"), scatter_dimension=1, tiled=True),
        lax.psum_scatter(spread[13], ("dp", "seq"), scatter_dimension=1, tiled=True),
    )
    return (
        output,
        d_inputs.astype(jnp.bfloat16),
        summed[0],
        summed[1],
        summed[2],
        summed[3],
        summed[4],
        summed[5],
        summed[6],
        summed[7],
        summed[8],
        summed[9],
        summed[10],
        summed[11],
        summed[12],
        summed[13],
    )


def solution(mesh):
    in_specs = (
        P("dp", "seq", None),
        P("dp", "seq", None),
        P("dp"),
        P("dp"),
        P(),
        P(),
        P(),
        P(),
        P(("dp", "seq"), None),
        P(("dp", "seq"), None),
        P(("dp", "seq"), None),
        P(("dp", "seq"), None),
        P(("dp", "seq"), None),
        P(("dp", "seq"), None),
        P(("dp", "seq"), None),
        P(None, ("dp", "seq"), None),
        P(None, ("dp", "seq"), None),
        P(None, ("dp", "seq"), None),
        P(None, ("dp", "seq"), None),
        P(None, ("dp", "seq"), None),
        P(None, ("dp", "seq"), None),
        P(None, ("dp", "seq"), None),
        P(None, ("dp", "seq"), None),
        P(None, ("dp", "seq"), None),
        P(None, ("dp", "seq"), None),
        P(None, ("dp", "seq"), None),
        P(None, ("dp", "seq"), None),
        P(None, ("dp", "seq"), None),
        P(None, ("dp", "seq"), None),
    )
    out_specs = (
        P("dp", "seq", None),
        P("dp", "seq", None),
        P(None, ("dp", "seq"), None),
        P(None, ("dp", "seq"), None),
        P(None, ("dp", "seq"), None),
        P(None, ("dp", "seq"), None),
        P(None, ("dp", "seq"), None),
        P(None, ("dp", "seq"), None),
        P(None, ("dp", "seq"), None),
        P(None, ("dp", "seq"), None),
        P(None, ("dp", "seq"), None),
        P(None, ("dp", "seq"), None),
        P(None, ("dp", "seq"), None),
        P(None, ("dp", "seq"), None),
        P(None, ("dp", "seq"), None),
        P(None, ("dp", "seq"), None),
    )
    return jax.shard_map(shards, mesh=mesh, in_specs=in_specs, out_specs=out_specs, check_vma=False)
```

profile of v0, /device:TPU:0, one launch (start us, length us, event | category | flops | bytes accessed | tf_op | source)
XLA Modules:
  0.0 3411.3 jit_solution(9352623528415871844)
XLA Ops:
  10.3 64.9 %all_gather.98 = bf16[8,2048,16]{2,0,1:T(8,128)(2,1)S(1)} all-gather(bf16[8,64,16]{2,0,1:T(8,128)(2,1)S(1)} %copy.99), channel_id=1, replica_groups=mesh['dp'=8,'seq'=4] {'dp','seq'}, dimensions={1}, use_global_device_ids=true | all-gather | bytes 540672 | tf_op jit(solution)/shard_map/all_gather | solution.py:113
  76.8 40.2 %all_gather.99 = bf16[8,512,16]{2,1,0:T(8,128)(2,1)S(1)} all-gather(bf16[8,16,16]{2,1,0:T(8,128)(2,1)S(1)} %copy-done.71), channel_id=1, replica_groups=mesh['dp'=8,'seq'=4] {'dp','seq'}, dimensions={1}, use_global_device_ids=true | all-gather | bytes 135168 | tf_op jit(solution)/shard_map/all_gather | solution.py:114
  123.9 70.1 %all_gather.94 = bf16[8,2048,16]{2,0,1:T(8,128)(2,1)S(1)} all-gather(bf16[8,64,16]{2,0,1:T(8,128)(2,1)S(1)} %copy.95), channel_id=1, replica_groups=mesh['dp'=8,'seq'=4] {'dp','seq'}, dimensions={1}, use_global_device_ids=true | all-gather | bytes 540672 | tf_op jit(solution)/shard_map/all_gather | solution.py:111
  195.6 45.1 %all_gather.95 = bf16[8,512,16]{2,1,0:T(8,128)(2,1)S(1)} all-gather(bf16[8,16,16]{2,1,0:T(8,128)(2,1)S(1)} %copy-done.73), channel_id=1, replica_groups=mesh['dp'=8,'seq'=4] {'dp','seq'}, dimensions={1}, use_global_device_ids=true | all-gather | bytes 135168 | tf_op jit(solution)/shard_map/all_gather | solution.py:112
  253.0 64.8 %all_gather.91 = bf16[8,2048,16]{2,0,1:T(8,128)(2,1)S(1)} all-gather(bf16[8,64,16]{2,0,1:T(8,128)(2,1)S(1)} %copy.88), channel_id=1, replica_groups=mesh['dp'=8,'seq'=4] {'dp','seq'}, dimensions={1}, use_global_device_ids=true | all-gather | bytes 540672 | tf_op jit(solution)/shard_map/all_gather | solution.py:109
  320.0 74.6 %all_gather.92 = bf16[8,2048,16]{2,0,1:T(8,128)(2,1)S(1)} all-gather(bf16[8,64,16]{2,0,1:T(8,128)(2,1)S(1)} %copy.90), channel_id=1, replica_groups=mesh['dp'=8,'seq'=4] {'dp','seq'}, dimensions={1}, use_global_device_ids=true | all-gather | bytes 540672 | tf_op jit(solution)/shard_map/all_gather | solution.py:110
  397.0 82.7 %all_gather.102 = bf16[8,2048,16]{2,0,1:T(8,128)(2,1)S(1)} all-gather(bf16[8,64,16]{2,0,1:T(8,128)(2,1)S(1)} %copy.103), channel_id=1, replica_groups=mesh['dp'=8,'seq'=4] {'dp','seq'}, dimensions={1}, use_global_device_ids=true | all-gather | bytes 540672 | tf_op jit(solution)/shard_map/all_gather | solution.py:115
  481.4 90.8 %all_gather.103 = bf16[8,2048,16]{2,0,1:T(8,128)(2,1)S(1)} all-gather(bf16[8,64,16]{2,0,1:T(8,128)(2,1)S(1)} %copy.105), channel_id=1, replica_groups=mesh['dp'=8,'seq'=4] {'dp','seq'}, dimensions={1}, use_global_device_ids=true | all-gather | bytes 540672 | tf_op jit(solution)/shard_map/all_gather | solution.py:116
  575.3 85.1 %all_gather.108 = bf16[8,2048,16]{2,0,1:T(8,128)(2,1)S(1)} all-gather(bf16[8,64,16]{2,0,1:T(8,128)(2,1)S(1)} %copy.109), channel_id=1, replica_groups=mesh['dp'=8,'seq'=4] {'dp','seq'}, dimensions={1}, use_global_device_ids=true | all-gather | bytes 540672 | tf_op jit(solution)/shard_map/all_gather | solution.py:119
  662.2 88.5 %all_gather.105 = bf16[8,2048,16]{2,0,1:T(8,128)(2,1)S(1)} all-gather(bf16[8,64,16]{2,0,1:T(8,128)(2,1)S(1)} %copy.107), channel_id=1, replica_groups=mesh['dp'=8,'seq'=4] {'dp','seq'}, dimensions={1}, use_global_device_ids=true | all-gather | bytes 540672 | tf_op jit(solution)/shard_map/all_gather | solution.py:117
  753.2 84.5 %all_gather.112 = bf16[8,2048,16]{2,0,1:T(8,128)(2,1)S(1)} all-gather(bf16[8,64,16]{2,0,1:T(8,128)(2,1)S(1)} %copy.111), channel_id=1, replica_groups=mesh['dp'=8,'seq'=4] {'dp','seq'}, dimensions={1}, use_global_device_ids=true | all-gather | bytes 540672 | tf_op jit(solution)/shard_map/all_gather | solution.py:122
  847.7 5.7 fusion.200
  860.0 51.4 %while.33 = (s32[]{:T(128)}, bf16[8,1,4,256,64]{3,4,2,1,0:T(8,128)(2,1)S(1)}, f32[8,1,4,256]{3,2,1,0:T(4,128)}, bf16[8,1,4,256,64]{3,4,2,1,0:T(8,128)(2,1)S(1)},...) while((s32[]{:T(128)}, ...), condition=%wide.region_6.9_spmd.clone.clone, body=%wide.region_3.0_spmd.clone.sunk.clone | while | flops 281541632 | bytes 14324309 | solution.py:173
  912.8 5.7 fusion.201
  920.3 25.9 fusion.203
  946.2 17.3 fusion.202
  966.2 8.1 convolution_add_fusion.1
  974.3 50.2 %all-gather.26.cloned.1.call-done = bf16[8,8192,16]{1,2,0:T(8,128)(2,1)} async-done(((bf16[8,256,16]{1,2,0:T(8,128)(2,1)}), bf16[8,8192,16]{1,2,0:T(8,128)(2,1)}) %all-gather.26.cloned.1.call-update) | async-done | bytes 2097168 | tf_op jit(solution)/shard_map/all_gather | solution.py:118
  1024.5 8.0 convolution_add_fusion.2
  1032.5 188.6 %all-gather.32.cloned.1.call-done = bf16[8192,2048]{1,0:T(8,128)(2,1)} async-done(((bf16[256,2048]{1,0:T(8,128)(2,1)}), bf16[8192,2048]{1,0:T(8,128)(2,1)}) %all-gather.32.cloned.1.call-update) | async-done | bytes 33554448 | tf_op jit(solution)/shard_map/all_gather | solution.py:108
  1221.1 18.7 fusion.198
  1239.8 38.9 %all-gather.34.cloned.1.call-done = bf16[8,8192,16]{1,2,0:T(8,128)(2,1)} async-done(((bf16[8,256,16]{1,2,0:T(8,128)(2,1)}), bf16[8,8192,16]{1,2,0:T(8,128)(2,1)}) %all-gather.34.cloned.1.call-update) | async-done | bytes 2097168 | tf_op jit(solution)/shard_map/all_gather | solution.py:121
  1278.7 13.7 multiply_convert_fusion.1
  1292.4 16.8 fusion.205
  1314.6 17.2 fusion.206
  1337.9 5.8 fusion.207
  1344.7 100.8 %while.34 = (s32[]{:T(128)}, f32[8,1,4,256,64]{3,4,2,1,0:T(8,128)}, bf16[8,1,1024,64]{2,3,1,0:T(8,128)(2,1)}, bf16[8,1,1024,64]{2,3,1,0:T(8,128)(2,1)}, bf16[8,1...) while((s32[]{:T(128)}, f32[8,1,4,256,64]{3,4,2,1,0:T(8,128)}, ...), condition=%wide.region_11.15_spmd.clone.clone, body=%wide.region_9.14_spmd.clone.sunk.clone | while | flops 687471616 | bytes 34245744 | solution.py:265
  1458.5 11.0 reduce-scatter.35.cloned.1.call-done
  1472.4 24.6 reduce-scatter.37.cloned.1.call-done
  1498.4 4.4 broadcast_multiply_fusion.5
  1502.8 6.0 copy.120
  1508.7 6.5 reshape.1306
  1515.3 6.0 copy.122
  1521.3 6.5 reshape.1308
  1527.8 6.0 copy.124
  1533.8 6.5 reshape.1310
  1540.3 6.0 copy.126
  1546.3 6.5 reshape.1312
  1552.9 6.0 copy.128
  1558.8 6.5 reshape.1314
  1565.4 6.0 copy.130
  1571.4 6.4 reshape.1316
  1578.1 6.0 copy.132
  1584.1 6.5 reshape.1318
  1590.6 6.0 copy.134
  1596.7 6.5 reshape.1320
  1603.2 4.6 copy.136
  1607.8 6.5 reshape.1322
  1625.1 4.9 broadcast_multiply_fusion
  1632.2 5.8 fusion.208
  1640.2 16.7 fusion.204
  1669.0 114.3 %reduce-scatter.51.cloned.1.call-done = f32[64,128]{1,0:T(8,128)} async-done(((f32[2048,128]{1,0:T(8,128)}), f32[64,128]{1,0:T(8,128)}) %reduce-scatter.51.cloned.1.call-update) | async-done | bytes 32784
  1785.0 131.2 %reduce-scatter.53.cloned.1.call-done = f32[64,128]{1,0:T(8,128)} async-done(((f32[2048,128]{1,0:T(8,128)}), f32[64,128]{1,0:T(8,128)}) %reduce-scatter.53.cloned.1.call-update) | async-done | bytes 32784
  1917.9 131.3 %reduce-scatter.55.cloned.1.call-done = f32[64,128]{1,0:T(8,128)} async-done(((f32[2048,128]{1,0:T(8,128)}), f32[64,128]{1,0:T(8,128)}) %reduce-scatter.55.cloned.1.call-update) | async-done | bytes 32784
  2050.9 131.4 %reduce-scatter.57.cloned.1.call-done = f32[64,128]{1,0:T(8,128)} async-done(((f32[2048,128]{1,0:T(8,128)}), f32[64,128]{1,0:T(8,128)}) %reduce-scatter.57.cloned.1.call-update) | async-done | bytes 32784
  2183.9 131.4 %reduce-scatter.59.cloned.1.call-done = f32[64,128]{1,0:T(8,128)} async-done(((f32[2048,128]{1,0:T(8,128)}), f32[64,128]{1,0:T(8,128)}) %reduce-scatter.59.cloned.1.call-update) | async-done | bytes 32784
  2317.0 131.5 %reduce-scatter.61.cloned.1.call-done = f32[64,128]{1,0:T(8,128)} async-done(((f32[2048,128]{1,0:T(8,128)}), f32[64,128]{1,0:T(8,128)}) %reduce-scatter.61.cloned.1.call-update) | async-done | bytes 32784
  2450.1 131.5 %reduce-scatter.63.cloned.1.call-done = f32[64,128]{1,0:T(8,128)} async-done(((f32[2048,128]{1,0:T(8,128)}), f32[64,128]{1,0:T(8,128)}) %reduce-scatter.63.cloned.1.call-update) | async-done | bytes 32784
  2583.2 131.5 %reduce-scatter.65.cloned.1.call-done = f32[64,128]{1,0:T(8,128)} async-done(((f32[2048,128]{1,0:T(8,128)}), f32[64,128]{1,0:T(8,128)}) %reduce-scatter.65.cloned.1.call-update) | async-done | bytes 32784
  2716.3 133.3 %reduce-scatter.39.cloned.1.call-done = f32[8,16,16]{2,1,0:T(8,128)} async-done(((f32[8,512,16]{2,1,0:T(8,128)}), f32[8,16,16]{2,1,0:T(8,128)}) %reduce-scatter.39.cloned.1.call-update) | async-done | bytes 8208 | tf_op jit(solution)/shard_map/reduce_scatter | solution.py:321
  2849.7 135.2 %reduce-scatter.41.cloned.1.call-done = f32[8,16,16]{2,1,0:T(8,128)} async-done(((f32[8,512,16]{2,1,0:T(8,128)}), f32[8,16,16]{2,1,0:T(8,128)}) %reduce-scatter.41.cloned.1.call-update) | async-done | bytes 8208 | tf_op jit(solution)/shard_map/reduce_scatter | solution.py:323
  2984.8 139.7 %reduce-scatter.43.cloned.1.call-done = f32[8,256,16]{1,2,0:T(8,128)} async-done(((f32[8,8192,16]{1,2,0:T(8,128)}), f32[8,256,16]{1,2,0:T(8,128)}) %reduce-scatter.43.cloned.1.call-update) | async-done | bytes 131088 | tf_op jit(solution)/shard_map/reduce_scatter | solution.py:327
  3124.5 139.6 %reduce-scatter.45.cloned.1.call-done = f32[8,256,16]{1,2,0:T(8,128)} async-done(((f32[8,8192,16]{1,2,0:T(8,128)}), f32[8,256,16]{1,2,0:T(8,128)}) %reduce-scatter.45.cloned.1.call-update) | async-done | bytes 131088 | tf_op jit(solution)/shard_map/reduce_scatter | solution.py:329
  3264.2 139.8 %reduce-scatter.47.cloned.1.call-done = f32[8,256,16]{1,2,0:T(8,128)} async-done(((f32[8,8192,16]{1,2,0:T(8,128)}), f32[8,256,16]{1,2,0:T(8,128)}) %reduce-scatter.47.cloned.1.call-update) | async-done | bytes 131088 | tf_op jit(solution)/shard_map/reduce_scatter | solution.py:330
  (499 shorter events, 281.4 us)
Async XLA Ops:
  7.2 112.6 %all-gather.20.cloned.1.call-start = ((), (), s32[]{:S(2)}) async-start(), calls=%async_computation.19 | async-start | bytes 2162688 | tf_op jit(solution)/shard_map/all_gather | solution.py:104
  7.9 234.4 %all-gather.16.cloned.1.call-start = ((), (), s32[]{:S(2)}) async-start(), calls=%async_computation.17 | async-start | bytes 2162688 | tf_op jit(solution)/shard_map/all_gather | solution.py:103
  8.7 836.8 %all-gather.36.cloned.1.call-start = ((), (), s32[]{:S(2)}) async-start(), calls=%async_computation.34 | async-start | bytes 1310720 | tf_op jit(solution)/shard_map/all_gather | solution.py:151
  75.2 41.9 %copy-start.6 = (bf16[1,256,2048]{2,1,0:T(8,128)(2,1)S(1)}, bf16[1,256,2048]{2,1,0:T(8,128)(2,1)}, u32[]{:S(2)}) copy-start(bf16[1,256,2048]{2,1,0:T(8,128)(2,1)} %param.39) | copy-start | bytes 3145732
  76.3 41.1 %copy-start.79 = (f32[2048]{0:T(1024)S(1)}, f32[2048]{0:T(1024)}, u32[]{:S(2)}) copy-start(f32[2048]{0:T(1024)} %param.43) | copy-start | bytes 24580
  76.8 40.9 %copy-start.37 = (bf16[1,2048,16]{1,2,0:T(8,128)(2,1)}, bf16[1,2048,16]{1,2,0:T(8,128)(2,1)S(1)}, u32[]{:S(2)}) copy-start(bf16[1,2048,16]{1,2,0:T(8,128)(2,1)S(1)} %copy.141) | copy-start | bytes 196612
  117.4 5.7 copy-start.89
  117.4 5.7 copy-start.87
  117.7 730.0 %copy-start.2 = (bf16[256,2048]{1,0:T(8,128)(2,1)}, bf16[256,2048]{1,0:T(8,128)(2,1)S(1)}, u32[]{:S(2)}) copy-start(bf16[256,2048]{1,0:T(8,128)(2,1)S(1)} %fusion.86) | copy-start | bytes 3145732
  123.1 724.6 %all-gather.14.cloned.1.call-start = ((), (), s32[]{:S(2)}) async-start(), calls=%async_computation.16 | async-start | bytes 8650752 | tf_op jit(solution)/shard_map/all_gather | solution.py:102
  123.7 735.3 %all-gather.18.cloned.1.call-start = ((), (), s32[]{:S(2)}) async-start(), calls=%async_computation.18 | async-start | bytes 1310720 | tf_op jit(solution)/shard_map/all_gather | solution.py:150
  195.6 49.0 %copy-start.39 = (bf16[1,2048,16]{1,2,0:T(8,128)(2,1)}, bf16[1,2048,16]{1,2,0:T(8,128)(2,1)S(1)}, u32[]{:S(2)}) copy-start(bf16[1,2048,16]{1,2,0:T(8,128)(2,1)S(1)} %copy.140) | copy-start | bytes 196612
  240.9 617.3 %copy-start.33 = (f32[256,32]{0,1:T(8,128)}, f32[256,32]{0,1:T(8,128)S(1)}, u32[]{:S(2)}) copy-start(f32[256,32]{0,1:T(8,128)S(1)} %get-tuple-element.305) | copy-start | bytes 98308
  240.9 617.3 %copy-start.35 = (f32[256,32]{0,1:T(8,128)}, f32[256,32]{0,1:T(8,128)S(1)}, u32[]{:S(2)}) copy-start(f32[256,32]{0,1:T(8,128)S(1)} %get-tuple-element.306) | copy-start | bytes 98308
  247.0 664.8 %all-gather.22.cloned.1.call-start = ((), (), s32[]{:S(2)}) async-start(), calls=%async_computation.20 | async-start | bytes 8650752 | tf_op jit(solution)/shard_map/all_gather | solution.py:105
  247.5 5.3 copy-start.74
  247.5 672.8 %all-gather.28.cloned.1.call-start = ((), (), s32[]{:S(2)}) async-start(), calls=%async_computation.23 | async-start | bytes 34603008 | tf_op jit(solution)/shard_map/all_gather | solution.py:107
  248.3 697.9 %all-gather.24.cloned.1.call-start = ((), (), s32[]{:S(2)}) async-start(), calls=%async_computation.21 | async-start | bytes 34603008 | tf_op jit(solution)/shard_map/all_gather | solution.py:106
  249.1 717.1 %all-gather.30.cloned.1.call-start = ((), (), s32[]{:S(2)}) async-start(), calls=%async_computation.24 | async-start | bytes 2162688 | tf_op jit(solution)/shard_map/all_gather | solution.py:120
  249.8 774.7 %all-gather.26.cloned.1.call-start = ((), (), s32[]{:S(2)}) async-start(), calls=%async_computation.22 | async-start | bytes 2162688 | tf_op jit(solution)/shard_map/all_gather | solution.py:118
  250.4 970.7 %all-gather.32.cloned.1.call-start = ((), (), s32[]{:S(2)}) async-start(), calls=%async_computation.25 | async-start | bytes 34603008 | tf_op jit(solution)/shard_map/all_gather | solution.py:108
  251.1 1027.6 %all-gather.34.cloned.1.call-start = ((), (), s32[]{:S(2)}) async-start(), calls=%async_computation.26 | async-start | bytes 2162688 | tf_op jit(solution)/shard_map/all_gather | solution.py:121
  251.7 1217.8 %reduce-scatter.35.cloned.1.call-start = ((), (), s32[]{:S(2)}) async-start(), calls=%async_computation.27 | async-start | bytes 1310720 | tf_op jit(solution)/shard_map/reduce_scatter | solution.py:272
  319.4 75.1 %copy-start.41 = (bf16[1,2048,16]{1,2,0:T(8,128)(2,1)}, bf16[1,2048,16]{1,2,0:T(8,128)(2,1)S(1)}, u32[]{:S(2)}) copy-start(bf16[1,2048,16]{1,2,0:T(8,128)(2,1)S(1)} %copy.138) | copy-start | bytes 196612
  319.8 533.6 %copy-start.56 = (bf16[256,16]{0,1:T(8,128)(2,1)}, bf16[256,16]{0,1:T(8,128)(2,1)S(1)}, u32[]{:S(2)}) copy-start(bf16[256,16]{0,1:T(8,128)(2,1)S(1)} %convolution_convert_fusion.8) | copy-start | bytes 24580
  396.1 457.3 %copy-start.43 = (bf16[1,2048,16]{1,2,0:T(8,128)(2,1)}, bf16[1,2048,16]{1,2,0:T(8,128)(2,1)S(1)}, u32[]{:S(2)}) copy-start(bf16[1,2048,16]{1,2,0:T(8,128)(2,1)S(1)} %copy.139) | copy-start | bytes 196612
  837.8 5.8 copy-start.17
  911.7 6.8 copy-start.58
  911.7 6.8 copy-start.81
  919.2 417.0 %copy-start = (f32[1,256,2048]{2,1,0:T(8,128)}, f32[1,256,2048]{2,1,0:T(8,128)S(1)}, u32[]{:S(2)}) copy-start(f32[1,256,2048]{2,1,0:T(8,128)S(1)} %get-tuple-element.322) | copy-start | bytes 6291460
  919.3 417.0 %copy-start.83 = (f32[256]{0:T(256)}, f32[256]{0:T(256)S(1)}, u32[]{:S(2)}) copy-start(f32[256]{0:T(256)S(1)} %fusion.166) | copy-start | bytes 3076
  919.9 46.3 %copy-start.52 = (bf16[256,16]{0,1:T(8,128)(2,1)}, bf16[256,16]{0,1:T(8,128)(2,1)S(1)}, u32[]{:S(2)}) copy-start(bf16[256,16]{0,1:T(8,128)(2,1)S(1)} %convolution_convert_fusion.4) | copy-start | bytes 24580
  920.3 104.2 %copy-start.54 = (bf16[256,16]{0,1:T(8,128)(2,1)}, bf16[256,16]{0,1:T(8,128)(2,1)S(1)}, u32[]{:S(2)}) copy-start(bf16[256,16]{0,1:T(8,128)(2,1)S(1)} %convolution_convert_fusion.5) | copy-start | bytes 24580
  1032.5 246.2 %copy-start.91 = (bf16[256,16]{0,1:T(8,128)(2,1)S(1)}, bf16[256,16]{0,1:T(8,128)(2,1)}, u32[]{:S(2)}) copy-start(bf16[256,16]{0,1:T(8,128)(2,1)} %convolution_convert_fusion.3) | copy-start | bytes 24580
  1337.5 6.2 copy-start.20
  1337.9 5.8 copy-start.60
  1344.7 100.9 %copy-start.34 = (f32[256,32]{0,1:T(8,128)S(1)}, f32[256,32]{0,1:T(8,128)}, u32[]{:S(2)}) copy-start(f32[256,32]{0,1:T(8,128)} %copy-done.33) | copy-start | bytes 98308
  1344.7 100.9 %copy-start.36 = (f32[256,32]{0,1:T(8,128)S(1)}, f32[256,32]{0,1:T(8,128)}, u32[]{:S(2)}) copy-start(f32[256,32]{0,1:T(8,128)} %copy-done.35) | copy-start | bytes 98308
  1445.6 51.4 %reduce-scatter.37.cloned.1.call-start = ((), (), s32[]{:S(2)}) async-start(), calls=%async_computation.28 | async-start | bytes 1310720 | tf_op jit(solution)/shard_map/reduce_scatter | solution.py:275
  1452.7 214.6 %reduce-scatter.49.cloned.1.call-start = ((), (), s32[]{:S(2)}) async-start(), calls=%async_computation.35 | async-start | bytes 1081344
  1457.4 13.2 copy-start.16
  1457.4 13.2 copy-start.94
  1457.4 13.3 copy-start.69
  1457.4 13.3 copy-start.63
  1470.8 27.6 copy-start.97
  1471.0 27.4 copy-start.45
  1471.0 27.4 copy-start.46
  1515.2 268.1 %reduce-scatter.51.cloned.1.call-start = ((), (), s32[]{:S(2)}) async-start(), calls=%async_computation.36 | async-start | bytes 1081344
  1527.7 388.5 %reduce-scatter.53.cloned.1.call-start = ((), (), s32[]{:S(2)}) async-start(), calls=%async_computation.37 | async-start | bytes 1081344
  1540.3 509.0 %reduce-scatter.55.cloned.1.call-start = ((), (), s32[]{:S(2)}) async-start(), calls=%async_computation.38 | async-start | bytes 1081344
  1552.8 629.5 %reduce-scatter.57.cloned.1.call-start = ((), (), s32[]{:S(2)}) async-start(), calls=%async_computation.39 | async-start | bytes 1081344
  1565.3 750.0 %reduce-scatter.59.cloned.1.call-start = ((), (), s32[]{:S(2)}) async-start(), calls=%async_computation.40 | async-start | bytes 1081344
  1577.9 870.6 %reduce-scatter.61.cloned.1.call-start = ((), (), s32[]{:S(2)}) async-start(), calls=%async_computation.41 | async-start | bytes 1081344
  1590.6 991.0 %reduce-scatter.63.cloned.1.call-start = ((), (), s32[]{:S(2)}) async-start(), calls=%async_computation.42 | async-start | bytes 1081344
  1603.1 1111.5 %reduce-scatter.65.cloned.1.call-start = ((), (), s32[]{:S(2)}) async-start(), calls=%async_computation.43 | async-start | bytes 1081344
  1607.8 6.6 copy-start.55
  1614.4 1235.3 %reduce-scatter.39.cloned.1.call-start = ((), (), s32[]{:S(2)}) async-start(), calls=%async_computation.29 | async-start | bytes 2162688 | tf_op jit(solution)/shard_map/reduce_scatter | solution.py:321
  1620.3 1364.6 %reduce-scatter.41.cloned.1.call-start = ((), (), s32[]{:S(2)}) async-start(), calls=%async_computation.30 | async-start | bytes 2162688 | tf_op jit(solution)/shard_map/reduce_scatter | solution.py:323
  1625.1 1499.5 %reduce-scatter.43.cloned.1.call-start = ((), (), s32[]{:S(2)}) async-start(), calls=%async_computation.31 | async-start | bytes 4325376 | tf_op jit(solution)/shard_map/reduce_scatter | solution.py:327
  1630.1 1634.1 %reduce-scatter.45.cloned.1.call-start = ((), (), s32[]{:S(2)}) async-start(), calls=%async_computation.32 | async-start | bytes 4325376 | tf_op jit(solution)/shard_map/reduce_scatter | solution.py:329
  1630.7 1773.3 %reduce-scatter.47.cloned.1.call-start = ((), (), s32[]{:S(2)}) async-start(), calls=%async_computation.33 | async-start | bytes 4325376 | tf_op jit(solution)/shard_map/reduce_scatter | solution.py:330
  1632.2 5.8 copy-start.42
  1640.2 16.7 copy-start.1
  1640.2 16.7 copy-start.51
  (62 other events, 112.5 us)
Sparse Core Ops, SparseCore 0:
  10.9 64.8 all-gather.19
  78.6 58.5 all-gather.15
  138.8 21.6 all-gather.35
  163.2 87.9 all-gather.13
  252.5 20.9 all-gather.17
  276.3 101.9 all-gather.21
  381.1 279.2 all-gather.27
  663.3 244.4 all-gather.23
  910.7 55.4 all-gather.29
  968.9 55.5 all-gather.25
  1027.4 193.6 all-gather.31
  1223.8 54.8 all-gather.33
  1445.7 23.7 reduce-scatter.34
  1472.1 24.8 reduce-scatter.36
  1515.3 134.8 reduce-scatter.48
  1652.4 130.8 reduce-scatter.50
  1785.4 130.7 reduce-scatter.52
  1918.4 130.7 reduce-scatter.54
  2051.5 130.7 reduce-scatter.56
  2184.5 130.7 reduce-scatter.58
  2317.6 130.8 reduce-scatter.60
  2450.8 130.7 reduce-scatter.62
  2583.8 130.8 reduce-scatter.64
  2717.5 132.1 reduce-scatter.38
  2852.5 132.2 reduce-scatter.40
  2987.6 136.8 reduce-scatter.42
  3127.3 136.8 reduce-scatter.44
  3267.1 136.8 reduce-scatter.46
where the time goes:
time: 3420 us; the launch traced here: 3410 us
  waiting for transfers between devices  2050 us (60%)
  blocking collectives  791 us (23%)
  matrix products  330 us (10%)
  local copies, waits for them, and re-layouts  171 us (5%)
  other arithmetic  53.4 us (2%)
    unnamed x37, waiting for transfers between devices  1040 us
    all_gather x1, waiting for transfers between devices, shards(): lax.all_gather(w_down, ('dp', 'seq'), axis=0, tiled=True)  189 us
    unnamed x250, local copies, waits for them, and re-layouts  150 us
    reduce_scatter x1, waiting for transfers between devices, shards(): lax.psum_scatter(spread[12], ('dp', 'seq'), scatter_dimension=1, tiled=True)  140 us
    reduce_scatter x1, waiting for transfers between devices, shards(): lax.psum_scatter(spread[9], ('dp', 'seq'), scatter_dimension=1, tiled=True)  140 us
    reduce_scatter x1, waiting for transfers between devices, shards(): lax.psum_scatter(spread[11], ('dp', 'seq'), scatter_dimension=1, tiled=True)  140 us
    reduce_scatter x1, waiting for transfers between devices, shards(): lax.psum_scatter(spread[5], ('dp', 'seq'), scatter_dimension=1, tiled=True)  135 us
    reduce_scatter x1, waiting for transfers between devices, shards(): lax.psum_scatter(spread[3], ('dp', 'seq'), scatter_dimension=1, tiled=True)  133 us
  transfers between devices with their start and end apart: 28, of which 19 were waited for; matrix products, arithmetic and copies ran while one was open for 10% of the time, Pallas kernels for 0%

commit v1 on v0

v1 whole, which is shorter than its diff:
```python
import functools

import jax
import jax.numpy as jnp
import numpy as np
from jax import lax
from jax.experimental import pallas as pl
from jax.experimental.pallas import tpu as pltpu
from jax.sharding import PartitionSpec as P

H = 32
KV = 8
HD = 64
GROUP = H // KV
ADAPT = 8
RANK = 16
EPS = 1e-05
F32 = jnp.float32
BF16 = jnp.bfloat16


def contract(left, right, left_dim, right_dim):
    return lax.dot_general(
        left, right, (((left_dim,), (right_dim,)), ((), ())), preferred_element_type=F32
    )


def rms_scale(operand, scaling, axis=-1):
    mean = jnp.mean(operand * operand, axis=axis, keepdims=True)
    return operand * lax.rsqrt(mean + EPS) * scaling


def rotary_tables(positions):
    frequency = jnp.power(1000000.0, -jnp.arange(HD // 2, dtype=F32) * 2.0 / HD)
    angles = frequency[:, None] * positions.astype(F32)[None, :]
    return jnp.cos(angles), jnp.sin(angles)


def prepare(linear, scaling, cosine, sine):
    normed = rms_scale(linear, scaling[:, None], axis=1)
    front, second = normed[:, : HD // 2], normed[:, HD // 2 :]
    return jnp.concatenate(
        [front * cosine - second * sine, second * cosine + front * sine], axis=1
    )


def ring_order(size):
    return list(range(0, size, 2)) + list(range(1, size, 2))[::-1]


def ring_pairs(size):
    order = ring_order(size)
    right = [(order[i], order[(i + 1) % size]) for i in range(size)]
    return right, [(b, a) for a, b in right]


def ring_pieces(own):
    size = lax.axis_size("dp")
    right, left = ring_pairs(size)
    pieces = [(0, own)]
    from_left = from_right = own
    for step in range(1, (size - 1) // 2 + 1):
        from_left = lax.ppermute(from_left, "dp", right)
        from_right = lax.ppermute(from_right, "dp", left)
        pieces += [(-step, from_left), (step, from_right)]
    half = own.shape[0] // 2
    top = lax.ppermute(from_left[:half], "dp", right)
    bottom = lax.ppermute(from_right[half:], "dp", left)
    return pieces, (size // 2, top, bottom)


def ring_source(offset):
    size = lax.axis_size("dp")
    order = ring_order(size)
    place = np.argsort(np.array(order))
    here = jnp.asarray(place)[lax.axis_index("dp")]
    return jnp.asarray(np.array(order))[(here + offset) % size]


def ring_gather(own):
    pieces, (far, top, bottom) = ring_pieces(own)
    whole = jnp.zeros((lax.axis_size("dp"),) + own.shape, own.dtype)
    for offset, piece in pieces:
        whole = lax.dynamic_update_slice(whole, piece[None], (ring_source(offset), 0, 0))
    whole = lax.dynamic_update_slice(whole, top[None], (ring_source(far), 0, 0))
    return lax.dynamic_update_slice(whole, bottom[None], (ring_source(far), top.shape[0], 0))


def partner(operand, bit):
    size = lax.axis_size("seq")
    return lax.ppermute(operand, "seq", [(i, i ^ bit) for i in range(size)])


def everywhere_gather(own):
    pieces, (far, top, bottom) = ring_pieces(own)
    pieces = pieces + [(far, jnp.concatenate([top, bottom], axis=0))]
    rows = []
    for _, piece in pieces:
        across = partner(piece, 2)
        rows += [piece, partner(piece, 1), across, partner(across, 1)]
    return jnp.concatenate(rows, axis=0)


def everywhere_order():
    size = lax.axis_size("dp")
    seq = lax.axis_index("seq")
    offsets = [0]
    for step in range(1, (size - 1) // 2 + 1):
        offsets += [-step, step]
    offsets += [size // 2]
    blocks = [ring_source(o) * lax.axis_size("seq") + (seq ^ j) for o in offsets for j in range(4)]
    return jnp.stack(blocks)


def seq_gather(own):
    seq = lax.axis_index("seq")
    side = partner(own, 1)
    across = partner(own, 2)
    corner = partner(across, 1)
    whole = jnp.zeros((lax.axis_size("seq"),) + own.shape, own.dtype)
    rest = (0,) * own.ndim
    for bit, piece in enumerate((own, side, across, corner)):
        whole = lax.dynamic_update_slice(whole, piece[None], (seq ^ bit,) + rest)
    return whole


def seq_exchange(slots):
    seq = lax.axis_index("seq")
    pick = lambda bit: lax.dynamic_index_in_dim(slots, seq ^ bit, 0, keepdims=False)
    got = [pick(0)] + [partner(pick(bit), bit) for bit in (1, 2, 3)]
    whole = jnp.zeros(slots.shape, slots.dtype)
    rest = (0,) * (slots.ndim - 1)
    for bit, piece in enumerate(got):
        whole = lax.dynamic_update_slice(whole, piece[None], (seq ^ bit,) + rest)
    return whole


def seq_reduce(partial, wire=BF16):
    seq = lax.axis_index("seq")
    x, core = seq // 2, seq % 2
    pairs = partial.reshape((2, 2) + partial.shape[1:])
    column = lambda c: lax.dynamic_index_in_dim(pairs, c, 1, keepdims=False)
    arrived = partner(column(1 - core).astype(wire), 1)
    both = column(core).astype(F32) + arrived.astype(F32)
    row = lambda r: lax.dynamic_index_in_dim(both, r, 0, keepdims=False)
    return row(x) + partner(row(1 - x).astype(wire), 2).astype(F32)


def attend_kernel(limit_ref, q_ref, k_ref, v_ref, o_ref, e_ref, r_ref):
    blocks, _, _, block = k_ref.shape
    heads = [q_ref[h * HD : (h + 1) * HD] for h in range(GROUP)]
    queries = jnp.concatenate(heads, axis=1)
    limit = limit_ref[...]
    total = jnp.zeros(limit.shape, F32)
    mixed = jnp.zeros(queries.shape, F32)
    for j in range(blocks):
        scores = contract(k_ref[j, 0], queries, 0, 0)
        places = j * block + lax.broadcasted_iota(jnp.int32, scores.shape, 0)
        raised = jnp.where(places <= limit, jnp.exp(scores), 0.0)
        total = total + jnp.sum(raised, axis=0, keepdims=True)
        low = raised.astype(BF16)
        e_ref[0, j] = low
        mixed = mixed + contract(v_ref[j, 0], low, 1, 0)
    inverse = 1.0 / total
    r_ref[0] = inverse
    mixed = (mixed * inverse).astype(BF16)
    width = q_ref.shape[1]
    for h in range(GROUP):
        o_ref[h * HD : (h + 1) * HD] = mixed[:, h * width : (h + 1) * width]


def attend_back_kernel(
    q_ref, k_ref, v_ref, e_ref, r_ref, o_ref, do_ref, dq_ref, dk_ref, dv_ref
):
    blocks = k_ref.shape[0]
    width = q_ref.shape[1]

    def wide(ref):
        return jnp.concatenate([ref[h * HD : (h + 1) * HD] for h in range(GROUP)], axis=1)

    queries = wide(q_ref)
    grads = wide(do_ref).astype(F32) * r_ref[0]
    dots = jnp.sum(grads * wide(o_ref).astype(F32), axis=0, keepdims=True)
    grads = grads.astype(BF16)
    d_queries = jnp.zeros(queries.shape, F32)
    for j in range(blocks):
        raised = e_ref[0, j]
        d_probs = contract(v_ref[j, 0], grads, 0, 0)
        d_scores = (raised.astype(F32) * (d_probs - dots)).astype(BF16)
        d_queries = d_queries + contract(k_ref[j, 0], d_scores, 1, 0)
        dk_ref[j] = contract(queries, d_scores, 1, 1).astype(BF16)
        dv_ref[j] = contract(grads, raised, 1, 1).astype(BF16)
    for h in range(GROUP):
        dq_ref[h * HD : (h + 1) * HD] = d_queries[:, h * width : (h + 1) * width]


def attend(limit, queries, keys_values):
    blocks, _, _, block = keys_values.shape
    width = queries.shape[1]
    wide = GROUP * width
    head_rows = pl.BlockSpec((GROUP * HD, width), lambda g: (g, 0))
    return pl.pallas_call(
        attend_kernel,
        grid=(KV,),
        in_specs=[
            pl.BlockSpec((1, wide), lambda g: (0, 0)),
            head_rows,
            pl.BlockSpec((blocks, 1, HD, block), lambda g: (0, 0, g, 0)),
            pl.BlockSpec((blocks, 1, HD, block), lambda g: (0, 1, g, 0)),
        ],
        out_specs=[
            head_rows,
            pl.BlockSpec((1, blocks, block, wide), lambda g: (g, 0, 0, 0)),
            pl.BlockSpec((1, 1, wide), lambda g: (g, 0, 0)),
        ],
        out_shape=[
            jax.ShapeDtypeStruct(queries.shape, BF16),
            jax.ShapeDtypeStruct((KV, blocks, block, wide), BF16),
            jax.ShapeDtypeStruct((KV, 1, wide), F32),
        ],
        compiler_params=pltpu.CompilerParams(vmem_limit_bytes=40 * 2**20),
        cost_estimate=pl.CostEstimate(
            flops=16 * H * width * blocks * block * HD,
            bytes_accessed=2 * KV * blocks * block * wide,
            transcendentals=H * width * blocks * block,
        ),
        name="attend",
    )(limit, queries, keys_values, keys_values)


def attend_back(queries, keys_values, raised, inverse, mixed, d_mixed):
    blocks, _, features, block = keys_values.shape
    width = queries.shape[1]
    wide = GROUP * width
    head_rows = pl.BlockSpec((GROUP * HD, width), lambda g: (g, 0))
    key_rows = pl.BlockSpec((blocks, HD, block), lambda g: (0, g, 0))
    return pl.pallas_call(
        attend_back_kernel,
        grid=(KV,),
        in_specs=[
            head_rows,
            pl.BlockSpec((blocks, 1, HD, block), lambda g: (0, 0, g, 0)),
            pl.BlockSpec((blocks, 1, HD, block), lambda g: (0, 1, g, 0)),
            pl.BlockSpec((1, blocks, block, wide), lambda g: (g, 0, 0, 0)),
            pl.BlockSpec((1, 1, wide), lambda g: (g, 0, 0)),
            head_rows,
            head_rows,
        ],
        out_specs=[head_rows, key_rows, key_rows],
        out_shape=[
            jax.ShapeDtypeStruct(queries.shape, F32),
            jax.ShapeDtypeStruct((blocks, features, block), BF16),
            jax.ShapeDtypeStruct((blocks, features, block), BF16),
        ],
        compiler_params=pltpu.CompilerParams(vmem_limit_bytes=40 * 2**20),
        cost_estimate=pl.CostEstimate(
            flops=32 * H * width * blocks * block * HD,
            bytes_accessed=2 * KV * blocks * block * wide,
            transcendentals=0,
        ),
        name="attend_back",
    )(queries, keys_values, keys_values, raised, inverse, mixed, d_mixed)


def shards(
    tokens,
    cotangent,
    lengths,
    adapter_ids,
    attn_gain,
    query_gain,
    key_gain,
    ffn_gain,
    w_query,
    w_key,
    w_value,
    w_out,
    gate_weight,
    w_up,
    w_down,
    a_query,
    b_query,
    a_key,
    b_key,
    a_value,
    b_value,
    a_out,
    b_out,
    a_gate,
    b_gate,
    a_up,
    b_up,
    a_down,
    b_down,
):
    n_dp, n_seq = lax.axis_size("dp"), lax.axis_size("seq")
    seq = lax.axis_index("seq")
    _, block, width = tokens.shape
    length = lengths[0]
    positions = seq * block + jnp.arange(block)
    valid = (positions < length).astype(F32)[:, None]

    w_in = everywhere_gather(jnp.concatenate([w_query, w_key, w_value], axis=1))
    w_back = everywhere_gather(w_out)
    order = everywhere_order()
    back_order = jnp.argsort(order)

    def reorder(rows, by):
        return rows.reshape(by.shape[0], -1, rows.shape[-1])[by].reshape(rows.shape)

    def columns_for_seq(matrix):
        rows = matrix.shape[0]
        slots = matrix.reshape(rows, n_dp, n_seq, -1).transpose(2, 0, 1, 3)
        own = seq_exchange(slots.reshape(n_seq, rows, -1))
        return own.reshape(n_seq * rows, -1)

    w_lower = ring_gather(w_down).reshape(-1, width)
    gate_part = ring_gather(columns_for_seq(gate_weight)).reshape(width, -1)
    up_part = ring_gather(columns_for_seq(w_up)).reshape(width, -1)

    shared = (a_query, a_key, a_value, b_query, b_key, b_value, a_out, b_out, a_gate, a_up, b_down)
    own_part = (b_gate, b_up, a_down)
    stack = jnp.concatenate(shared + own_part, axis=1)
    ids = lax.all_gather(adapter_ids, "dp", tiled=True)
    sent = jnp.take(stack, ids, axis=0).transpose(0, 2, 1)
    mine = lax.all_to_all(sent, "dp", 0, 0, tiled=True)
    edges = np.cumsum([0] + [m.shape[1] for m in shared + own_part])
    cut = int(edges[len(shared)])
    spread = seq_gather(mine[..., :cut])
    whole = []
    for i, member in enumerate(shared):
        part = spread[..., edges[i] : edges[i + 1]]
        whole.append(part.transpose(2, 1, 0, 3).reshape(RANK, -1))
    for i, member in enumerate(own_part, len(shared)):
        part = mine[..., edges[i] : edges[i + 1]]
        whole.append(part.transpose(1, 0, 2).reshape(RANK, -1))
    aq, ak, av, bq, bk, bv, ao, bo, ag, au, bd, bg, bu, ad = whole
    a_in = jnp.concatenate([aq, ak, av], axis=0)
    none = lambda m: jnp.zeros_like(m)
    b_in = jnp.concatenate(
        [
            jnp.concatenate([bq, none(bk), none(bv)], axis=1),
            jnp.concatenate([none(bq), bk, none(bv)], axis=1),
            jnp.concatenate([none(bq), none(bk), bv], axis=1),
        ],
        axis=0,
    )
    a_gu = jnp.concatenate([ag, au], axis=0)

    inputs = tokens[0].astype(F32)
    normed = rms_scale(inputs, attn_gain).astype(BF16)
    normed_t = normed.T
    inner = contract(a_in, normed_t, 1, 0).astype(BF16)
    linear = contract(w_in, reorder(normed_t, order), 0, 0) + contract(b_in, inner, 0, 0)
    n_query, n_key = H * HD, KV * HD
    query_lin = linear[:n_query].reshape(H, HD, block)
    key_lin = linear[n_query : n_query + n_key].reshape(KV, HD, block)
    value_lin = linear[n_query + n_key :]
    cosine, sine = rotary_tables(positions)
    scale = HD**-0.5
    query_prep = lambda v: prepare(v, query_gain, cosine, sine)
    key_prep = lambda v: prepare(v, key_gain, cosine, sine)
    queries = (query_prep(query_lin) * scale).astype(BF16).reshape(n_query, block)
    keys = key_prep(key_lin).astype(BF16).reshape(n_key, block)
    keys_values = seq_gather(jnp.stack([keys, value_lin.astype(BF16)]))

    limit = jnp.minimum(positions, length - 1).astype(jnp.int32)
    limit = jnp.tile(limit, GROUP)[None, :]
    mixed, raised, inverse = attend(limit, queries, keys_values)

    inner_out = contract(ao, mixed, 1, 0).astype(BF16)
    update = contract(reorder(mixed, order), w_back, 0, 0) + contract(inner_out, bo, 0, 0)
    hidden = inputs + valid * update
    normed_two = rms_scale(hidden, ffn_gain).astype(BF16)

    cot = cotangent[0].astype(F32)
    n2 = seq_gather(normed_two).reshape(-1, width)
    gf = seq_gather((valid * cot).astype(BF16)).reshape(-1, width)
    inner_gu = contract(n2, a_gu, 1, 1).astype(BF16)
    gate = contract(n2, gate_part, 1, 0) + contract(inner_gu[:, :RANK], bg, 1, 0)
    up = contract(n2, up_part, 1, 0) + contract(inner_gu[:, RANK:], bu, 1, 0)
    d_inner_down = contract(gf, bd, 1, 1).astype(BF16)
    d_act = contract(gf, w_lower, 1, 1) + contract(d_inner_down, ad, 1, 0)
    sig = jax.nn.sigmoid(gate)
    act = (gate * sig * up).astype(BF16)
    d_gate = (d_act * up * sig * (1.0 + gate * (1.0 - sig))).astype(BF16)
    d_up = (d_act * gate * sig).astype(BF16)
    inner_down = contract(act, ad, 1, 1).astype(BF16)
    lowered = contract(act, w_lower, 1, 0) + contract(inner_down, bd, 1, 0)
    lowered = seq_reduce(lowered.reshape(n_seq, block, width))
    output = (hidden + valid * lowered).astype(BF16)

    d_inner_gu = jnp.concatenate(
        [contract(d_gate, bg, 1, 1), contract(d_up, bu, 1, 1)], axis=1
    ).astype(BF16)
    d_n2 = (
        contract(d_gate, gate_part, 1, 1)
        + contract(d_up, up_part, 1, 1)
        + contract(d_inner_gu, a_gu, 1, 0)
    )
    d_n2 = seq_reduce(d_n2.reshape(n_seq, block, width))
    grad_a_gu = contract(d_inner_gu, n2, 0, 0)
    grad_bg = contract(inner_gu[:, :RANK], d_gate, 0, 0)
    grad_bu = contract(inner_gu[:, RANK:], d_up, 0, 0)
    grad_bd = contract(inner_down, gf, 0, 0)
    grad_ad = contract(d_inner_down, act, 0, 0)

    d_hidden = cot + jax.vjp(lambda v: rms_scale(v, ffn_gain), hidden)[1](d_n2)[0]
    grad_update = (valid * d_hidden).astype(BF16)
    d_inner_out = contract(bo, grad_update, 1, 1).astype(BF16)
    d_mixed = reorder(contract(w_back, grad_update, 1, 1), back_order)
    d_mixed = (d_mixed + contract(ao, d_inner_out, 0, 0)).astype(BF16)
    grad_ao = contract(d_inner_out, mixed, 1, 1)
    grad_bo = contract(inner_out, grad_update, 1, 0)

    d_queries, d_keys, d_values = attend_back(
        queries, keys_values, raised, inverse, mixed, d_mixed
    )
    d_kv = seq_reduce(jnp.stack([d_keys, d_values], axis=1))
    d_query_lin = jax.vjp(query_prep, query_lin)[1](d_queries.reshape(H, HD, block) * scale)[0]
    d_key_lin = jax.vjp(key_prep, key_lin)[1](d_kv[0].reshape(KV, HD, block))[0]
    d_linear = jnp.concatenate(
        [d_query_lin.reshape(n_query, block), d_key_lin.reshape(n_key, block), d_kv[1]], axis=0
    ).astype(BF16)
    d_inner = contract(b_in, d_linear, 1, 0).astype(BF16)
    d_normed = reorder(contract(w_in, d_linear, 1, 0), back_order) + contract(a_in, d_inner, 0, 0)
    d_inputs = d_hidden + jax.vjp(lambda v: rms_scale(v, attn_gain), inputs)[1](d_normed.T)[0]
    grad_a_in = contract(d_inner, normed, 1, 0)
    grad_b_in = contract(inner, d_linear, 1, 1)

    q_end, k_end = n_query, n_query + n_key
    partial = (
        grad_a_in[:RANK],
        grad_a_in[RANK : 2 * RANK],
        grad_a_in[2 * RANK :],
        grad_b_in[:RANK, :q_end],
        grad_b_in[RANK : 2 * RANK, q_end:k_end],
        grad_b_in[2 * RANK :, k_end:],
        grad_ao,
        grad_bo,
        grad_a_gu[:RANK],
        grad_a_gu[RANK:],
        grad_bd,
    )
    partial = jnp.concatenate(
        [g.reshape(RANK, n_dp, n_seq, -1).transpose(2, 1, 0, 3) for g in partial], axis=-1
    )
    complete = [g.reshape(RANK, n_dp, -1).transpose(1, 0, 2) for g in (grad_bg, grad_bu, grad_ad)]
    gathered = jnp.concatenate([seq_reduce(partial, F32)] + complete, axis=-1)
    arrived = lax.all_to_all(gathered, "dp", 0, 0, tiled=True)
    chosen = (ids[:, None] == jnp.arange(ADAPT)[None, :]).astype(F32)
    summed = jnp.sum(chosen[:, :, None, None] * arrived[:, None], axis=0).transpose(0, 2, 1)
    parts = [summed[:, edges[i] : edges[i + 1]] for i in range(len(edges) - 1)]
    gaq, gak, gav, gbq, gbk, gbv, gao, gbo, gag, gau, gbd, gbg, gbu, gad = parts
    return (
        output[None],
        d_inputs.astype(BF16)[None],
        gaq,
        gbq,
        gak,
        gbk,
        gav,
        gbv,
        gao,
        gbo,
        gag,
        gbg,
        gau,
        gbu,
        gad,
        gbd,
    )


def solution(mesh):
    tokens = P("dp", "seq", None)
    matrix = P(("dp", "seq"), None)
    stack = P(None, ("dp", "seq"), None)
    in_specs = (tokens, tokens, P("dp"), P("dp")) + (P(),) * 4 + (matrix,) * 7 + (stack,) * 14
    out_specs = (tokens, tokens) + (stack,) * 14
    return jax.shard_map(shards, mesh=mesh, in_specs=in_specs, out_specs=out_specs, check_vma=False)
```

time: 3420 us -> 936 us (0.27)
  waiting for transfers between devices: 2050 us -> 315 us
  blocking collectives: 791 us -> 15.9 us
  matrix products: 330 us -> 173 us
  starting transfers between devices: 1.76 us -> 82.7 us
  local copies, waits for them, and re-layouts: 171 us -> 243 us
  Pallas kernels: 0 us -> 35.7 us
    unnamed x37 -> x0, waiting for transfers between devices: 1040 us -> none
    all_gather x11 -> x0, blocking collectives: 791 us -> none  [the longest x1 90.8 us: shards(): lax.all_gather(b_out, ('dp', 'seq'), axis=1, tiled=True)]
    reduce_scatter x7 -> x0, waiting for transfers between devices: 723 us -> none  [the longest x1 140 us: shards(): lax.psum_scatter(spread[12], ('dp', 'seq'), scatter_dimension=1, tiled=True)]
    ppermute x0 -> x114, waiting for transfers between devices: none -> 311 us  [the longest x74 167 us: partner(): return lax.ppermute(operand, 'seq', [(i, i ^ bit) for i in range(size)])]
    all_gather x12 -> x0, waiting for transfers between devices: 280 us -> none  [the longest x1 189 us: shards(): lax.all_gather(w_down, ('dp', 'seq'), axis=0, tiled=True)]
    dot_general x112 -> x37, matrix products: 330 us -> 173 us  [contract(): lax.dot_general(left, right, (((left_dim,), (right_dim,)), ((), ())), pre...]
    unnamed x250 -> x287, local copies, waits for them, and re-layouts: 150 us -> 72.5 us
    ppermute x0 -> x114, starting transfers between devices: none -> 74.9 us  [the longest x74 31.3 us: partner(): return lax.ppermute(operand, 'seq', [(i, i ^ bit) for i in range(size)])]
  transfers between devices with their start and end apart: 28 -> 116, of which waited for: 19 -> 41; matrix products, arithmetic and copies ran while one was open for 10% -> 33% of each run, Pallas kernels for 0% -> 2%
where the time goes in v1:
time: 936 us; the launch traced here: 925 us
  waiting for transfers between devices  315 us (34%)
  local copies, waits for them, and re-layouts  243 us (26%)
  matrix products  173 us (18%)
  starting transfers between devices  82.7 us (9%)
  Pallas kernels  35.7 us (4%)
  between operations  31.5 us (3%)
  other arithmetic  28.1 us (3%)
  blocking collectives  15.9 us (2%)
    dot_general x37, matrix products, contract(): lax.dot_general(left, right, (((left_dim,), (right_dim,)), ((), ())), pre...  173 us
    ppermute x74, waiting for transfers between devices, partner(): return lax.ppermute(operand, 'seq', [(i, i ^ bit) for i in range(size)])  167 us
    ppermute x15, waiting for transfers between devices, ring_pieces(): from_left = lax.ppermute(from_left, 'dp', right)  73.6 us
    unnamed x287, local copies, waits for them, and re-layouts  72.5 us
    ppermute x74, starting transfers between devices, partner(): return lax.ppermute(operand, 'seq', [(i, i ^ bit) for i in range(size)])  31.3 us
    ppermute x15, waiting for transfers between devices, ring_pieces(): from_right = lax.ppermute(from_right, 'dp', left)  27.6 us
    dynamic_update_slice x21, local copies, waits for them, and re-layouts, ring_gather(): lax.dynamic_update_slice(whole, piece[None], (ring_source(offset), 0, 0))  26.1 us
    ppermute x5, waiting for transfers between devices, ring_pieces(): top = lax.ppermute(from_left[:half], 'dp', right)  22.4 us
  transfers between devices with their start and end apart: 116, of which 41 were waited for; matrix products, arithmetic and copies ran while one was open for 33% of the time, Pallas kernels for 2%

profile of v1, /device:TPU:0, one launch (start us, length us, event | category | flops | bytes accessed | tf_op | source)
XLA Modules:
  0.0 924.9 jit_solution(4013393826243042136)
XLA Ops:
  0.6 3.1 collective-permute-start.41
  8.3 15.9 %all-reduce.5 = s32[8]{0:T(128)S(1)} all-reduce(s32[8]{0:T(128)S(1)} %dynamic-update-slice), channel_id=1, replica_groups=mesh['dp'=8,'seq'=4] {'dp'}, use_global_device_ids=true, to_apply=%add.5 | all-reduce | flops 8 | bytes 64
  29.4 3.4 all-to-all-start
  32.8 2.6 reshape.1817
  67.8 4.3 broadcast.347.clone
  102.7 6.7 collective-permute-done.85
  110.2 8.0 collective-permute-done.86
  120.3 7.7 collective-permute-done.74
  128.0 8.1 collective-permute-done.75
  137.2 4.4 broadcast.347.clone.1
  144.1 4.3 broadcast.347.clone.2
  157.7 4.0 collective-permute-done.43
  198.3 3.8 collective-permute-done.61
  211.2 18.8 %collective-permute-done.5 = bf16[64,3072]{1,0:T(8,128)(2,1)S(1)} collective-permute-done((bf16[64,3072]{1,0:T(8,128)(2,1)}, bf16[64,3072]{1,0:T(8,128)(2,1)S(1)}, u32[]{:S(2)}, u32[]{:S(2)}) %collective-permute-start.5) | collective-permute-done | bytes 393248 | tf_op jit(solution)/shard_map/ppermute | solution.py:91
  282.5 14.7 %collective-permute-done.96 = bf16[256,2048]{1,0:T(8,128)(2,1)S(1)} collective-permute-done((bf16[256,2048]{1,0:T(8,128)(2,1)S(1)}, bf16[256,2048]{1,0:T(8,128)(2,1)S(1)}, u32[]{:S(2)}, u32[]{:S(2)}) %collective-permute-start.96) | collective-permute-done | bytes 1048608 | tf_op jit(solution)/shard_map/ppermute | solution.py:64
  298.3 7.5 collective-permute-done.11
  315.1 9.1 collective-permute-done.23
  338.5 13.0 %collective-permute-done.65 = bf16[32,2048]{1,0:T(8,128)(2,1)S(1)} collective-permute-done((bf16[32,2048]{1,0:T(8,128)(2,1)S(1)}, bf16[32,2048]{1,0:T(8,128)(2,1)S(1)}, u32[]{:S(2)}, u32[]{:S(2)}) %collective-permute-start.65) | collective-permute-done | bytes 131104 | tf_op jit(solution)/shard_map/ppermute | solution.py:67
  353.1 20.7 %collective-permute-done.66 = bf16[32,2048]{1,0:T(8,128)(2,1)S(1)} collective-permute-done((bf16[32,2048]{1,0:T(8,128)(2,1)S(1)}, bf16[32,2048]{1,0:T(8,128)(2,1)S(1)}, u32[]{:S(2)}, u32[]{:S(2)}) %collective-permute-start.66) | collective-permute-done | bytes 131104 | tf_op jit(solution)/shard_map/ppermute | solution.py:68
  389.0 5.5 collective-permute-done.21
  395.3 3.7 collective-permute-done.68
  404.4 7.9 collective-permute-done.25
  416.8 4.8 collective-permute-done.27
  431.1 3.4 convolution_convert_fusion.3
  435.8 35.0 %collective-permute-done.89 = bf16[256,2048]{1,0:T(8,128)(2,1)S(1)} collective-permute-done((bf16[256,2048]{1,0:T(8,128)(2,1)S(1)}, bf16[256,2048]{1,0:T(8,128)(2,1)S(1)}, u32[]{:S(2)}, u32[]{:S(2)}) %collective-permute-start.89) | collective-permute-done | bytes 1048608 | tf_op jit(solution)/shard_map/ppermute | solution.py:63
  483.0 6.8 convolution_add_fusion.4
  493.6 6.7 collective-permute-done.99
  504.2 11.6 %collective-permute-done.36 = bf16[2,512,256]{2,1,0:T(8,128)(2,1)S(1)} collective-permute-done((bf16[2,512,256]{2,1,0:T(8,128)(2,1)S(1)}, bf16[2,512,256]{2,1,0:T(8,128)(2,1)S(1)}, u32[]{:S(2)}, u32[]{:S(2)}) %collective-permute-start.36) | collective-permute-done | bytes 524320 | tf_op jit(solution)/shard_map/ppermute | solution.py:91
  517.4 5.4 collective-permute-done.80
  526.4 18.9 %collective-permute-done.91 = bf16[256,2048]{1,0:T(8,128)(2,1)S(1)} collective-permute-done((bf16[256,2048]{1,0:T(8,128)(2,1)S(1)}, bf16[256,2048]{1,0:T(8,128)(2,1)S(1)}, u32[]{:S(2)}, u32[]{:S(2)}) %collective-permute-start.91) | collective-permute-done | bytes 1048608 | tf_op jit(solution)/shard_map/ppermute | solution.py:63
  551.9 4.6 collective-permute-done.101
  560.4 14.6 %convolution_add_fusion = f32[1024,2048]{1,0:T(8,128)} fusion(f32[1024,2048]{1,0:T(8,128)S(1)} %fusion.79, bf16[1024,2048]{1,0:T(8,128)(2,1)} %bitcast.155, bf16[2048,2048]{1,0:T(8,128)(2,1)} %bitcast.142), kind=kOutput, calls=%fused_computation.20 | convolution fusion | flops 8592031744 | bytes 29360128 | tf_op jit(solution)/shard_map/dot_general | solution.py:23
  575.0 14.4 %attend.1 = (bf16[2048,256]{1,0:T(8,128)(2,1)S(1)}, bf16[8,4,256,1024]{3,2,1,0:T(8,128)(2,1)}, f32[8,1,1024]{2,1,0:T(1,128)S(1)}) custom-call(s32[1,1024]{1,0:T(1,128)S(1)} %bitcast.490, bf16[2048,256]{1,0:T(8,128)(2,1)S(1)} %bitcast.488, bf16[4,2,512,256]{3,2,1,0:T(8,128)(2,1)S(1)} %bitcast_dynamic-update-slice_fusion.34.k_ref.v_ref, ...), custom_call_target="tpu_custom_call" | custom-call | flops 8589934592 | bytes 16777216 | tf_op jit(solution)/shard_map/attend/pallas_call | solution.py:202
  591.9 6.5 multiply_reduce_fusion.3
  606.0 18.9 %collective-permute-done.71 = bf16[256,2048]{1,0:T(8,128)(2,1)S(1)} collective-permute-done((bf16[256,2048]{1,0:T(8,128)(2,1)S(1)}, bf16[256,2048]{1,0:T(8,128)(2,1)S(1)}, u32[]{:S(2)}, u32[]{:S(2)}) %collective-permute-start.71) | collective-permute-done | bytes 1048608 | tf_op jit(solution)/shard_map/ppermute | solution.py:91
  630.3 4.5 fusion.48
  634.9 13.5 %convolution_add_fusion.2 = f32[1024,2048]{1,0:T(8,128)} fusion(f32[1024,2048]{1,0:T(8,128)S(1)} %fusion.44, bf16[1024,2048]{1,0:T(8,128)(2,1)S(1)} %bitcast.492, bf16[2048,2048]{1,0:T(8,128)(2,1)} %bitcast.131), kind=kOutput, calls=%fused_computation.22 | convolution fusion | flops 8592031744 | bytes 29360128 | tf_op jit(solution)/shard_map/dot_general | solution.py:23
  648.4 24.6 %multiply_convert_fusion.1 = (bf16[1024,2048]{1,0:T(8,128)(2,1)}, bf16[1024,2048]{1,0:T(8,128)(2,1)}, bf16[1024,2048]{1,0:T(8,128)(2,1)}) fusion(f32[1024,2048]{1,0:T(8,128)} %convolution_add_fusion, f32[1024,2048]{1,0:T(8,128)} %convolution_add_fusion.2, f32[1024,2048]{1,0:T(8,128)} %fusion.48, bf16[1024,2048]{1,0:T(8,128)(2,1)} %bitcast.493, ...), kind=kOutput, calls=%fused_computation.7 | convolution fusion | flops 8625586176 | bytes 50331648 | tf_op jit(solution)/shard_map/dot_general | solution.py:23
  672.9 3.4 convolution_convert_fusion.1
  676.3 14.8 %fusion.80 = f32[1024,2048]{1,0:T(8,128)} fusion(bf16[1024,2048]{1,0:T(8,128)(2,1)} %get-tuple-element.100, bf16[2048,2048]{1,0:T(8,128)(2,1)} %bitcast.131), kind=kOutput, calls=%fused_computation.345 | convolution fusion | flops 8589934592 | bytes 20971520 | tf_op jit(solution)/shard_map/dot_general | solution.py:23
  693.5 4.6 fusion.39
  698.2 18.1 %add_add_fusion = f32[1024,2048]{1,0:T(8,128)} fusion(f32[1024,2048]{1,0:T(8,128)} %fusion.39, f32[1024,2048]{1,0:T(8,128)} %fusion.80, bf16[1024,2048]{1,0:T(8,128)(2,1)} %get-tuple-element.98, bf16[2048,2048]{1,0:T(8,128)(2,1)} %bitcast.110), kind=kOutput, calls=%fused_computation.5 | convolution fusion | flops 8594128896 | bytes 37748736 | tf_op jit(solution)/shard_map/dot_general | solution.py:23
  716.3 3.8 fusion.15
  721.5 13.3 %convolution_add_fusion.1 = f32[1024,2048]{1,0:T(8,128)} fusion(f32[1024,2048]{1,0:T(8,128)S(1)} %fusion.78, bf16[1024,2048]{1,0:T(8,128)(2,1)S(1)} %copy-done.12, bf16[2048,2048]{1,0:T(8,128)(2,1)} %bitcast.142), kind=kOutput, calls=%fused_computation.21 | convolution fusion | flops 8592031744 | bytes 29360128 | tf_op jit(solution)/shard_map/dot_general | solution.py:23
  734.8 3.8 fusion.14
  739.1 6.6 copy.271
  745.7 3.0 fusion.38
  749.8 3.4 bitcast_add_fusion
  754.3 3.6 bitcast_add_fusion.1
  762.0 17.5 %collective-permute-done.109 = bf16[256,2048]{1,0:T(8,128)(2,1)S(1)} collective-permute-done((bf16[256,2048]{1,0:T(8,128)(2,1)S(1)}, bf16[256,2048]{1,0:T(8,128)(2,1)S(1)}, u32[]{:S(2)}, u32[]{:S(2)}) %collective-permute-start.109) | collective-permute-done | bytes 1048608 | tf_op jit(solution)/shard_map/ppermute | solution.py:91
  780.0 21.1 %collective-permute-done.104 = bf16[256,2048]{1,0:T(8,128)(2,1)S(1)} collective-permute-done((bf16[256,2048]{1,0:T(8,128)(2,1)S(1)}, bf16[256,2048]{1,0:T(8,128)(2,1)S(1)}, u32[]{:S(2)}, u32[]{:S(2)}) %collective-permute-start.104) | collective-permute-done | bytes 1048608 | tf_op jit(solution)/shard_map/ppermute | solution.py:91
  801.1 2.8 multiply_convert_fusion.3
  803.9 7.2 fusion.81
  813.4 3.6 gather_fusion.3
  817.0 3.0 fusion.17.do_ref
  826.0 21.3 %attend_back.1 = (f32[2048,256]{1,0:T(8,128)S(1)}, bf16[4,512,256]{2,1,0:T(8,128)(2,1)S(1)}, bf16[4,512,256]{2,1,0:T(8,128)(2,1)S(1)}) custom-call(bf16[2048,256]{1,0:T(8,128)(2,1)S(1)} %bitcast.489, bf16[4,2,512,256]{3,2,1,0:T(8,128)(2,1)S(1)} %copy-done.3, bf16[4,2,512,256]{3,2,1,0:T(8,128)(2,1)S(1)} %copy-done.3, ...), custom_call_target="tpu_custom_call" | custom-call | flops 17179869184 | bytes 16777216 | tf_op jit(solution)/shard_map/attend_back/pallas_call | solution.py:237
  852.2 12.4 %collective-permute-done.111 = bf16[2,512,256]{2,1,0:T(8,128)(2,1)S(1)} collective-permute-done((bf16[2,512,256]{2,1,0:T(8,128)(2,1)S(1)}, bf16[2,512,256]{2,1,0:T(8,128)(2,1)S(1)}, u32[]{:S(2)}, u32[]{:S(2)}) %collective-permute-start.111) | collective-permute-done | bytes 524320 | tf_op jit(solution)/shard_map/ppermute | solution.py:91
  879.2 3.0 fusion.42
  882.3 2.8 fusion.46
  887.1 8.3 collective-permute-done.113
  896.5 4.4 all-to-all-start.1
  900.9 6.9 fusion.63
  912.8 3.1 fusion.25
  915.9 3.8 all-to-all-done.1
  (705 shorter events, 322.3 us)
Async XLA Ops:
  0.6 148.8 %collective-permute-start.41 = (bf16[64,2048]{1,0:T(8,128)(2,1)}, bf16[64,2048]{1,0:T(8,128)(2,1)}, u32[]{:S(2)}, u32[]{:S(2)}) collective-permute-start(bf16[64,2048]{1,0:T(8,128)(2,1)} %param.158), channel_id=1, source_target_pairs={{0,8},{8,16},{16,24},{24,28},{28,20},{20,12},{12,4},{4,0},{1,9},{9... | collective-permute-start | bytes 786440 | tf_op jit(solution)/shard_map/ppermute | solution.py:63
  3.7 149.3 %collective-permute-start.39 = (bf16[64,2048]{1,0:T(8,128)(2,1)}, bf16[64,2048]{1,0:T(8,128)(2,1)}, u32[]{:S(2)}, u32[]{:S(2)}) collective-permute-start(bf16[64,2048]{1,0:T(8,128)(2,1)} %param.158), channel_id=1, source_target_pairs={{0,2},{1,3},{2,0},{3,1},{4,6},{5,7},{6,4},{7,5},{8,10},{9,11},{10,... | collective-permute-start | bytes 786440 | tf_op jit(solution)/shard_map/ppermute | solution.py:91
  5.2 144.3 %collective-permute-start.38 = (bf16[64,2048]{1,0:T(8,128)(2,1)}, bf16[64,2048]{1,0:T(8,128)(2,1)}, u32[]{:S(2)}, u32[]{:S(2)}) collective-permute-start(bf16[64,2048]{1,0:T(8,128)(2,1)} %param.158), channel_id=1, source_target_pairs={{0,1},{1,0},{2,3},{3,2},{4,5},{5,4},{6,7},{7,6},{8,9},{9,8},{10,11... | collective-permute-start | bytes 786440 | tf_op jit(solution)/shard_map/ppermute | solution.py:91
  7.9 165.7 %collective-permute-start.45 = (bf16[64,2048]{1,0:T(8,128)(2,1)}, bf16[64,2048]{1,0:T(8,128)(2,1)}, u32[]{:S(2)}, u32[]{:S(2)}) collective-permute-start(bf16[64,2048]{1,0:T(8,128)(2,1)} %param.158), channel_id=1, source_target_pairs={{8,0},{16,8},{24,16},{28,24},{20,28},{12,20},{4,12},{0,4},{9,1},{1... | collective-permute-start | bytes 786440 | tf_op jit(solution)/shard_map/ppermute | solution.py:64
  29.4 137.1 %all-to-all-start = ((bf16[8,16,1376]{2,1,0:T(8,128)(2,1)}), bf16[8,16,1376]{2,1,0:T(8,128)(2,1)S(1)}, u32[]{:S(2)}, u32[]{:S(2)}) async-start(bf16[8,16,1376]{2,1,0:T(8,128)(2,1)} %select_bitcast_fusion), calls=%async_computation | async-start | bytes 720896 | tf_op jit(solution)/shard_map/all_to_all | solution.py:326
  43.5 57.0 %collective-permute-start.84 = (bf16[64,2048]{1,0:T(8,128)(2,1)}, bf16[64,2048]{1,0:T(8,128)(2,1)}, u32[]{:S(2)}, u32[]{:S(2)}) collective-permute-start(bf16[64,2048]{1,0:T(8,128)(2,1)} %get-tuple-element.112), channel_id=1, source_target_pairs={{0,1},{1,0},{2,3},{3,2},{4,5},{5,4},{6,7},{7,6},{8,9},{9,8},{10,11... | collective-permute-start | bytes 786440 | tf_op jit(solution)/shard_map/ppermute | solution.py:91
  136.1 20.3 %collective-permute-start.1 = (bf16[64,3072]{1,0:T(8,128)(2,1)}, bf16[64,3072]{1,0:T(8,128)(2,1)S(1)}, u32[]{:S(2)}, u32[]{:S(2)}) collective-permute-start(bf16[64,3072]{1,0:T(8,128)(2,1)} %copy-done.64), channel_id=1, source_target_pairs={{0,2},{1,3},{2,0},{3,1},{4,6},{5,7},{6,4},{7,5},{8,10},{9,11},{10,... | collective-permute-start | bytes 1179656 | tf_op jit(solution)/shard_map/ppermute | solution.py:91
  149.5 35.2 %collective-permute-start.49 = (bf16[64,2048]{1,0:T(8,128)(2,1)}, bf16[64,2048]{1,0:T(8,128)(2,1)}, u32[]{:S(2)}, u32[]{:S(2)}) collective-permute-start(bf16[64,2048]{1,0:T(8,128)(2,1)} %collective-permute-done.41), channel_id=1, source_target_pairs={{0,8},{8,16},{16,24},{24,28},{28,20},{20,12},{12,4},{4,0},{1,9},{9... | collective-permute-start | bytes 786440 | tf_op jit(solution)/shard_map/ppermute | solution.py:63
  161.7 23.1 %collective-permute-start.44 = (bf16[64,2048]{1,0:T(8,128)(2,1)}, bf16[64,2048]{1,0:T(8,128)(2,1)}, u32[]{:S(2)}, u32[]{:S(2)}) collective-permute-start(bf16[64,2048]{1,0:T(8,128)(2,1)} %collective-permute-done.43), channel_id=1, source_target_pairs={{0,1},{1,0},{2,3},{3,2},{4,5},{5,4},{6,7},{7,6},{8,9},{9,8},{10,11... | collective-permute-start | bytes 786440 | tf_op jit(solution)/shard_map/ppermute | solution.py:91
  173.6 30.4 %collective-permute-start.3 = (bf16[64,3072]{1,0:T(8,128)(2,1)}, bf16[64,3072]{1,0:T(8,128)(2,1)}, u32[]{:S(2)}, u32[]{:S(2)}) collective-permute-start(bf16[64,3072]{1,0:T(8,128)(2,1)} %copy-done.64), channel_id=1, source_target_pairs={{0,8},{8,16},{16,24},{24,28},{28,20},{20,12},{12,4},{4,0},{1,9},{9... | collective-permute-start | bytes 1179656 | tf_op jit(solution)/shard_map/ppermute | solution.py:63
  175.2 17.9 %collective-permute-start.53 = (bf16[64,2048]{1,0:T(8,128)(2,1)}, bf16[64,2048]{1,0:T(8,128)(2,1)}, u32[]{:S(2)}, u32[]{:S(2)}) collective-permute-start(bf16[64,2048]{1,0:T(8,128)(2,1)} %collective-permute-done.45), channel_id=1, source_target_pairs={{8,0},{16,8},{24,16},{28,24},{20,28},{12,20},{4,12},{0,4},{9,1},{1... | collective-permute-start | bytes 786440 | tf_op jit(solution)/shard_map/ppermute | solution.py:64
  177.4 12.4 %collective-permute-start.47 = (bf16[64,2048]{1,0:T(8,128)(2,1)}, bf16[64,2048]{1,0:T(8,128)(2,1)}, u32[]{:S(2)}, u32[]{:S(2)}) collective-permute-start(bf16[64,2048]{1,0:T(8,128)(2,1)} %collective-permute-done.45), channel_id=1, source_target_pairs={{0,2},{1,3},{2,0},{3,1},{4,6},{5,7},{6,4},{7,5},{8,10},{9,11},{10,... | collective-permute-start | bytes 786440 | tf_op jit(solution)/shard_map/ppermute | solution.py:91
  189.8 15.6 %collective-permute-start.51 = (bf16[64,2048]{1,0:T(8,128)(2,1)}, bf16[64,2048]{1,0:T(8,128)(2,1)S(1)}, u32[]{:S(2)}, u32[]{:S(2)}) collective-permute-start(bf16[64,2048]{1,0:T(8,128)(2,1)} %collective-permute-done.49), channel_id=1, source_target_pairs={{0,2},{1,3},{2,0},{3,1},{4,6},{5,7},{6,4},{7,5},{8,10},{9,11},{10,... | collective-permute-start | bytes 786440 | tf_op jit(solution)/shard_map/ppermute | solution.py:91
  196.5 78.7 %collective-permute-start.106 = (bf16[256,2048]{1,0:T(8,128)(2,1)}, bf16[256,2048]{1,0:T(8,128)(2,1)}, u32[]{:S(2)}, u32[]{:S(2)}) collective-permute-start(bf16[256,2048]{1,0:T(8,128)(2,1)} %fusion.5), channel_id=1, source_target_pairs={{0,2},{1,3},{2,0},{3,1},{4,6},{5,7},{6,4},{7,5},{8,10},{9,11},{10,... | collective-permute-start | bytes 3145736 | tf_op jit(solution)/shard_map/ppermute | solution.py:91
  202.1 58.5 %collective-permute-start.105 = (bf16[256,2048]{1,0:T(8,128)(2,1)}, bf16[256,2048]{1,0:T(8,128)(2,1)}, u32[]{:S(2)}, u32[]{:S(2)}) collective-permute-start(bf16[256,2048]{1,0:T(8,128)(2,1)} %fusion.5), channel_id=1, source_target_pairs={{0,1},{1,0},{2,3},{3,2},{4,5},{5,4},{6,7},{7,6},{8,9},{9,8},{10,11... | collective-permute-start | bytes 3145736 | tf_op jit(solution)/shard_map/ppermute | solution.py:91
  204.0 74.5 %collective-permute-start.95 = (bf16[256,2048]{1,0:T(8,128)(2,1)}, bf16[256,2048]{1,0:T(8,128)(2,1)}, u32[]{:S(2)}, u32[]{:S(2)}) collective-permute-start(bf16[256,2048]{1,0:T(8,128)(2,1)} %param.161), channel_id=1, source_target_pairs={{0,8},{8,16},{16,24},{24,28},{28,20},{20,12},{12,4},{4,0},{1,9},{9... | collective-permute-start | bytes 3145736 | tf_op jit(solution)/shard_map/ppermute | solution.py:63
  205.4 24.6 %collective-permute-start.5 = (bf16[64,3072]{1,0:T(8,128)(2,1)}, bf16[64,3072]{1,0:T(8,128)(2,1)S(1)}, u32[]{:S(2)}, u32[]{:S(2)}) collective-permute-start(bf16[64,3072]{1,0:T(8,128)(2,1)} %collective-permute-done.3), channel_id=1, source_target_pairs={{0,2},{1,3},{2,0},{3,1},{4,6},{5,7},{6,4},{7,5},{8,10},{9,11},{10,... | collective-permute-start | bytes 1179656 | tf_op jit(solution)/shard_map/ppermute | solution.py:91
  209.8 62.5 %collective-permute-start.7 = (bf16[64,3072]{1,0:T(8,128)(2,1)}, bf16[64,3072]{1,0:T(8,128)(2,1)}, u32[]{:S(2)}, u32[]{:S(2)}) collective-permute-start(bf16[64,3072]{1,0:T(8,128)(2,1)} %copy-done.64), channel_id=1, source_target_pairs={{8,0},{16,8},{24,16},{28,24},{20,28},{12,20},{4,12},{0,4},{9,1},{1... | collective-permute-start | bytes 1179656 | tf_op jit(solution)/shard_map/ppermute | solution.py:64
  231.6 34.3 %collective-permute-start.55 = (bf16[64,2048]{1,0:T(8,128)(2,1)}, bf16[64,2048]{1,0:T(8,128)(2,1)}, u32[]{:S(2)}, u32[]{:S(2)}) collective-permute-start(bf16[64,2048]{1,0:T(8,128)(2,1)} %collective-permute-done.53), channel_id=1, source_target_pairs={{0,2},{1,3},{2,0},{3,1},{4,6},{5,7},{6,4},{7,5},{8,10},{9,11},{10,... | collective-permute-start | bytes 786440 | tf_op jit(solution)/shard_map/ppermute | solution.py:91
  271.1 26.1 %collective-permute-start.96 = (bf16[256,2048]{1,0:T(8,128)(2,1)S(1)}, bf16[256,2048]{1,0:T(8,128)(2,1)S(1)}, u32[]{:S(2)}, u32[]{:S(2)}) collective-permute-start(bf16[256,2048]{1,0:T(8,128)(2,1)S(1)} %copy-done.18), channel_id=1, source_target_pairs={{8,0},{16,8},{24,16},{28,24},{20,28},{12,20},{4,12},{0,4},{9,1},{1... | collective-permute-start | bytes 3145736 | tf_op jit(solution)/shard_map/ppermute | solution.py:64
  272.3 57.0 %collective-permute-start.87 = (bf16[256,2048]{1,0:T(8,128)(2,1)}, bf16[256,2048]{1,0:T(8,128)(2,1)S(1)}, u32[]{:S(2)}, u32[]{:S(2)}) collective-permute-start(bf16[256,2048]{1,0:T(8,128)(2,1)} %bitcast.122), channel_id=1, source_target_pairs={{0,8},{8,16},{16,24},{24,28},{28,20},{20,12},{12,4},{4,0},{1,9},{9... | collective-permute-start | bytes 3145736 | tf_op jit(solution)/shard_map/ppermute | solution.py:63
  274.1 38.5 %collective-permute-start.15 = (bf16[64,3072]{1,0:T(8,128)(2,1)}, bf16[64,3072]{1,0:T(8,128)(2,1)S(1)}, u32[]{:S(2)}, u32[]{:S(2)}) collective-permute-start(bf16[64,3072]{1,0:T(8,128)(2,1)} %collective-permute-done.7), channel_id=1, source_target_pairs={{8,0},{16,8},{24,16},{28,24},{20,28},{12,20},{4,12},{0,4},{9,1},{1... | collective-permute-start | bytes 1179656 | tf_op jit(solution)/shard_map/ppermute | solution.py:64
  275.2 34.7 %collective-permute-start.9 = (bf16[64,3072]{1,0:T(8,128)(2,1)}, bf16[64,3072]{1,0:T(8,128)(2,1)S(1)}, u32[]{:S(2)}, u32[]{:S(2)}) collective-permute-start(bf16[64,3072]{1,0:T(8,128)(2,1)} %collective-permute-done.7), channel_id=1, source_target_pairs={{0,2},{1,3},{2,0},{3,1},{4,6},{5,7},{6,4},{7,5},{8,10},{9,11},{10,... | collective-permute-start | bytes 1179656 | tf_op jit(solution)/shard_map/ppermute | solution.py:91
  278.5 27.3 %collective-permute-start.11 = (bf16[64,3072]{1,0:T(8,128)(2,1)}, bf16[64,3072]{1,0:T(8,128)(2,1)S(1)}, u32[]{:S(2)}, u32[]{:S(2)}) collective-permute-start(bf16[64,3072]{1,0:T(8,128)(2,1)} %collective-permute-done.3), channel_id=1, source_target_pairs={{0,8},{8,16},{16,24},{24,28},{28,20},{20,12},{12,4},{4,0},{1,9},{9... | collective-permute-start | bytes 1179656 | tf_op jit(solution)/shard_map/ppermute | solution.py:63
  305.8 18.8 %collective-permute-start.19 = (bf16[64,3072]{1,0:T(8,128)(2,1)S(1)}, bf16[64,3072]{1,0:T(8,128)(2,1)S(1)}, u32[]{:S(2)}, u32[]{:S(2)}) collective-permute-start(bf16[64,3072]{1,0:T(8,128)(2,1)S(1)} %collective-permute-done.11), channel_id=1, source_target_pairs={{0,8},{8,16},{16,24},{24,28},{28,20},{20,12},{12,4},{4,0},{1,9},{9... | collective-permute-start | bytes 1179656 | tf_op jit(solution)/shard_map/ppermute | solution.py:63
  310.0 17.6 %collective-permute-start.13 = (bf16[64,3072]{1,0:T(8,128)(2,1)S(1)}, bf16[64,3072]{1,0:T(8,128)(2,1)S(1)}, u32[]{:S(2)}, u32[]{:S(2)}) collective-permute-start(bf16[64,3072]{1,0:T(8,128)(2,1)S(1)} %collective-permute-done.11), channel_id=1, source_target_pairs={{0,2},{1,3},{2,0},{3,1},{4,6},{5,7},{6,4},{7,5},{8,10},{9,11},{10,... | collective-permute-start | bytes 1179656 | tf_op jit(solution)/shard_map/ppermute | solution.py:91
  312.7 13.7 %collective-permute-start.12 = (bf16[64,3072]{1,0:T(8,128)(2,1)S(1)}, bf16[64,3072]{1,0:T(8,128)(2,1)S(1)}, u32[]{:S(2)}, u32[]{:S(2)}) collective-permute-start(bf16[64,3072]{1,0:T(8,128)(2,1)S(1)} %collective-permute-done.11), channel_id=1, source_target_pairs={{0,1},{1,0},{2,3},{3,2},{4,5},{5,4},{6,7},{7,6},{8,9},{9,8},{10,11... | collective-permute-start | bytes 1179656 | tf_op jit(solution)/shard_map/ppermute | solution.py:91
  324.2 53.3 %collective-permute-start.77 = (bf16[256,2048]{1,0:T(8,128)(2,1)S(1)}, bf16[256,2048]{1,0:T(8,128)(2,1)S(1)}, u32[]{:S(2)}, u32[]{:S(2)}) collective-permute-start(bf16[256,2048]{1,0:T(8,128)(2,1)S(1)} %bitcast.510), channel_id=1, source_target_pairs={{8,0},{16,8},{24,16},{28,24},{20,28},{12,20},{4,12},{0,4},{9,1},{1... | collective-permute-start | bytes 3145736 | tf_op jit(solution)/shard_map/ppermute | solution.py:64
  324.6 51.4 %collective-permute-start.76 = (bf16[256,2048]{1,0:T(8,128)(2,1)S(1)}, bf16[256,2048]{1,0:T(8,128)(2,1)S(1)}, u32[]{:S(2)}, u32[]{:S(2)}) collective-permute-start(bf16[256,2048]{1,0:T(8,128)(2,1)S(1)} %bitcast.511), channel_id=1, source_target_pairs={{0,8},{8,16},{16,24},{24,28},{28,20},{20,12},{12,4},{4,0},{1,9},{9... | collective-permute-start | bytes 3145736 | tf_op jit(solution)/shard_map/ppermute | solution.py:63
  326.4 48.1 %collective-permute-start.88 = (bf16[256,2048]{1,0:T(8,128)(2,1)}, bf16[256,2048]{1,0:T(8,128)(2,1)S(1)}, u32[]{:S(2)}, u32[]{:S(2)}) collective-permute-start(bf16[256,2048]{1,0:T(8,128)(2,1)} %bitcast.122), channel_id=1, source_target_pairs={{8,0},{16,8},{24,16},{28,24},{20,28},{12,20},{4,12},{0,4},{9,1},{1... | collective-permute-start | bytes 3145736 | tf_op jit(solution)/shard_map/ppermute | solution.py:64
  334.2 17.3 %collective-permute-start.65 = (bf16[32,2048]{1,0:T(8,128)(2,1)S(1)}, bf16[32,2048]{1,0:T(8,128)(2,1)S(1)}, u32[]{:S(2)}, u32[]{:S(2)}) collective-permute-start(bf16[32,2048]{1,0:T(8,128)(2,1)S(1)} %copy-done.67), channel_id=1, source_target_pairs={{0,8},{8,16},{16,24},{24,28},{28,20},{20,12},{12,4},{4,0},{1,9},{9... | collective-permute-start | bytes 393224 | tf_op jit(solution)/shard_map/ppermute | solution.py:67
  337.4 36.4 %collective-permute-start.66 = (bf16[32,2048]{1,0:T(8,128)(2,1)S(1)}, bf16[32,2048]{1,0:T(8,128)(2,1)S(1)}, u32[]{:S(2)}, u32[]{:S(2)}) collective-permute-start(bf16[32,2048]{1,0:T(8,128)(2,1)S(1)} %copy-done.66), channel_id=1, source_target_pairs={{8,0},{16,8},{24,16},{28,24},{20,28},{12,20},{4,12},{0,4},{9,1},{1... | collective-permute-start | bytes 393224 | tf_op jit(solution)/shard_map/ppermute | solution.py:68
  351.5 31.0 %collective-permute-start.17 = (bf16[64,3072]{1,0:T(8,128)(2,1)S(1)}, bf16[64,3072]{1,0:T(8,128)(2,1)S(1)}, u32[]{:S(2)}, u32[]{:S(2)}) collective-permute-start(bf16[64,3072]{1,0:T(8,128)(2,1)S(1)} %collective-permute-done.15), channel_id=1, source_target_pairs={{0,2},{1,3},{2,0},{3,1},{4,6},{5,7},{6,4},{7,5},{8,10},{9,11},{10,... | collective-permute-start | bytes 1179656 | tf_op jit(solution)/shard_map/ppermute | solution.py:91
  374.5 50.6 %collective-permute-start.107 = (bf16[256,2048]{1,0:T(8,128)(2,1)}, bf16[256,2048]{1,0:T(8,128)(2,1)S(1)}, u32[]{:S(2)}, u32[]{:S(2)}) collective-permute-start(bf16[256,2048]{1,0:T(8,128)(2,1)} %collective-permute-done.106), channel_id=1, source_target_pairs={{0,1},{1,0},{2,3},{3,2},{4,5},{5,4},{6,7},{7,6},{8,9},{9,8},{10,11... | collective-permute-start | bytes 3145736 | tf_op jit(solution)/shard_map/ppermute | solution.py:91
  376.0 53.2 %collective-permute-start.98 = (bf16[256,2048]{1,0:T(8,128)(2,1)S(1)}, bf16[256,2048]{1,0:T(8,128)(2,1)S(1)}, u32[]{:S(2)}, u32[]{:S(2)}) collective-permute-start(bf16[256,2048]{1,0:T(8,128)(2,1)S(1)} %collective-permute-done.96), channel_id=1, source_target_pairs={{8,0},{16,8},{24,16},{28,24},{20,28},{12,20},{4,12},{0,4},{9,1},{1... | collective-permute-start | bytes 3145736 | tf_op jit(solution)/shard_map/ppermute | solution.py:64
  379.3 48.5 %collective-permute-start.97 = (bf16[256,2048]{1,0:T(8,128)(2,1)}, bf16[256,2048]{1,0:T(8,128)(2,1)S(1)}, u32[]{:S(2)}, u32[]{:S(2)}) collective-permute-start(bf16[256,2048]{1,0:T(8,128)(2,1)} %collective-permute-done.95), channel_id=1, source_target_pairs={{0,8},{8,16},{16,24},{24,28},{28,20},{20,12},{12,4},{4,0},{1,9},{9... | collective-permute-start | bytes 3145736 | tf_op jit(solution)/shard_map/ppermute | solution.py:63
  382.5 12.0 %collective-permute-start.21 = (bf16[64,3072]{1,0:T(8,128)(2,1)S(1)}, bf16[64,3072]{1,0:T(8,128)(2,1)S(1)}, u32[]{:S(2)}, u32[]{:S(2)}) collective-permute-start(bf16[64,3072]{1,0:T(8,128)(2,1)S(1)} %collective-permute-done.19), channel_id=1, source_target_pairs={{0,2},{1,3},{2,0},{3,1},{4,6},{5,7},{6,4},{7,5},{8,10},{9,11},{10,... | collective-permute-start | bytes 1179656 | tf_op jit(solution)/shard_map/ppermute | solution.py:91
  421.7 52.7 %collective-permute-start.79 = (bf16[256,2048]{1,0:T(8,128)(2,1)S(1)}, bf16[256,2048]{1,0:T(8,128)(2,1)S(1)}, u32[]{:S(2)}, u32[]{:S(2)}) collective-permute-start(bf16[256,2048]{1,0:T(8,128)(2,1)S(1)} %collective-permute-done.77), channel_id=1, source_target_pairs={{8,0},{16,8},{24,16},{28,24},{20,28},{12,20},{4,12},{0,4},{9,1},{1... | collective-permute-start | bytes 3145736 | tf_op jit(solution)/shard_map/ppermute | solution.py:64
  424.0 47.9 %collective-permute-start.78 = (bf16[256,2048]{1,0:T(8,128)(2,1)S(1)}, bf16[256,2048]{1,0:T(8,128)(2,1)S(1)}, u32[]{:S(2)}, u32[]{:S(2)}) collective-permute-start(bf16[256,2048]{1,0:T(8,128)(2,1)S(1)} %collective-permute-done.76), channel_id=1, source_target_pairs={{0,8},{8,16},{16,24},{24,28},{28,20},{20,12},{12,4},{4,0},{1,9},{9... | collective-permute-start | bytes 3145736 | tf_op jit(solution)/shard_map/ppermute | solution.py:63
  425.1 50.9 %collective-permute-start.90 = (bf16[256,2048]{1,0:T(8,128)(2,1)S(1)}, bf16[256,2048]{1,0:T(8,128)(2,1)S(1)}, u32[]{:S(2)}, u32[]{:S(2)}) collective-permute-start(bf16[256,2048]{1,0:T(8,128)(2,1)S(1)} %collective-permute-done.88), channel_id=1, source_target_pairs={{8,0},{16,8},{24,16},{28,24},{20,28},{12,20},{4,12},{0,4},{9,1},{1... | collective-permute-start | bytes 3145736 | tf_op jit(solution)/shard_map/ppermute | solution.py:64
  427.8 43.0 %collective-permute-start.89 = (bf16[256,2048]{1,0:T(8,128)(2,1)S(1)}, bf16[256,2048]{1,0:T(8,128)(2,1)S(1)}, u32[]{:S(2)}, u32[]{:S(2)}) collective-permute-start(bf16[256,2048]{1,0:T(8,128)(2,1)S(1)} %collective-permute-done.87), channel_id=1, source_target_pairs={{0,8},{8,16},{16,24},{24,28},{28,20},{20,12},{12,4},{4,0},{1,9},{9... | collective-permute-start | bytes 3145736 | tf_op jit(solution)/shard_map/ppermute | solution.py:63
  429.2 49.3 %collective-permute-start.30 = (bf16[64,3072]{1,0:T(8,128)(2,1)S(1)}, bf16[64,3072]{1,0:T(8,128)(2,1)S(1)}, u32[]{:S(2)}, u32[]{:S(2)}) collective-permute-start(bf16[64,3072]{1,0:T(8,128)(2,1)S(1)} %get-tuple-element.157), channel_id=1, source_target_pairs={{0,2},{1,3},{2,0},{3,1},{4,6},{5,7},{6,4},{7,5},{8,10},{9,11},{10,... | collective-permute-start | bytes 1179656 | tf_op jit(solution)/shard_map/ppermute | solution.py:91
  471.9 29.5 %collective-permute-start.100 = (bf16[256,2048]{1,0:T(8,128)(2,1)S(1)}, bf16[256,2048]{1,0:T(8,128)(2,1)S(1)}, u32[]{:S(2)}, u32[]{:S(2)}) collective-permute-start(bf16[256,2048]{1,0:T(8,128)(2,1)S(1)} %collective-permute-done.98), channel_id=1, source_target_pairs={{8,0},{16,8},{24,16},{28,24},{20,28},{12,20},{4,12},{0,4},{9,1},{1... | collective-permute-start | bytes 3145736 | tf_op jit(solution)/shard_map/ppermute | solution.py:64
  474.3 26.0 %collective-permute-start.99 = (bf16[256,2048]{1,0:T(8,128)(2,1)S(1)}, bf16[256,2048]{1,0:T(8,128)(2,1)S(1)}, u32[]{:S(2)}, u32[]{:S(2)}) collective-permute-start(bf16[256,2048]{1,0:T(8,128)(2,1)S(1)} %collective-permute-done.97), channel_id=1, source_target_pairs={{0,8},{8,16},{16,24},{24,28},{28,20},{20,12},{12,4},{4,0},{1,9},{9... | collective-permute-start | bytes 3145736 | tf_op jit(solution)/shard_map/ppermute | solution.py:63
  476.0 48.5 %collective-permute-start.81 = (bf16[256,2048]{1,0:T(8,128)(2,1)S(1)}, bf16[256,2048]{1,0:T(8,128)(2,1)S(1)}, u32[]{:S(2)}, u32[]{:S(2)}) collective-permute-start(bf16[256,2048]{1,0:T(8,128)(2,1)S(1)} %collective-permute-done.79), channel_id=1, source_target_pairs={{8,0},{16,8},{24,16},{28,24},{20,28},{12,20},{4,12},{0,4},{9,1},{1... | collective-permute-start | bytes 3145736 | tf_op jit(solution)/shard_map/ppermute | solution.py:64
  478.5 44.3 %collective-permute-start.80 = (bf16[256,2048]{1,0:T(8,128)(2,1)S(1)}, bf16[256,2048]{1,0:T(8,128)(2,1)S(1)}, u32[]{:S(2)}, u32[]{:S(2)}) collective-permute-start(bf16[256,2048]{1,0:T(8,128)(2,1)S(1)} %collective-permute-done.78), channel_id=1, source_target_pairs={{0,8},{8,16},{16,24},{24,28},{28,20},{20,12},{12,4},{4,0},{1,9},{9... | collective-permute-start | bytes 3145736 | tf_op jit(solution)/shard_map/ppermute | solution.py:63
  480.9 68.0 %collective-permute-start.92 = (bf16[256,2048]{1,0:T(8,128)(2,1)S(1)}, bf16[256,2048]{1,0:T(8,128)(2,1)S(1)}, u32[]{:S(2)}, u32[]{:S(2)}) collective-permute-start(bf16[256,2048]{1,0:T(8,128)(2,1)S(1)} %collective-permute-done.90), channel_id=1, source_target_pairs={{8,0},{16,8},{24,16},{28,24},{20,28},{12,20},{4,12},{0,4},{9,1},{1... | collective-permute-start | bytes 3145736 | tf_op jit(solution)/shard_map/ppermute | solution.py:64
  501.4 14.3 %collective-permute-start.36 = (bf16[2,512,256]{2,1,0:T(8,128)(2,1)S(1)}, bf16[2,512,256]{2,1,0:T(8,128)(2,1)S(1)}, u32[]{:S(2)}, u32[]{:S(2)}) collective-permute-start(bf16[2,512,256]{2,1,0:T(8,128)(2,1)S(1)} %pad_maximum_fusion.1), channel_id=1, source_target_pairs={{0,2},{1,3},{2,0},{3,1},{4,6},{5,7},{6,4},{7,5},{8,10},{9,11},{10,... | collective-permute-start | bytes 1572872 | tf_op jit(solution)/shard_map/ppermute | solution.py:91
  503.4 41.9 %collective-permute-start.91 = (bf16[256,2048]{1,0:T(8,128)(2,1)S(1)}, bf16[256,2048]{1,0:T(8,128)(2,1)S(1)}, u32[]{:S(2)}, u32[]{:S(2)}) collective-permute-start(bf16[256,2048]{1,0:T(8,128)(2,1)S(1)} %collective-permute-done.89), channel_id=1, source_target_pairs={{0,8},{8,16},{16,24},{24,28},{28,20},{20,12},{12,4},{4,0},{1,9},{9... | collective-permute-start | bytes 3145736 | tf_op jit(solution)/shard_map/ppermute | solution.py:63
  515.7 43.2 %collective-permute-start.102 = (bf16[128,2048]{1,0:T(8,128)(2,1)S(1)}, bf16[128,2048]{1,0:T(8,128)(2,1)S(1)}, u32[]{:S(2)}, u32[]{:S(2)}) collective-permute-start(bf16[128,2048]{1,0:T(8,128)(2,1)S(1)} %slice.277), channel_id=1, source_target_pairs={{8,0},{16,8},{24,16},{28,24},{20,28},{12,20},{4,12},{0,4},{9,1},{1... | collective-permute-start | bytes 1572872 | tf_op jit(solution)/shard_map/ppermute | solution.py:68
  522.8 33.7 %collective-permute-start.101 = (bf16[128,2048]{1,0:T(8,128)(2,1)S(1)}, bf16[128,2048]{1,0:T(8,128)(2,1)S(1)}, u32[]{:S(2)}, u32[]{:S(2)}) collective-permute-start(bf16[128,2048]{1,0:T(8,128)(2,1)S(1)} %slice.276), channel_id=1, source_target_pairs={{0,8},{8,16},{16,24},{24,28},{28,20},{20,12},{12,4},{4,0},{1,9},{9... | collective-permute-start | bytes 1572872 | tf_op jit(solution)/shard_map/ppermute | solution.py:67
  524.5 50.5 %collective-permute-start.37 = (bf16[2,512,256]{2,1,0:T(8,128)(2,1)S(1)}, bf16[2,512,256]{2,1,0:T(8,128)(2,1)S(1)}, u32[]{:S(2)}, u32[]{:S(2)}) collective-permute-start(bf16[2,512,256]{2,1,0:T(8,128)(2,1)S(1)} %collective-permute-done.36), channel_id=1, source_target_pairs={{0,1},{1,0},{2,3},{3,2},{4,5},{5,4},{6,7},{7,6},{8,9},{9,8},{10,11... | collective-permute-start | bytes 1572872 | tf_op jit(solution)/shard_map/ppermute | solution.py:91
  545.3 79.6 %collective-permute-start.83 = (bf16[128,2048]{1,0:T(8,128)(2,1)}, bf16[128,2048]{1,0:T(8,128)(2,1)}, u32[]{:S(2)}, u32[]{:S(2)}) collective-permute-start(bf16[128,2048]{1,0:T(8,128)(2,1)} %slice.267), channel_id=1, source_target_pairs={{8,0},{16,8},{24,16},{28,24},{20,28},{12,20},{4,12},{0,4},{9,1},{1... | collective-permute-start | bytes 1572872 | tf_op jit(solution)/shard_map/ppermute | solution.py:68
  548.8 55.2 %collective-permute-start.82 = (bf16[128,2048]{1,0:T(8,128)(2,1)}, bf16[128,2048]{1,0:T(8,128)(2,1)}, u32[]{:S(2)}, u32[]{:S(2)}) collective-permute-start(bf16[128,2048]{1,0:T(8,128)(2,1)} %slice.266), channel_id=1, source_target_pairs={{0,8},{8,16},{16,24},{24,28},{28,20},{20,12},{12,4},{4,0},{1,9},{9... | collective-permute-start | bytes 1572872 | tf_op jit(solution)/shard_map/ppermute | solution.py:67
  556.5 45.7 %collective-permute-start.94 = (bf16[128,2048]{1,0:T(8,128)(2,1)}, bf16[128,2048]{1,0:T(8,128)(2,1)}, u32[]{:S(2)}, u32[]{:S(2)}) collective-permute-start(bf16[128,2048]{1,0:T(8,128)(2,1)} %slice.273), channel_id=1, source_target_pairs={{8,0},{16,8},{24,16},{28,24},{20,28},{12,20},{4,12},{0,4},{9,1},{1... | collective-permute-start | bytes 1572872 | tf_op jit(solution)/shard_map/ppermute | solution.py:68
  559.0 40.4 %collective-permute-start.93 = (bf16[128,2048]{1,0:T(8,128)(2,1)}, bf16[128,2048]{1,0:T(8,128)(2,1)}, u32[]{:S(2)}, u32[]{:S(2)}) collective-permute-start(bf16[128,2048]{1,0:T(8,128)(2,1)} %slice.272), channel_id=1, source_target_pairs={{0,8},{8,16},{16,24},{24,28},{28,20},{20,12},{12,4},{4,0},{1,9},{9... | collective-permute-start | bytes 1572872 | tf_op jit(solution)/shard_map/ppermute | solution.py:67
  599.2 27.5 %collective-permute-start.70 = (bf16[256,2048]{1,0:T(8,128)(2,1)S(1)}, bf16[256,2048]{1,0:T(8,128)(2,1)S(1)}, u32[]{:S(2)}, u32[]{:S(2)}) collective-permute-start(bf16[256,2048]{1,0:T(8,128)(2,1)S(1)} %get-tuple-element.97), channel_id=1, source_target_pairs={{0,1},{1,0},{2,3},{3,2},{4,5},{5,4},{6,7},{7,6},{8,9},{9,8},{10,11... | collective-permute-start | bytes 3145736 | tf_op jit(solution)/shard_map/ppermute | solution.py:91
  599.3 25.6 %collective-permute-start.71 = (bf16[256,2048]{1,0:T(8,128)(2,1)S(1)}, bf16[256,2048]{1,0:T(8,128)(2,1)S(1)}, u32[]{:S(2)}, u32[]{:S(2)}) collective-permute-start(bf16[256,2048]{1,0:T(8,128)(2,1)S(1)} %get-tuple-element.97), channel_id=1, source_target_pairs={{0,2},{1,3},{2,0},{3,1},{4,6},{5,7},{6,4},{7,5},{8,10},{9,11},{10,... | collective-permute-start | bytes 3145736 | tf_op jit(solution)/shard_map/ppermute | solution.py:91
  720.1 29.7 %collective-permute-start.108 = (bf16[2,256,2048]{2,1,0:T(8,128)(2,1)}, bf16[2,256,2048]{2,1,0:T(8,128)(2,1)}, u32[]{:S(2)}, u32[]{:S(2)}) collective-permute-start(bf16[2,256,2048]{2,1,0:T(8,128)(2,1)} %fusion.15), channel_id=1, source_target_pairs={{0,1},{1,0},{2,3},{3,2},{4,5},{5,4},{6,7},{7,6},{8,9},{9,8},{10,11... | collective-permute-start | bytes 6291464 | tf_op jit(solution)/shard_map/ppermute | solution.py:91
  738.6 15.7 %collective-permute-start.103 = (bf16[2,256,2048]{2,1,0:T(8,128)(2,1)}, bf16[2,256,2048]{2,1,0:T(8,128)(2,1)}, u32[]{:S(2)}, u32[]{:S(2)}) collective-permute-start(bf16[2,256,2048]{2,1,0:T(8,128)(2,1)} %fusion.14), channel_id=1, source_target_pairs={{0,1},{1,0},{2,3},{3,2},{4,5},{5,4},{6,7},{7,6},{8,9},{9,8},{10,11... | collective-permute-start | bytes 6291464 | tf_op jit(solution)/shard_map/ppermute | solution.py:91
  753.3 26.1 %collective-permute-start.109 = (bf16[256,2048]{1,0:T(8,128)(2,1)S(1)}, bf16[256,2048]{1,0:T(8,128)(2,1)S(1)}, u32[]{:S(2)}, u32[]{:S(2)}) collective-permute-start(bf16[256,2048]{1,0:T(8,128)(2,1)S(1)} %fusion.23), channel_id=1, source_target_pairs={{0,2},{1,3},{2,0},{3,1},{4,6},{5,7},{6,4},{7,5},{8,10},{9,11},{10,... | collective-permute-start | bytes 3145736 | tf_op jit(solution)/shard_map/ppermute | solution.py:91
  758.1 43.0 %collective-permute-start.104 = (bf16[256,2048]{1,0:T(8,128)(2,1)S(1)}, bf16[256,2048]{1,0:T(8,128)(2,1)S(1)}, u32[]{:S(2)}, u32[]{:S(2)}) collective-permute-start(bf16[256,2048]{1,0:T(8,128)(2,1)S(1)} %fusion.22), channel_id=1, source_target_pairs={{0,2},{1,3},{2,0},{3,1},{4,6},{5,7},{6,4},{7,5},{8,10},{9,11},{10,... | collective-permute-start | bytes 3145736 | tf_op jit(solution)/shard_map/ppermute | solution.py:91
  850.6 14.0 %collective-permute-start.111 = (bf16[2,512,256]{2,1,0:T(8,128)(2,1)S(1)}, bf16[2,512,256]{2,1,0:T(8,128)(2,1)S(1)}, u32[]{:S(2)}, u32[]{:S(2)}) collective-permute-start(bf16[2,512,256]{2,1,0:T(8,128)(2,1)S(1)} %fusion.33), channel_id=1, source_target_pairs={{0,2},{1,3},{2,0},{3,1},{4,6},{5,7},{6,4},{7,5},{8,10},{9,11},{10,... | collective-permute-start | bytes 1572872 | tf_op jit(solution)/shard_map/ppermute | solution.py:91
  896.5 23.1 %all-to-all-start.1 = ((f32[8,16,1376]{2,1,0:T(8,128)}), f32[8,16,1376]{2,1,0:T(8,128)}, u32[]{:S(2)}, u32[]{:S(2)}) async-start(f32[8,16,1376]{2,1,0:T(8,128)} %concatenate.97), calls=%async_computation.1 | async-start | bytes 1441792 | tf_op jit(solution)/shard_map/all_to_all | solution.py:450
  (156 other events, 3234.6 us)

commit v2 on v1

v2 whole, which is shorter than its diff:
```python
import functools

import jax
import jax.numpy as jnp
import numpy as np
from jax import lax
from jax.experimental import pallas as pl
from jax.experimental.pallas import tpu as pltpu
from jax.sharding import PartitionSpec as P

H = 32
KV = 8
HD = 64
GROUP = H // KV
ADAPT = 8
RANK = 16
EPS = 1e-05
F32 = jnp.float32
BF16 = jnp.bfloat16


def contract(left, right, left_dim, right_dim):
    return lax.dot_general(
        left, right, (((left_dim,), (right_dim,)), ((), ())), preferred_element_type=F32
    )


def rms_scale(operand, scaling, axis=-1):
    mean = jnp.mean(operand * operand, axis=axis, keepdims=True)
    return operand * lax.rsqrt(mean + EPS) * scaling


def rotary_tables(positions):
    frequency = jnp.power(1000000.0, -jnp.arange(HD // 2, dtype=F32) * 2.0 / HD)
    angles = frequency[:, None] * positions.astype(F32)[None, :]
    return jnp.cos(angles), jnp.sin(angles)


def prepare(linear, scaling, cosine, sine):
    normed = rms_scale(linear, scaling[:, None], axis=1)
    front, second = normed[:, : HD // 2], normed[:, HD // 2 :]
    return jnp.concatenate(
        [front * cosine - second * sine, second * cosine + front * sine], axis=1
    )


def after(value, *others):
    return lax.optimization_barrier((value, others))[0]


def ring_order(size):
    return list(range(0, size, 2)) + list(range(1, size, 2))[::-1]


def ring_pairs(size):
    order = ring_order(size)
    right = [(order[i], order[(i + 1) % size]) for i in range(size)]
    return right, [(b, a) for a, b in right]


def ring_offsets():
    offsets = [0]
    for step in range(1, (lax.axis_size("dp") - 1) // 2 + 1):
        offsets += [-step, step]
    return offsets + [lax.axis_size("dp") // 2]


class Ring:
    def __init__(self, own):
        self.pieces = [own]
        self.left = self.right = own
        self.steps = lax.axis_size("dp") // 2

    def complete(self):
        return len(self.pieces) == lax.axis_size("dp")

    def step(self, clock):
        size = lax.axis_size("dp")
        right, left = ring_pairs(size)
        if len(self.pieces) < size - 1:
            self.left = lax.ppermute(clock(self.left), "dp", right)
            self.right = lax.ppermute(clock(self.right), "dp", left)
            self.pieces += [self.left, self.right]
            return self.left, self.right
        half = self.left.shape[0] // 2
        top = lax.ppermute(clock(self.left[:half]), "dp", right)
        bottom = lax.ppermute(clock(self.right[half:]), "dp", left)
        self.pieces.append((top, bottom))
        return top, bottom


def ring_sources():
    size = lax.axis_size("dp")
    here = lax.axis_index("dp")
    place = jnp.where(here % 2 == 0, here // 2, size - 1 - here // 2)
    sources = []
    for offset in ring_offsets():
        at = (place + offset + size) % size
        sources.append(jnp.where(at < size // 2, 2 * at, 2 * (size - 1 - at) + 1).astype(jnp.int32))
    return sources


class Clock:
    def __init__(self):
        self.done = ()

    def tick(self, *done):
        self.done = done

    def __call__(self, value):
        return after(value, self.done) if self.done else value


class Conveyor:
    def __init__(self, clock, ring, waiting):
        self.clock = clock
        self.waiting = list(waiting)
        self.going = [(ring.step(clock), ring)]

    def push(self):
        ring = Ring(self.waiting.pop(0)())
        self.going.append((ring.step(self.clock), ring))
        return ring

    def advance(self, *computed):
        came, ring = self.going.pop(0)
        self.clock.tick(came, *computed)
        if not ring.complete():
            self.going.append((ring.step(self.clock), ring))
        elif self.waiting:
            self.push()

    def until(self, ring, *computed):
        while not ring.complete() or any(r is ring for _, r in self.going):
            self.advance(*computed)


def partner(operand, bit):
    size = lax.axis_size("seq")
    return lax.ppermute(operand, "seq", [(i, i ^ bit) for i in range(size)])


def seq_pieces(own):
    across = partner(own, 2)
    return [own, partner(own, 1), across, partner(across, 1)]


def seq_reduce(keep, give):
    arrived = partner(give, 1)
    sent = (keep[1].astype(F32) + arrived[1].astype(F32)).astype(BF16)
    own = keep[0].astype(F32) + arrived[0].astype(F32)
    return own + partner(sent, 2).astype(F32), sent


def everywhere_order(sources):
    seq = lax.axis_index("seq")
    return jnp.stack([s * 4 + (seq ^ bit) for s in sources for bit in range(4)]).astype(jnp.int32)


VMEM_LIMIT = 56 * 2**20
SMEM = pl.BlockSpec(memory_space=pltpu.SMEM)
VMEM = pl.BlockSpec(memory_space=pltpu.VMEM)


def call(kernel, name, flops=0, moved=0, **options):
    return pl.pallas_call(
        kernel,
        compiler_params=pltpu.CompilerParams(vmem_limit_bytes=VMEM_LIMIT),
        cost_estimate=pl.CostEstimate(flops=0, bytes_accessed=0, transcendentals=0),
        name=name,
        **options,
    )


def shape(dims, dtype):
    return jax.ShapeDtypeStruct(dims, dtype)


def fixed(*dims):
    return pl.BlockSpec(dims, lambda *_: (0,) * len(dims))


def columns_kernel(n_dp, gate_ref, up_ref, *out_refs):
    size = gate_ref.shape[1] // (4 * n_dp)
    for half, out in enumerate(out_refs):
        for m, ref in enumerate((gate_ref, up_ref)):
            for q in range(n_dp // 2):
                place = (m * (n_dp // 2) + q) * size
                for j in range(4):
                    start = ((half * (n_dp // 2) + q) * 4 + j) * size
                    out[j, :, place : place + size] = ref[:, start : start + size]


def columns_for_seq(gate, up, n_dp):
    rows, total = gate.shape
    return call(
        functools.partial(columns_kernel, n_dp),
        "columns",
        moved=8 * rows * total,
        in_specs=[VMEM] * 2,
        out_shape=[shape((4, rows, total // 4), BF16)] * 2,
    )(gate, up)


ANY = pl.BlockSpec(memory_space=pl.ANY)


def place_kernel(sources_ref, *refs):
    pieces, (out_ref, sems) = refs[:-2], refs[-2:]
    copies = []
    for i, piece in enumerate(pieces):
        rows = piece.shape[0]
        start = pl.multiple_of(sources_ref[i] * rows, rows)
        copies.append(pltpu.make_async_copy(piece, out_ref.at[pl.ds(start, rows)], sems.at[i]))
    for copy in copies:
        copy.start()
    for copy in copies:
        copy.wait()


def finish_kernel(source_ref, whole_ref, top_ref, bottom_ref, out_ref, sems):
    rows = top_ref.shape[0]
    copies = []
    for i, piece in enumerate((top_ref, bottom_ref)):
        start = pl.multiple_of(source_ref[0] * (2 * rows), 2 * rows) + i * rows
        copies.append(pltpu.make_async_copy(piece, out_ref.at[pl.ds(start, rows)], sems.at[i]))
    for copy in copies:
        copy.start()
    for copy in copies:
        copy.wait()


def assemble(pieces, sources):
    rows, columns = pieces[0].shape
    most = len(pieces) - 1
    whole = shape(((most + 1) * rows, columns), BF16)
    begun = call(
        place_kernel,
        "place",
        moved=4 * most * rows * columns,
        in_specs=[SMEM] + [VMEM] * most,
        out_specs=ANY,
        out_shape=whole,
        scratch_shapes=[pltpu.SemaphoreType.DMA((most,))],
    )(jnp.stack(sources[:-1]), *pieces[:-1])
    return call(
        finish_kernel,
        "finish",
        moved=4 * rows * columns,
        in_specs=[SMEM, ANY] + [VMEM] * 2,
        out_specs=ANY,
        out_shape=whole,
        scratch_shapes=[pltpu.SemaphoreType.DMA((2,))],
        input_output_aliases={1: 0},
    )(sources[-1][None], begun, *pieces[-1])


def gather_rows(order_ref, source_ref, target_ref, rows):
    total = source_ref.shape[0]
    wide = min(256, total)
    each = wide // rows
    for i in range(total // wide):
        blocks = []
        for j in range(each):
            start = pl.multiple_of(order_ref[i * each + j] * rows, rows)
            blocks.append(source_ref[pl.ds(start, rows), :])
        target_ref[:, i * wide : (i + 1) * wide] = jnp.concatenate(blocks, axis=0).T


def qkv_kernel(order_ref, normed_ref, inner_ref, b_ref, *refs):
    pieces, (out_ref, left_ref) = refs[:-2], refs[-2:]

    @pl.when(pl.program_id(0) == 0)
    def _():
        gather_rows(order_ref, normed_ref, left_ref, pieces[0].shape[0])

    width = pieces[0].shape[1]
    step = 512
    for c in range(0, width, step):
        right = jnp.concatenate([p[:, c : c + step] for p in pieces], axis=0)
        sums = contract(left_ref[...], right, 1, 0)
        sums = sums + contract(inner_ref[...], b_ref[:, c : c + step], 1, 0)
        out_ref[c : c + step, :] = sums.T


def project_in(order, normed_t, inner, b_in, pieces):
    width, tokens = normed_t.shape
    total = b_in.shape[1]
    step = 1024
    rows = pieces[0].shape[0]
    return call(
        qkv_kernel,
        "project_in",
        flops=2 * width * tokens * total,
        moved=2 * width * total,
        grid=(total // step,),
        in_specs=[
            SMEM,
            fixed(width, tokens),
            fixed(*inner.shape),
            pl.BlockSpec((b_in.shape[0], step), lambda c: (0, c)),
        ]
        + [pl.BlockSpec((rows, step), lambda c: (0, c))] * len(pieces),
        out_specs=pl.BlockSpec((step, tokens), lambda c: (c, 0)),
        out_shape=shape((total, tokens), F32),
        scratch_shapes=[pltpu.VMEM((tokens, width), BF16)],
    )(order, normed_t, inner, b_in, *pieces)


def out_kernel(order_ref, mixed_ref, inner_ref, b_ref, tokens_ref, valid_ref, gain_ref, *refs):
    pieces, (hidden_ref, normed_ref, left_ref) = refs[:-3], refs[-3:]
    c = pl.program_id(0)

    @pl.when(c == 0)
    def _():
        gather_rows(order_ref, mixed_ref, left_ref, pieces[0].shape[0])

    width = pieces[0].shape[1]
    right = jnp.concatenate([p[...] for p in pieces], axis=0)
    sums = contract(left_ref[...], right, 1, 0) + contract(inner_ref[...], b_ref[...], 0, 0)
    sums = tokens_ref[...].astype(F32) + valid_ref[...] * sums
    hidden_ref[:, pl.ds(pl.multiple_of(c * width, width), width)] = sums

    @pl.when(c == pl.num_programs(0) - 1)
    def _():
        hidden = hidden_ref[...]
        normed_ref[...] = rms_scale(hidden, gain_ref[...]).astype(BF16)


def project_out(order, mixed, inner, bo, tokens, valid, gain, pieces):
    features, block = mixed.shape
    width = tokens.shape[1]
    step = 1024
    rows = pieces[0].shape[0]
    skip = (pieces[0].shape[1] - width) // step
    return call(
        out_kernel,
        "project_out",
        flops=2 * features * block * width,
        moved=2 * features * width,
        grid=(width // step,),
        in_specs=[
            SMEM,
            fixed(features, block),
            fixed(*inner.shape),
            pl.BlockSpec((RANK, step), lambda c: (0, c)),
            pl.BlockSpec((block, step), lambda c: (0, c)),
            fixed(block, 1),
            fixed(1, width),
        ]
        + [pl.BlockSpec((rows, step), lambda c: (0, c + skip))] * len(pieces),
        out_specs=[fixed(block, width), fixed(block, width)],
        out_shape=[shape((block, width), F32), shape((block, width), BF16)],
        scratch_shapes=[pltpu.VMEM((block, features), BF16)],
    )(order, mixed, inner, bo, tokens, valid, gain, *pieces)


def scatter_products(order_ref, pieces, right, sums_ref, form):
    rows = pieces[0].shape[0]
    each = max(1, 256 // rows)
    for i in range(0, len(pieces), each):
        left = jnp.concatenate([p[...] for p in pieces[i : i + each]], axis=0)
        product = contract(left, right, 1, form)
        for j in range(each):
            start = pl.multiple_of(order_ref[i + j] * rows, rows)
            sums_ref[pl.ds(start, rows), :] += product[j * rows : (j + 1) * rows]


def out_back_kernel(order_ref, grad_ref, a_ref, inner_ref, *refs):
    pieces, (out_ref, sums_ref) = refs[:-2], refs[-2:]
    c = pl.program_id(0)

    @pl.when(c == 0)
    def _():
        sums_ref[...] = contract(a_ref[...], inner_ref[...], 0, 1)

    scatter_products(order_ref, pieces, grad_ref[...], sums_ref, 1)

    @pl.when(c == pl.num_programs(0) - 1)
    def _():
        out_ref[...] = sums_ref[...].astype(BF16)


def project_out_back(order, grad, ao, d_inner, pieces):
    block, width = grad.shape
    features = ao.shape[1]
    step = 1024
    rows = pieces[0].shape[0]
    skip = (pieces[0].shape[1] - width) // step
    return call(
        out_back_kernel,
        "project_out_back",
        flops=2 * features * block * width,
        moved=2 * features * width,
        grid=(width // step,),
        in_specs=[
            SMEM,
            pl.BlockSpec((block, step), lambda c: (0, c)),
            fixed(*ao.shape),
            fixed(*d_inner.shape),
        ]
        + [pl.BlockSpec((rows, step), lambda c: (0, c + skip))] * len(pieces),
        out_specs=fixed(features, block),
        out_shape=shape((features, block), BF16),
        scratch_shapes=[pltpu.VMEM((features, block), F32)],
    )(order, grad, ao, d_inner, *pieces)


def in_back_kernel(order_ref, grad_ref, a_ref, inner_ref, tokens_ref, gain_ref, base_ref, *refs):
    pieces, (out_ref, sums_ref, turned_ref) = refs[:-3], refs[-3:]
    c = pl.program_id(0)

    @pl.when(c == 0)
    def _():
        sums_ref[...] = contract(a_ref[...], inner_ref[...], 0, 0)

    scatter_products(order_ref, pieces, grad_ref[...], sums_ref, 0)

    @pl.when(c == pl.num_programs(0) - 1)
    def _():
        size = sums_ref.shape[1]
        for i in range(0, sums_ref.shape[0], size):
            turned_ref[:, i : i + size] = sums_ref[i : i + size, :].T
        inputs = tokens_ref[...].astype(F32)
        grad = turned_ref[...] * gain_ref[...]
        scale = lax.rsqrt(jnp.mean(inputs * inputs, axis=-1, keepdims=True) + EPS)
        along = jnp.mean(inputs * grad, axis=-1, keepdims=True) * scale * scale
        out_ref[...] = (base_ref[...] + scale * (grad - inputs * along)).astype(BF16)


def project_in_back(order, d_linear, a_in, d_inner, tokens, gain, base, pieces):
    total, block = d_linear.shape
    width = tokens.shape[1]
    step = 1024
    rows = pieces[0].shape[0]
    return call(
        in_back_kernel,
        "project_in_back",
        flops=2 * total * block * width,
        moved=2 * total * width,
        grid=(total // step,),
        in_specs=[
            SMEM,
            pl.BlockSpec((step, block), lambda c: (c, 0)),
            fixed(*a_in.shape),
            fixed(*d_inner.shape),
            fixed(block, width),
            fixed(1, width),
            fixed(block, width),
        ]
        + [pl.BlockSpec((rows, step), lambda c: (0, c))] * len(pieces),
        out_specs=fixed(block, width),
        out_shape=shape((block, width), BF16),
        scratch_shapes=[pltpu.VMEM((width, block), F32), pltpu.VMEM((block, width), F32)],
    )(order, d_linear, a_in, d_inner, tokens, gain, base, *pieces)


def gather_tokens(refs, whole_ref):
    block = refs[0].shape[0]
    for i, ref in enumerate(refs):
        whole_ref[i * block : (i + 1) * block, :] = ref[...]


def lower_back_kernel(g0, g1, g2, g3, weight_ref, b_ref, a_ref, out_ref, inner_ref, whole_ref):
    @pl.when(pl.program_id(0) == 0)
    def _():
        gather_tokens((g0, g1, g2, g3), whole_ref)
        inner_ref[...] = contract(whole_ref[...], b_ref[...], 1, 1).astype(BF16)

    sums = contract(whole_ref[...], weight_ref[...], 1, 1)
    out_ref[...] = (sums + contract(inner_ref[...], a_ref[...], 1, 0)).astype(BF16)


def lower_back(grads, weight, bd, ad):
    block, width = grads[0].shape
    units = weight.shape[0]
    step = 256
    tokens = 4 * block
    return call(
        lower_back_kernel,
        "lower_back",
        flops=2 * tokens * width * units,
        moved=2 * width * units,
        grid=(units // step,),
        in_specs=[fixed(block, width)] * 4
        + [
            pl.BlockSpec((step, width), lambda j: (j, 0)),
            fixed(RANK, width),
            pl.BlockSpec((RANK, step), lambda j: (0, j)),
        ],
        out_specs=[pl.BlockSpec((tokens, step), lambda j: (0, j)), fixed(tokens, RANK)],
        out_shape=[shape((tokens, units), BF16), shape((tokens, RANK), BF16)],
        scratch_shapes=[pltpu.VMEM((tokens, width), BF16)],
    )(*grads, weight, bd, ad)


def tokens_kernel(n0, n1, n2, n3, a_ref, whole_ref, low_ref):
    gather_tokens((n0, n1, n2, n3), whole_ref)
    low_ref[...] = contract(whole_ref[...], a_ref[...], 1, 1).astype(BF16)


def all_tokens(normed, a_gu):
    block, width = normed[0].shape
    return call(
        tokens_kernel,
        "all_tokens",
        flops=16 * block * width * RANK,
        moved=16 * block * width,
        out_shape=[shape((4 * block, width), BF16), shape((4 * block, 2 * RANK), BF16)],
    )(*normed, a_gu)


def units_kernel(
    whole_ref,
    low_ref,
    gate_ref,
    up_ref,
    bg_ref,
    bu_ref,
    ad_ref,
    d_act_ref,
    act_ref,
    dg_ref,
    du_ref,
    inner_ref,
):
    @pl.when(pl.program_id(0) == 0)
    def _():
        inner_ref[...] = jnp.zeros(inner_ref.shape, F32)

    low_gate, low_up = low_ref[:, :RANK], low_ref[:, RANK:]
    gate = contract(whole_ref[...], gate_ref[...], 1, 0) + contract(low_gate, bg_ref[...], 1, 0)
    up = contract(whole_ref[...], up_ref[...], 1, 0) + contract(low_up, bu_ref[...], 1, 0)
    d_act = d_act_ref[...].astype(F32)
    sig = jax.nn.sigmoid(gate)
    silu = gate * sig
    act = (silu * up).astype(BF16)
    d_gate = (d_act * up * (sig + silu * (1.0 - sig))).astype(BF16)
    d_up = (d_act * silu).astype(BF16)
    act_ref[...] = act
    dg_ref[...] = d_gate
    du_ref[...] = d_up
    inner_ref[:, :RANK] += contract(d_gate, bg_ref[...], 1, 1)
    inner_ref[:, RANK : 2 * RANK] += contract(d_up, bu_ref[...], 1, 1)
    inner_ref[:, 2 * RANK :] += contract(act, ad_ref[...], 1, 1)


def units(part, whole, low, both, bg, bu, ad, d_act):
    tokens, width = whole.shape
    half = both.shape[1] // 2
    step = 256
    steps = half // step
    here = pl.BlockSpec((RANK, step), lambda j: (0, part * steps + j))
    tile = pl.BlockSpec((tokens, step), lambda j: (0, j))
    return call(
        units_kernel,
        "units",
        flops=4 * tokens * width * half,
        moved=4 * width * half,
        grid=(steps,),
        in_specs=[
            fixed(tokens, width),
            fixed(tokens, 2 * RANK),
            pl.BlockSpec((width, step), lambda j: (0, j)),
            pl.BlockSpec((width, step), lambda j: (0, steps + j)),
            here,
            here,
            here,
            pl.BlockSpec((tokens, step), lambda j: (0, part * steps + j)),
        ],
        out_specs=[tile] * 3 + [fixed(tokens, 3 * RANK)],
        out_shape=[shape((tokens, half), BF16)] * 3 + [shape((tokens, 3 * RANK), F32)],
    )(whole, low, both, both, bg, bu, ad, d_act)


def units_grads_kernel(low_ref, d_down_ref, act_ref, dg_ref, du_ref, gbg_ref, gbu_ref, gad_ref):
    gbg_ref[...] = contract(low_ref[:, :RANK], dg_ref[...], 0, 0)
    gbu_ref[...] = contract(low_ref[:, RANK:], du_ref[...], 0, 0)
    gad_ref[...] = contract(d_down_ref[...], act_ref[...], 0, 0)


def units_grads(low, d_down, act, d_gate, d_up):
    tokens, half = act.shape
    step = 256
    tile = pl.BlockSpec((tokens, step), lambda j: (0, j))
    thin = pl.BlockSpec((RANK, step), lambda j: (0, j))
    return call(
        units_grads_kernel,
        "units_grads",
        flops=6 * tokens * half * RANK,
        moved=6 * tokens * half,
        grid=(half // step,),
        in_specs=[fixed(tokens, 2 * RANK), fixed(tokens, RANK), tile, tile, tile],
        out_specs=[thin] * 3,
        out_shape=[shape((RANK, half), F32)] * 3,
    )(low, d_down, act, d_gate, d_up)


def units_back_first_kernel(g_ref, u_ref, w_ref, out_ref):
    half = g_ref.shape[1]
    sums = contract(g_ref[...], w_ref[:, :half], 1, 1) + contract(u_ref[...], w_ref[:, half:], 1, 1)
    out_ref[...] = sums.astype(BF16)


def units_back_first(d_gate, d_up, both):
    tokens, half = d_gate.shape
    width = both.shape[0]
    step = 256
    return call(
        units_back_first_kernel,
        "units_back_first",
        flops=4 * tokens * half * width,
        moved=4 * half * width,
        grid=(width // step,),
        in_specs=[fixed(tokens, half)] * 2 + [pl.BlockSpec((step, 2 * half), lambda n: (n, 0))],
        out_specs=pl.BlockSpec((tokens, step), lambda n: (0, n)),
        out_shape=shape((tokens, width), BF16),
    )(d_gate, d_up, both)


def units_back_kernel(first_ref, g_ref, u_ref, w_ref, low_ref, a_ref, keep_ref, give_ref):
    half = g_ref.shape[1]
    sums = first_ref[...].astype(F32) + contract(low_ref[...], a_ref[...], 1, 0)
    sums = sums + contract(g_ref[...], w_ref[:, :half], 1, 1)
    sums = sums + contract(u_ref[...], w_ref[:, half:], 1, 1)
    sums = sums.astype(BF16)
    block = keep_ref.shape[1]
    keep_ref[0] = sums[:block]
    give_ref[0] = sums[block : 2 * block]
    keep_ref[1] = sums[2 * block : 3 * block]
    give_ref[1] = sums[3 * block :]


def units_back(part, parts, first, d_gate, d_up, both, low, a_gu):
    tokens, half = d_gate.shape
    width = both.shape[0]
    step = 256
    steps = width // parts // step
    place = lambda n: part * steps + n
    out = pl.BlockSpec((2, tokens // 4, step), lambda n: (0, 0, n))
    return call(
        units_back_kernel,
        "units_back",
        flops=4 * tokens * half * width // parts,
        moved=4 * half * width // parts,
        grid=(steps,),
        in_specs=[
            pl.BlockSpec((tokens, step), lambda n: (0, place(n))),
            fixed(tokens, half),
            fixed(tokens, half),
            pl.BlockSpec((step, 2 * half), lambda n: (place(n), 0)),
            fixed(tokens, 2 * RANK),
            pl.BlockSpec((2 * RANK, step), lambda n: (0, place(n))),
        ],
        out_specs=[out, out],
        out_shape=[shape((2, tokens // 4, width // parts), BF16)] * 2,
    )(first, d_gate, d_up, both, low, a_gu)


def lower_kernel(
    aa_ref, ab_ref, weight_ref, low_ref, b_ref, whole_ref, lowgu_ref, g0, g1, g2, g3, keep_ref, give_ref, grad_ref, grad_gu_ref
):
    half = aa_ref.shape[1]
    sums = contract(low_ref[...], b_ref[...], 1, 0)
    sums = sums + contract(aa_ref[...], weight_ref[:half], 1, 0)
    sums = sums + contract(ab_ref[...], weight_ref[half:], 1, 0)
    sums = sums.astype(BF16)
    block = g0.shape[0]
    low = low_ref[...]
    grad = jnp.zeros(grad_ref.shape, F32)
    for i, g in enumerate((g0, g1, g2, g3)):
        out = give_ref if i % 2 else keep_ref
        out[i // 2] = sums[i * block : (i + 1) * block]
        grad = grad + contract(low[i * block : (i + 1) * block], g[...], 0, 0)
    grad_ref[...] = grad
    grad_gu_ref[...] = contract(lowgu_ref[...], whole_ref[...], 0, 0)


def lower(act_a, act_b, weight, low, bd, grads, whole, low_gu):
    block, width = grads[0].shape
    tokens, half = act_a.shape
    step = 256
    tile = pl.BlockSpec((block, step), lambda n: (0, n))
    thin = pl.BlockSpec((RANK, step), lambda n: (0, n))
    out = pl.BlockSpec((2, block, step), lambda n: (0, 0, n))
    return call(
        lower_kernel,
        "lower",
        flops=4 * tokens * half * width,
        moved=4 * half * width,
        grid=(width // step,),
        in_specs=[
            fixed(tokens, half),
            fixed(tokens, half),
            pl.BlockSpec((2 * half, step), lambda n: (0, n)),
            fixed(tokens, RANK),
            thin,
            pl.BlockSpec((tokens, step), lambda n: (0, n)),
            fixed(tokens, 2 * RANK),
        ]
        + [tile] * 4,
        out_specs=[out, out, thin, pl.BlockSpec((2 * RANK, step), lambda n: (0, n))],
        out_shape=[shape((2, block, width), BF16)] * 2
        + [shape((RANK, width), F32), shape((2 * RANK, width), F32)],
    )(act_a, act_b, weight, low, bd, whole, low_gu, *grads)


def wide_heads(ref):
    return jnp.concatenate([ref[h * HD : (h + 1) * HD] for h in range(GROUP)], axis=1)


def attend_kernel(seq_ref, limit_ref, q_ref, kv0, kv1, kv2, kv3, o_ref, e_ref, r_ref):
    queries = wide_heads(q_ref)
    limit = limit_ref[...]
    total = jnp.zeros(limit.shape, F32)
    mixed = jnp.zeros(queries.shape, F32)
    for bit, ref in enumerate((kv0, kv1, kv2, kv3)):
        block = ref.shape[2]
        scores = contract(ref[0, :HD], queries, 0, 0)
        places = (seq_ref[0] ^ bit) * block + lax.broadcasted_iota(jnp.int32, scores.shape, 0)
        raised = jnp.where(places <= limit, jnp.exp(scores), 0.0)
        total = total + jnp.sum(raised, axis=0, keepdims=True)
        low = raised.astype(BF16)
        e_ref[0, bit] = low
        mixed = mixed + contract(ref[0, HD:], low, 1, 0)
    inverse = 1.0 / total
    r_ref[0] = inverse
    mixed = (mixed * inverse).astype(BF16)
    width = q_ref.shape[1]
    for h in range(GROUP):
        o_ref[h * HD : (h + 1) * HD] = mixed[:, h * width : (h + 1) * width]


def attend(seq, limit, queries, keys_values):
    block = keys_values[0].shape[2]
    width = queries.shape[1]
    wide = GROUP * width
    head_rows = pl.BlockSpec((GROUP * HD, width), lambda g: (g, 0))
    return call(
        attend_kernel,
        "attend",
        flops=16 * H * width * 4 * block * HD,
        moved=2 * KV * 4 * block * wide,
        grid=(KV,),
        in_specs=[SMEM, fixed(1, wide), head_rows]
        + [pl.BlockSpec((1, 2 * HD, block), lambda g: (g, 0, 0))] * 4,
        out_specs=[
            head_rows,
            pl.BlockSpec((1, 4, block, wide), lambda g: (g, 0, 0, 0)),
            pl.BlockSpec((1, 1, wide), lambda g: (g, 0, 0)),
        ],
        out_shape=[
            shape(queries.shape, BF16),
            shape((KV, 4, block, wide), BF16),
            shape((KV, 1, wide), F32),
        ],
    )(seq[None], limit, queries, *keys_values)


def attend_back_kernel(q_ref, kv0, kv1, kv2, kv3, e_ref, r_ref, o_ref, do_ref, dq_ref, keep_ref, give_ref):
    width = q_ref.shape[1]
    queries = wide_heads(q_ref)
    grads = wide_heads(do_ref).astype(F32) * r_ref[0]
    dots = jnp.sum(grads * wide_heads(o_ref).astype(F32), axis=0, keepdims=True)
    grads = grads.astype(BF16)
    d_queries = jnp.zeros(queries.shape, F32)
    for bit, ref in enumerate((kv0, kv1, kv2, kv3)):
        out = give_ref if bit % 2 else keep_ref
        raised = e_ref[0, bit]
        d_probs = contract(ref[0, HD:], grads, 0, 0)
        d_scores = (raised.astype(F32) * (d_probs - dots)).astype(BF16)
        d_queries = d_queries + contract(ref[0, :HD], d_scores, 1, 0)
        out[bit // 2, 0, :HD] = contract(queries, d_scores, 1, 1).astype(BF16)
        out[bit // 2, 0, HD:] = contract(grads, raised, 1, 1).astype(BF16)
    for h in range(GROUP):
        dq_ref[h * HD : (h + 1) * HD] = d_queries[:, h * width : (h + 1) * width]


def attend_back(first, count, queries, keys_values, raised, inverse, mixed, d_mixed):
    block = keys_values[0].shape[2]
    width = queries.shape[1]
    wide = GROUP * width
    head_rows = pl.BlockSpec((GROUP * HD, width), lambda g: (first + g, 0))
    shares = pl.BlockSpec((2, 1, 2 * HD, block), lambda g: (0, g, 0, 0))
    return call(
        attend_back_kernel,
        "attend_back",
        flops=32 * count * GROUP * width * 4 * block * HD,
        moved=2 * count * 4 * block * wide,
        grid=(count,),
        in_specs=[head_rows]
        + [pl.BlockSpec((1, 2 * HD, block), lambda g: (first + g, 0, 0))] * 4
        + [
            pl.BlockSpec((1, 4, block, wide), lambda g: (first + g, 0, 0, 0)),
            pl.BlockSpec((1, 1, wide), lambda g: (first + g, 0, 0)),
            head_rows,
            head_rows,
        ],
        out_specs=[pl.BlockSpec((GROUP * HD, width), lambda g: (g, 0)), shares, shares],
        out_shape=[
            shape((count * GROUP * HD, width), F32),
            shape((2, count, 2 * HD, block), BF16),
            shape((2, count, 2 * HD, block), BF16),
        ],
    )(queries, *keys_values, raised, inverse, mixed, d_mixed)


def pick_kernel(ids_ref, *refs):
    out_ref = refs[-1]
    for d in range(out_ref.shape[0]):
        parts = [ref[ids_ref[d]] for ref in refs[:-1]]
        out_ref[d] = jnp.concatenate(parts, axis=1)


def pick(ids, stacks):
    columns = sum(stack.shape[2] for stack in stacks)
    n_dp = ids.shape[0]
    return call(
        pick_kernel,
        "pick",
        moved=4 * n_dp * RANK * columns,
        in_specs=[SMEM] + [VMEM] * len(stacks),
        out_shape=shape((n_dp, RANK, columns), BF16),
    )(ids, *stacks)


def spread_kernel(widths, seq_ref, mine_ref, p1, p2, p3, *refs):
    (in_ref, grow_ref, ao_ref, bo_ref, gu_ref, bd_ref, bg_ref, bu_ref, ad_ref, all_ref) = refs
    local, each, thin = widths
    n_dp = mine_ref.shape[0]
    seq = seq_ref[0]
    base = 3 * local
    all_ref[seq] = mine_ref[:, :, base:]
    for bit, ref in ((1, p1), (2, p2), (3, p3)):
        all_ref[seq ^ bit] = ref[...]

    def factor(start, width):
        parts = [all_ref[j, d, :, start : start + width] for d in range(n_dp) for j in range(4)]
        return jnp.concatenate(parts, axis=1)

    wide = lambda m: factor(m * each, each)
    for i in range(3):
        in_ref[i * RANK : (i + 1) * RANK] = wide(i)
    grow_ref[...] = jnp.zeros(grow_ref.shape, BF16)
    n_query, n_key = 4 * n_dp * each, 4 * n_dp * thin
    grow_ref[:RANK, :n_query] = wide(3)
    for i in range(2):
        start = n_query + i * n_key
        grow_ref[(i + 1) * RANK : (i + 2) * RANK, start : start + n_key] = factor(9 * each + i * thin, thin)
    ao_ref[...] = wide(4)
    bo_ref[...] = wide(5)
    gu_ref[:RANK] = wide(6)
    gu_ref[RANK:] = wide(7)
    bd_ref[...] = wide(8)
    for i, ref in enumerate((bg_ref, bu_ref, ad_ref)):
        for d in range(n_dp):
            ref[:, d * local : (d + 1) * local] = mine_ref[d, :, i * local : (i + 1) * local]


def spread(seq, mine, others, widths):
    local, each, thin = widths
    n_dp = mine.shape[0]
    total = 4 * n_dp * each
    grown = total + 8 * n_dp * thin
    rows = [(3 * RANK, total), (3 * RANK, grown), (RANK, total), (RANK, total), (2 * RANK, total), (RANK, total)]
    rows += [(RANK, n_dp * local)] * 3
    return call(
        functools.partial(spread_kernel, widths),
        "spread",
        moved=4 * 4 * mine.size,
        in_specs=[SMEM] + [VMEM] * 4,
        out_shape=[shape(dims, BF16) for dims in rows],
        scratch_shapes=[pltpu.VMEM((4,) + others[0].shape, BF16)],
    )(seq[None], mine, *others)


def pack_kernel(n_dp, count, seq_ref, *refs):
    ins, (keep_ref, give_ref, all_ref) = refs[:count], refs[count:]
    for d in range(n_dp):
        for j in range(4):
            parts = []
            for ref in ins:
                each = ref.shape[1] // (4 * n_dp)
                at = (d * 4 + j) * each
                parts.append(ref[:, at : at + each])
            all_ref[j, d] = jnp.concatenate(parts, axis=1)
    seq = seq_ref[0]
    for bit in range(4):
        out = give_ref if bit % 2 else keep_ref
        out[bit // 2] = all_ref[seq ^ bit]


def pack(seq, grads, n_dp):
    columns = sum(g.shape[1] for g in grads) // (4 * n_dp)
    dims = (n_dp, RANK, columns)
    return call(
        functools.partial(pack_kernel, n_dp, len(grads)),
        "pack",
        moved=16 * n_dp * RANK * columns * 4,
        in_specs=[SMEM] + [VMEM] * len(grads),
        out_shape=[shape((2,) + dims, F32)] * 2,
        scratch_shapes=[pltpu.VMEM((4,) + dims, F32)],
    )(seq[None], *grads)


def sort_kernel(widths, ids_ref, came_ref, *out_refs):
    came = [came_ref[d] for d in range(came_ref.shape[0])]
    for a in range(ADAPT):
        total = jnp.zeros(came[0].shape, F32)
        for d, value in enumerate(came):
            total = total + jnp.where(ids_ref[d] == a, value, 0.0)
        at = 0
        for ref, width in zip(out_refs, widths):
            ref[a] = total[:, at : at + width]
            at += width


def sort(ids, came, widths):
    outs = call(
        functools.partial(sort_kernel, widths),
        "sort",
        moved=8 * came.size,
        in_specs=[SMEM, VMEM],
        out_shape=[shape((ADAPT, RANK, w), F32) for w in widths],
    )(ids, came)
    return [o.transpose(0, 2, 1) for o in outs]


def shards(
    tokens,
    cotangent,
    lengths,
    adapter_ids,
    attn_gain,
    query_gain,
    key_gain,
    ffn_gain,
    w_query,
    w_key,
    w_value,
    w_out,
    gate_weight,
    w_up,
    w_down,
    a_query,
    b_query,
    a_key,
    b_key,
    a_value,
    b_value,
    a_out,
    b_out,
    a_gate,
    b_gate,
    a_up,
    b_up,
    a_down,
    b_down,
):
    n_dp = lax.axis_size("dp")
    seq = lax.axis_index("seq")
    _, block, width = tokens.shape
    length = lengths[0]
    positions = seq * block + jnp.arange(block)
    valid = (positions < length).astype(F32)[:, None]
    sources = ring_sources()
    clock = Clock()
    n_query, n_key = H * HD, KV * HD
    local, each, thin = b_gate.shape[1], a_query.shape[1], b_key.shape[1]
    widths = (local, each, thin)

    attn = Ring(jnp.concatenate([w_query, w_key, w_value, w_out], axis=1))
    sides, acrosses, corners = [], [], []

    def share(piece):
        sides.append(partner(clock(piece), 1))
        acrosses.append(partner(clock(piece), 2))

    def pass_on(count):
        for _ in range(count):
            corners.append(partner(clock(acrosses[len(corners)]), 1))

    came = attn.step(clock)
    share(attn.pieces[0])
    ids = lax.all_to_all(
        jnp.broadcast_to(adapter_ids[None], (n_dp, 128)), "dp", 0, 0, tiled=True
    )[:, 0]
    slots_a, slots_b = columns_for_seq(gate_weight, w_up, n_dp)
    inputs = tokens[0].astype(F32)
    normed = rms_scale(inputs, attn_gain).astype(BF16)
    cot = cotangent[0].astype(F32)
    grad_out = (valid * cot).astype(BF16)
    stacks = (b_gate, b_up, a_down, a_query, a_key, a_value, b_query, a_out, b_out)
    stacks += (a_gate, a_up, b_down, b_key, b_value)
    ids = after(ids, slots_a, normed, grad_out)
    sent = pick(ids, [m.transpose(0, 2, 1) for m in stacks])
    clock.tick(came, slots_a, slots_b, normed, grad_out, sent)

    came = attn.step(clock)
    share(attn.pieces[1])
    share(attn.pieces[2])
    mine = lax.all_to_all(clock(sent), "dp", 0, 0, tiled=True)
    normed_t = clock(normed).T
    clock.tick(came, normed_t)

    came = attn.step(clock)
    share(attn.pieces[3])
    share(attn.pieces[4])
    swap = lambda slots: lax.all_to_all(clock(slots), "seq", 0, 0, tiled=True)
    swapped_a = swap(slots_a)
    mine = clock(mine)
    others = seq_pieces(mine[..., 3 * local :])[1:]
    pass_on(1)
    clock.tick(came)
    while len(attn.pieces) < n_dp - 1:
        came = attn.step(clock)
        share(attn.pieces[-4])
        share(attn.pieces[-3])
        clock.tick(came)

    came = attn.step(clock)
    lower_ring = Ring(w_down)
    belt = Conveyor(clock, lower_ring, [lambda: clock(swapped_a).reshape(-1, width), lambda: clock(swapped_b).reshape(-1, width)])
    share(attn.pieces[-3])
    share(attn.pieces[-2])
    clock.tick(came)
    attn.pieces.append(jnp.concatenate(attn.pieces.pop(), axis=0))
    share(attn.pieces[-1])
    pass_on(3)
    belt.advance()
    ring_a = belt.push()
    swapped_b = swap(slots_b)
    pass_on(2)
    order = everywhere_order(sources)
    a_in, b_in, ao, bo, a_gu, bd, bg, bu, ad = spread(seq, *clock((mine, others)), widths)
    inner = contract(clock(normed), a_in, 1, 1).astype(BF16)
    belt.advance(inner)
    pass_on(2)
    belt.advance()
    pass_on(len(acrosses) - len(corners))
    attn_pieces = []
    for group in zip(attn.pieces, sides, acrosses, corners):
        attn_pieces += group

    linear = project_in(order, normed_t, inner, b_in, attn_pieces)
    query_lin = linear[:n_query].reshape(H, HD, block)
    key_lin = linear[n_query : n_query + n_key].reshape(KV, HD, block)
    value_lin = linear[n_query + n_key :].reshape(KV, HD, block)
    cosine, sine = rotary_tables(positions)
    scale = HD**-0.5
    query_prep = lambda v: prepare(v, query_gain, cosine, sine)
    key_prep = lambda v: prepare(v, key_gain, cosine, sine)
    keys_values = jnp.concatenate([key_prep(key_lin), value_lin], axis=1).astype(BF16)
    belt.advance(keys_values)
    keys_values = seq_pieces(clock(keys_values))
    queries = (query_prep(clock(query_lin)) * scale).astype(BF16).reshape(n_query, block)
    limit = jnp.minimum(positions, length - 1).astype(jnp.int32)
    limit = jnp.tile(limit, GROUP)[None, :]
    belt.advance(queries)
    grads = seq_pieces(after(clock(grad_out), keys_values[0], keys_values[2]))
    mixed, raised, inverse = attend(seq, limit, clock(queries), keys_values)

    belt.until(lower_ring, mixed)
    w_lower = assemble(clock(lower_ring.pieces), sources)
    inner_out = contract(ao, clock(mixed), 1, 0).astype(BF16)
    hidden, normed_two = project_out(
        order, clock(mixed), inner_out, bo, tokens[0], valid, ffn_gain[None], attn_pieces
    )
    belt.advance(normed_two)

    n2 = seq_pieces(clock(normed_two))
    d_act, d_down = lower_back(grads, clock(w_lower), bd, ad)
    belt.until(ring_a, d_act)
    ring_b = belt.going[-1][1]
    n2, low_n2 = all_tokens(clock(n2), a_gu)
    both_a = assemble(clock(ring_a.pieces), sources)
    act_a, dg_a, du_a, inner_a = units(0, n2, low_n2, both_a, bg, bu, ad, d_act)
    belt.advance(act_a)
    first = units_back_first(clock(dg_a), du_a, both_a)
    belt.advance(first)
    gbg_a, gbu_a, gad_a = units_grads(low_n2, d_down, clock(act_a), dg_a, du_a)
    belt.until(ring_b, gbg_a)
    both_b = assemble(clock(ring_b.pieces), sources)
    act_b, dg_b, du_b, inner_b = units(1, n2, low_n2, both_b, bg, bu, ad, d_act)
    low = (inner_a + inner_b).astype(BF16)
    low_gu, low_down = low[:, : 2 * RANK], low[:, 2 * RANK :]
    d_n2, parts = [], 2
    for part in range(parts):
        keep, give = units_back(part, parts, first, dg_b, du_b, both_b, low_gu, a_gu)
        first = after(first, keep)
        reduced, sent = seq_reduce(keep, give)
        d_n2.append(reduced)
    d_n2 = jnp.concatenate(d_n2, axis=1)

    act_b = after(act_b, sent)
    gbg_b, gbu_b, gad_b = units_grads(low_n2, d_down, act_b, dg_b, du_b)
    keep, give, grad_bd, grad_a_gu = lower(act_a, act_b, w_lower, low_down, bd, grads, n2, low_gu)
    lowered, _ = seq_reduce(keep, give)
    output = (hidden + valid * lowered).astype(BF16)

    d_hidden = cot + jax.vjp(lambda v: rms_scale(v, ffn_gain), hidden)[1](d_n2)[0]
    grad_update = (valid * d_hidden).astype(BF16)
    d_inner_out = contract(grad_update, bo, 1, 1).astype(BF16)
    d_mixed = project_out_back(order, grad_update, ao, d_inner_out, attn_pieces)
    d_queries, d_kv = [], []
    for part in range(2):
        count = KV // 2
        d_query, keep, give = attend_back(
            part * count, count, queries, keys_values, raised, inverse, mixed, d_mixed
        )
        d_kv.append(seq_reduce(keep, give)[0])
        d_queries.append(d_query)
    d_queries = jnp.concatenate(d_queries, axis=0).reshape(H, HD, block) * scale
    d_kv = jnp.concatenate(d_kv, axis=0)
    d_query_lin = jax.vjp(query_prep, query_lin)[1](d_queries)[0]
    d_key_lin = jax.vjp(key_prep, key_lin)[1](d_kv[:, :HD])[0]
    d_linear = jnp.concatenate(
        [
            d_query_lin.reshape(n_query, block),
            d_key_lin.reshape(n_key, block),
            d_kv[:, HD:].reshape(n_key, block),
        ],
        axis=0,
    ).astype(BF16)
    d_inner = contract(b_in, d_linear, 1, 0).astype(BF16)
    grad_tokens = project_in_back(
        order, d_linear, a_in, d_inner, tokens[0], attn_gain[None], d_hidden, attn_pieces
    )

    def owners(grads, alone):
        keep, give = pack(seq, grads, n_dp)
        both = keep + partner(give, 1)
        summed = both[0] + partner(both[1], 2)
        sizes = [g.shape[1] // (4 * n_dp) for g in grads]
        if alone:
            summed = jnp.concatenate([summed] + alone, axis=2)
            sizes += [g.shape[2] for g in alone]
        return sort(ids, lax.all_to_all(summed, "dp", 0, 0, tiled=True), sizes)

    grad_ao = contract(d_inner_out, mixed, 0, 1)
    grad_bo = contract(inner_out, grad_update, 1, 0)
    cat = lambda a, b: jnp.concatenate([a, b], axis=1).reshape(RANK, n_dp, -1).transpose(1, 0, 2)
    gao, gbo, gag, gau, gbd, gbg, gbu, gad = owners(
        [grad_ao, grad_bo, grad_a_gu[:RANK], grad_a_gu[RANK:], grad_bd],
        [cat(gbg_a, gbg_b), cat(gbu_a, gbu_b), cat(gad_a, gad_b)],
    )
    grad_a_in = contract(d_inner, normed, 1, 0)
    grad_b_in = contract(inner, d_linear, 0, 1)
    q_end, k_end = n_query, n_query + n_key
    gaq, gak, gav, gbq, gbk, gbv = owners(
        [
            grad_a_in[:RANK],
            grad_a_in[RANK : 2 * RANK],
            grad_a_in[2 * RANK :],
            grad_b_in[:RANK, :q_end],
            grad_b_in[RANK : 2 * RANK, q_end:k_end],
            grad_b_in[2 * RANK :, k_end:],
        ],
        [],
    )
    return (
        output[None],
        grad_tokens[None],
        gaq,
        gbq,
        gak,
        gbk,
        gav,
        gbv,
        gao,
        gbo,
        gag,
        gbg,
        gau,
        gbu,
        gad,
        gbd,
    )


def solution(mesh):
    tokens = P("dp", "seq", None)
    matrix = P(("dp", "seq"), None)
    stack = P(None, ("dp", "seq"), None)
    in_specs = (tokens, tokens, P("dp"), P("dp")) + (P(),) * 4 + (matrix,) * 7 + (stack,) * 14
    out_specs = (tokens, tokens) + (stack,) * 14
    return jax.shard_map(shards, mesh=mesh, in_specs=in_specs, out_specs=out_specs, check_vma=False)
```

time: 936 us -> 671 us (0.72)
  local copies, waits for them, and re-layouts: 243 us -> 40.1 us
  Pallas kernels: 35.7 us -> 235 us
  matrix products: 173 us -> 7.97 us
  waiting for transfers between devices: 315 us -> 252 us
  between operations: 31.5 us -> 3.86 us
  blocking collectives: 15.9 us -> 0 us
    pallas_call x2 -> x30, Pallas kernels: 35.7 us -> 235 us  [the longest x2 36.2 us: units(): call(units_kernel, 'units', flops=4 * tokens * width * half, moved=4 * wi...]
    dot_general x37 -> x8, matrix products: 173 us -> 7.97 us  [contract(): lax.dot_general(left, right, (((left_dim,), (right_dim,)), ((), ())), pre...]
    unnamed x287 -> x164, local copies, waits for them, and re-layouts: 72.5 us -> 17.5 us
    dynamic_update_slice x46 -> x0, local copies, waits for them, and re-layouts: 54.6 us -> none  [the longest x21 26.1 us: ring_gather(): lax.dynamic_update_slice(whole, piece[None], (ring_source(offset), 0, 0))]
    reshape x31 -> x3, local copies, waits for them, and re-layouts: 39.1 us -> 1.35 us  [shards(): jnp.concatenate([a, b], axis=1).reshape(RANK, n_dp, -1).transpose(1, 0, 2)]
    ppermute x40 -> x32, waiting for transfers between devices: 144 us -> 108 us  [the longest x4 47.8 us: step(): bottom = lax.ppermute(clock(self.right[half:]), 'dp', left)]
    ppermute x74 -> x50, waiting for transfers between devices: 167 us -> 142 us  [partner(): return lax.ppermute(operand, 'seq', [(i, i ^ bit) for i in range(size)])]
    all_to_all x2 -> x6, starting transfers between devices: 7.82 us -> 27.5 us  [the longest x2 8.51 us: shards(): swap = lambda slots: lax.all_to_all(clock(slots), 'seq', 0, 0, tiled=True)]
  transfers between devices with their start and end apart: 116 -> 88, of which waited for: 41 -> 34; matrix products, arithmetic and copies ran while one was open for 33% -> 8% of each run, Pallas kernels for 2% -> 26%
where the time goes in v2:
time: 671 us; the launch traced here: 659 us
  waiting for transfers between devices  252 us (38%)
  Pallas kernels  235 us (35%)
  starting transfers between devices  91.1 us (14%)
  local copies, waits for them, and re-layouts  40.1 us (6%)
  other arithmetic  29.6 us (4%)
  matrix products  7.97 us (1%)
    ppermute x50, waiting for transfers between devices, partner(): return lax.ppermute(operand, 'seq', [(i, i ^ bit) for i in range(size)])  142 us
    ppermute x4, waiting for transfers between devices, step(): bottom = lax.ppermute(clock(self.right[half:]), 'dp', left)  47.8 us
    pallas_call x2, Pallas kernels, units(): call(units_kernel, 'units', flops=4 * tokens * width * half, moved=4 * wi...  36.2 us
    ppermute x50, starting transfers between devices, partner(): return lax.ppermute(operand, 'seq', [(i, i ^ bit) for i in range(size)])  30.5 us
    ppermute x12, waiting for transfers between devices, step(): self.left = lax.ppermute(clock(self.left), 'dp', right)  30.4 us
    pallas_call x2, Pallas kernels, attend_back(): call(attend_back_kernel, 'attend_back', flops=32 * count * GROUP * width...  24.2 us
    ppermute x12, waiting for transfers between devices, step(): self.right = lax.ppermute(clock(self.right), 'dp', left)  22 us
    pallas_call x2, Pallas kernels, units_back(): call(units_back_kernel, 'units_back', flops=4 * tokens * half * width //...  18.9 us
  transfers between devices with their start and end apart: 88, of which 34 were waited for; matrix products, arithmetic and copies ran while one was open for 8% of the time, Pallas kernels for 26%

profile of v2, /device:TPU:0, one launch (start us, length us, event | category | flops | bytes accessed | tf_op | source)
XLA Modules:
  0.0 659.5 jit_solution(7010711374727775466)
XLA Ops:
  4.4 3.0 collective-permute-start.1
  8.8 6.2 all-to-all-start
  17.8 2.9 fusion.2
  22.1 3.1 columns.1
  33.3 11.0 %collective-permute-done.2.refs_12_ = bf16[64,5120]{1,0:T(8,128)(2,1)} collective-permute-done((bf16[64,5120]{1,0:T(8,128)(2,1)S(1)}, bf16[64,5120]{1,0:T(8,128)(2,1)}, u32[]{:S(2)}, u32[]{:S(2)}) %collective-permute-start.2) | collective-permute-done | bytes 655392 | tf_op jit(solution)/shard_map/ppermute | solution.py:81
  44.3 4.9 all-to-all-start.1
  50.8 2.0 collective-permute-start.4
  52.9 10.2 %collective-permute-done.15.refs_6_ = bf16[64,5120]{1,0:T(8,128)(2,1)} collective-permute-done((bf16[64,5120]{1,0:T(8,128)(2,1)S(1)}, bf16[64,5120]{1,0:T(8,128)(2,1)}, u32[]{:S(2)}, u32[]{:S(2)}) %collective-permute-start.15) | collective-permute-done | bytes 655392 | tf_op jit(solution)/shard_map/ppermute | solution.py:140
  65.6 11.5 %collective-permute-done.20.refs_10_ = bf16[64,5120]{1,0:T(8,128)(2,1)} collective-permute-done((bf16[64,5120]{1,0:T(8,128)(2,1)S(1)}, bf16[64,5120]{1,0:T(8,128)(2,1)}, u32[]{:S(2)}, u32[]{:S(2)}) %collective-permute-start.20) | collective-permute-done | bytes 655392 | tf_op jit(solution)/shard_map/ppermute | solution.py:140
  84.9 10.2 %collective-permute-done.23.refs_14_ = bf16[64,5120]{1,0:T(8,128)(2,1)} collective-permute-done((bf16[64,5120]{1,0:T(8,128)(2,1)}, bf16[64,5120]{1,0:T(8,128)(2,1)}, u32[]{:S(2)}, u32[]{:S(2)}) %collective-permute-start.23) | collective-permute-done | bytes 655392 | tf_op jit(solution)/shard_map/ppermute | solution.py:140
  96.4 9.1 %collective-permute-done.26.refs_18_ = bf16[64,5120]{1,0:T(8,128)(2,1)} collective-permute-done((bf16[64,5120]{1,0:T(8,128)(2,1)S(1)}, bf16[64,5120]{1,0:T(8,128)(2,1)}, u32[]{:S(2)}, u32[]{:S(2)}) %collective-permute-start.26) | collective-permute-done | bytes 655392 | tf_op jit(solution)/shard_map/ppermute | solution.py:140
  108.7 4.2 all-to-all-start.2
  118.5 8.5 %collective-permute-done.17 = bf16[32,5120]{1,0:T(8,128)(2,1)S(1)} collective-permute-done((bf16[32,5120]{1,0:T(8,128)(2,1)S(1)}, bf16[32,5120]{1,0:T(8,128)(2,1)S(1)}, u32[]{:S(2)}, u32[]{:S(2)}) %collective-permute-start.17) | collective-permute-done | bytes 327712 | tf_op jit(solution)/shard_map/ppermute | solution.py:87
  129.7 20.1 %collective-permute-done.32.refs_26_ = bf16[64,5120]{1,0:T(8,128)(2,1)S(1)} collective-permute-done((bf16[64,5120]{1,0:T(8,128)(2,1)S(1)}, bf16[64,5120]{1,0:T(8,128)(2,1)S(1)}, u32[]{:S(2)}, u32[]{:S(2)}) %collective-permute-start.32) | collective-permute-done | bytes 655392 | tf_op jit(solution)/shard_map/ppermute | solution.py:140
  150.3 9.4 %collective-permute-done.37.refs_30_ = bf16[64,5120]{1,0:T(8,128)(2,1)S(1)} collective-permute-done((bf16[64,5120]{1,0:T(8,128)(2,1)S(1)}, bf16[64,5120]{1,0:T(8,128)(2,1)S(1)}, u32[]{:S(2)}, u32[]{:S(2)}) %collective-permute-start.37) | collective-permute-done | bytes 655392 | tf_op jit(solution)/shard_map/ppermute | solution.py:140
  163.9 2.3 spread.1
  166.2 2.3 convolution_convert_fusion.inner_ref
  169.1 18.2 %collective-permute-done.42.refs_2_ = bf16[256,2048]{1,0:T(8,128)(2,1)} collective-permute-done((bf16[256,2048]{1,0:T(8,128)(2,1)}, bf16[256,2048]{1,0:T(8,128)(2,1)}, u32[]{:S(2)}, u32[]{:S(2)}) %collective-permute-start.42) | collective-permute-done | bytes 1048608 | tf_op jit(solution)/shard_map/ppermute | solution.py:82
  190.4 2.3 copy.88.normed_ref
  194.8 10.1 %project_in.1 = f32[3072,256]{1,0:T(8,128)} custom-call(s32[32]{0:T(128)} %stack.171.order_ref, bf16[2048,256]{1,0:T(8,128)(2,1)} %copy.88.normed_ref, bf16[256,48]{1,0:T(8,128)(2,1)} %convolution_convert_fusion.inner_ref, bf16[48,3072]{1,0:T(8,128)(2,1)} %get-tuple-element.193.b_ref, bf16[64,5120]{1,0:T(8,128)(2,1)} %copy-done.7, ...), custom_call_target="tpu_custom_call" | custom-call | tf_op jit(solution)/shard_map/project_in/pallas_call | solution.py:291
  209.6 4.1 collective-permute-done.39.refs_5_
  217.4 7.9 %collective-permute-done.46.kv2 = bf16[8,128,256]{2,1,0:T(8,128)(2,1)} collective-permute-done((bf16[8,128,256]{2,1,0:T(8,128)(2,1)}, bf16[8,128,256]{2,1,0:T(8,128)(2,1)}, u32[]{:S(2)}, u32[]{:S(2)}) %collective-permute-start.46) | collective-permute-done | bytes 524320 | tf_op jit(solution)/shard_map/ppermute | solution.py:140
  227.0 7.4 %collective-permute-done.43.refs_3_ = bf16[256,2048]{1,0:T(8,128)(2,1)} collective-permute-done((bf16[256,2048]{1,0:T(8,128)(2,1)}, bf16[256,2048]{1,0:T(8,128)(2,1)}, u32[]{:S(2)}, u32[]{:S(2)}) %collective-permute-start.43) | collective-permute-done | bytes 1048608 | tf_op jit(solution)/shard_map/ppermute | solution.py:81
  239.1 4.3 all-to-all-start.3
  249.4 14.9 %attend.1 = (bf16[2048,256]{1,0:T(8,128)(2,1)}, bf16[8,4,256,1024]{3,2,1,0:T(8,128)(2,1)}, f32[8,1,1024]{2,1,0:T(1,128)}) custom-call(s32[1]{0:T(128)} %bitcast.32.seq_ref, s32[1,1024]{1,0:T(1,128)} %bitcast.230, bf16[2048,256]{1,0:T(8,128)(2,1)} %bitcast.193, bf16[8,128,256]{2,1,0:T(8,128)(2,1)} %pad_maximum_fusion.2.kv0, ...), custom_call_target="tpu_custom_call" | custom-call | tf_op jit(solution)/shard_map/attend/pallas_call | solution.py:739
  264.4 5.9 collective-permute-done.48.top_ref
  271.4 2.1 convolution_convert_fusion.3.inner_ref
  273.5 8.0 %project_out.1 = (f32[256,2048]{1,0:T(8,128)}, bf16[256,2048]{1,0:T(8,128)(2,1)}) custom-call(s32[32]{0:T(128)} %stack.171.order_ref, bf16[2048,256]{1,0:T(8,128)(2,1)} %get-tuple-element.222.mixed_ref.o_ref, bf16[16,256]{1,0:T(8,128)(2,1)} %convolution_convert_fusion.3.inner_ref, bf16[16,2048]{1,0:T(8,128)(2,1)} %get-tuple-element.224.b_ref, ...), custom_call_target="tpu_custom_call" | custom-call | tf_op jit(solution)/shard_map/project_out/pallas_call | solution.py:336
  289.1 6.1 place.3.whole_ref
  295.2 2.3 finish.3.weight_ref
  297.5 8.8 %collective-permute-done.53.n2 = bf16[256,2048]{1,0:T(8,128)(2,1)} collective-permute-done((bf16[256,2048]{1,0:T(8,128)(2,1)}, bf16[256,2048]{1,0:T(8,128)(2,1)}, u32[]{:S(2)}, u32[]{:S(2)}) %collective-permute-start.53) | collective-permute-done | bytes 1048608 | tf_op jit(solution)/shard_map/ppermute | solution.py:140
  306.8 15.8 %lower_back.1 = (bf16[1024,2048]{1,0:T(8,128)(2,1)}, bf16[1024,16]{1,0:T(8,128)(2,1)}) custom-call(bf16[256,2048]{1,0:T(8,128)(2,1)} %get-tuple-element.233.g0, bf16[256,2048]{1,0:T(8,128)(2,1)} %collective-permute-done.57.g1, bf16[256,2048]{1,0:T(8,128)(2,1)} %collective-permute-done.58.g2, bf16[256,2048]{1,0:T(8,128)(2,1)} %collective-permute-done.59.g3, ...), custom_call_target="tpu_custom_call" | custom-call | tf_op jit(solution)/shard_map/lower_back/pallas_call | solution.py:479
  326.4 34.1 %collective-permute-done.56.bottom_ref = bf16[128,2048]{1,0:T(8,128)(2,1)} collective-permute-done((bf16[128,2048]{1,0:T(8,128)(2,1)S(1)}, bf16[128,2048]{1,0:T(8,128)(2,1)}, u32[]{:S(2)}, u32[]{:S(2)}) %collective-permute-start.56) | collective-permute-done | bytes 524320 | tf_op jit(solution)/shard_map/ppermute | solution.py:87
  360.5 6.2 place.4.whole_ref
  366.8 2.2 finish.4.gate_ref.up_ref.w_ref
  370.0 5.3 all_tokens.1
  375.3 18.1 %units.2 = (bf16[1024,1024]{1,0:T(8,128)(2,1)}, bf16[1024,1024]{1,0:T(8,128)(2,1)}, bf16[1024,1024]{1,0:T(8,128)(2,1)}, f32[1024,48]{1,0:T(8,128)}) custom-call(bf16[1024,2048]{1,0:T(8,128)(2,1)} %get-tuple-element.252.whole_ref, bf16[1024,32]{1,0:T(8,128)(2,1)} %get-tuple-element.253.low_ref, bf16[2048,2048]{1,0:T(8,128)(2,1)} %finish.4.gate_ref.up_ref.w_ref, ...), custom_call_target="tpu_custom_call" | custom-call | tf_op jit(solution)/shard_map/units/pallas_call | solution.py:555
  395.5 14.2 %units_back_first.1.first_ref = bf16[1024,2048]{1,0:T(8,128)(2,1)} custom-call(bf16[1024,1024]{1,0:T(8,128)(2,1)} %get-tuple-element.274.g_ref.dg_ref, bf16[1024,1024]{1,0:T(8,128)(2,1)} %get-tuple-element.275.u_ref.du_ref, bf16[2048,2048]{1,0:T(8,128)(2,1)} %finish.4.gate_ref.up_ref.w_ref), custom_call_target="tpu_custom_call" | custom-call | tf_op jit(solution)/shard_map/units_back_first/pallas_call | solution.py:609
  409.7 7.8 %collective-permute-done.64.refs_5_ = bf16[256,2048]{1,0:T(8,128)(2,1)S(1)} collective-permute-done((bf16[256,2048]{1,0:T(8,128)(2,1)S(1)}, bf16[256,2048]{1,0:T(8,128)(2,1)S(1)}, u32[]{:S(2)}, u32[]{:S(2)}) %collective-permute-start.64) | collective-permute-done | bytes 1048608 | tf_op jit(solution)/shard_map/ppermute | solution.py:81
  420.9 5.4 units_grads.2
  426.3 4.0 collective-permute-done.67.bottom_ref
  430.8 6.4 place.5.whole_ref
  437.2 2.2 finish.5.gate_ref.up_ref.w_ref
  439.4 18.0 %units.3 = (bf16[1024,1024]{1,0:T(8,128)(2,1)}, bf16[1024,1024]{1,0:T(8,128)(2,1)}, bf16[1024,1024]{1,0:T(8,128)(2,1)}, f32[1024,48]{1,0:T(8,128)}) custom-call(bf16[1024,2048]{1,0:T(8,128)(2,1)} %get-tuple-element.252.whole_ref, bf16[1024,32]{1,0:T(8,128)(2,1)} %get-tuple-element.253.low_ref, bf16[2048,2048]{1,0:T(8,128)(2,1)} %finish.5.gate_ref.up_ref.w_ref, ...), custom_call_target="tpu_custom_call" | custom-call | tf_op jit(solution)/shard_map/units/pallas_call | solution.py:555
  459.2 9.5 %units_back.2 = (bf16[2,256,1024]{2,1,0:T(8,128)(2,1)}, bf16[2,256,1024]{2,1,0:T(8,128)(2,1)}) custom-call(bf16[1024,2048]{1,0:T(8,128)(2,1)} %units_back_first.1.first_ref, bf16[1024,1024]{1,0:T(8,128)(2,1)} %get-tuple-element.291.g_ref.dg_ref, bf16[1024,1024]{1,0:T(8,128)(2,1)} %get-tuple-element.292.u_ref.du_ref, ...), custom_call_target="tpu_custom_call" | custom-call | tf_op jit(solution)/shard_map/units_back/pallas_call | solution.py:641
  468.7 9.5 %units_back.3 = (bf16[2,256,1024]{2,1,0:T(8,128)(2,1)}, bf16[2,256,1024]{2,1,0:T(8,128)(2,1)}) custom-call(bf16[1024,2048]{1,0:T(8,128)(2,1)} %units_back_first.1.first_ref, bf16[1024,1024]{1,0:T(8,128)(2,1)} %get-tuple-element.291.g_ref.dg_ref, bf16[1024,1024]{1,0:T(8,128)(2,1)} %get-tuple-element.292.u_ref.du_ref, ...), custom_call_target="tpu_custom_call" | custom-call | tf_op jit(solution)/shard_map/units_back/pallas_call | solution.py:641
  482.7 16.7 %lower.1 = (bf16[2,256,2048]{2,1,0:T(8,128)(2,1)}, bf16[2,256,2048]{2,1,0:T(8,128)(2,1)}, f32[16,2048]{1,0:T(8,128)}, f32[32,2048]{1,0:T(8,128)}) custom-call(bf16[1024,1024]{1,0:T(8,128)(2,1)} %get-tuple-element.279.act_ref.aa_ref, bf16[1024,1024]{1,0:T(8,128)(2,1)} %get-tuple-element.299.ab_ref.act_ref, bf16[2048,2048]{1,0:T(8,128)(2,1)} %finish.3.weight_ref, ...), custom_call_target="tpu_custom_call" | custom-call | tf_op jit(solution)/shard_map/lower/pallas_call | solution.py:686
  500.1 5.4 units_grads.3
  515.5 4.8 collective-permute-done.73
  520.6 11.0 %collective-permute-done.72 = bf16[256,1024]{1,0:T(8,128)(2,1)S(1)} collective-permute-done((bf16[256,1024]{1,0:T(8,128)(2,1)S(1)}, bf16[256,1024]{1,0:T(8,128)(2,1)S(1)}, u32[]{:S(2)}, u32[]{:S(2)}) %collective-permute-start.72) | collective-permute-done | bytes 524320 | tf_op jit(solution)/shard_map/ppermute | solution.py:140
  532.4 21.0 %collective-permute-done.70 = bf16[256,2048]{1,0:T(8,128)(2,1)S(1)} collective-permute-done((bf16[256,2048]{1,0:T(8,128)(2,1)S(1)}, bf16[256,2048]{1,0:T(8,128)(2,1)S(1)}, u32[]{:S(2)}, u32[]{:S(2)}) %collective-permute-start.70) | collective-permute-done | bytes 1048608 | tf_op jit(solution)/shard_map/ppermute | solution.py:140
  553.4 2.7 multiply_convert_fusion
  558.8 2.3 pack.3
  561.1 7.1 %project_out_back.1.do_ref = bf16[2048,256]{1,0:T(8,128)(2,1)} custom-call(s32[32]{0:T(128)} %stack.171.order_ref, bf16[256,2048]{1,0:T(8,128)(2,1)} %copy-done.19, bf16[16,2048]{1,0:T(8,128)(2,1)} %get-tuple-element.223.a_ref, bf16[256,16]{1,0:T(8,128)(2,1)} %copy-done.54, bf16[64,5120]{1,0:T(8,128)(2,1)} %copy-done.7, ...), custom_call_target="tpu_custom_call" | custom-call | tf_op jit(solution)/shard_map/project_out_back/pallas_call | solution.py:390
  568.2 12.1 %attend_back.3 = (f32[1024,256]{1,0:T(8,128)}, bf16[2,4,128,256]{3,2,1,0:T(8,128)(2,1)}, bf16[2,4,128,256]{3,2,1,0:T(8,128)(2,1)}) custom-call(bf16[2048,256]{1,0:T(8,128)(2,1)} %bitcast.194, bf16[8,128,256]{2,1,0:T(8,128)(2,1)} %pad_maximum_fusion.2.kv0, bf16[8,128,256]{2,1,0:T(8,128)(2,1)} %collective-permute-done.45.kv1, ...), custom_call_target="tpu_custom_call" | custom-call | tf_op jit(solution)/shard_map/attend_back/pallas_call | solution.py:785
  580.2 12.1 %attend_back.2 = (f32[1024,256]{1,0:T(8,128)}, bf16[2,4,128,256]{3,2,1,0:T(8,128)(2,1)}, bf16[2,4,128,256]{3,2,1,0:T(8,128)(2,1)}) custom-call(bf16[2048,256]{1,0:T(8,128)(2,1)} %bitcast.195, bf16[8,128,256]{2,1,0:T(8,128)(2,1)} %pad_maximum_fusion.2.kv0, bf16[8,128,256]{2,1,0:T(8,128)(2,1)} %collective-permute-done.45.kv1, ...), custom_call_target="tpu_custom_call" | custom-call | tf_op jit(solution)/shard_map/attend_back/pallas_call | solution.py:785
  603.1 2.5 collective-permute-done.81
  607.6 4.2 all-to-all-start.5
  613.0 3.3 collective-permute-done.75
  623.1 2.3 pack.2
  630.0 5.5 collective-permute-done.79
  636.2 3.7 all-to-all-start.4
  639.8 11.3 %project_in_back.1 = bf16[256,2048]{1,0:T(8,128)(2,1)} custom-call(s32[32]{0:T(128)} %stack.171.order_ref, bf16[3072,256]{1,0:T(8,128)(2,1)} %copy-done.2, bf16[48,2048]{1,0:T(8,128)(2,1)} %get-tuple-element.192.a_ref, bf16[48,256]{1,0:T(8,128)(2,1)} %copy-done.56, bf16[256,2048]{1,0:T(8,128)(2,1)} %bitcast.192, f32[1,2048]{1,0:T(1,128)} %bitcast.220, ...), custom_call_target="tpu_custom_call" | custom-call | tf_op jit(solution)/shard_map/project_in_back/pallas_call | solution.py:436
  651.1 2.3 sort.3
  (392 shorter events, 143.5 us)
Async XLA Ops:
  4.4 24.8 %collective-permute-start.1 = (bf16[64,5120]{1,0:T(8,128)(2,1)S(1)}, bf16[64,5120]{1,0:T(8,128)(2,1)S(1)}, u32[]{:S(2)}, u32[]{:S(2)}) collective-permute-start(bf16[64,5120]{1,0:T(8,128)(2,1)S(1)} %constant_dynamic-update-slice_fusion.refs_0_), channel_id=1, source_target_pairs={{8,0},{16,8},{24,16},{28,24},{20,28},{12,20},{4,12},{0,4},{9,1},{1... | collective-permute-start | bytes 1966088 | tf_op jit(solution)/shard_map/ppermute | solution.py:82
  7.4 21.7 %collective-permute-start = (bf16[64,5120]{1,0:T(8,128)(2,1)S(1)}, bf16[64,5120]{1,0:T(8,128)(2,1)S(1)}, u32[]{:S(2)}, u32[]{:S(2)}) collective-permute-start(bf16[64,5120]{1,0:T(8,128)(2,1)S(1)} %constant_dynamic-update-slice_fusion.refs_0_), channel_id=1, source_target_pairs={{0,8},{8,16},{16,24},{24,28},{28,20},{20,12},{12,4},{4,0},{1,9},{9... | collective-permute-start | bytes 1966088 | tf_op jit(solution)/shard_map/ppermute | solution.py:81
  8.8 17.9 %all-to-all-start = ((s32[8,1,128]{2,1,0:T(1,128)}), s32[8,1,128]{2,1,0:T(1,128)S(1)}, u32[]{:S(2)}, u32[]{:S(2)}) async-start(s32[8,1,128]{2,1,0:T(1,128)} %broadcast_in_dim.24), calls=%async_computation | async-start | bytes 8192 | tf_op jit(solution)/shard_map/all_to_all | solution.py:985
  29.2 15.1 %collective-permute-start.2 = (bf16[64,5120]{1,0:T(8,128)(2,1)S(1)}, bf16[64,5120]{1,0:T(8,128)(2,1)}, u32[]{:S(2)}, u32[]{:S(2)}) collective-permute-start(bf16[64,5120]{1,0:T(8,128)(2,1)S(1)} %collective-permute-done.refs_4_), channel_id=1, source_target_pairs={{0,8},{8,16},{16,24},{24,28},{28,20},{20,12},{12,4},{4,0},{1,9},{9... | collective-permute-start | bytes 1966088 | tf_op jit(solution)/shard_map/ppermute | solution.py:81
  29.8 19.4 %collective-permute-start.3 = (bf16[64,5120]{1,0:T(8,128)(2,1)S(1)}, bf16[64,5120]{1,0:T(8,128)(2,1)S(1)}, u32[]{:S(2)}, u32[]{:S(2)}) collective-permute-start(bf16[64,5120]{1,0:T(8,128)(2,1)S(1)} %collective-permute-done.1.refs_8_), channel_id=1, source_target_pairs={{8,0},{16,8},{24,16},{28,24},{20,28},{12,20},{4,12},{0,4},{9,1},{1... | collective-permute-start | bytes 1966088 | tf_op jit(solution)/shard_map/ppermute | solution.py:82
  31.3 19.5 %collective-permute-start.12 = (bf16[64,5120]{1,0:T(8,128)(2,1)S(1)}, bf16[64,5120]{1,0:T(8,128)(2,1)}, u32[]{:S(2)}, u32[]{:S(2)}) collective-permute-start(bf16[64,5120]{1,0:T(8,128)(2,1)S(1)} %constant_dynamic-update-slice_fusion.refs_0_), channel_id=1, source_target_pairs={{0,2},{1,3},{2,0},{3,1},{4,6},{5,7},{6,4},{7,5},{8,10},{9,11},{10,... | collective-permute-start | bytes 1966088 | tf_op jit(solution)/shard_map/ppermute | solution.py:140
  32.8 20.1 %collective-permute-start.11 = (bf16[64,5120]{1,0:T(8,128)(2,1)S(1)}, bf16[64,5120]{1,0:T(8,128)(2,1)}, u32[]{:S(2)}, u32[]{:S(2)}) collective-permute-start(bf16[64,5120]{1,0:T(8,128)(2,1)S(1)} %constant_dynamic-update-slice_fusion.refs_0_), channel_id=1, source_target_pairs={{0,1},{1,0},{2,3},{3,2},{4,5},{5,4},{6,7},{7,6},{8,9},{9,8},{10,11... | collective-permute-start | bytes 1966088 | tf_op jit(solution)/shard_map/ppermute | solution.py:140
  32.8 30.3 %collective-permute-start.15 = (bf16[64,5120]{1,0:T(8,128)(2,1)S(1)}, bf16[64,5120]{1,0:T(8,128)(2,1)}, u32[]{:S(2)}, u32[]{:S(2)}) collective-permute-start(bf16[64,5120]{1,0:T(8,128)(2,1)S(1)} %collective-permute-done.refs_4_), channel_id=1, source_target_pairs={{0,2},{1,3},{2,0},{3,1},{4,6},{5,7},{6,4},{7,5},{8,10},{9,11},{10,... | collective-permute-start | bytes 1966088 | tf_op jit(solution)/shard_map/ppermute | solution.py:140
  44.3 19.7 %collective-permute-start.14 = (bf16[64,5120]{1,0:T(8,128)(2,1)S(1)}, bf16[64,5120]{1,0:T(8,128)(2,1)}, u32[]{:S(2)}, u32[]{:S(2)}) collective-permute-start(bf16[64,5120]{1,0:T(8,128)(2,1)S(1)} %collective-permute-done.refs_4_), channel_id=1, source_target_pairs={{0,1},{1,0},{2,3},{3,2},{4,5},{5,4},{6,7},{7,6},{8,9},{9,8},{10,11... | collective-permute-start | bytes 1966088 | tf_op jit(solution)/shard_map/ppermute | solution.py:140
  44.3 18.8 %all-to-all-start.1 = ((bf16[8,16,1376]{2,1,0:T(8,128)(2,1)}), bf16[8,16,1376]{2,1,0:T(8,128)(2,1)}, u32[]{:S(2)}, u32[]{:S(2)}) async-start(bf16[8,16,1376]{2,1,0:T(8,128)(2,1)} %pick.1), calls=%async_computation.1 | async-start | bytes 720896 | tf_op jit(solution)/shard_map/all_to_all | solution.py:1002
  49.2 27.9 %collective-permute-start.20 = (bf16[64,5120]{1,0:T(8,128)(2,1)S(1)}, bf16[64,5120]{1,0:T(8,128)(2,1)}, u32[]{:S(2)}, u32[]{:S(2)}) collective-permute-start(bf16[64,5120]{1,0:T(8,128)(2,1)S(1)} %collective-permute-done.1.refs_8_), channel_id=1, source_target_pairs={{0,2},{1,3},{2,0},{3,1},{4,6},{5,7},{6,4},{7,5},{8,10},{9,11},{10,... | collective-permute-start | bytes 1966088 | tf_op jit(solution)/shard_map/ppermute | solution.py:140
  50.8 29.8 %collective-permute-start.4 = (bf16[64,5120]{1,0:T(8,128)(2,1)}, bf16[64,5120]{1,0:T(8,128)(2,1)S(1)}, u32[]{:S(2)}, u32[]{:S(2)}) collective-permute-start(bf16[64,5120]{1,0:T(8,128)(2,1)} %collective-permute-done.2.refs_12_), channel_id=1, source_target_pairs={{0,8},{8,16},{16,24},{24,28},{28,20},{20,12},{12,4},{4,0},{1,9},{9... | collective-permute-start | bytes 1966088 | tf_op jit(solution)/shard_map/ppermute | solution.py:81
  52.8 28.2 %collective-permute-start.5 = (bf16[64,5120]{1,0:T(8,128)(2,1)S(1)}, bf16[64,5120]{1,0:T(8,128)(2,1)S(1)}, u32[]{:S(2)}, u32[]{:S(2)}) collective-permute-start(bf16[64,5120]{1,0:T(8,128)(2,1)S(1)} %collective-permute-done.3.refs_16_), channel_id=1, source_target_pairs={{8,0},{16,8},{24,16},{28,24},{20,28},{12,20},{4,12},{0,4},{9,1},{1... | collective-permute-start | bytes 1966088 | tf_op jit(solution)/shard_map/ppermute | solution.py:82
  63.1 18.1 %collective-permute-start.19 = (bf16[64,5120]{1,0:T(8,128)(2,1)S(1)}, bf16[64,5120]{1,0:T(8,128)(2,1)}, u32[]{:S(2)}, u32[]{:S(2)}) collective-permute-start(bf16[64,5120]{1,0:T(8,128)(2,1)S(1)} %collective-permute-done.1.refs_8_), channel_id=1, source_target_pairs={{0,1},{1,0},{2,3},{3,2},{4,5},{5,4},{6,7},{7,6},{8,9},{9,8},{10,11... | collective-permute-start | bytes 1966088 | tf_op jit(solution)/shard_map/ppermute | solution.py:140
  64.0 16.5 %collective-permute-start.9 = (bf16[8,16,608]{2,1,0:T(8,128)(2,1)S(1)}, bf16[8,16,608]{2,1,0:T(8,128)(2,1)S(1)}, u32[]{:S(2)}, u32[]{:S(2)}) collective-permute-start(bf16[8,16,608]{2,1,0:T(8,128)(2,1)S(1)} %slice.162), channel_id=1, source_target_pairs={{0,2},{1,3},{2,0},{3,1},{4,6},{5,7},{6,4},{7,5},{8,10},{9,11},{10,... | collective-permute-start | bytes 466952 | tf_op jit(solution)/shard_map/ppermute | solution.py:140
  77.1 18.0 %collective-permute-start.23 = (bf16[64,5120]{1,0:T(8,128)(2,1)}, bf16[64,5120]{1,0:T(8,128)(2,1)}, u32[]{:S(2)}, u32[]{:S(2)}) collective-permute-start(bf16[64,5120]{1,0:T(8,128)(2,1)} %collective-permute-done.2.refs_12_), channel_id=1, source_target_pairs={{0,2},{1,3},{2,0},{3,1},{4,6},{5,7},{6,4},{7,5},{8,10},{9,11},{10,... | collective-permute-start | bytes 1966088 | tf_op jit(solution)/shard_map/ppermute | solution.py:140
  81.1 35.8 %collective-permute-start.7 = (bf16[256,2048]{1,0:T(8,128)(2,1)}, bf16[256,2048]{1,0:T(8,128)(2,1)}, u32[]{:S(2)}, u32[]{:S(2)}) collective-permute-start(bf16[256,2048]{1,0:T(8,128)(2,1)} %refs_0_), channel_id=1, source_target_pairs={{8,0},{16,8},{24,16},{28,24},{20,28},{12,20},{4,12},{0,4},{9,1},{1... | collective-permute-start | bytes 3145736 | tf_op jit(solution)/shard_map/ppermute | solution.py:82
  82.9 34.0 %collective-permute-start.6 = (bf16[256,2048]{1,0:T(8,128)(2,1)}, bf16[256,2048]{1,0:T(8,128)(2,1)}, u32[]{:S(2)}, u32[]{:S(2)}) collective-permute-start(bf16[256,2048]{1,0:T(8,128)(2,1)} %refs_0_), channel_id=1, source_target_pairs={{0,8},{8,16},{16,24},{24,28},{28,20},{20,12},{12,4},{4,0},{1,9},{9... | collective-permute-start | bytes 3145736 | tf_op jit(solution)/shard_map/ppermute | solution.py:81
  83.4 22.1 %collective-permute-start.26 = (bf16[64,5120]{1,0:T(8,128)(2,1)S(1)}, bf16[64,5120]{1,0:T(8,128)(2,1)}, u32[]{:S(2)}, u32[]{:S(2)}) collective-permute-start(bf16[64,5120]{1,0:T(8,128)(2,1)S(1)} %collective-permute-done.3.refs_16_), channel_id=1, source_target_pairs={{0,2},{1,3},{2,0},{3,1},{4,6},{5,7},{6,4},{7,5},{8,10},{9,11},{10,... | collective-permute-start | bytes 1966088 | tf_op jit(solution)/shard_map/ppermute | solution.py:140
  95.1 17.9 %collective-permute-start.13 = (bf16[64,5120]{1,0:T(8,128)(2,1)}, bf16[64,5120]{1,0:T(8,128)(2,1)}, u32[]{:S(2)}, u32[]{:S(2)}) collective-permute-start(bf16[64,5120]{1,0:T(8,128)(2,1)} %collective-permute-done.12.refs_2_), channel_id=1, source_target_pairs={{0,1},{1,0},{2,3},{3,2},{4,5},{5,4},{6,7},{7,6},{8,9},{9,8},{10,11... | collective-permute-start | bytes 1966088 | tf_op jit(solution)/shard_map/ppermute | solution.py:140
  107.2 20.4 %collective-permute-start.29 = (bf16[64,5120]{1,0:T(8,128)(2,1)S(1)}, bf16[64,5120]{1,0:T(8,128)(2,1)}, u32[]{:S(2)}, u32[]{:S(2)}) collective-permute-start(bf16[64,5120]{1,0:T(8,128)(2,1)S(1)} %collective-permute-done.4.refs_20_), channel_id=1, source_target_pairs={{0,2},{1,3},{2,0},{3,1},{4,6},{5,7},{6,4},{7,5},{8,10},{9,11},{10,... | collective-permute-start | bytes 1966088 | tf_op jit(solution)/shard_map/ppermute | solution.py:140
  108.7 53.2 %all-to-all-start.2 = ((bf16[4,64,2048]{2,1,0:T(8,128)(2,1)}), bf16[4,64,2048]{2,1,0:T(8,128)(2,1)}, u32[]{:S(2)}, u32[]{:S(2)}) async-start(bf16[4,64,2048]{2,1,0:T(8,128)(2,1)} %get-tuple-element.212), calls=%async_computation.2 | async-start | bytes 2097152 | tf_op jit(solution)/shard_map/all_to_all | solution.py:1009
  113.0 16.1 %collective-permute-start.28 = (bf16[64,5120]{1,0:T(8,128)(2,1)S(1)}, bf16[64,5120]{1,0:T(8,128)(2,1)S(1)}, u32[]{:S(2)}, u32[]{:S(2)}) collective-permute-start(bf16[64,5120]{1,0:T(8,128)(2,1)S(1)} %collective-permute-done.4.refs_20_), channel_id=1, source_target_pairs={{0,1},{1,0},{2,3},{3,2},{4,5},{5,4},{6,7},{7,6},{8,9},{9,8},{10,11... | collective-permute-start | bytes 1966088 | tf_op jit(solution)/shard_map/ppermute | solution.py:140
  115.4 34.4 %collective-permute-start.32 = (bf16[64,5120]{1,0:T(8,128)(2,1)S(1)}, bf16[64,5120]{1,0:T(8,128)(2,1)S(1)}, u32[]{:S(2)}, u32[]{:S(2)}) collective-permute-start(bf16[64,5120]{1,0:T(8,128)(2,1)S(1)} %collective-permute-done.5.refs_24_), channel_id=1, source_target_pairs={{0,2},{1,3},{2,0},{3,1},{4,6},{5,7},{6,4},{7,5},{8,10},{9,11},{10,... | collective-permute-start | bytes 1966088 | tf_op jit(solution)/shard_map/ppermute | solution.py:140
  116.9 32.9 %collective-permute-start.31 = (bf16[64,5120]{1,0:T(8,128)(2,1)S(1)}, bf16[64,5120]{1,0:T(8,128)(2,1)S(1)}, u32[]{:S(2)}, u32[]{:S(2)}) collective-permute-start(bf16[64,5120]{1,0:T(8,128)(2,1)S(1)} %collective-permute-done.5.refs_24_), channel_id=1, source_target_pairs={{0,1},{1,0},{2,3},{3,2},{4,5},{5,4},{6,7},{7,6},{8,9},{9,8},{10,11... | collective-permute-start | bytes 1966088 | tf_op jit(solution)/shard_map/ppermute | solution.py:140
  127.0 34.9 %collective-permute-start.33 = (bf16[256,2048]{1,0:T(8,128)(2,1)}, bf16[256,2048]{1,0:T(8,128)(2,1)}, u32[]{:S(2)}, u32[]{:S(2)}) collective-permute-start(bf16[256,2048]{1,0:T(8,128)(2,1)} %collective-permute-done.6.refs_1_), channel_id=1, source_target_pairs={{0,8},{8,16},{16,24},{24,28},{28,20},{20,12},{12,4},{4,0},{1,9},{9... | collective-permute-start | bytes 3145736 | tf_op jit(solution)/shard_map/ppermute | solution.py:81
  127.6 35.1 %collective-permute-start.34 = (bf16[256,2048]{1,0:T(8,128)(2,1)}, bf16[256,2048]{1,0:T(8,128)(2,1)}, u32[]{:S(2)}, u32[]{:S(2)}) collective-permute-start(bf16[256,2048]{1,0:T(8,128)(2,1)} %collective-permute-done.7.refs_2_), channel_id=1, source_target_pairs={{8,0},{16,8},{24,16},{28,24},{20,28},{12,20},{4,12},{0,4},{9,1},{1... | collective-permute-start | bytes 3145736 | tf_op jit(solution)/shard_map/ppermute | solution.py:82
  129.1 30.6 %collective-permute-start.37 = (bf16[64,5120]{1,0:T(8,128)(2,1)S(1)}, bf16[64,5120]{1,0:T(8,128)(2,1)S(1)}, u32[]{:S(2)}, u32[]{:S(2)}) collective-permute-start(bf16[64,5120]{1,0:T(8,128)(2,1)S(1)} %constant_dynamic-update-slice_fusion.4.refs_28_), channel_id=1, source_target_pairs={{0,2},{1,3},{2,0},{3,1},{4,6},{5,7},{6,4},{7,5},{8,10},{9,11},{10,... | collective-permute-start | bytes 1966088 | tf_op jit(solution)/shard_map/ppermute | solution.py:140
  161.9 25.4 %collective-permute-start.42 = (bf16[256,2048]{1,0:T(8,128)(2,1)}, bf16[256,2048]{1,0:T(8,128)(2,1)}, u32[]{:S(2)}, u32[]{:S(2)}) collective-permute-start(bf16[256,2048]{1,0:T(8,128)(2,1)} %bitcast.57.refs_0_), channel_id=1, source_target_pairs={{8,0},{16,8},{24,16},{28,24},{20,28},{12,20},{4,12},{0,4},{9,1},{1... | collective-permute-start | bytes 3145736 | tf_op jit(solution)/shard_map/ppermute | solution.py:82
  162.6 26.2 %collective-permute-start.41 = (bf16[256,2048]{1,0:T(8,128)(2,1)}, bf16[256,2048]{1,0:T(8,128)(2,1)}, u32[]{:S(2)}, u32[]{:S(2)}) collective-permute-start(bf16[256,2048]{1,0:T(8,128)(2,1)} %bitcast.57.refs_0_), channel_id=1, source_target_pairs={{0,8},{8,16},{16,24},{24,28},{28,20},{20,12},{12,4},{4,0},{1,9},{9... | collective-permute-start | bytes 3145736 | tf_op jit(solution)/shard_map/ppermute | solution.py:81
  168.5 24.2 %collective-permute-start.30 = (bf16[64,5120]{1,0:T(8,128)(2,1)}, bf16[64,5120]{1,0:T(8,128)(2,1)}, u32[]{:S(2)}, u32[]{:S(2)}) collective-permute-start(bf16[64,5120]{1,0:T(8,128)(2,1)} %collective-permute-done.29.refs_22_), channel_id=1, source_target_pairs={{0,1},{1,0},{2,3},{3,2},{4,5},{5,4},{6,7},{7,6},{8,9},{9,8},{10,11... | collective-permute-start | bytes 1966088 | tf_op jit(solution)/shard_map/ppermute | solution.py:140
  168.5 25.7 %collective-permute-start.35 = (bf16[64,5120]{1,0:T(8,128)(2,1)S(1)}, bf16[64,5120]{1,0:T(8,128)(2,1)}, u32[]{:S(2)}, u32[]{:S(2)}) collective-permute-start(bf16[64,5120]{1,0:T(8,128)(2,1)S(1)} %copy-done.14), channel_id=1, source_target_pairs={{0,1},{1,0},{2,3},{3,2},{4,5},{5,4},{6,7},{7,6},{8,9},{9,8},{10,11... | collective-permute-start | bytes 1966088 | tf_op jit(solution)/shard_map/ppermute | solution.py:140
  169.0 25.8 %collective-permute-start.38 = (bf16[64,5120]{1,0:T(8,128)(2,1)S(1)}, bf16[64,5120]{1,0:T(8,128)(2,1)}, u32[]{:S(2)}, u32[]{:S(2)}) collective-permute-start(bf16[64,5120]{1,0:T(8,128)(2,1)S(1)} %collective-permute-done.37.refs_30_), channel_id=1, source_target_pairs={{0,1},{1,0},{2,3},{3,2},{4,5},{5,4},{6,7},{7,6},{8,9},{9,8},{10,11... | collective-permute-start | bytes 1966088 | tf_op jit(solution)/shard_map/ppermute | solution.py:140
  187.3 26.4 %collective-permute-start.39 = (bf16[256,2048]{1,0:T(8,128)(2,1)}, bf16[256,2048]{1,0:T(8,128)(2,1)}, u32[]{:S(2)}, u32[]{:S(2)}) collective-permute-start(bf16[256,2048]{1,0:T(8,128)(2,1)} %collective-permute-done.33.refs_3_), channel_id=1, source_target_pairs={{0,8},{8,16},{16,24},{24,28},{28,20},{20,12},{12,4},{4,0},{1,9},{9... | collective-permute-start | bytes 3145736 | tf_op jit(solution)/shard_map/ppermute | solution.py:81
  188.8 26.4 %collective-permute-start.40 = (bf16[256,2048]{1,0:T(8,128)(2,1)}, bf16[256,2048]{1,0:T(8,128)(2,1)}, u32[]{:S(2)}, u32[]{:S(2)}) collective-permute-start(bf16[256,2048]{1,0:T(8,128)(2,1)} %collective-permute-done.34.refs_4_), channel_id=1, source_target_pairs={{8,0},{16,8},{24,16},{28,24},{20,28},{12,20},{4,12},{0,4},{9,1},{1... | collective-permute-start | bytes 3145736 | tf_op jit(solution)/shard_map/ppermute | solution.py:82
  192.7 41.7 %collective-permute-start.43 = (bf16[256,2048]{1,0:T(8,128)(2,1)}, bf16[256,2048]{1,0:T(8,128)(2,1)}, u32[]{:S(2)}, u32[]{:S(2)}) collective-permute-start(bf16[256,2048]{1,0:T(8,128)(2,1)} %collective-permute-done.41.refs_1_), channel_id=1, source_target_pairs={{0,8},{8,16},{16,24},{24,28},{28,20},{20,12},{12,4},{4,0},{1,9},{9... | collective-permute-start | bytes 3145736 | tf_op jit(solution)/shard_map/ppermute | solution.py:81
  194.3 41.4 %collective-permute-start.44 = (bf16[256,2048]{1,0:T(8,128)(2,1)}, bf16[256,2048]{1,0:T(8,128)(2,1)}, u32[]{:S(2)}, u32[]{:S(2)}) collective-permute-start(bf16[256,2048]{1,0:T(8,128)(2,1)} %collective-permute-done.42.refs_2_), channel_id=1, source_target_pairs={{8,0},{16,8},{24,16},{28,24},{20,28},{12,20},{4,12},{0,4},{9,1},{1... | collective-permute-start | bytes 3145736 | tf_op jit(solution)/shard_map/ppermute | solution.py:82
  216.7 28.9 %collective-permute-start.45 = (bf16[8,128,256]{2,1,0:T(8,128)(2,1)}, bf16[8,128,256]{2,1,0:T(8,128)(2,1)}, u32[]{:S(2)}, u32[]{:S(2)}) collective-permute-start(bf16[8,128,256]{2,1,0:T(8,128)(2,1)} %pad_maximum_fusion.2.kv0), channel_id=1, source_target_pairs={{0,1},{1,0},{2,3},{3,2},{4,5},{5,4},{6,7},{7,6},{8,9},{9,8},{10,11... | collective-permute-start | bytes 1572872 | tf_op jit(solution)/shard_map/ppermute | solution.py:140
  225.3 21.9 %collective-permute-start.47 = (bf16[8,128,256]{2,1,0:T(8,128)(2,1)}, bf16[8,128,256]{2,1,0:T(8,128)(2,1)}, u32[]{:S(2)}, u32[]{:S(2)}) collective-permute-start(bf16[8,128,256]{2,1,0:T(8,128)(2,1)} %collective-permute-done.46.kv2), channel_id=1, source_target_pairs={{0,1},{1,0},{2,3},{3,2},{4,5},{5,4},{6,7},{7,6},{8,9},{9,8},{10,11... | collective-permute-start | bytes 1572872 | tf_op jit(solution)/shard_map/ppermute | solution.py:140
  235.6 45.9 %collective-permute-start.50 = (bf16[256,2048]{1,0:T(8,128)(2,1)}, bf16[256,2048]{1,0:T(8,128)(2,1)}, u32[]{:S(2)}, u32[]{:S(2)}) collective-permute-start(bf16[256,2048]{1,0:T(8,128)(2,1)} %collective-permute-done.43.refs_3_), channel_id=1, source_target_pairs={{0,8},{8,16},{16,24},{24,28},{28,20},{20,12},{12,4},{4,0},{1,9},{9... | collective-permute-start | bytes 3145736 | tf_op jit(solution)/shard_map/ppermute | solution.py:81
  237.1 44.5 %collective-permute-start.51 = (bf16[256,2048]{1,0:T(8,128)(2,1)}, bf16[256,2048]{1,0:T(8,128)(2,1)}, u32[]{:S(2)}, u32[]{:S(2)}) collective-permute-start(bf16[256,2048]{1,0:T(8,128)(2,1)} %collective-permute-done.44.refs_4_), channel_id=1, source_target_pairs={{8,0},{16,8},{24,16},{28,24},{20,28},{12,20},{4,12},{0,4},{9,1},{1... | collective-permute-start | bytes 3145736 | tf_op jit(solution)/shard_map/ppermute | solution.py:82
  237.6 45.5 %collective-permute-start.58 = (bf16[256,2048]{1,0:T(8,128)(2,1)}, bf16[256,2048]{1,0:T(8,128)(2,1)}, u32[]{:S(2)}, u32[]{:S(2)}) collective-permute-start(bf16[256,2048]{1,0:T(8,128)(2,1)} %get-tuple-element.233.g0), channel_id=1, source_target_pairs={{0,2},{1,3},{2,0},{3,1},{4,6},{5,7},{6,4},{7,5},{8,10},{9,11},{10,... | collective-permute-start | bytes 3145736 | tf_op jit(solution)/shard_map/ppermute | solution.py:140
  239.1 34.4 %all-to-all-start.3 = ((bf16[4,64,2048]{2,1,0:T(8,128)(2,1)}), bf16[4,64,2048]{2,1,0:T(8,128)(2,1)}, u32[]{:S(2)}, u32[]{:S(2)}) async-start(bf16[4,64,2048]{2,1,0:T(8,128)(2,1)} %get-tuple-element.266), calls=%async_computation.3 | async-start | bytes 2097152 | tf_op jit(solution)/shard_map/all_to_all | solution.py:1009
  245.6 24.6 %collective-permute-start.48 = (bf16[128,2048]{1,0:T(8,128)(2,1)S(1)}, bf16[128,2048]{1,0:T(8,128)(2,1)}, u32[]{:S(2)}, u32[]{:S(2)}) collective-permute-start(bf16[128,2048]{1,0:T(8,128)(2,1)S(1)} %slice.222), channel_id=1, source_target_pairs={{0,8},{8,16},{16,24},{24,28},{28,20},{20,12},{12,4},{4,0},{1,9},{9... | collective-permute-start | bytes 1572872 | tf_op jit(solution)/shard_map/ppermute | solution.py:86
  247.2 24.3 %collective-permute-start.49 = (bf16[128,2048]{1,0:T(8,128)(2,1)S(1)}, bf16[128,2048]{1,0:T(8,128)(2,1)}, u32[]{:S(2)}, u32[]{:S(2)}) collective-permute-start(bf16[128,2048]{1,0:T(8,128)(2,1)S(1)} %slice.223), channel_id=1, source_target_pairs={{8,0},{16,8},{24,16},{28,24},{20,28},{12,20},{4,12},{0,4},{9,1},{1... | collective-permute-start | bytes 1572872 | tf_op jit(solution)/shard_map/ppermute | solution.py:87
  270.2 17.4 %collective-permute-start.57 = (bf16[256,2048]{1,0:T(8,128)(2,1)}, bf16[256,2048]{1,0:T(8,128)(2,1)}, u32[]{:S(2)}, u32[]{:S(2)}) collective-permute-start(bf16[256,2048]{1,0:T(8,128)(2,1)} %get-tuple-element.233.g0), channel_id=1, source_target_pairs={{0,1},{1,0},{2,3},{3,2},{4,5},{5,4},{6,7},{7,6},{8,9},{9,8},{10,11... | collective-permute-start | bytes 3145736 | tf_op jit(solution)/shard_map/ppermute | solution.py:140
  281.5 24.8 %collective-permute-start.53 = (bf16[256,2048]{1,0:T(8,128)(2,1)}, bf16[256,2048]{1,0:T(8,128)(2,1)}, u32[]{:S(2)}, u32[]{:S(2)}) collective-permute-start(bf16[256,2048]{1,0:T(8,128)(2,1)} %get-tuple-element.247.n0), channel_id=1, source_target_pairs={{0,2},{1,3},{2,0},{3,1},{4,6},{5,7},{6,4},{7,5},{8,10},{9,11},{10,... | collective-permute-start | bytes 3145736 | tf_op jit(solution)/shard_map/ppermute | solution.py:140
  283.1 23.2 %collective-permute-start.59 = (bf16[256,2048]{1,0:T(8,128)(2,1)}, bf16[256,2048]{1,0:T(8,128)(2,1)}, u32[]{:S(2)}, u32[]{:S(2)}) collective-permute-start(bf16[256,2048]{1,0:T(8,128)(2,1)} %collective-permute-done.58.g2), channel_id=1, source_target_pairs={{0,1},{1,0},{2,3},{3,2},{4,5},{5,4},{6,7},{7,6},{8,9},{9,8},{10,11... | collective-permute-start | bytes 3145736 | tf_op jit(solution)/shard_map/ppermute | solution.py:140
  283.1 39.5 %collective-permute-start.61 = (bf16[256,2048]{1,0:T(8,128)(2,1)}, bf16[256,2048]{1,0:T(8,128)(2,1)}, u32[]{:S(2)}, u32[]{:S(2)}) collective-permute-start(bf16[256,2048]{1,0:T(8,128)(2,1)} %bitcast.67.refs_0_), channel_id=1, source_target_pairs={{8,0},{16,8},{24,16},{28,24},{20,28},{12,20},{4,12},{0,4},{9,1},{1... | collective-permute-start | bytes 3145736 | tf_op jit(solution)/shard_map/ppermute | solution.py:82
  283.7 38.9 %collective-permute-start.60 = (bf16[256,2048]{1,0:T(8,128)(2,1)}, bf16[256,2048]{1,0:T(8,128)(2,1)}, u32[]{:S(2)}, u32[]{:S(2)}) collective-permute-start(bf16[256,2048]{1,0:T(8,128)(2,1)} %bitcast.67.refs_0_), channel_id=1, source_target_pairs={{0,8},{8,16},{16,24},{24,28},{28,20},{20,12},{12,4},{4,0},{1,9},{9... | collective-permute-start | bytes 3145736 | tf_op jit(solution)/shard_map/ppermute | solution.py:81
  287.6 38.2 %collective-permute-start.55 = (bf16[128,2048]{1,0:T(8,128)(2,1)}, bf16[128,2048]{1,0:T(8,128)(2,1)S(1)}, u32[]{:S(2)}, u32[]{:S(2)}) collective-permute-start(bf16[128,2048]{1,0:T(8,128)(2,1)} %slice.224), channel_id=1, source_target_pairs={{0,8},{8,16},{16,24},{24,28},{28,20},{20,12},{12,4},{4,0},{1,9},{9... | collective-permute-start | bytes 1572872 | tf_op jit(solution)/shard_map/ppermute | solution.py:86
  306.3 62.7 %collective-permute-start.52 = (bf16[256,2048]{1,0:T(8,128)(2,1)S(1)}, bf16[256,2048]{1,0:T(8,128)(2,1)S(1)}, u32[]{:S(2)}, u32[]{:S(2)}) collective-permute-start(bf16[256,2048]{1,0:T(8,128)(2,1)S(1)} %copy-done.39), channel_id=1, source_target_pairs={{0,1},{1,0},{2,3},{3,2},{4,5},{5,4},{6,7},{7,6},{8,9},{9,8},{10,11... | collective-permute-start | bytes 3145736 | tf_op jit(solution)/shard_map/ppermute | solution.py:140
  306.3 62.7 %collective-permute-start.54 = (bf16[256,2048]{1,0:T(8,128)(2,1)}, bf16[256,2048]{1,0:T(8,128)(2,1)}, u32[]{:S(2)}, u32[]{:S(2)}) collective-permute-start(bf16[256,2048]{1,0:T(8,128)(2,1)} %collective-permute-done.53.n2), channel_id=1, source_target_pairs={{0,1},{1,0},{2,3},{3,2},{4,5},{5,4},{6,7},{7,6},{8,9},{9,8},{10,11... | collective-permute-start | bytes 3145736 | tf_op jit(solution)/shard_map/ppermute | solution.py:140
  322.6 70.8 %collective-permute-start.62 = (bf16[256,2048]{1,0:T(8,128)(2,1)}, bf16[256,2048]{1,0:T(8,128)(2,1)S(1)}, u32[]{:S(2)}, u32[]{:S(2)}) collective-permute-start(bf16[256,2048]{1,0:T(8,128)(2,1)} %collective-permute-done.60.refs_1_), channel_id=1, source_target_pairs={{0,8},{8,16},{16,24},{24,28},{28,20},{20,12},{12,4},{4,0},{1,9},{9... | collective-permute-start | bytes 3145736 | tf_op jit(solution)/shard_map/ppermute | solution.py:81
  324.1 69.3 %collective-permute-start.63 = (bf16[256,2048]{1,0:T(8,128)(2,1)}, bf16[256,2048]{1,0:T(8,128)(2,1)S(1)}, u32[]{:S(2)}, u32[]{:S(2)}) collective-permute-start(bf16[256,2048]{1,0:T(8,128)(2,1)} %collective-permute-done.61.refs_2_), channel_id=1, source_target_pairs={{8,0},{16,8},{24,16},{28,24},{20,28},{12,20},{4,12},{0,4},{9,1},{1... | collective-permute-start | bytes 3145736 | tf_op jit(solution)/shard_map/ppermute | solution.py:82
  325.8 34.7 %collective-permute-start.56 = (bf16[128,2048]{1,0:T(8,128)(2,1)S(1)}, bf16[128,2048]{1,0:T(8,128)(2,1)}, u32[]{:S(2)}, u32[]{:S(2)}) collective-permute-start(bf16[128,2048]{1,0:T(8,128)(2,1)S(1)} %slice.225), channel_id=1, source_target_pairs={{8,0},{16,8},{24,16},{28,24},{20,28},{12,20},{4,12},{0,4},{9,1},{1... | collective-permute-start | bytes 1572872 | tf_op jit(solution)/shard_map/ppermute | solution.py:87
  393.5 24.0 %collective-permute-start.64 = (bf16[256,2048]{1,0:T(8,128)(2,1)S(1)}, bf16[256,2048]{1,0:T(8,128)(2,1)S(1)}, u32[]{:S(2)}, u32[]{:S(2)}) collective-permute-start(bf16[256,2048]{1,0:T(8,128)(2,1)S(1)} %collective-permute-done.62.refs_3_), channel_id=1, source_target_pairs={{0,8},{8,16},{16,24},{24,28},{28,20},{20,12},{12,4},{4,0},{1,9},{9... | collective-permute-start | bytes 3145736 | tf_op jit(solution)/shard_map/ppermute | solution.py:81
  395.0 23.7 %collective-permute-start.65 = (bf16[256,2048]{1,0:T(8,128)(2,1)S(1)}, bf16[256,2048]{1,0:T(8,128)(2,1)S(1)}, u32[]{:S(2)}, u32[]{:S(2)}) collective-permute-start(bf16[256,2048]{1,0:T(8,128)(2,1)S(1)} %collective-permute-done.63.refs_4_), channel_id=1, source_target_pairs={{8,0},{16,8},{24,16},{28,24},{20,28},{12,20},{4,12},{0,4},{9,1},{1... | collective-permute-start | bytes 3145736 | tf_op jit(solution)/shard_map/ppermute | solution.py:82
  505.5 14.8 %collective-permute-start.73 = (bf16[256,1024]{1,0:T(8,128)(2,1)S(1)}, bf16[256,1024]{1,0:T(8,128)(2,1)S(1)}, u32[]{:S(2)}, u32[]{:S(2)}) collective-permute-start(bf16[256,1024]{1,0:T(8,128)(2,1)S(1)} %fusion.12), channel_id=1, source_target_pairs={{0,2},{1,3},{2,0},{3,1},{4,6},{5,7},{6,4},{7,5},{8,10},{9,11},{10,... | collective-permute-start | bytes 1572872 | tf_op jit(solution)/shard_map/ppermute | solution.py:140
  512.2 19.4 %collective-permute-start.72 = (bf16[256,1024]{1,0:T(8,128)(2,1)S(1)}, bf16[256,1024]{1,0:T(8,128)(2,1)S(1)}, u32[]{:S(2)}, u32[]{:S(2)}) collective-permute-start(bf16[256,1024]{1,0:T(8,128)(2,1)S(1)} %fusion.13), channel_id=1, source_target_pairs={{0,2},{1,3},{2,0},{3,1},{4,6},{5,7},{6,4},{7,5},{8,10},{9,11},{10,... | collective-permute-start | bytes 1572872 | tf_op jit(solution)/shard_map/ppermute | solution.py:140
  514.0 39.3 %collective-permute-start.70 = (bf16[256,2048]{1,0:T(8,128)(2,1)S(1)}, bf16[256,2048]{1,0:T(8,128)(2,1)S(1)}, u32[]{:S(2)}, u32[]{:S(2)}) collective-permute-start(bf16[256,2048]{1,0:T(8,128)(2,1)S(1)} %fusion.9), channel_id=1, source_target_pairs={{0,2},{1,3},{2,0},{3,1},{4,6},{5,7},{6,4},{7,5},{8,10},{9,11},{10,... | collective-permute-start | bytes 3145736 | tf_op jit(solution)/shard_map/ppermute | solution.py:140
  561.1 36.6 %collective-permute-start.80 = (f32[2,8,16,320]{3,2,1,0:T(8,128)}, f32[2,8,16,320]{3,2,1,0:T(8,128)S(1)}, u32[]{:S(2)}, u32[]{:S(2)}) collective-permute-start(f32[2,8,16,320]{3,2,1,0:T(8,128)} %get-tuple-element.322), channel_id=1, source_target_pairs={{0,1},{1,0},{2,3},{3,2},{4,5},{5,4},{6,7},{7,6},{8,9},{9,8},{10,11... | collective-permute-start | bytes 983048 | tf_op jit(solution)/shard_map/ppermute | solution.py:140
  607.6 28.6 %all-to-all-start.5 = ((f32[8,16,1088]{2,1,0:T(8,128)}), f32[8,16,1088]{2,1,0:T(8,128)}, u32[]{:S(2)}, u32[]{:S(2)}) async-start(f32[8,16,1088]{2,1,0:T(8,128)} %concatenate.49), calls=%async_computation.5 | async-start | bytes 1179648 | tf_op jit(solution)/shard_map/all_to_all | solution.py:1138
  636.2 17.2 %all-to-all-start.4 = ((f32[8,16,288]{2,1,0:T(8,128)}), f32[8,16,288]{2,1,0:T(8,128)S(1)}, u32[]{:S(2)}, u32[]{:S(2)}) async-start(f32[8,16,288]{2,1,0:T(8,128)} %fusion.20), calls=%async_computation.4 | async-start | bytes 393216 | tf_op jit(solution)/shard_map/all_to_all | solution.py:1138
  (101 other events, 1438.3 us)

commit v3 on v2

--- a/solution.py
+++ b/solution.py
@@ -112,27 +112,33 @@
 
 
 class Conveyor:
-    def __init__(self, clock, ring, waiting):
+    def __init__(self, clock, waiting):
         self.clock = clock
         self.waiting = list(waiting)
-        self.going = [(ring.step(clock), ring)]
+        self.going = []
+        self.rings = []
 
     def push(self):
         ring = Ring(self.waiting.pop(0)())
         self.going.append((ring.step(self.clock), ring))
+        self.rings.append(ring)
         return ring
 
     def advance(self, *computed):
+        if not self.going:
+            self.clock.tick(self.clock.done, computed)
+            return
         came, ring = self.going.pop(0)
         self.clock.tick(came, *computed)
         if not ring.complete():
             self.going.append((ring.step(self.clock), ring))
-        elif self.waiting:
-            self.push()
+            if ring.complete() and self.waiting:
+                self.push()
 
     def until(self, ring, *computed):
+        self.clock.tick(self.clock.done, computed)
         while not ring.complete() or any(r is ring for _, r in self.going):
-            self.advance(*computed)
+            self.advance(self.clock.done)
 
 
 def partner(operand, bit):
@@ -205,54 +211,64 @@
 ANY = pl.BlockSpec(memory_space=pl.ANY)
 
 
-def place_kernel(sources_ref, *refs):
-    pieces, (out_ref, sems) = refs[:-2], refs[-2:]
+def place_kernel(count, sources_ref, *refs):
+    pieces, outs, sems = refs[: -count - 1], refs[-count - 1 : -1], refs[-1]
     copies = []
     for i, piece in enumerate(pieces):
-        rows = piece.shape[0]
+        rows = piece.shape[0] // count
         start = pl.multiple_of(sources_ref[i] * rows, rows)
-        copies.append(pltpu.make_async_copy(piece, out_ref.at[pl.ds(start, rows)], sems.at[i]))
+        for j, out in enumerate(outs):
+            part = piece.at[pl.ds(j * rows, rows)]
+            copies.append(pltpu.make_async_copy(part, out.at[pl.ds(start, rows)], sems.at[i, j]))
     for copy in copies:
         copy.start()
     for copy in copies:
         copy.wait()
 
 
-def finish_kernel(source_ref, whole_ref, top_ref, bottom_ref, out_ref, sems):
-    rows = top_ref.shape[0]
+def finish_kernel(count, source_ref, *refs):
+    (top_ref, bottom_ref), outs, sems = refs[count : count + 2], refs[count + 2 : -1], refs[-1]
     copies = []
-    for i, piece in enumerate((top_ref, bottom_ref)):
-        start = pl.multiple_of(source_ref[0] * (2 * rows), 2 * rows) + i * rows
-        copies.append(pltpu.make_async_copy(piece, out_ref.at[pl.ds(start, rows)], sems.at[i]))
+    if count == 2:
+        rows = top_ref.shape[0]
+        start = pl.multiple_of(source_ref[0] * rows, rows)
+        for i, piece in enumerate((top_ref, bottom_ref)):
+            copies.append(pltpu.make_async_copy(piece, outs[i].at[pl.ds(start, rows)], sems.at[i]))
+    else:
+        rows = top_ref.shape[0]
+        for i, piece in enumerate((top_ref, bottom_ref)):
+            start = pl.multiple_of(source_ref[0] * (2 * rows), 2 * rows) + i * rows
+            copies.append(pltpu.make_async_copy(piece, outs[0].at[pl.ds(start, rows)], sems.at[i]))
     for copy in copies:
         copy.start()
     for copy in copies:
         copy.wait()
 
 
-def assemble(pieces, sources):
+def place(pieces, sources, count):
     rows, columns = pieces[0].shape
-    most = len(pieces) - 1
-    whole = shape(((most + 1) * rows, columns), BF16)
-    begun = call(
-        place_kernel,
+    most = len(pieces)
+    return call(
+        functools.partial(place_kernel, count),
         "place",
-        moved=4 * most * rows * columns,
         in_specs=[SMEM] + [VMEM] * most,
-        out_specs=ANY,
-        out_shape=whole,
-        scratch_shapes=[pltpu.SemaphoreType.DMA((most,))],
-    )(jnp.stack(sources[:-1]), *pieces[:-1])
-    return call(
-        finish_kernel,
+        out_specs=[ANY] * count,
+        out_shape=[shape(((most + 1) * rows // count, columns), BF16)] * count,
+        scratch_shapes=[pltpu.SemaphoreType.DMA((most, count))],
+    )(jnp.stack(sources[:-1]), *pieces)
+
+
+def finish(begun, pieces, sources):
+    count = len(begun)
+    return call(
+        functools.partial(finish_kernel, count),
         "finish",
-        moved=4 * rows * columns,
-        in_specs=[SMEM, ANY] + [VMEM] * 2,
-        out_specs=ANY,
-        out_shape=whole,
+        in_specs=[SMEM] + [ANY] * count + [VMEM] * 2,
+        out_specs=[ANY] * count,
+        out_shape=[shape(m.shape, BF16) for m in begun],
         scratch_shapes=[pltpu.SemaphoreType.DMA((2,))],
-        input_output_aliases={1: 0},
-    )(sources[-1][None], begun, *pieces[-1])
+        input_output_aliases={i + 1: i for i in range(count)},
+    )(sources[-1][None], *begun, *pieces[-1])
 
 
 def gather_rows(order_ref, source_ref, target_ref, rows):
@@ -911,7 +927,8 @@
             total = total + jnp.where(ids_ref[d] == a, value, 0.0)
         at = 0
         for ref, width in zip(out_refs, widths):
-            ref[a] = total[:, at : at + width]
+            part = total[:, at : at + width]
+            ref[a] = part.T if width < 64 else part
             at += width
 
 
@@ -921,9 +938,9 @@
         "sort",
         moved=8 * came.size,
         in_specs=[SMEM, VMEM],
-        out_shape=[shape((ADAPT, RANK, w), F32) for w in widths],
+        out_shape=[shape((ADAPT, w, RANK) if w < 64 else (ADAPT, RANK, w), F32) for w in widths],
     )(ids, came)
-    return [o.transpose(0, 2, 1) for o in outs]
+    return [o if w < 64 else o.transpose(0, 2, 1) for o, w in zip(outs, widths)]
 
 
 def shards(
@@ -970,77 +987,83 @@
     widths = (local, each, thin)
 
     attn = Ring(jnp.concatenate([w_query, w_key, w_value, w_out], axis=1))
-    sides, acrosses, corners = [], [], []
-
-    def share(piece):
-        sides.append(partner(clock(piece), 1))
-        acrosses.append(partner(clock(piece), 2))
-
-    def pass_on(count):
-        for _ in range(count):
-            corners.append(partner(clock(acrosses[len(corners)]), 1))
-
-    came = attn.step(clock)
-    share(attn.pieces[0])
-    ids = lax.all_to_all(
-        jnp.broadcast_to(adapter_ids[None], (n_dp, 128)), "dp", 0, 0, tiled=True
-    )[:, 0]
-    slots_a, slots_b = columns_for_seq(gate_weight, w_up, n_dp)
-    inputs = tokens[0].astype(F32)
-    normed = rms_scale(inputs, attn_gain).astype(BF16)
-    cot = cotangent[0].astype(F32)
-    grad_out = (valid * cot).astype(BF16)
-    stacks = (b_gate, b_up, a_down, a_query, a_key, a_value, b_query, a_out, b_out)
-    stacks += (a_gate, a_up, b_down, b_key, b_value)
-    ids = after(ids, slots_a, normed, grad_out)
-    sent = pick(ids, [m.transpose(0, 2, 1) for m in stacks])
-    clock.tick(came, slots_a, slots_b, normed, grad_out, sent)
-
-    came = attn.step(clock)
-    share(attn.pieces[1])
-    share(attn.pieces[2])
-    mine = lax.all_to_all(clock(sent), "dp", 0, 0, tiled=True)
-    normed_t = clock(normed).T
-    clock.tick(came, normed_t)
-
-    came = attn.step(clock)
-    share(attn.pieces[3])
-    share(attn.pieces[4])
-    swap = lambda slots: lax.all_to_all(clock(slots), "seq", 0, 0, tiled=True)
-    swapped_a = swap(slots_a)
-    mine = clock(mine)
-    others = seq_pieces(mine[..., 3 * local :])[1:]
-    pass_on(1)
-    clock.tick(came)
-    while len(attn.pieces) < n_dp - 1:
-        came = attn.step(clock)
-        share(attn.pieces[-4])
-        share(attn.pieces[-3])
-        clock.tick(came)
-
-    came = attn.step(clock)
-    lower_ring = Ring(w_down)
-    belt = Conveyor(clock, lower_ring, [lambda: clock(swapped_a).reshape(-1, width), lambda: clock(swapped_b).reshape(-1, width)])
-    share(attn.pieces[-3])
-    share(attn.pieces[-2])
-    clock.tick(came)
-    attn.pieces.append(jnp.concatenate(attn.pieces.pop(), axis=0))
-    share(attn.pieces[-1])
-    pass_on(3)
-    belt.advance()
-    ring_a = belt.push()
-    swapped_b = swap(slots_b)
-    pass_on(2)
+    first_came, age = None, 0
+    queue = [attn.pieces[0]]
+    sides, acrosses, corners, going = [], [], [], []
+    arrived = slot = 0
+    last = attn.steps - 1
+    while len(corners) < n_dp + 1:
+        waits, new = [], []
+        if not attn.complete():
+            new = attn.step(clock)
+            waits += new
+            if attn.complete():
+                ended = new
+                new = [new]
+        elif first_came is not None:
+            age += 1
+            if age == 3:
+                waits += first_came
+                first_came = None
+        elif not first_ring.complete():
+            first_came, age = first_ring.step(lambda v: after(v, ended) if len(first_ring.pieces) == 1 else clock(v)), 0
+        while len(acrosses) < len(queue) and len(going) < 2:
+            acrosses.append(partner(clock(queue[len(acrosses)]), 2))
+            going.append(len(acrosses))
+        for _ in range(3):
+            if len(corners) < arrived:
+                corners.append(partner(clock(acrosses[len(corners)]), 1))
+                waits.append(corners[-1])
+            elif len(sides) < len(queue):
+                sides.append(partner(clock(queue[len(sides)]), 1))
+                waits.append(sides[-1])
+        if slot == 0:
+            slots_a, slots_b = columns_for_seq(gate_weight, w_up, n_dp)
+            ids = lax.all_to_all(
+                jnp.broadcast_to(adapter_ids[None], (n_dp, 128)), "dp", 0, 0, tiled=True
+            )[:, 0]
+            stacks = (b_gate, b_up, a_down, a_query, a_key, a_value, b_query, a_out, b_out)
+            stacks += (a_gate, a_up, b_down, b_key, b_value)
+            sent = pick(ids, [m.transpose(0, 2, 1) for m in stacks])
+            waits += [sent, slots_a]
+        if slot == 1:
+            swapped_a = lax.all_to_all(clock(slots_a), "seq", 0, 0, tiled=True)
+        if slot == 2:
+            mine = lax.all_to_all(clock(sent), "dp", 0, 0, tiled=True)
+            first_ring = Ring(jnp.concatenate([w_down, swapped_a.reshape(-1, width)], axis=0))
+            waits.append(first_ring.pieces[0])
+        if slot == last + 2:
+            inputs = clock(tokens)[0].astype(F32)
+            normed = rms_scale(inputs, attn_gain).astype(BF16)
+            normed_t = normed.T
+            cot = cotangent[0].astype(F32)
+            grad_out = (valid * clock(cot)).astype(BF16)
+            waits += [normed_t, grad_out]
+        if going and (slot == 0 or len(going) == 2 or len(queue) == n_dp + 1):
+            waits.append(acrosses[going[0] - 1])
+        else:
+            going = going[:0] + going
+        clock.tick(*waits)
+        if going and any(w is acrosses[going[0] - 1] for w in waits):
+            arrived = going.pop(0)
+        if slot == 2:
+            queue.append(clock(mine)[..., 3 * local :])
+        queue += [jnp.concatenate(p, axis=0) if isinstance(p, tuple) else p for p in new]
+        slot += 1
+    others = [sides.pop(5), acrosses.pop(5), corners.pop(5)]
+    queue.pop(5)
+    attn_pieces = []
+    for group in zip(queue, sides, acrosses, corners):
+        attn_pieces += group
     order = everywhere_order(sources)
-    a_in, b_in, ao, bo, a_gu, bd, bg, bu, ad = spread(seq, *clock((mine, others)), widths)
-    inner = contract(clock(normed), a_in, 1, 1).astype(BF16)
-    belt.advance(inner)
-    pass_on(2)
-    belt.advance()
-    pass_on(len(acrosses) - len(corners))
-    attn_pieces = []
-    for group in zip(attn.pieces, sides, acrosses, corners):
-        attn_pieces += group
+
+    belt = Conveyor(clock, [lambda: swapped_b.reshape(-1, width)])
+    if first_came is None and not first_ring.complete():
+        first_came = first_ring.step(clock)
+    if first_came is not None:
+        belt.going.append((first_came, first_ring))
+    a_in, b_in, ao, bo, a_gu, bd, bg, bu, ad = spread(seq, mine, clock(others), widths)
+    inner = contract(normed, a_in, 1, 1).astype(BF16)
 
     linear = project_in(order, normed_t, inner, b_in, attn_pieces)
     query_lin = linear[:n_query].reshape(H, HD, block)
@@ -1051,67 +1074,95 @@
     query_prep = lambda v: prepare(v, query_gain, cosine, sine)
     key_prep = lambda v: prepare(v, key_gain, cosine, sine)
     keys_values = jnp.concatenate([key_prep(key_lin), value_lin], axis=1).astype(BF16)
-    belt.advance(keys_values)
-    keys_values = seq_pieces(clock(keys_values))
-    queries = (query_prep(clock(query_lin)) * scale).astype(BF16).reshape(n_query, block)
+    keys_values = seq_pieces(keys_values)
+    queries = (query_prep(query_lin) * scale).astype(BF16).reshape(n_query, block)
     limit = jnp.minimum(positions, length - 1).astype(jnp.int32)
     limit = jnp.tile(limit, GROUP)[None, :]
     belt.advance(queries)
-    grads = seq_pieces(after(clock(grad_out), keys_values[0], keys_values[2]))
-    mixed, raised, inverse = attend(seq, limit, clock(queries), keys_values)
-
-    belt.until(lower_ring, mixed)
-    w_lower = assemble(clock(lower_ring.pieces), sources)
-    inner_out = contract(ao, clock(mixed), 1, 0).astype(BF16)
+    grads = seq_pieces(after(grad_out, keys_values[2]))
+    mixed, raised, inverse = attend(seq, limit, queries, keys_values)
+    swapped_b = lax.all_to_all(after(slots_b, queries), "seq", 0, 0, tiled=True)
+    belt.advance(mixed)
+
+    inner_out = contract(ao, mixed, 1, 0).astype(BF16)
     hidden, normed_two = project_out(
-        order, clock(mixed), inner_out, bo, tokens[0], valid, ffn_gain[None], attn_pieces
+        order, mixed, inner_out, bo, tokens[0], valid, ffn_gain[None], attn_pieces
     )
-    belt.advance(normed_two)
-
-    n2 = seq_pieces(clock(normed_two))
-    d_act, d_down = lower_back(grads, clock(w_lower), bd, ad)
-    belt.until(ring_a, d_act)
-    ring_b = belt.going[-1][1]
-    n2, low_n2 = all_tokens(clock(n2), a_gu)
-    both_a = assemble(clock(ring_a.pieces), sources)
+
+    n2 = seq_pieces(normed_two)
+    while not first_ring.complete():
+        belt.advance(normed_two)
+    ring_b = belt.rings[0]
+    begun = place(clock(first_ring.pieces[:-1]), sources, 2)
+    belt.until(first_ring, begun)
+    w_lower, both_a = finish(begun, first_ring.pieces, sources)
+    d_act, d_down = lower_back(clock(grads), w_lower, bd, ad)
+    belt.advance(d_act)
+    n2, low_n2 = all_tokens(n2, a_gu)
     act_a, dg_a, du_a, inner_a = units(0, n2, low_n2, both_a, bg, bu, ad, d_act)
     belt.advance(act_a)
     first = units_back_first(clock(dg_a), du_a, both_a)
-    belt.advance(first)
-    gbg_a, gbu_a, gad_a = units_grads(low_n2, d_down, clock(act_a), dg_a, du_a)
-    belt.until(ring_b, gbg_a)
-    both_b = assemble(clock(ring_b.pieces), sources)
+    gbg_a, gbu_a, gad_a = units_grads(low_n2, d_down, after(act_a, first), dg_a, du_a)
+    while not ring_b.complete():
+        belt.advance(gbg_a)
+    begun = place(clock(ring_b.pieces[:-1]), sources, 1)
+    belt.until(ring_b, begun)
+    (both_b,) = finish(begun, ring_b.pieces, sources)
     act_b, dg_b, du_b, inner_b = units(1, n2, low_n2, both_b, bg, bu, ad, d_act)
     low = (inner_a + inner_b).astype(BF16)
     low_gu, low_down = low[:, : 2 * RANK], low[:, 2 * RANK :]
-    d_n2, parts = [], 2
-    for part in range(parts):
-        keep, give = units_back(part, parts, first, dg_b, du_b, both_b, low_gu, a_gu)
-        first = after(first, keep)
-        reduced, sent = seq_reduce(keep, give)
-        d_n2.append(reduced)
-    d_n2 = jnp.concatenate(d_n2, axis=1)
-
-    act_b = after(act_b, sent)
-    gbg_b, gbu_b, gad_b = units_grads(low_n2, d_down, act_b, dg_b, du_b)
+    keep, give = units_back(0, 2, first, dg_b, du_b, both_b, low_gu, a_gu)
+    left, sent = seq_reduce(keep, give)
+    keep, give = units_back(1, 2, after(first, sent), dg_b, du_b, both_b, low_gu, a_gu)
+    right, sent = seq_reduce(keep, give)
+    gbg_b, gbu_b, gad_b = units_grads(low_n2, d_down, after(act_b, sent), dg_b, du_b)
+
+    act_b = after(act_b, left, gbg_b)
     keep, give, grad_bd, grad_a_gu = lower(act_a, act_b, w_lower, low_down, bd, grads, n2, low_gu)
-    lowered, _ = seq_reduce(keep, give)
-    output = (hidden + valid * lowered).astype(BF16)
-
+    left, right = after((left, right), keep)
+
+    d_n2 = jnp.concatenate([left, right], axis=1)
     d_hidden = cot + jax.vjp(lambda v: rms_scale(v, ffn_gain), hidden)[1](d_n2)[0]
     grad_update = (valid * d_hidden).astype(BF16)
+    keep, give = after((keep, give), grad_update)
+    lowered, sent = seq_reduce(keep, give)
     d_inner_out = contract(grad_update, bo, 1, 1).astype(BF16)
-    d_mixed = project_out_back(order, grad_update, ao, d_inner_out, attn_pieces)
+    d_mixed = project_out_back(order, after(grad_update, sent), ao, d_inner_out, attn_pieces)
     d_queries, d_kv = [], []
     for part in range(2):
         count = KV // 2
         d_query, keep, give = attend_back(
             part * count, count, queries, keys_values, raised, inverse, mixed, d_mixed
         )
-        d_kv.append(seq_reduce(keep, give)[0])
+        if part == 0:
+            give = after(give, lowered)
+        reduced, sent = seq_reduce(keep, give)
+        d_mixed = after(d_mixed, sent)
+        d_kv.append(reduced)
         d_queries.append(d_query)
+    def owners(grads, alone):
+        keep, give = pack(seq, grads, n_dp)
+        both = keep + partner(give, 1)
+        summed = both[0] + partner(both[1], 2)
+        sizes = [g.shape[1] // (4 * n_dp) for g in grads]
+        if alone:
+            summed = jnp.concatenate([summed] + alone, axis=2)
+            sizes += [g.shape[2] for g in alone]
+        return sort(ids, lax.all_to_all(summed, "dp", 0, 0, tiled=True), sizes)
+
+    grad_ao = contract(d_inner_out, mixed, 0, 1)
+    grad_bo = contract(inner_out, grad_update, 1, 0)
+    cat = lambda a, b: jnp.concatenate([a, b], axis=1).reshape(RANK, n_dp, -1).transpose(1, 0, 2)
+    some = [grad_ao, grad_bo, grad_a_gu[:RANK], grad_a_gu[RANK:], grad_bd]
+    owned = owners(
+        after(some, d_query),
+        [cat(gbg_a, gbg_b), cat(gbu_a, gbu_b), cat(gad_a, gad_b)],
+    )
+    gao, gbo, gag, gau, gbd, gbg, gbu, gad = owned
+
     d_queries = jnp.concatenate(d_queries, axis=0).reshape(H, HD, block) * scale
-    d_kv = jnp.concatenate(d_kv, axis=0)
+    output = (hidden + valid * after(lowered, d_queries)).astype(BF16)
+    d_kv = jnp.concatenate(after(d_kv, output), axis=0)
     d_query_lin = jax.vjp(query_prep, query_lin)[1](d_queries)[0]
     d_key_lin = jax.vjp(key_prep, key_lin)[1](d_kv[:, :HD])[0]
     d_linear = jnp.concatenate(
@@ -1124,26 +1175,9 @@
     ).astype(BF16)
     d_inner = contract(b_in, d_linear, 1, 0).astype(BF16)
     grad_tokens = project_in_back(
-        order, d_linear, a_in, d_inner, tokens[0], attn_gain[None], d_hidden, attn_pieces
+        order, d_linear, a_in, d_inner, tokens[0], attn_gain[None], after(d_hidden, *owned), attn_pieces
     )
 
-    def owners(grads, alone):
-        keep, give = pack(seq, grads, n_dp)
-        both = keep + partner(give, 1)
-        summed = both[0] + partner(both[1], 2)
-        sizes = [g.shape[1] // (4 * n_dp) for g in grads]
-        if alone:
-            summed = jnp.concatenate([summed] + alone, axis=2)
-            sizes += [g.shape[2] for g in alone]
-        return sort(ids, lax.all_to_all(summed, "dp", 0, 0, tiled=True), sizes)
-
-    grad_ao = contract(d_inner_out, mixed, 0, 1)
-    grad_bo = contract(inner_out, grad_update, 1, 0)
-    cat = lambda a, b: jnp.concatenate([a, b], axis=1).reshape(RANK, n_dp, -1).transpose(1, 0, 2)
-    gao, gbo, gag, gau, gbd, gbg, gbu, gad = owners(
-        [grad_ao, grad_bo, grad_a_gu[:RANK], grad_a_gu[RANK:], grad_bd],
-        [cat(gbg_a, gbg_b), cat(gbu_a, gbu_b), cat(gad_a, gad_b)],
-    )
     grad_a_in = contract(d_inner, normed, 1, 0)
     grad_b_in = contract(inner, d_linear, 0, 1)
     q_end, k_end = n_query, n_query + n_key

time: 671 us -> 598 us (0.89)
  waiting for transfers between devices: 252 us -> 174 us
  other arithmetic: 29.6 us -> 46.1 us
  starting transfers between devices: 91.1 us -> 81.5 us
    ppermute x50, waiting for transfers between devices: 142 us -> 58.4 us  [partner(): return lax.ppermute(operand, 'seq', [(i, i ^ bit) for i in range(size)])]
    ppermute x4 -> x3, waiting for transfers between devices: 47.8 us -> 4.56 us  [step(): bottom = lax.ppermute(clock(self.right[half:]), 'dp', left)]
    ppermute x12 -> x9, waiting for transfers between devices: 22 us -> 53.9 us  [step(): self.right = lax.ppermute(clock(self.right), 'dp', left)]
    all_to_all x2, waiting for transfers between devices: 0.01 us -> 17.8 us  [the longest x1 14.4 us: shards(): swapped_b = lax.all_to_all(after(slots_b, queries), 'seq', 0, 0, tiled=True)]
    ppermute x12 -> x9, starting transfers between devices: 14 us -> 9.24 us  [step(): self.left = lax.ppermute(clock(self.left), 'dp', right)]
    pallas_call x6 -> x4, Pallas kernels: 25.4 us -> 22.1 us  [the longest x2 17 us: place(): call(functools.partial(place_kernel, count), 'place', in_specs=[SMEM] + [...]
    unnamed x164 -> x187, local copies, waits for them, and re-layouts: 17.5 us -> 19.5 us
    ppermute x12 -> x9, waiting for transfers between devices: 30.4 us -> 30.8 us  [step(): self.left = lax.ppermute(clock(self.left), 'dp', right)]
  transfers between devices with their start and end apart: 88 -> 80, of which waited for: 34 -> 32; matrix products, arithmetic and copies ran while one was open for 8% -> 12% of each run, Pallas kernels for 26% -> 32%
where the time goes in v3:
time: 598 us; the launch traced here: 588 us
  Pallas kernels  232 us (39%)
  waiting for transfers between devices  174 us (29%)
  starting transfers between devices  81.5 us (14%)
  other arithmetic  46.1 us (8%)
  local copies, waits for them, and re-layouts  41.5 us (7%)
  matrix products  9.27 us (2%)
    ppermute x50, waiting for transfers between devices, partner(): return lax.ppermute(operand, 'seq', [(i, i ^ bit) for i in range(size)])  58.4 us
    ppermute x9, waiting for transfers between devices, step(): self.right = lax.ppermute(clock(self.right), 'dp', left)  53.9 us
    pallas_call x2, Pallas kernels, units(): call(units_kernel, 'units', flops=4 * tokens * width * half, moved=4 * wi...  36.1 us
    ppermute x9, waiting for transfers between devices, step(): self.left = lax.ppermute(clock(self.left), 'dp', right)  30.8 us
    ppermute x50, starting transfers between devices, partner(): return lax.ppermute(operand, 'seq', [(i, i ^ bit) for i in range(size)])  25.5 us
    pallas_call x2, Pallas kernels, attend_back(): call(attend_back_kernel, 'attend_back', flops=32 * count * GROUP * width...  24.3 us
    unnamed x187, local copies, waits for them, and re-layouts  19.5 us
    pallas_call x2, Pallas kernels, units_back(): call(units_back_kernel, 'units_back', flops=4 * tokens * half * width //...  19 us
  transfers between devices with their start and end apart: 80, of which 32 were waited for; matrix products, arithmetic and copies ran while one was open for 12% of the time, Pallas kernels for 32%

profile of v3, /device:TPU:0, one launch (start us, length us, event | category | flops | bytes accessed | tf_op | source)
XLA Modules:
  0.0 587.7 jit_solution(2107488492331394355)
XLA Ops:
  4.3 3.1 collective-permute-start
  10.6 5.8 all-to-all-start
  19.3 3.0 columns.1
  22.3 3.3 all-to-all-done
  32.0 11.2 %collective-permute-done.5.refs_16_ = bf16[64,5120]{1,0:T(8,128)(2,1)S(1)} collective-permute-done((bf16[64,5120]{1,0:T(8,128)(2,1)S(1)}, bf16[64,5120]{1,0:T(8,128)(2,1)S(1)}, u32[]{:S(2)}, u32[]{:S(2)}) %collective-permute-start.5) | collective-permute-done | bytes 655392 | tf_op jit(solution)/shard_map/ppermute | solution.py:82
  43.3 3.7 collective-permute-done.4.refs_12_
  49.7 4.2 all-to-all-start.1
  57.6 7.9 %collective-permute-done.11.refs_20_ = bf16[64,5120]{1,0:T(8,128)(2,1)S(1)} collective-permute-done((bf16[64,5120]{1,0:T(8,128)(2,1)}, bf16[64,5120]{1,0:T(8,128)(2,1)S(1)}, u32[]{:S(2)}, u32[]{:S(2)}) %collective-permute-start.11) | collective-permute-done | bytes 655392 | tf_op jit(solution)/shard_map/ppermute | solution.py:81
  65.6 3.4 all-to-all-done.1
  69.0 4.1 all-to-all-start.2
  73.1 3.2 pad_maximum_fusion.refs_0_
  77.0 5.5 collective-permute-done.16.refs_10_
  88.4 3.7 collective-permute-done.17
  95.8 5.3 collective-permute-done.10.refs_14_
  103.3 2.8 bitcast_convert_fusion
  107.6 6.0 %collective-permute-done.25.refs_18_ = bf16[64,5120]{1,0:T(8,128)(2,1)} collective-permute-done((bf16[64,5120]{1,0:T(8,128)(2,1)S(1)}, bf16[64,5120]{1,0:T(8,128)(2,1)}, u32[]{:S(2)}, u32[]{:S(2)}) %collective-permute-start.25) | collective-permute-done | bytes 655392 | tf_op jit(solution)/shard_map/ppermute | solution.py:146
  117.1 2.3 copy.79
  121.0 2.8 multiply_convert_fusion.1.g0
  126.3 9.9 %collective-permute-done.29.refs_22_ = bf16[64,5120]{1,0:T(8,128)(2,1)S(1)} collective-permute-done((bf16[64,5120]{1,0:T(8,128)(2,1)S(1)}, bf16[64,5120]{1,0:T(8,128)(2,1)S(1)}, u32[]{:S(2)}, u32[]{:S(2)}) %collective-permute-start.29) | collective-permute-done | bytes 655392 | tf_op jit(solution)/shard_map/ppermute | solution.py:146
  137.0 17.0 %collective-permute-done.32.refs_1_ = bf16[512,2048]{1,0:T(8,128)(2,1)} collective-permute-done((bf16[512,2048]{1,0:T(8,128)(2,1)}, bf16[512,2048]{1,0:T(8,128)(2,1)}, u32[]{:S(2)}, u32[]{:S(2)}) %collective-permute-start.32) | collective-permute-done | bytes 2097184 | tf_op jit(solution)/shard_map/ppermute | solution.py:81
  153.9 6.0 %collective-permute-done.33.refs_2_ = bf16[512,2048]{1,0:T(8,128)(2,1)} collective-permute-done((bf16[512,2048]{1,0:T(8,128)(2,1)}, bf16[512,2048]{1,0:T(8,128)(2,1)}, u32[]{:S(2)}, u32[]{:S(2)}) %collective-permute-start.33) | collective-permute-done | bytes 2097184 | tf_op jit(solution)/shard_map/ppermute | solution.py:82
  165.2 2.5 spread.1
  167.7 2.7 convolution_convert_fusion.inner_ref
  170.5 10.1 %project_in.1 = f32[3072,256]{1,0:T(8,128)} custom-call(s32[32]{0:T(128)} %stack.163.order_ref, bf16[2048,256]{1,0:T(8,128)(2,1)} %fusion.23.normed_ref, bf16[256,48]{1,0:T(8,128)(2,1)} %convolution_convert_fusion.inner_ref, bf16[48,3072]{1,0:T(8,128)(2,1)} %get-tuple-element.208.b_ref, bf16[64,5120]{1,0:T(8,128)(2,1)} %copy-done.7, ...), custom_call_target="tpu_custom_call" | custom-call | tf_op jit(solution)/shard_map/project_in/pallas_call | solution.py:307
  187.5 23.8 %collective-permute-done.44.refs_4_ = bf16[512,2048]{1,0:T(8,128)(2,1)} collective-permute-done((bf16[512,2048]{1,0:T(8,128)(2,1)}, bf16[512,2048]{1,0:T(8,128)(2,1)}, u32[]{:S(2)}, u32[]{:S(2)}) %collective-permute-start.44) | collective-permute-done | bytes 2097184 | tf_op jit(solution)/shard_map/ppermute | solution.py:82
  218.6 14.9 %attend.1 = (bf16[2048,256]{1,0:T(8,128)(2,1)}, bf16[8,4,256,1024]{3,2,1,0:T(8,128)(2,1)}, f32[8,1,1024]{2,1,0:T(1,128)}) custom-call(s32[1]{0:T(128)} %bitcast.32.seq_ref, s32[1,1024]{1,0:T(1,128)} %bitcast.222, bf16[2048,256]{1,0:T(8,128)(2,1)} %bitcast.185, bf16[8,128,256]{2,1,0:T(8,128)(2,1)} %copy-done.29, bf16[8,128,256]{2,1,0:T(8,128)(2,1)} %copy-done.33, ...), custom_call_target="tpu_custom_call" | custom-call | tf_op jit(solution)/shard_map/attend/pallas_call | solution.py:755
  235.6 8.1 %project_out.1 = (f32[256,2048]{1,0:T(8,128)}, bf16[256,2048]{1,0:T(8,128)(2,1)}) custom-call(s32[32]{0:T(128)} %stack.163.order_ref, bf16[2048,256]{1,0:T(8,128)(2,1)} %get-tuple-element.209.mixed_ref.o_ref, bf16[16,256]{1,0:T(8,128)(2,1)} %convolution_convert_fusion.3.inner_ref, bf16[16,2048]{1,0:T(8,128)(2,1)} %get-tuple-element.211.b_ref, ...), custom_call_target="tpu_custom_call" | custom-call | tf_op jit(solution)/shard_map/project_out/pallas_call | solution.py:352
  244.9 4.3 all-to-all-start.3
  249.6 9.9 %collective-permute-done.46.refs_6_ = bf16[512,2048]{1,0:T(8,128)(2,1)} collective-permute-done((bf16[512,2048]{1,0:T(8,128)(2,1)}, bf16[512,2048]{1,0:T(8,128)(2,1)}, u32[]{:S(2)}, u32[]{:S(2)}) %collective-permute-start.46) | collective-permute-done | bytes 2097184 | tf_op jit(solution)/shard_map/ppermute | solution.py:82
  259.5 2.4 slice.215
  263.4 2.3 slice.214
  266.3 14.4 %all-to-all-done.3 = bf16[4,64,2048]{2,1,0:T(8,128)(2,1)} async-done(((bf16[4,64,2048]{2,1,0:T(8,128)(2,1)}), bf16[4,64,2048]{2,1,0:T(8,128)(2,1)}, u32[]{:S(2)}, u32[]{:S(2)}) %all-to-all-start.3) | async-done | bytes 1048608 | tf_op jit(solution)/shard_map/all_to_all | solution.py:1084
  283.3 10.7 %place.2 = (bf16[2048,2048]{1,0:T(8,128)(2,1)}, bf16[2048,2048]{1,0:T(8,128)(2,1)}) custom-call(s32[7]{0:T(128)} %stack.171.sources_ref, bf16[512,2048]{1,0:T(8,128)(2,1)} %pad_maximum_fusion.refs_0_, bf16[512,2048]{1,0:T(8,128)(2,1)} %collective-permute-done.32.refs_1_, bf16[512,2048]{1,0:T(8,128)(2,1)} %collective-permute-done.33.refs_2_, ...), custom_call_target="tpu_custom_call" | custom-call | tf_op jit(solution)/shard_map/place/pallas_call | solution.py:251
  294.7 2.9 finish.2
  297.6 15.8 %lower_back.1 = (bf16[1024,2048]{1,0:T(8,128)(2,1)}, bf16[1024,16]{1,0:T(8,128)(2,1)}) custom-call(bf16[256,2048]{1,0:T(8,128)(2,1)} %multiply_convert_fusion.1.g0, bf16[256,2048]{1,0:T(8,128)(2,1)} %collective-permute-done.49.g1, bf16[256,2048]{1,0:T(8,128)(2,1)} %collective-permute-done.50.g2, bf16[256,2048]{1,0:T(8,128)(2,1)} %collective-permute-done.51.g3, ...), custom_call_target="tpu_custom_call" | custom-call | tf_op jit(solution)/shard_map/lower_back/pallas_call | solution.py:495
  316.5 5.3 all_tokens.1
  321.8 18.1 %units.2 = (bf16[1024,1024]{1,0:T(8,128)(2,1)}, bf16[1024,1024]{1,0:T(8,128)(2,1)}, bf16[1024,1024]{1,0:T(8,128)(2,1)}, f32[1024,48]{1,0:T(8,128)}) custom-call(bf16[1024,2048]{1,0:T(8,128)(2,1)} %get-tuple-element.215.whole_ref, bf16[1024,32]{1,0:T(8,128)(2,1)} %get-tuple-element.216.low_ref, bf16[2048,2048]{1,0:T(8,128)(2,1)} %get-tuple-element.232.gate_ref.up_ref.w_ref, ...), custom_call_target="tpu_custom_call" | custom-call | tf_op jit(solution)/shard_map/units/pallas_call | solution.py:571
  342.0 14.2 %units_back_first.1.first_ref = bf16[1024,2048]{1,0:T(8,128)(2,1)} custom-call(bf16[1024,1024]{1,0:T(8,128)(2,1)} %get-tuple-element.254.g_ref.dg_ref, bf16[1024,1024]{1,0:T(8,128)(2,1)} %get-tuple-element.255.u_ref.du_ref, bf16[2048,2048]{1,0:T(8,128)(2,1)} %get-tuple-element.232.gate_ref.up_ref.w_ref), custom_call_target="tpu_custom_call" | custom-call | tf_op jit(solution)/shard_map/units_back_first/pallas_call | solution.py:625
  356.3 5.4 units_grads.2
  361.7 2.9 collective-permute-done.57.refs_6_
  368.0 6.2 %place.3.refs_0_ = bf16[2048,2048]{1,0:T(8,128)(2,1)} custom-call(s32[7]{0:T(128)} %stack.171.sources_ref, bf16[256,2048]{1,0:T(8,128)(2,1)} %bitcast.69.refs_0_, bf16[256,2048]{1,0:T(8,128)(2,1)} %collective-permute-done.52.refs_1_, bf16[256,2048]{1,0:T(8,128)(2,1)} %collective-permute-done.53.refs_2_, bf16[256,2048]{1,0:T(8,128)(2,1)} %copy-done.43, ...), custom_call_target="tpu_custom_call" | custom-call | tf_op jit(solution)/shard_map/place/pallas_call | solution.py:251
  374.3 3.6 collective-permute-done.59.refs_2_
  380.1 2.2 finish.3.gate_ref.up_ref.w_ref
  382.3 18.0 %units.3 = (bf16[1024,1024]{1,0:T(8,128)(2,1)}, bf16[1024,1024]{1,0:T(8,128)(2,1)}, bf16[1024,1024]{1,0:T(8,128)(2,1)}, f32[1024,48]{1,0:T(8,128)}) custom-call(bf16[1024,2048]{1,0:T(8,128)(2,1)} %get-tuple-element.215.whole_ref, bf16[1024,32]{1,0:T(8,128)(2,1)} %get-tuple-element.216.low_ref, bf16[2048,2048]{1,0:T(8,128)(2,1)} %finish.3.gate_ref.up_ref.w_ref, ...), custom_call_target="tpu_custom_call" | custom-call | tf_op jit(solution)/shard_map/units/pallas_call | solution.py:571
  402.1 9.5 %units_back.2 = (bf16[2,256,1024]{2,1,0:T(8,128)(2,1)}, bf16[2,256,1024]{2,1,0:T(8,128)(2,1)}) custom-call(bf16[1024,2048]{1,0:T(8,128)(2,1)} %units_back_first.1.first_ref, bf16[1024,1024]{1,0:T(8,128)(2,1)} %get-tuple-element.268.g_ref.dg_ref, bf16[1024,1024]{1,0:T(8,128)(2,1)} %get-tuple-element.269.u_ref.du_ref, ...), custom_call_target="tpu_custom_call" | custom-call | tf_op jit(solution)/shard_map/units_back/pallas_call | solution.py:657
  411.6 2.9 collective-permute-done.60
  415.7 9.5 %units_back.3 = (bf16[2,256,1024]{2,1,0:T(8,128)(2,1)}, bf16[2,256,1024]{2,1,0:T(8,128)(2,1)}) custom-call(bf16[1024,2048]{1,0:T(8,128)(2,1)} %units_back_first.1.first_ref, bf16[1024,1024]{1,0:T(8,128)(2,1)} %get-tuple-element.268.g_ref.dg_ref, bf16[1024,1024]{1,0:T(8,128)(2,1)} %get-tuple-element.269.u_ref.du_ref, ...), custom_call_target="tpu_custom_call" | custom-call | tf_op jit(solution)/shard_map/units_back/pallas_call | solution.py:657
  428.1 2.4 fusion.9
  432.4 7.6 %collective-permute-done.61 = bf16[256,1024]{1,0:T(8,128)(2,1)S(1)} collective-permute-done((bf16[256,1024]{1,0:T(8,128)(2,1)S(1)}, bf16[256,1024]{1,0:T(8,128)(2,1)S(1)}, u32[]{:S(2)}, u32[]{:S(2)}) %collective-permute-start.61) | collective-permute-done | bytes 524320 | tf_op jit(solution)/shard_map/ppermute | solution.py:146
  440.4 5.4 units_grads.3
  445.8 16.8 %lower.1 = (bf16[2,256,2048]{2,1,0:T(8,128)(2,1)}, bf16[2,256,2048]{2,1,0:T(8,128)(2,1)}, f32[16,2048]{1,0:T(8,128)}, f32[32,2048]{1,0:T(8,128)}) custom-call(bf16[1024,1024]{1,0:T(8,128)(2,1)} %get-tuple-element.256.act_ref.aa_ref, bf16[1024,1024]{1,0:T(8,128)(2,1)} %get-tuple-element.279.act_ref.ab_ref, bf16[2048,2048]{1,0:T(8,128)(2,1)} %get-tuple-element.241.weight_ref, ...), custom_call_target="tpu_custom_call" | custom-call | tf_op jit(solution)/shard_map/lower/pallas_call | solution.py:702
  468.0 4.1 collective-permute-done.64
  477.4 6.7 %project_out_back.1.do_ref = bf16[2048,256]{1,0:T(8,128)(2,1)} custom-call(s32[32]{0:T(128)} %stack.163.order_ref, bf16[256,2048]{1,0:T(8,128)(2,1)} %copy-done.27, bf16[16,2048]{1,0:T(8,128)(2,1)} %get-tuple-element.210.a_ref, bf16[256,16]{1,0:T(8,128)(2,1)} %convolution_convert_fusion.1.inner_ref, bf16[64,5120]{1,0:T(8,128)(2,1)} %copy-done.7, ...), custom_call_target="tpu_custom_call" | custom-call | tf_op jit(solution)/shard_map/project_out_back/pallas_call | solution.py:406
  484.1 12.2 %attend_back.2 = (f32[1024,256]{1,0:T(8,128)}, bf16[2,4,128,256]{3,2,1,0:T(8,128)(2,1)}, bf16[2,4,128,256]{3,2,1,0:T(8,128)(2,1)}) custom-call(bf16[2048,256]{1,0:T(8,128)(2,1)} %bitcast.186, bf16[8,128,256]{2,1,0:T(8,128)(2,1)} %copy-done.29, bf16[8,128,256]{2,1,0:T(8,128)(2,1)} %copy-done.33, bf16[8,128,256]{2,1,0:T(8,128)(2,1)} %copy-done.32, ...), custom_call_target="tpu_custom_call" | custom-call | tf_op jit(solution)/shard_map/attend_back/pallas_call | solution.py:801
  496.5 2.7 collective-permute-done.65
  499.2 3.4 bitcast_add_fusion
  508.8 12.0 %attend_back.3 = (f32[1024,256]{1,0:T(8,128)}, bf16[2,4,128,256]{3,2,1,0:T(8,128)(2,1)}, bf16[2,4,128,256]{3,2,1,0:T(8,128)(2,1)}) custom-call(bf16[2048,256]{1,0:T(8,128)(2,1)} %bitcast.187, bf16[8,128,256]{2,1,0:T(8,128)(2,1)} %copy-done.29, bf16[8,128,256]{2,1,0:T(8,128)(2,1)} %copy-done.33, bf16[8,128,256]{2,1,0:T(8,128)(2,1)} %copy-done.32, ...), custom_call_target="tpu_custom_call" | custom-call | tf_op jit(solution)/shard_map/attend_back/pallas_call | solution.py:801
  525.0 2.3 pack.2
  539.6 4.2 all-to-all-start.4
  551.9 2.3 pack.3
  558.3 6.0 %collective-permute-done.73 = f32[8,16,288]{2,1,0:T(8,128)S(1)} collective-permute-done((f32[8,16,288]{2,1,0:T(8,128)S(1)}, f32[8,16,288]{2,1,0:T(8,128)S(1)}, u32[]{:S(2)}, u32[]{:S(2)}) %collective-permute-start.73) | collective-permute-done | bytes 147488 | tf_op jit(solution)/shard_map/ppermute | solution.py:146
  565.0 6.2 %all-to-all-start.5 = ((f32[8,16,288]{2,1,0:T(8,128)}), f32[8,16,288]{2,1,0:T(8,128)S(1)}, u32[]{:S(2)}, u32[]{:S(2)}) async-start(f32[8,16,288]{2,1,0:T(8,128)} %fusion.12), calls=%async_computation.5 | async-start | bytes 393216 | tf_op jit(solution)/shard_map/all_to_all | solution.py:1151
  571.2 2.3 sort.2
  573.5 11.2 %project_in_back.1 = bf16[256,2048]{1,0:T(8,128)(2,1)} custom-call(s32[32]{0:T(128)} %stack.163.order_ref, bf16[3072,256]{1,0:T(8,128)(2,1)} %copy-done.2, bf16[48,2048]{1,0:T(8,128)(2,1)} %get-tuple-element.207.a_ref, bf16[48,256]{1,0:T(8,128)(2,1)} %copy-done.67, bf16[256,2048]{1,0:T(8,128)(2,1)} %bitcast.189, f32[1,2048]{1,0:T(1,128)} %bitcast.212, ...), custom_call_target="tpu_custom_call" | custom-call | tf_op jit(solution)/shard_map/project_in_back/pallas_call | solution.py:452
  (400 shorter events, 138.7 us)
Async XLA Ops:
  4.3 23.8 %collective-permute-start = (bf16[64,5120]{1,0:T(8,128)(2,1)S(1)}, bf16[64,5120]{1,0:T(8,128)(2,1)S(1)}, u32[]{:S(2)}, u32[]{:S(2)}) collective-permute-start(bf16[64,5120]{1,0:T(8,128)(2,1)S(1)} %constant_dynamic-update-slice_fusion.refs_0_), channel_id=1, source_target_pairs={{0,8},{8,16},{16,24},{24,28},{28,20},{20,12},{12,4},{4,0},{1,9},{9... | collective-permute-start | bytes 1966088 | tf_op jit(solution)/shard_map/ppermute | solution.py:81
  7.4 20.8 %collective-permute-start.1 = (bf16[64,5120]{1,0:T(8,128)(2,1)S(1)}, bf16[64,5120]{1,0:T(8,128)(2,1)S(1)}, u32[]{:S(2)}, u32[]{:S(2)}) collective-permute-start(bf16[64,5120]{1,0:T(8,128)(2,1)S(1)} %constant_dynamic-update-slice_fusion.refs_0_), channel_id=1, source_target_pairs={{8,0},{16,8},{24,16},{28,24},{20,28},{12,20},{4,12},{0,4},{9,1},{1... | collective-permute-start | bytes 1966088 | tf_op jit(solution)/shard_map/ppermute | solution.py:82
  7.4 20.8 %collective-permute-start.2 = (bf16[64,5120]{1,0:T(8,128)(2,1)S(1)}, bf16[64,5120]{1,0:T(8,128)(2,1)S(1)}, u32[]{:S(2)}, u32[]{:S(2)}) collective-permute-start(bf16[64,5120]{1,0:T(8,128)(2,1)S(1)} %constant_dynamic-update-slice_fusion.refs_0_), channel_id=1, source_target_pairs={{0,1},{1,0},{2,3},{3,2},{4,5},{5,4},{6,7},{7,6},{8,9},{9,8},{10,11... | collective-permute-start | bytes 1966088 | tf_op jit(solution)/shard_map/ppermute | solution.py:146
  7.4 20.8 %collective-permute-start.3 = (bf16[64,5120]{1,0:T(8,128)(2,1)S(1)}, bf16[64,5120]{1,0:T(8,128)(2,1)S(1)}, u32[]{:S(2)}, u32[]{:S(2)}) collective-permute-start(bf16[64,5120]{1,0:T(8,128)(2,1)S(1)} %constant_dynamic-update-slice_fusion.refs_0_), channel_id=1, source_target_pairs={{0,2},{1,3},{2,0},{3,1},{4,6},{5,7},{6,4},{7,5},{8,10},{9,11},{10,... | collective-permute-start | bytes 1966088 | tf_op jit(solution)/shard_map/ppermute | solution.py:146
  10.6 15.1 %all-to-all-start = ((s32[8,1,128]{2,1,0:T(1,128)}), s32[8,1,128]{2,1,0:T(1,128)S(1)}, u32[]{:S(2)}, u32[]{:S(2)}) async-start(s32[8,1,128]{2,1,0:T(1,128)} %broadcast_in_dim.24), calls=%async_computation | async-start | bytes 8192 | tf_op jit(solution)/shard_map/all_to_all | solution.py:1022
  28.2 15.0 %collective-permute-start.5 = (bf16[64,5120]{1,0:T(8,128)(2,1)S(1)}, bf16[64,5120]{1,0:T(8,128)(2,1)S(1)}, u32[]{:S(2)}, u32[]{:S(2)}) collective-permute-start(bf16[64,5120]{1,0:T(8,128)(2,1)S(1)} %collective-permute-done.1.refs_8_), channel_id=1, source_target_pairs={{8,0},{16,8},{24,16},{28,24},{20,28},{12,20},{4,12},{0,4},{9,1},{1... | collective-permute-start | bytes 1966088 | tf_op jit(solution)/shard_map/ppermute | solution.py:82
  29.7 13.5 %collective-permute-start.8 = (bf16[64,5120]{1,0:T(8,128)(2,1)S(1)}, bf16[64,5120]{1,0:T(8,128)(2,1)S(1)}, u32[]{:S(2)}, u32[]{:S(2)}) collective-permute-start(bf16[64,5120]{1,0:T(8,128)(2,1)S(1)} %collective-permute-done.1.refs_8_), channel_id=1, source_target_pairs={{0,1},{1,0},{2,3},{3,2},{4,5},{5,4},{6,7},{7,6},{8,9},{9,8},{10,11... | collective-permute-start | bytes 1966088 | tf_op jit(solution)/shard_map/ppermute | solution.py:146
  29.7 17.3 %collective-permute-start.4 = (bf16[64,5120]{1,0:T(8,128)(2,1)S(1)}, bf16[64,5120]{1,0:T(8,128)(2,1)}, u32[]{:S(2)}, u32[]{:S(2)}) collective-permute-start(bf16[64,5120]{1,0:T(8,128)(2,1)S(1)} %collective-permute-done.refs_4_), channel_id=1, source_target_pairs={{0,8},{8,16},{16,24},{24,28},{28,20},{20,12},{12,4},{4,0},{1,9},{9... | collective-permute-start | bytes 1966088 | tf_op jit(solution)/shard_map/ppermute | solution.py:81
  30.3 16.7 %collective-permute-start.7 = (bf16[64,5120]{1,0:T(8,128)(2,1)S(1)}, bf16[64,5120]{1,0:T(8,128)(2,1)S(1)}, u32[]{:S(2)}, u32[]{:S(2)}) collective-permute-start(bf16[64,5120]{1,0:T(8,128)(2,1)S(1)} %collective-permute-done.refs_4_), channel_id=1, source_target_pairs={{0,1},{1,0},{2,3},{3,2},{4,5},{5,4},{6,7},{7,6},{8,9},{9,8},{10,11... | collective-permute-start | bytes 1966088 | tf_op jit(solution)/shard_map/ppermute | solution.py:146
  30.5 16.9 %collective-permute-start.9 = (bf16[64,5120]{1,0:T(8,128)(2,1)S(1)}, bf16[64,5120]{1,0:T(8,128)(2,1)S(1)}, u32[]{:S(2)}, u32[]{:S(2)}) collective-permute-start(bf16[64,5120]{1,0:T(8,128)(2,1)S(1)} %collective-permute-done.refs_4_), channel_id=1, source_target_pairs={{0,2},{1,3},{2,0},{3,1},{4,6},{5,7},{6,4},{7,5},{8,10},{9,11},{10,... | collective-permute-start | bytes 1966088 | tf_op jit(solution)/shard_map/ppermute | solution.py:146
  49.1 16.4 %collective-permute-start.11 = (bf16[64,5120]{1,0:T(8,128)(2,1)}, bf16[64,5120]{1,0:T(8,128)(2,1)S(1)}, u32[]{:S(2)}, u32[]{:S(2)}) collective-permute-start(bf16[64,5120]{1,0:T(8,128)(2,1)} %collective-permute-done.4.refs_12_), channel_id=1, source_target_pairs={{0,8},{8,16},{16,24},{24,28},{28,20},{20,12},{12,4},{4,0},{1,9},{9... | collective-permute-start | bytes 1966088 | tf_op jit(solution)/shard_map/ppermute | solution.py:81
  49.7 19.3 %all-to-all-start.1 = ((bf16[4,64,2048]{2,1,0:T(8,128)(2,1)}), bf16[4,64,2048]{2,1,0:T(8,128)(2,1)}, u32[]{:S(2)}, u32[]{:S(2)}) async-start(bf16[4,64,2048]{2,1,0:T(8,128)(2,1)} %get-tuple-element.180), calls=%async_computation.1 | async-start | bytes 2097152 | tf_op jit(solution)/shard_map/all_to_all | solution.py:1030
  54.0 28.6 %collective-permute-start.16 = (bf16[64,5120]{1,0:T(8,128)(2,1)S(1)}, bf16[64,5120]{1,0:T(8,128)(2,1)}, u32[]{:S(2)}, u32[]{:S(2)}) collective-permute-start(bf16[64,5120]{1,0:T(8,128)(2,1)S(1)} %collective-permute-done.1.refs_8_), channel_id=1, source_target_pairs={{0,2},{1,3},{2,0},{3,1},{4,6},{5,7},{6,4},{7,5},{8,10},{9,11},{10,... | collective-permute-start | bytes 1966088 | tf_op jit(solution)/shard_map/ppermute | solution.py:146
  56.0 26.6 %collective-permute-start.14 = (bf16[64,5120]{1,0:T(8,128)(2,1)}, bf16[64,5120]{1,0:T(8,128)(2,1)}, u32[]{:S(2)}, u32[]{:S(2)}) collective-permute-start(bf16[64,5120]{1,0:T(8,128)(2,1)} %collective-permute-done.4.refs_12_), channel_id=1, source_target_pairs={{0,1},{1,0},{2,3},{3,2},{4,5},{5,4},{6,7},{7,6},{8,9},{9,8},{10,11... | collective-permute-start | bytes 1966088 | tf_op jit(solution)/shard_map/ppermute | solution.py:146
  56.0 26.6 %collective-permute-start.12 = (bf16[64,5120]{1,0:T(8,128)(2,1)}, bf16[64,5120]{1,0:T(8,128)(2,1)S(1)}, u32[]{:S(2)}, u32[]{:S(2)}) collective-permute-start(bf16[64,5120]{1,0:T(8,128)(2,1)} %copy-done.12), channel_id=1, source_target_pairs={{8,0},{16,8},{24,16},{28,24},{20,28},{12,20},{4,12},{0,4},{9,1},{1... | collective-permute-start | bytes 1966088 | tf_op jit(solution)/shard_map/ppermute | solution.py:82
  57.4 25.1 %collective-permute-start.15 = (bf16[64,5120]{1,0:T(8,128)(2,1)}, bf16[64,5120]{1,0:T(8,128)(2,1)}, u32[]{:S(2)}, u32[]{:S(2)}) collective-permute-start(bf16[64,5120]{1,0:T(8,128)(2,1)} %copy-done.12), channel_id=1, source_target_pairs={{0,1},{1,0},{2,3},{3,2},{4,5},{5,4},{6,7},{7,6},{8,9},{9,8},{10,11... | collective-permute-start | bytes 1966088 | tf_op jit(solution)/shard_map/ppermute | solution.py:146
  65.6 17.0 %collective-permute-start.13 = (bf16[64,5120]{1,0:T(8,128)(2,1)}, bf16[64,5120]{1,0:T(8,128)(2,1)}, u32[]{:S(2)}, u32[]{:S(2)}) collective-permute-start(bf16[64,5120]{1,0:T(8,128)(2,1)} %copy-done.16), channel_id=1, source_target_pairs={{0,1},{1,0},{2,3},{3,2},{4,5},{5,4},{6,7},{7,6},{8,9},{9,8},{10,11... | collective-permute-start | bytes 1966088 | tf_op jit(solution)/shard_map/ppermute | solution.py:146
  69.0 18.5 %all-to-all-start.2 = ((bf16[8,16,1376]{2,1,0:T(8,128)(2,1)}), bf16[8,16,1376]{2,1,0:T(8,128)(2,1)}, u32[]{:S(2)}, u32[]{:S(2)}) async-start(bf16[8,16,1376]{2,1,0:T(8,128)(2,1)} %pick.1), calls=%async_computation.2 | async-start | bytes 720896 | tf_op jit(solution)/shard_map/all_to_all | solution.py:1032
  82.6 9.5 %collective-permute-start.17 = (bf16[32,5120]{1,0:T(8,128)(2,1)}, bf16[32,5120]{1,0:T(8,128)(2,1)S(1)}, u32[]{:S(2)}, u32[]{:S(2)}) collective-permute-start(bf16[32,5120]{1,0:T(8,128)(2,1)} %slice.205), channel_id=1, source_target_pairs={{0,8},{8,16},{16,24},{24,28},{28,20},{20,12},{12,4},{4,0},{1,9},{9... | collective-permute-start | bytes 983048 | tf_op jit(solution)/shard_map/ppermute | solution.py:86
  83.3 17.9 %collective-permute-start.10 = (bf16[64,5120]{1,0:T(8,128)(2,1)}, bf16[64,5120]{1,0:T(8,128)(2,1)S(1)}, u32[]{:S(2)}, u32[]{:S(2)}) collective-permute-start(bf16[64,5120]{1,0:T(8,128)(2,1)} %collective-permute-done.4.refs_12_), channel_id=1, source_target_pairs={{0,2},{1,3},{2,0},{3,1},{4,6},{5,7},{6,4},{7,5},{8,10},{9,11},{10,... | collective-permute-start | bytes 1966088 | tf_op jit(solution)/shard_map/ppermute | solution.py:146
  83.6 30.0 %collective-permute-start.25 = (bf16[64,5120]{1,0:T(8,128)(2,1)S(1)}, bf16[64,5120]{1,0:T(8,128)(2,1)}, u32[]{:S(2)}, u32[]{:S(2)}) collective-permute-start(bf16[64,5120]{1,0:T(8,128)(2,1)S(1)} %copy-done.13), channel_id=1, source_target_pairs={{0,2},{1,3},{2,0},{3,1},{4,6},{5,7},{6,4},{7,5},{8,10},{9,11},{10,... | collective-permute-start | bytes 1966088 | tf_op jit(solution)/shard_map/ppermute | solution.py:146
  86.0 8.7 %collective-permute-start.18 = (bf16[32,5120]{1,0:T(8,128)(2,1)}, bf16[32,5120]{1,0:T(8,128)(2,1)}, u32[]{:S(2)}, u32[]{:S(2)}) collective-permute-start(bf16[32,5120]{1,0:T(8,128)(2,1)} %slice.206), channel_id=1, source_target_pairs={{8,0},{16,8},{24,16},{28,24},{20,28},{12,20},{4,12},{0,4},{9,1},{1... | collective-permute-start | bytes 983048 | tf_op jit(solution)/shard_map/ppermute | solution.py:87
  87.4 13.7 %collective-permute-start.21 = (bf16[64,5120]{1,0:T(8,128)(2,1)S(1)}, bf16[64,5120]{1,0:T(8,128)(2,1)}, u32[]{:S(2)}, u32[]{:S(2)}) collective-permute-start(bf16[64,5120]{1,0:T(8,128)(2,1)S(1)} %collective-permute-done.11.refs_20_), channel_id=1, source_target_pairs={{0,1},{1,0},{2,3},{3,2},{4,5},{5,4},{6,7},{7,6},{8,9},{9,8},{10,11... | collective-permute-start | bytes 1966088 | tf_op jit(solution)/shard_map/ppermute | solution.py:146
  92.8 8.3 %collective-permute-start.19 = (bf16[64,5120]{1,0:T(8,128)(2,1)}, bf16[64,5120]{1,0:T(8,128)(2,1)S(1)}, u32[]{:S(2)}, u32[]{:S(2)}) collective-permute-start(bf16[64,5120]{1,0:T(8,128)(2,1)} %collective-permute-done.16.refs_10_), channel_id=1, source_target_pairs={{0,1},{1,0},{2,3},{3,2},{4,5},{5,4},{6,7},{7,6},{8,9},{9,8},{10,11... | collective-permute-start | bytes 1966088 | tf_op jit(solution)/shard_map/ppermute | solution.py:146
  101.2 13.8 %collective-permute-start.24 = (bf16[64,5120]{1,0:T(8,128)(2,1)S(1)}, bf16[64,5120]{1,0:T(8,128)(2,1)}, u32[]{:S(2)}, u32[]{:S(2)}) collective-permute-start(bf16[64,5120]{1,0:T(8,128)(2,1)S(1)} %constant_dynamic-update-slice_fusion.4.refs_28_), channel_id=1, source_target_pairs={{0,1},{1,0},{2,3},{3,2},{4,5},{5,4},{6,7},{7,6},{8,9},{9,8},{10,11... | collective-permute-start | bytes 1966088 | tf_op jit(solution)/shard_map/ppermute | solution.py:146
  102.1 13.6 %collective-permute-start.23 = (bf16[64,5120]{1,0:T(8,128)(2,1)S(1)}, bf16[64,5120]{1,0:T(8,128)(2,1)}, u32[]{:S(2)}, u32[]{:S(2)}) collective-permute-start(bf16[64,5120]{1,0:T(8,128)(2,1)S(1)} %collective-permute-done.12.refs_24_), channel_id=1, source_target_pairs={{0,1},{1,0},{2,3},{3,2},{4,5},{5,4},{6,7},{7,6},{8,9},{9,8},{10,11... | collective-permute-start | bytes 1966088 | tf_op jit(solution)/shard_map/ppermute | solution.py:146
  102.1 13.6 %collective-permute-start.22 = (bf16[64,5120]{1,0:T(8,128)(2,1)S(1)}, bf16[64,5120]{1,0:T(8,128)(2,1)}, u32[]{:S(2)}, u32[]{:S(2)}) collective-permute-start(bf16[64,5120]{1,0:T(8,128)(2,1)S(1)} %collective-permute-done.10.refs_14_), channel_id=1, source_target_pairs={{0,1},{1,0},{2,3},{3,2},{4,5},{5,4},{6,7},{7,6},{8,9},{9,8},{10,11... | collective-permute-start | bytes 1966088 | tf_op jit(solution)/shard_map/ppermute | solution.py:146
  106.1 47.9 %collective-permute-start.32 = (bf16[512,2048]{1,0:T(8,128)(2,1)}, bf16[512,2048]{1,0:T(8,128)(2,1)}, u32[]{:S(2)}, u32[]{:S(2)}) collective-permute-start(bf16[512,2048]{1,0:T(8,128)(2,1)} %pad_maximum_fusion.refs_0_), channel_id=1, source_target_pairs={{0,8},{8,16},{16,24},{24,28},{28,20},{20,12},{12,4},{4,0},{1,9},{9... | collective-permute-start | bytes 6291464 | tf_op jit(solution)/shard_map/ppermute | solution.py:81
  113.6 46.3 %collective-permute-start.33 = (bf16[512,2048]{1,0:T(8,128)(2,1)}, bf16[512,2048]{1,0:T(8,128)(2,1)}, u32[]{:S(2)}, u32[]{:S(2)}) collective-permute-start(bf16[512,2048]{1,0:T(8,128)(2,1)} %pad_maximum_fusion.refs_0_), channel_id=1, source_target_pairs={{8,0},{16,8},{24,16},{28,24},{20,28},{12,20},{4,12},{0,4},{9,1},{1... | collective-permute-start | bytes 6291464 | tf_op jit(solution)/shard_map/ppermute | solution.py:82
  115.0 10.2 %collective-permute-start.26 = (bf16[8,16,608]{2,1,0:T(8,128)(2,1)S(1)}, bf16[8,16,608]{2,1,0:T(8,128)(2,1)}, u32[]{:S(2)}, u32[]{:S(2)}) collective-permute-start(bf16[8,16,608]{2,1,0:T(8,128)(2,1)S(1)} %slice.158), channel_id=1, source_target_pairs={{0,2},{1,3},{2,0},{3,1},{4,6},{5,7},{6,4},{7,5},{8,10},{9,11},{10,... | collective-permute-start | bytes 466952 | tf_op jit(solution)/shard_map/ppermute | solution.py:146
  115.6 20.5 %collective-permute-start.29 = (bf16[64,5120]{1,0:T(8,128)(2,1)S(1)}, bf16[64,5120]{1,0:T(8,128)(2,1)S(1)}, u32[]{:S(2)}, u32[]{:S(2)}) collective-permute-start(bf16[64,5120]{1,0:T(8,128)(2,1)S(1)} %collective-permute-done.11.refs_20_), channel_id=1, source_target_pairs={{0,2},{1,3},{2,0},{3,1},{4,6},{5,7},{6,4},{7,5},{8,10},{9,11},{10,... | collective-permute-start | bytes 1966088 | tf_op jit(solution)/shard_map/ppermute | solution.py:146
  125.2 11.0 %collective-permute-start.28 = (bf16[8,16,608]{2,1,0:T(8,128)(2,1)}, bf16[8,16,608]{2,1,0:T(8,128)(2,1)S(1)}, u32[]{:S(2)}, u32[]{:S(2)}) collective-permute-start(bf16[8,16,608]{2,1,0:T(8,128)(2,1)} %collective-permute-done.26.p2), channel_id=1, source_target_pairs={{0,1},{1,0},{2,3},{3,2},{4,5},{5,4},{6,7},{7,6},{8,9},{9,8},{10,11... | collective-permute-start | bytes 466952 | tf_op jit(solution)/shard_map/ppermute | solution.py:146
  125.7 34.2 %collective-permute-start.31 = (bf16[64,5120]{1,0:T(8,128)(2,1)S(1)}, bf16[64,5120]{1,0:T(8,128)(2,1)S(1)}, u32[]{:S(2)}, u32[]{:S(2)}) collective-permute-start(bf16[64,5120]{1,0:T(8,128)(2,1)S(1)} %collective-permute-done.12.refs_24_), channel_id=1, source_target_pairs={{0,2},{1,3},{2,0},{3,1},{4,6},{5,7},{6,4},{7,5},{8,10},{9,11},{10,... | collective-permute-start | bytes 1966088 | tf_op jit(solution)/shard_map/ppermute | solution.py:146
  136.2 23.7 %collective-permute-start.34 = (bf16[64,5120]{1,0:T(8,128)(2,1)S(1)}, bf16[64,5120]{1,0:T(8,128)(2,1)S(1)}, u32[]{:S(2)}, u32[]{:S(2)}) collective-permute-start(bf16[64,5120]{1,0:T(8,128)(2,1)S(1)} %collective-permute-done.29.refs_22_), channel_id=1, source_target_pairs={{0,1},{1,0},{2,3},{3,2},{4,5},{5,4},{6,7},{7,6},{8,9},{9,8},{10,11... | collective-permute-start | bytes 1966088 | tf_op jit(solution)/shard_map/ppermute | solution.py:146
  136.3 25.2 %collective-permute-start.30 = (bf16[64,5120]{1,0:T(8,128)(2,1)S(1)}, bf16[64,5120]{1,0:T(8,128)(2,1)}, u32[]{:S(2)}, u32[]{:S(2)}) collective-permute-start(bf16[64,5120]{1,0:T(8,128)(2,1)S(1)} %constant_dynamic-update-slice_fusion.4.refs_28_), channel_id=1, source_target_pairs={{0,2},{1,3},{2,0},{3,1},{4,6},{5,7},{6,4},{7,5},{8,10},{9,11},{10,... | collective-permute-start | bytes 1966088 | tf_op jit(solution)/shard_map/ppermute | solution.py:146
  163.1 48.3 %collective-permute-start.44 = (bf16[512,2048]{1,0:T(8,128)(2,1)}, bf16[512,2048]{1,0:T(8,128)(2,1)}, u32[]{:S(2)}, u32[]{:S(2)}) collective-permute-start(bf16[512,2048]{1,0:T(8,128)(2,1)} %collective-permute-done.33.refs_2_), channel_id=1, source_target_pairs={{8,0},{16,8},{24,16},{28,24},{20,28},{12,20},{4,12},{0,4},{9,1},{1... | collective-permute-start | bytes 6291464 | tf_op jit(solution)/shard_map/ppermute | solution.py:82
  164.5 47.9 %collective-permute-start.43 = (bf16[512,2048]{1,0:T(8,128)(2,1)}, bf16[512,2048]{1,0:T(8,128)(2,1)}, u32[]{:S(2)}, u32[]{:S(2)}) collective-permute-start(bf16[512,2048]{1,0:T(8,128)(2,1)} %collective-permute-done.32.refs_1_), channel_id=1, source_target_pairs={{0,8},{8,16},{16,24},{24,28},{28,20},{20,12},{12,4},{4,0},{1,9},{9... | collective-permute-start | bytes 6291464 | tf_op jit(solution)/shard_map/ppermute | solution.py:81
  184.3 30.6 %collective-permute-start.38 = (bf16[8,128,256]{2,1,0:T(8,128)(2,1)S(1)}, bf16[8,128,256]{2,1,0:T(8,128)(2,1)S(1)}, u32[]{:S(2)}, u32[]{:S(2)}) collective-permute-start(bf16[8,128,256]{2,1,0:T(8,128)(2,1)S(1)} %pad_maximum_fusion.2.kv0), channel_id=1, source_target_pairs={{0,2},{1,3},{2,0},{3,1},{4,6},{5,7},{6,4},{7,5},{8,10},{9,11},{10,... | collective-permute-start | bytes 1572872 | tf_op jit(solution)/shard_map/ppermute | solution.py:146
  212.5 47.1 %collective-permute-start.46 = (bf16[512,2048]{1,0:T(8,128)(2,1)}, bf16[512,2048]{1,0:T(8,128)(2,1)}, u32[]{:S(2)}, u32[]{:S(2)}) collective-permute-start(bf16[512,2048]{1,0:T(8,128)(2,1)} %collective-permute-done.44.refs_4_), channel_id=1, source_target_pairs={{8,0},{16,8},{24,16},{28,24},{20,28},{12,20},{4,12},{0,4},{9,1},{1... | collective-permute-start | bytes 6291464 | tf_op jit(solution)/shard_map/ppermute | solution.py:82
  213.9 48.0 %collective-permute-start.45 = (bf16[512,2048]{1,0:T(8,128)(2,1)}, bf16[512,2048]{1,0:T(8,128)(2,1)}, u32[]{:S(2)}, u32[]{:S(2)}) collective-permute-start(bf16[512,2048]{1,0:T(8,128)(2,1)} %collective-permute-done.43.refs_3_), channel_id=1, source_target_pairs={{0,8},{8,16},{16,24},{24,28},{28,20},{20,12},{12,4},{4,0},{1,9},{9... | collective-permute-start | bytes 6291464 | tf_op jit(solution)/shard_map/ppermute | solution.py:81
  216.7 32.4 %collective-permute-start.50 = (bf16[256,2048]{1,0:T(8,128)(2,1)}, bf16[256,2048]{1,0:T(8,128)(2,1)}, u32[]{:S(2)}, u32[]{:S(2)}) collective-permute-start(bf16[256,2048]{1,0:T(8,128)(2,1)} %multiply_convert_fusion.1.g0), channel_id=1, source_target_pairs={{0,2},{1,3},{2,0},{3,1},{4,6},{5,7},{6,4},{7,5},{8,10},{9,11},{10,... | collective-permute-start | bytes 3145736 | tf_op jit(solution)/shard_map/ppermute | solution.py:146
  217.6 63.1 %collective-permute-start.49 = (bf16[256,2048]{1,0:T(8,128)(2,1)}, bf16[256,2048]{1,0:T(8,128)(2,1)}, u32[]{:S(2)}, u32[]{:S(2)}) collective-permute-start(bf16[256,2048]{1,0:T(8,128)(2,1)} %multiply_convert_fusion.1.g0), channel_id=1, source_target_pairs={{0,1},{1,0},{2,3},{3,2},{4,5},{5,4},{6,7},{7,6},{8,9},{9,8},{10,11... | collective-permute-start | bytes 3145736 | tf_op jit(solution)/shard_map/ppermute | solution.py:146
  243.7 37.7 %collective-permute-start.41 = (bf16[256,2048]{1,0:T(8,128)(2,1)}, bf16[256,2048]{1,0:T(8,128)(2,1)}, u32[]{:S(2)}, u32[]{:S(2)}) collective-permute-start(bf16[256,2048]{1,0:T(8,128)(2,1)} %get-tuple-element.213.n0), channel_id=1, source_target_pairs={{0,2},{1,3},{2,0},{3,1},{4,6},{5,7},{6,4},{7,5},{8,10},{9,11},{10,... | collective-permute-start | bytes 3145736 | tf_op jit(solution)/shard_map/ppermute | solution.py:146
  244.9 35.8 %all-to-all-start.3 = ((bf16[4,64,2048]{2,1,0:T(8,128)(2,1)}), bf16[4,64,2048]{2,1,0:T(8,128)(2,1)}, u32[]{:S(2)}, u32[]{:S(2)}) async-start(bf16[4,64,2048]{2,1,0:T(8,128)(2,1)} %get-tuple-element.246), calls=%async_computation.3 | async-start | bytes 2097152 | tf_op jit(solution)/shard_map/all_to_all | solution.py:1084
  249.2 44.9 %collective-permute-start.51 = (bf16[256,2048]{1,0:T(8,128)(2,1)}, bf16[256,2048]{1,0:T(8,128)(2,1)}, u32[]{:S(2)}, u32[]{:S(2)}) collective-permute-start(bf16[256,2048]{1,0:T(8,128)(2,1)} %collective-permute-done.50.g2), channel_id=1, source_target_pairs={{0,1},{1,0},{2,3},{3,2},{4,5},{5,4},{6,7},{7,6},{8,9},{9,8},{10,11... | collective-permute-start | bytes 3145736 | tf_op jit(solution)/shard_map/ppermute | solution.py:146
  261.9 32.3 %collective-permute-start.48 = (bf16[256,2048]{1,0:T(8,128)(2,1)}, bf16[256,2048]{1,0:T(8,128)(2,1)}, u32[]{:S(2)}, u32[]{:S(2)}) collective-permute-start(bf16[256,2048]{1,0:T(8,128)(2,1)} %slice.215), channel_id=1, source_target_pairs={{8,0},{16,8},{24,16},{28,24},{20,28},{12,20},{4,12},{0,4},{9,1},{1... | collective-permute-start | bytes 3145736 | tf_op jit(solution)/shard_map/ppermute | solution.py:87
  265.7 29.0 %collective-permute-start.47 = (bf16[256,2048]{1,0:T(8,128)(2,1)}, bf16[256,2048]{1,0:T(8,128)(2,1)}, u32[]{:S(2)}, u32[]{:S(2)}) collective-permute-start(bf16[256,2048]{1,0:T(8,128)(2,1)} %slice.214), channel_id=1, source_target_pairs={{0,8},{8,16},{16,24},{24,28},{28,20},{20,12},{12,4},{4,0},{1,9},{9... | collective-permute-start | bytes 3145736 | tf_op jit(solution)/shard_map/ppermute | solution.py:86
  280.7 32.7 %collective-permute-start.52 = (bf16[256,2048]{1,0:T(8,128)(2,1)}, bf16[256,2048]{1,0:T(8,128)(2,1)}, u32[]{:S(2)}, u32[]{:S(2)}) collective-permute-start(bf16[256,2048]{1,0:T(8,128)(2,1)} %bitcast.69.refs_0_), channel_id=1, source_target_pairs={{0,8},{8,16},{16,24},{24,28},{28,20},{20,12},{12,4},{4,0},{1,9},{9... | collective-permute-start | bytes 3145736 | tf_op jit(solution)/shard_map/ppermute | solution.py:81
  281.3 32.1 %collective-permute-start.53 = (bf16[256,2048]{1,0:T(8,128)(2,1)}, bf16[256,2048]{1,0:T(8,128)(2,1)}, u32[]{:S(2)}, u32[]{:S(2)}) collective-permute-start(bf16[256,2048]{1,0:T(8,128)(2,1)} %bitcast.69.refs_0_), channel_id=1, source_target_pairs={{8,0},{16,8},{24,16},{28,24},{20,28},{12,20},{4,12},{0,4},{9,1},{1... | collective-permute-start | bytes 3145736 | tf_op jit(solution)/shard_map/ppermute | solution.py:82
  294.1 21.4 %collective-permute-start.40 = (bf16[256,2048]{1,0:T(8,128)(2,1)S(1)}, bf16[256,2048]{1,0:T(8,128)(2,1)S(1)}, u32[]{:S(2)}, u32[]{:S(2)}) collective-permute-start(bf16[256,2048]{1,0:T(8,128)(2,1)S(1)} %copy-done.47), channel_id=1, source_target_pairs={{0,1},{1,0},{2,3},{3,2},{4,5},{5,4},{6,7},{7,6},{8,9},{9,8},{10,11... | collective-permute-start | bytes 3145736 | tf_op jit(solution)/shard_map/ppermute | solution.py:146
  294.2 21.3 %collective-permute-start.42 = (bf16[256,2048]{1,0:T(8,128)(2,1)}, bf16[256,2048]{1,0:T(8,128)(2,1)}, u32[]{:S(2)}, u32[]{:S(2)}) collective-permute-start(bf16[256,2048]{1,0:T(8,128)(2,1)} %collective-permute-done.41.n2), channel_id=1, source_target_pairs={{0,1},{1,0},{2,3},{3,2},{4,5},{5,4},{6,7},{7,6},{8,9},{9,8},{10,11... | collective-permute-start | bytes 3145736 | tf_op jit(solution)/shard_map/ppermute | solution.py:146
  313.4 26.5 %collective-permute-start.55 = (bf16[256,2048]{1,0:T(8,128)(2,1)}, bf16[256,2048]{1,0:T(8,128)(2,1)S(1)}, u32[]{:S(2)}, u32[]{:S(2)}) collective-permute-start(bf16[256,2048]{1,0:T(8,128)(2,1)} %collective-permute-done.53.refs_2_), channel_id=1, source_target_pairs={{8,0},{16,8},{24,16},{28,24},{20,28},{12,20},{4,12},{0,4},{9,1},{1... | collective-permute-start | bytes 3145736 | tf_op jit(solution)/shard_map/ppermute | solution.py:82
  314.9 25.1 %collective-permute-start.54 = (bf16[256,2048]{1,0:T(8,128)(2,1)}, bf16[256,2048]{1,0:T(8,128)(2,1)S(1)}, u32[]{:S(2)}, u32[]{:S(2)}) collective-permute-start(bf16[256,2048]{1,0:T(8,128)(2,1)} %collective-permute-done.52.refs_1_), channel_id=1, source_target_pairs={{0,8},{8,16},{16,24},{24,28},{28,20},{20,12},{12,4},{4,0},{1,9},{9... | collective-permute-start | bytes 3145736 | tf_op jit(solution)/shard_map/ppermute | solution.py:81
  340.0 24.6 %collective-permute-start.57 = (bf16[256,2048]{1,0:T(8,128)(2,1)S(1)}, bf16[256,2048]{1,0:T(8,128)(2,1)S(1)}, u32[]{:S(2)}, u32[]{:S(2)}) collective-permute-start(bf16[256,2048]{1,0:T(8,128)(2,1)S(1)} %collective-permute-done.55.refs_4_), channel_id=1, source_target_pairs={{8,0},{16,8},{24,16},{28,24},{20,28},{12,20},{4,12},{0,4},{9,1},{1... | collective-permute-start | bytes 3145736 | tf_op jit(solution)/shard_map/ppermute | solution.py:82
  341.4 24.3 %collective-permute-start.56 = (bf16[256,2048]{1,0:T(8,128)(2,1)S(1)}, bf16[256,2048]{1,0:T(8,128)(2,1)S(1)}, u32[]{:S(2)}, u32[]{:S(2)}) collective-permute-start(bf16[256,2048]{1,0:T(8,128)(2,1)S(1)} %collective-permute-done.54.refs_3_), channel_id=1, source_target_pairs={{0,8},{8,16},{16,24},{24,28},{28,20},{20,12},{12,4},{4,0},{1,9},{9... | collective-permute-start | bytes 3145736 | tf_op jit(solution)/shard_map/ppermute | solution.py:81
  365.7 12.2 %collective-permute-start.59 = (bf16[128,2048]{1,0:T(8,128)(2,1)S(1)}, bf16[128,2048]{1,0:T(8,128)(2,1)S(1)}, u32[]{:S(2)}, u32[]{:S(2)}) collective-permute-start(bf16[128,2048]{1,0:T(8,128)(2,1)S(1)} %slice.217), channel_id=1, source_target_pairs={{8,0},{16,8},{24,16},{28,24},{20,28},{12,20},{4,12},{0,4},{9,1},{1... | collective-permute-start | bytes 1572872 | tf_op jit(solution)/shard_map/ppermute | solution.py:87
  367.1 12.1 %collective-permute-start.58 = (bf16[128,2048]{1,0:T(8,128)(2,1)S(1)}, bf16[128,2048]{1,0:T(8,128)(2,1)S(1)}, u32[]{:S(2)}, u32[]{:S(2)}) collective-permute-start(bf16[128,2048]{1,0:T(8,128)(2,1)S(1)} %slice.216), channel_id=1, source_target_pairs={{0,8},{8,16},{16,24},{24,28},{28,20},{20,12},{12,4},{4,0},{1,9},{9... | collective-permute-start | bytes 1572872 | tf_op jit(solution)/shard_map/ppermute | solution.py:86
  425.3 14.8 %collective-permute-start.61 = (bf16[256,1024]{1,0:T(8,128)(2,1)S(1)}, bf16[256,1024]{1,0:T(8,128)(2,1)S(1)}, u32[]{:S(2)}, u32[]{:S(2)}) collective-permute-start(bf16[256,1024]{1,0:T(8,128)(2,1)S(1)} %fusion.8), channel_id=1, source_target_pairs={{0,2},{1,3},{2,0},{3,1},{4,6},{5,7},{6,4},{7,5},{8,10},{9,11},{10,... | collective-permute-start | bytes 1572872 | tf_op jit(solution)/shard_map/ppermute | solution.py:146
  430.5 32.2 %collective-permute-start.63 = (bf16[256,1024]{1,0:T(8,128)(2,1)}, bf16[256,1024]{1,0:T(8,128)(2,1)}, u32[]{:S(2)}, u32[]{:S(2)}) collective-permute-start(bf16[256,1024]{1,0:T(8,128)(2,1)} %fusion.9), channel_id=1, source_target_pairs={{0,2},{1,3},{2,0},{3,1},{4,6},{5,7},{6,4},{7,5},{8,10},{9,11},{10,... | collective-permute-start | bytes 1572872 | tf_op jit(solution)/shard_map/ppermute | solution.py:146
  473.8 25.4 %collective-permute-start.65 = (bf16[256,2048]{1,0:T(8,128)(2,1)}, bf16[256,2048]{1,0:T(8,128)(2,1)S(1)}, u32[]{:S(2)}, u32[]{:S(2)}) collective-permute-start(bf16[256,2048]{1,0:T(8,128)(2,1)} %fusion.6), channel_id=1, source_target_pairs={{0,2},{1,3},{2,0},{3,1},{4,6},{5,7},{6,4},{7,5},{8,10},{9,11},{10,... | collective-permute-start | bytes 3145736 | tf_op jit(solution)/shard_map/ppermute | solution.py:146
  507.6 26.0 %collective-permute-start.67 = (bf16[4,128,256]{2,1,0:T(8,128)(2,1)}, bf16[4,128,256]{2,1,0:T(8,128)(2,1)}, u32[]{:S(2)}, u32[]{:S(2)}) collective-permute-start(bf16[4,128,256]{2,1,0:T(8,128)(2,1)} %fusion.10), channel_id=1, source_target_pairs={{0,2},{1,3},{2,0},{3,1},{4,6},{5,7},{6,4},{7,5},{8,10},{9,11},{10,... | collective-permute-start | bytes 786440 | tf_op jit(solution)/shard_map/ppermute | solution.py:146
  532.5 11.3 %collective-permute-start.69 = (bf16[4,128,256]{2,1,0:T(8,128)(2,1)}, bf16[4,128,256]{2,1,0:T(8,128)(2,1)}, u32[]{:S(2)}, u32[]{:S(2)}) collective-permute-start(bf16[4,128,256]{2,1,0:T(8,128)(2,1)} %fusion.11), channel_id=1, source_target_pairs={{0,2},{1,3},{2,0},{3,1},{4,6},{5,7},{6,4},{7,5},{8,10},{9,11},{10,... | collective-permute-start | bytes 786440 | tf_op jit(solution)/shard_map/ppermute | solution.py:146
  539.6 25.4 %all-to-all-start.4 = ((f32[8,16,1088]{2,1,0:T(8,128)}), f32[8,16,1088]{2,1,0:T(8,128)}, u32[]{:S(2)}, u32[]{:S(2)}) async-start(f32[8,16,1088]{2,1,0:T(8,128)} %concatenate.53), calls=%async_computation.4 | async-start | bytes 1179648 | tf_op jit(solution)/shard_map/all_to_all | solution.py:1151
  565.0 19.7 %all-to-all-start.5 = ((f32[8,16,288]{2,1,0:T(8,128)}), f32[8,16,288]{2,1,0:T(8,128)S(1)}, u32[]{:S(2)}, u32[]{:S(2)}) async-start(f32[8,16,288]{2,1,0:T(8,128)} %fusion.12), calls=%async_computation.5 | async-start | bytes 393216 | tf_op jit(solution)/shard_map/all_to_all | solution.py:1151
  (105 other events, 1007.1 us)

commit v4 on v3

--- a/solution.py
+++ b/solution.py
@@ -151,11 +151,15 @@
     return [own, partner(own, 1), across, partner(across, 1)]
 
 
-def seq_reduce(keep, give):
+def seq_shares(keep, give):
     arrived = partner(give, 1)
     sent = (keep[1].astype(F32) + arrived[1].astype(F32)).astype(BF16)
-    own = keep[0].astype(F32) + arrived[0].astype(F32)
-    return own + partner(sent, 2).astype(F32), sent
+    return (keep, arrived, partner(sent, 2)), sent
+
+
+def total(shares):
+    keep, arrived, across = shares
+    return keep[0].astype(F32) + arrived[0].astype(F32) + across.astype(F32)
 
 
 def everywhere_order(sources):
@@ -168,11 +172,11 @@
 VMEM = pl.BlockSpec(memory_space=pltpu.VMEM)
 
 
-def call(kernel, name, flops=0, moved=0, **options):
+def call(kernel, name, flops=0, **options):
     return pl.pallas_call(
         kernel,
         compiler_params=pltpu.CompilerParams(vmem_limit_bytes=VMEM_LIMIT),
-        cost_estimate=pl.CostEstimate(flops=0, bytes_accessed=0, transcendentals=0),
+        cost_estimate=pl.CostEstimate(flops=int(flops), bytes_accessed=0, transcendentals=0),
         name=name,
         **options,
     )
@@ -202,7 +206,6 @@
     return call(
         functools.partial(columns_kernel, n_dp),
         "columns",
-        moved=8 * rows * total,
         in_specs=[VMEM] * 2,
         out_shape=[shape((4, rows, total // 4), BF16)] * 2,
     )(gate, up)
@@ -307,8 +310,6 @@
     return call(
         qkv_kernel,
         "project_in",
-        flops=2 * width * tokens * total,
-        moved=2 * width * total,
         grid=(total // step,),
         in_specs=[
             SMEM,
@@ -352,8 +353,6 @@
     return call(
         out_kernel,
         "project_out",
-        flops=2 * features * block * width,
-        moved=2 * features * width,
         grid=(width // step,),
         in_specs=[
             SMEM,
@@ -406,8 +405,6 @@
     return call(
         out_back_kernel,
         "project_out_back",
-        flops=2 * features * block * width,
-        moved=2 * features * width,
         grid=(width // step,),
         in_specs=[
             SMEM,
@@ -452,8 +449,6 @@
     return call(
         in_back_kernel,
         "project_in_back",
-        flops=2 * total * block * width,
-        moved=2 * total * width,
         grid=(total // step,),
         in_specs=[
             SMEM,
@@ -471,6 +466,32 @@
     )(order, d_linear, a_in, d_inner, tokens, gain, base, *pieces)
 
 
+def hidden_back_kernel(l0, l1, l2, r0, r1, r2, hidden_ref, cot_ref, valid_ref, gain_ref, b_ref, dh_ref, gu_ref, inner_ref):
+    half = l2.shape[1]
+    for i, refs in enumerate(((l0, l1, l2), (r0, r1, r2))):
+        part = slice(i * half, (i + 1) * half)
+        grad = refs[0][0].astype(F32) + refs[1][0].astype(F32) + refs[2][...].astype(F32)
+        dh_ref[:, part] = grad * gain_ref[:, part]
+    hidden, grad = hidden_ref[...], dh_ref[...]
+    scale = lax.rsqrt(jnp.mean(hidden * hidden, axis=-1, keepdims=True) + EPS)
+    along = jnp.mean(hidden * grad, axis=-1, keepdims=True) * scale * scale
+    grad = cot_ref[...].astype(F32) + scale * (grad - hidden * along)
+    dh_ref[...] = grad
+    low = (valid_ref[...] * grad).astype(BF16)
+    gu_ref[...] = low
+    inner_ref[...] = contract(low, b_ref[...], 1, 1).astype(BF16)
+
+
+def hidden_back(left, right, hidden, cot, valid, gain, bo):
+    block, width = hidden.shape
+    return call(
+        hidden_back_kernel,
+        "hidden_back",
+        flops=7e9,
+        out_shape=[shape((block, width), F32), shape((block, width), BF16), shape((block, RANK), BF16)],
+    )(*left, *right, hidden, cot, valid, gain, bo)
+
+
 def gather_tokens(refs, whole_ref):
     block = refs[0].shape[0]
     for i, ref in enumerate(refs):
@@ -495,8 +516,6 @@
     return call(
         lower_back_kernel,
         "lower_back",
-        flops=2 * tokens * width * units,
-        moved=2 * width * units,
         grid=(units // step,),
         in_specs=[fixed(block, width)] * 4
         + [
@@ -520,8 +539,6 @@
     return call(
         tokens_kernel,
         "all_tokens",
-        flops=16 * block * width * RANK,
-        moved=16 * block * width,
         out_shape=[shape((4 * block, width), BF16), shape((4 * block, 2 * RANK), BF16)],
     )(*normed, a_gu)
 
@@ -571,8 +588,6 @@
     return call(
         units_kernel,
         "units",
-        flops=4 * tokens * width * half,
-        moved=4 * width * half,
         grid=(steps,),
         in_specs=[
             fixed(tokens, width),
@@ -603,8 +618,6 @@
     return call(
         units_grads_kernel,
         "units_grads",
-        flops=6 * tokens * half * RANK,
-        moved=6 * tokens * half,
         grid=(half // step,),
         in_specs=[fixed(tokens, 2 * RANK), fixed(tokens, RANK), tile, tile, tile],
         out_specs=[thin] * 3,
@@ -625,8 +638,6 @@
     return call(
         units_back_first_kernel,
         "units_back_first",
-        flops=4 * tokens * half * width,
-        moved=4 * half * width,
         grid=(width // step,),
         in_specs=[fixed(tokens, half)] * 2 + [pl.BlockSpec((step, 2 * half), lambda n: (n, 0))],
         out_specs=pl.BlockSpec((tokens, step), lambda n: (0, n)),
@@ -634,9 +645,10 @@
     )(d_gate, d_up, both)
 
 
-def units_back_kernel(first_ref, g_ref, u_ref, w_ref, low_ref, a_ref, keep_ref, give_ref):
+def units_back_kernel(first_ref, g_ref, u_ref, w_ref, ia_ref, ib_ref, a_ref, keep_ref, give_ref):
     half = g_ref.shape[1]
-    sums = first_ref[...].astype(F32) + contract(low_ref[...], a_ref[...], 1, 0)
+    low = (ia_ref[...] + ib_ref[...]).astype(BF16)[:, : 2 * RANK]
+    sums = first_ref[...].astype(F32) + contract(low, a_ref[...], 1, 0)
     sums = sums + contract(g_ref[...], w_ref[:, :half], 1, 1)
     sums = sums + contract(u_ref[...], w_ref[:, half:], 1, 1)
     sums = sums.astype(BF16)
@@ -647,7 +659,7 @@
     give_ref[1] = sums[3 * block :]
 
 
-def units_back(part, parts, first, d_gate, d_up, both, low, a_gu):
+def units_back(part, parts, first, d_gate, d_up, both, inners, a_gu):
     tokens, half = d_gate.shape
     width = both.shape[0]
     step = 256
@@ -657,42 +669,42 @@
     return call(
         units_back_kernel,
         "units_back",
-        flops=4 * tokens * half * width // parts,
-        moved=4 * half * width // parts,
         grid=(steps,),
         in_specs=[
             pl.BlockSpec((tokens, step), lambda n: (0, place(n))),
             fixed(tokens, half),
             fixed(tokens, half),
             pl.BlockSpec((step, 2 * half), lambda n: (place(n), 0)),
-            fixed(tokens, 2 * RANK),
+            fixed(tokens, 3 * RANK),
+            fixed(tokens, 3 * RANK),
             pl.BlockSpec((2 * RANK, step), lambda n: (0, place(n))),
         ],
         out_specs=[out, out],
         out_shape=[shape((2, tokens // 4, width // parts), BF16)] * 2,
-    )(first, d_gate, d_up, both, low, a_gu)
+    )(first, d_gate, d_up, both, *inners, a_gu)
 
 
 def lower_kernel(
-    aa_ref, ab_ref, weight_ref, low_ref, b_ref, whole_ref, lowgu_ref, g0, g1, g2, g3, keep_ref, give_ref, grad_ref, grad_gu_ref
+    aa_ref, ab_ref, weight_ref, ia_ref, ib_ref, b_ref, whole_ref, g0, g1, g2, g3, keep_ref, give_ref, grad_ref, grad_gu_ref
 ):
+    inner = (ia_ref[...] + ib_ref[...]).astype(BF16)
+    low = inner[:, 2 * RANK :]
     half = aa_ref.shape[1]
-    sums = contract(low_ref[...], b_ref[...], 1, 0)
+    sums = contract(low, b_ref[...], 1, 0)
     sums = sums + contract(aa_ref[...], weight_ref[:half], 1, 0)
     sums = sums + contract(ab_ref[...], weight_ref[half:], 1, 0)
     sums = sums.astype(BF16)
     block = g0.shape[0]
-    low = low_ref[...]
     grad = jnp.zeros(grad_ref.shape, F32)
     for i, g in enumerate((g0, g1, g2, g3)):
         out = give_ref if i % 2 else keep_ref
         out[i // 2] = sums[i * block : (i + 1) * block]
         grad = grad + contract(low[i * block : (i + 1) * block], g[...], 0, 0)
     grad_ref[...] = grad
-    grad_gu_ref[...] = contract(lowgu_ref[...], whole_ref[...], 0, 0)
-
-
-def lower(act_a, act_b, weight, low, bd, grads, whole, low_gu):
+    grad_gu_ref[...] = contract(inner[:, : 2 * RANK], whole_ref[...], 0, 0)
+
+
+def lower(act_a, act_b, weight, inners, bd, grads, whole):
     block, width = grads[0].shape
     tokens, half = act_a.shape
     step = 256
@@ -702,23 +714,21 @@
     return call(
         lower_kernel,
         "lower",
-        flops=4 * tokens * half * width,
-        moved=4 * half * width,
         grid=(width // step,),
         in_specs=[
             fixed(tokens, half),
             fixed(tokens, half),
             pl.BlockSpec((2 * half, step), lambda n: (0, n)),
-            fixed(tokens, RANK),
+            fixed(tokens, 3 * RANK),
+            fixed(tokens, 3 * RANK),
             thin,
             pl.BlockSpec((tokens, step), lambda n: (0, n)),
-            fixed(tokens, 2 * RANK),
         ]
         + [tile] * 4,
         out_specs=[out, out, thin, pl.BlockSpec((2 * RANK, step), lambda n: (0, n))],
         out_shape=[shape((2, block, width), BF16)] * 2
         + [shape((RANK, width), F32), shape((2 * RANK, width), F32)],
-    )(act_a, act_b, weight, low, bd, whole, low_gu, *grads)
+    )(act_a, act_b, weight, *inners, bd, whole, *grads)
 
 
 def wide_heads(ref):
@@ -755,8 +765,6 @@
     return call(
         attend_kernel,
         "attend",
-        flops=16 * H * width * 4 * block * HD,
-        moved=2 * KV * 4 * block * wide,
         grid=(KV,),
         in_specs=[SMEM, fixed(1, wide), head_rows]
         + [pl.BlockSpec((1, 2 * HD, block), lambda g: (g, 0, 0))] * 4,
@@ -801,8 +809,6 @@
     return call(
         attend_back_kernel,
         "attend_back",
-        flops=32 * count * GROUP * width * 4 * block * HD,
-        moved=2 * count * 4 * block * wide,
         grid=(count,),
         in_specs=[head_rows]
         + [pl.BlockSpec((1, 2 * HD, block), lambda g: (first + g, 0, 0))] * 4
@@ -834,7 +840,6 @@
     return call(
         pick_kernel,
         "pick",
-        moved=4 * n_dp * RANK * columns,
         in_specs=[SMEM] + [VMEM] * len(stacks),
         out_shape=shape((n_dp, RANK, columns), BF16),
     )(ids, *stacks)
@@ -883,7 +888,6 @@
     return call(
         functools.partial(spread_kernel, widths),
         "spread",
-        moved=4 * 4 * mine.size,
         in_specs=[SMEM] + [VMEM] * 4,
         out_shape=[shape(dims, BF16) for dims in rows],
         scratch_shapes=[pltpu.VMEM((4,) + others[0].shape, BF16)],
@@ -891,7 +895,8 @@
 
 
 def pack_kernel(n_dp, count, seq_ref, *refs):
-    ins, (keep_ref, give_ref, all_ref) = refs[:count], refs[count:]
+    ins, refs = refs[:count], refs[count:]
+    alone, (keep_ref, give_ref, alone_ref, all_ref) = refs[:-4], refs[-4:]
     for d in range(n_dp):
         for j in range(4):
             parts = []
@@ -899,28 +904,36 @@
                 each = ref.shape[1] // (4 * n_dp)
                 at = (d * 4 + j) * each
                 parts.append(ref[:, at : at + each])
-            all_ref[j, d] = jnp.concatenate(parts, axis=1)
+            all_ref[j, d] = jnp.concatenate(parts, axis=1).astype(BF16)
     seq = seq_ref[0]
     for bit in range(4):
         out = give_ref if bit % 2 else keep_ref
         out[bit // 2] = all_ref[seq ^ bit]
-
-
-def pack(seq, grads, n_dp):
+    for i in range(0, len(alone), 2):
+        for half in range(2):
+            size = alone[i].shape[1] // (n_dp // 2)
+            for d in range(n_dp // 2):
+                place = slice((i // 2) * size, (i // 2 + 1) * size)
+                part = alone[i + half][:, d * size : (d + 1) * size]
+                alone_ref[half * (n_dp // 2) + d, :, place] = part.astype(BF16)
+
+
+def pack(seq, grads, n_dp, alone):
     columns = sum(g.shape[1] for g in grads) // (4 * n_dp)
     dims = (n_dp, RANK, columns)
+    outs = [shape((2,) + dims, BF16)] * 2
+    outs.append(shape((n_dp, RANK, sum(g.shape[1] for g in alone) // n_dp), BF16))
     return call(
         functools.partial(pack_kernel, n_dp, len(grads)),
         "pack",
-        moved=16 * n_dp * RANK * columns * 4,
-        in_specs=[SMEM] + [VMEM] * len(grads),
-        out_shape=[shape((2,) + dims, F32)] * 2,
-        scratch_shapes=[pltpu.VMEM((4,) + dims, F32)],
-    )(seq[None], *grads)
+        in_specs=[SMEM] + [VMEM] * (len(grads) + len(alone)),
+        out_shape=outs,
+        scratch_shapes=[pltpu.VMEM((4,) + dims, BF16)],
+    )(seq[None], *grads, *alone)
 
 
 def sort_kernel(widths, ids_ref, came_ref, *out_refs):
-    came = [came_ref[d] for d in range(came_ref.shape[0])]
+    came = [came_ref[d].astype(F32) for d in range(came_ref.shape[0])]
     for a in range(ADAPT):
         total = jnp.zeros(came[0].shape, F32)
         for d, value in enumerate(came):
@@ -936,7 +949,6 @@
     outs = call(
         functools.partial(sort_kernel, widths),
         "sort",
-        moved=8 * came.size,
         in_specs=[SMEM, VMEM],
         out_shape=[shape((ADAPT, w, RANK) if w < 64 else (ADAPT, RANK, w), F32) for w in widths],
     )(ids, came)
@@ -1109,60 +1121,36 @@
     belt.until(ring_b, begun)
     (both_b,) = finish(begun, ring_b.pieces, sources)
     act_b, dg_b, du_b, inner_b = units(1, n2, low_n2, both_b, bg, bu, ad, d_act)
-    low = (inner_a + inner_b).astype(BF16)
-    low_gu, low_down = low[:, : 2 * RANK], low[:, 2 * RANK :]
-    keep, give = units_back(0, 2, first, dg_b, du_b, both_b, low_gu, a_gu)
-    left, sent = seq_reduce(keep, give)
-    keep, give = units_back(1, 2, after(first, sent), dg_b, du_b, both_b, low_gu, a_gu)
-    right, sent = seq_reduce(keep, give)
-    gbg_b, gbu_b, gad_b = units_grads(low_n2, d_down, after(act_b, sent), dg_b, du_b)
-
-    act_b = after(act_b, left, gbg_b)
-    keep, give, grad_bd, grad_a_gu = lower(act_a, act_b, w_lower, low_down, bd, grads, n2, low_gu)
-    left, right = after((left, right), keep)
-
-    d_n2 = jnp.concatenate([left, right], axis=1)
-    d_hidden = cot + jax.vjp(lambda v: rms_scale(v, ffn_gain), hidden)[1](d_n2)[0]
-    grad_update = (valid * d_hidden).astype(BF16)
-    keep, give = after((keep, give), grad_update)
-    lowered, sent = seq_reduce(keep, give)
-    d_inner_out = contract(grad_update, bo, 1, 1).astype(BF16)
+    inners = (inner_a, inner_b)
+    keep, give = units_back(0, 2, first, dg_b, du_b, both_b, inners, a_gu)
+    left, sent = seq_shares(keep, give)
+    keep, give = units_back(1, 2, after(first, sent), dg_b, du_b, both_b, inners, a_gu)
+    right, sent = seq_shares(keep, give)
+
+    keep, give, grad_bd, grad_a_gu = lower(
+        act_a, after(act_b, sent), w_lower, inners, bd, grads, n2
+    )
+
+    d_hidden, grad_update, d_inner_out = hidden_back(
+        after(left[:2], keep) + left[2:], after(right[:2], keep) + right[2:], hidden, cotangent[0], valid, ffn_gain[None], bo
+    )
+    lowered, sent = seq_shares(*after((keep, give), grad_update))
     d_mixed = project_out_back(order, after(grad_update, sent), ao, d_inner_out, attn_pieces)
-    d_queries, d_kv = [], []
-    for part in range(2):
-        count = KV // 2
-        d_query, keep, give = attend_back(
-            part * count, count, queries, keys_values, raised, inverse, mixed, d_mixed
-        )
-        if part == 0:
-            give = after(give, lowered)
-        reduced, sent = seq_reduce(keep, give)
-        d_mixed = after(d_mixed, sent)
-        d_kv.append(reduced)
-        d_queries.append(d_query)
-    def owners(grads, alone):
-        keep, give = pack(seq, grads, n_dp)
-        both = keep + partner(give, 1)
-        summed = both[0] + partner(both[1], 2)
-        sizes = [g.shape[1] // (4 * n_dp) for g in grads]
-        if alone:
-            summed = jnp.concatenate([summed] + alone, axis=2)
-            sizes += [g.shape[2] for g in alone]
-        return sort(ids, lax.all_to_all(summed, "dp", 0, 0, tiled=True), sizes)
-
-    grad_ao = contract(d_inner_out, mixed, 0, 1)
-    grad_bo = contract(inner_out, grad_update, 1, 0)
-    cat = lambda a, b: jnp.concatenate([a, b], axis=1).reshape(RANK, n_dp, -1).transpose(1, 0, 2)
-    some = [grad_ao, grad_bo, grad_a_gu[:RANK], grad_a_gu[RANK:], grad_bd]
-    owned = owners(
-        after(some, d_query),
-        [cat(gbg_a, gbg_b), cat(gbu_a, gbu_b), cat(gad_a, gad_b)],
+    count = KV // 2
+    back = lambda part, d_mixed: attend_back(
+        part * count, count, queries, keys_values, raised, inverse, mixed, d_mixed
     )
-    gao, gbo, gag, gau, gbd, gbg, gbu, gad = owned
-
-    d_queries = jnp.concatenate(d_queries, axis=0).reshape(H, HD, block) * scale
-    output = (hidden + valid * after(lowered, d_queries)).astype(BF16)
-    d_kv = jnp.concatenate(after(d_kv, output), axis=0)
+    d_query, keep, give = back(0, d_mixed)
+    gbg_b, gbu_b, gad_b = units_grads(low_n2, d_down, after(act_b, d_query), dg_b, du_b)
+    give, gbg_b = after((give, gbg_b), lowered[2])
+    first_kv, sent = seq_shares(keep, give)
+    other_query, keep, give = back(1, after(d_mixed, sent))
+    other_kv, sent = seq_shares(keep, give)
+
+    first_kv = total(after(first_kv, other_query))
+    d_query = after(jnp.concatenate([d_query, other_query], axis=0), first_kv)
+    d_queries = d_query.reshape(H, HD, block) * scale
+    d_kv = jnp.concatenate([first_kv, total(other_kv)], axis=0)
     d_query_lin = jax.vjp(query_prep, query_lin)[1](d_queries)[0]
     d_key_lin = jax.vjp(key_prep, key_lin)[1](d_kv[:, :HD])[0]
     d_linear = jnp.concatenate(
@@ -1173,25 +1161,29 @@
         ],
         axis=0,
     ).astype(BF16)
+    output = (hidden + valid * total(after(lowered, d_linear))).astype(BF16)
     d_inner = contract(b_in, d_linear, 1, 0).astype(BF16)
     grad_tokens = project_in_back(
-        order, d_linear, a_in, d_inner, tokens[0], attn_gain[None], after(d_hidden, *owned), attn_pieces
+        order, d_linear, a_in, d_inner, tokens[0], attn_gain[None], d_hidden, attn_pieces
     )
 
+    grad_ao = contract(d_inner_out, mixed, 0, 1)
+    grad_bo = contract(inner_out, grad_update, 1, 0)
     grad_a_in = contract(d_inner, normed, 1, 0)
     grad_b_in = contract(inner, d_linear, 0, 1)
     q_end, k_end = n_query, n_query + n_key
-    gaq, gak, gav, gbq, gbk, gbv = owners(
-        [
-            grad_a_in[:RANK],
-            grad_a_in[RANK : 2 * RANK],
-            grad_a_in[2 * RANK :],
-            grad_b_in[:RANK, :q_end],
-            grad_b_in[RANK : 2 * RANK, q_end:k_end],
-            grad_b_in[2 * RANK :, k_end:],
-        ],
-        [],
-    )
+    partial = [grad_ao, grad_bo, grad_a_gu[:RANK], grad_a_gu[RANK:], grad_bd]
+    partial += [grad_a_in[i * RANK : (i + 1) * RANK] for i in range(3)]
+    partial += [grad_b_in[:RANK, :q_end]]
+    partial += [grad_b_in[RANK : 2 * RANK, q_end:k_end], grad_b_in[2 * RANK :, k_end:]]
+    whole = (gbg_a, gbg_b, gbu_a, gbu_b, gad_a, gad_b)
+    keep, give, whole = pack(seq, partial, n_dp, whole)
+    (keep, arrived, across), _ = seq_shares(keep, give)
+    summed = total((keep, arrived, across)).astype(BF16)
+    summed = after(jnp.concatenate([summed, whole], axis=2), grad_tokens)
+    sizes = [each] * 9 + [thin] * 2 + [local] * 3
+    came = lax.all_to_all(summed, "dp", 0, 0, tiled=True)
+    gao, gbo, gag, gau, gbd, gaq, gak, gav, gbq, gbk, gbv, gbg, gbu, gad = sort(ids, came, sizes)
     return (
         output[None],
         grad_tokens[None],

time: 598 us -> 569 us (0.952)
  other arithmetic: 46.1 us -> 31.5 us
  starting transfers between devices: 81.5 us -> 73.6 us
  local copies, waits for them, and re-layouts: 41.5 us -> 33.7 us
    add x9 -> x2, other arithmetic: 10.2 us -> 0.18 us  [total(): return keep[0].astype(F32) + arrived[0].astype(F32) + across.astype(F32)]
    ppermute x50 -> x48, waiting for transfers between devices: 58.4 us -> 49.5 us  [partner(): return lax.ppermute(operand, 'seq', [(i, i ^ bit) for i in range(size)])]
    all_to_all x2 -> x1, waiting for transfers between devices: 0.01 us -> 7.66 us  [shards(): came = lax.all_to_all(summed, 'dp', 0, 0, tiled=True)]
    all_to_all x2 -> x1, starting transfers between devices: 10.4 us -> 3.44 us  [shards(): came = lax.all_to_all(summed, 'dp', 0, 0, tiled=True)]
    convert_element_type x8 -> x7, other arithmetic: 12.9 us -> 6.08 us  [the longest x6 6.01 us: seq_shares(): sent = (keep[1].astype(F32) + arrived[1].astype(F32)).astype(BF16)]
    pallas_call x24 -> x23, Pallas kernels: 210 us -> 214 us  [the longest x2 36.1 us: units(): call(units_kernel, 'units', grid=(steps,), in_specs=[fixed(tokens, width)...]
    unnamed x187 -> x140, local copies, waits for them, and re-layouts: 19.5 us -> 15.9 us
    ppermute x50 -> x48, starting transfers between devices: 25.5 us -> 24.6 us  [partner(): return lax.ppermute(operand, 'seq', [(i, i ^ bit) for i in range(size)])]
  transfers between devices with their start and end apart: 80 -> 77, of which waited for: 32 -> 32; matrix products, arithmetic and copies ran while one was open for 12% -> 9% of each run, Pallas kernels for 32% -> 33%
where the time goes in v4:
time: 569 us; the launch traced here: 558 us
  Pallas kernels  235 us (41%)
  waiting for transfers between devices  173 us (30%)
  starting transfers between devices  73.6 us (13%)
  local copies, waits for them, and re-layouts  33.7 us (6%)
  other arithmetic  31.5 us (6%)
  matrix products  8.22 us (1%)
    ppermute x9, waiting for transfers between devices, step(): self.right = lax.ppermute(clock(self.right), 'dp', left)  53.8 us
    ppermute x48, waiting for transfers between devices, partner(): return lax.ppermute(operand, 'seq', [(i, i ^ bit) for i in range(size)])  49.5 us
    pallas_call x2, Pallas kernels, units(): call(units_kernel, 'units', grid=(steps,), in_specs=[fixed(tokens, width)...  36.1 us
    ppermute x9, waiting for transfers between devices, step(): self.left = lax.ppermute(clock(self.left), 'dp', right)  31.3 us
    ppermute x48, starting transfers between devices, partner(): return lax.ppermute(operand, 'seq', [(i, i ^ bit) for i in range(size)])  24.6 us
    pallas_call x2, Pallas kernels, attend_back(): call(attend_back_kernel, 'attend_back', grid=(count,), in_specs=[head_row...  24.2 us
    pallas_call x2, Pallas kernels, units_back(): call(units_back_kernel, 'units_back', grid=(steps,), in_specs=[pl.BlockSp...  19.5 us
    pallas_call x1, Pallas kernels, lower(): call(lower_kernel, 'lower', grid=(width // step,), in_specs=[fixed(tokens...  17.3 us
  transfers between devices with their start and end apart: 77, of which 32 were waited for; matrix products, arithmetic and copies ran while one was open for 9% of the time, Pallas kernels for 33%

profile of v4, /device:TPU:0, one launch (start us, length us, event | category | flops | bytes accessed | tf_op | source)
XLA Modules:
  0.0 558.4 jit_solution(7862585210479838656)
XLA Ops:
  4.3 3.1 collective-permute-start
  10.6 5.8 %all-to-all-start = ((s32[8,1,128]{2,1,0:T(1,128)}), s32[8,1,128]{2,1,0:T(1,128)S(1)}, u32[]{:S(2)}, u32[]{:S(2)}) async-start(s32[8,1,128]{2,1,0:T(1,128)} %broadcast_in_dim.22), calls=%async_computation | async-start | bytes 8192 | tf_op jit(solution)/shard_map/all_to_all | solution.py:1034
  19.3 3.0 columns.1
  22.3 3.3 all-to-all-done
  32.1 11.2 %collective-permute-done.5.refs_16_ = bf16[64,5120]{1,0:T(8,128)(2,1)S(1)} collective-permute-done((bf16[64,5120]{1,0:T(8,128)(2,1)S(1)}, bf16[64,5120]{1,0:T(8,128)(2,1)S(1)}, u32[]{:S(2)}, u32[]{:S(2)}) %collective-permute-start.5) | collective-permute-done | bytes 655392 | tf_op jit(solution)/shard_map/ppermute | solution.py:82
  43.3 3.7 collective-permute-done.4.refs_12_
  49.8 4.2 all-to-all-start.1
  54.0 2.0 collective-permute-start.16
  57.7 7.9 %collective-permute-done.11.refs_20_ = bf16[64,5120]{1,0:T(8,128)(2,1)S(1)} collective-permute-done((bf16[64,5120]{1,0:T(8,128)(2,1)}, bf16[64,5120]{1,0:T(8,128)(2,1)S(1)}, u32[]{:S(2)}, u32[]{:S(2)}) %collective-permute-start.11) | collective-permute-done | bytes 655392 | tf_op jit(solution)/shard_map/ppermute | solution.py:81
  65.6 3.4 all-to-all-done.1
  69.0 4.1 all-to-all-start.2
  73.1 3.2 pad_maximum_fusion.refs_0_
  77.1 5.5 collective-permute-done.16.refs_10_
  88.4 3.7 collective-permute-done.17
  95.8 5.4 collective-permute-done.10.refs_14_
  103.3 2.8 bitcast_convert_fusion
  107.6 6.1 %collective-permute-done.25.refs_18_ = bf16[64,5120]{1,0:T(8,128)(2,1)} collective-permute-done((bf16[64,5120]{1,0:T(8,128)(2,1)S(1)}, bf16[64,5120]{1,0:T(8,128)(2,1)}, u32[]{:S(2)}, u32[]{:S(2)}) %collective-permute-start.25) | collective-permute-done | bytes 655392 | tf_op jit(solution)/shard_map/ppermute | solution.py:146
  117.2 2.3 copy.58
  121.1 2.7 multiply_convert_fusion.g0
  126.3 10.0 %collective-permute-done.29.refs_22_ = bf16[64,5120]{1,0:T(8,128)(2,1)S(1)} collective-permute-done((bf16[64,5120]{1,0:T(8,128)(2,1)S(1)}, bf16[64,5120]{1,0:T(8,128)(2,1)S(1)}, u32[]{:S(2)}, u32[]{:S(2)}) %collective-permute-start.29) | collective-permute-done | bytes 655392 | tf_op jit(solution)/shard_map/ppermute | solution.py:146
  137.0 16.9 %collective-permute-done.32.refs_1_ = bf16[512,2048]{1,0:T(8,128)(2,1)} collective-permute-done((bf16[512,2048]{1,0:T(8,128)(2,1)}, bf16[512,2048]{1,0:T(8,128)(2,1)}, u32[]{:S(2)}, u32[]{:S(2)}) %collective-permute-start.32) | collective-permute-done | bytes 2097184 | tf_op jit(solution)/shard_map/ppermute | solution.py:81
  154.0 6.0 %collective-permute-done.33.refs_2_ = bf16[512,2048]{1,0:T(8,128)(2,1)} collective-permute-done((bf16[512,2048]{1,0:T(8,128)(2,1)}, bf16[512,2048]{1,0:T(8,128)(2,1)}, u32[]{:S(2)}, u32[]{:S(2)}) %collective-permute-start.33) | collective-permute-done | bytes 2097184 | tf_op jit(solution)/shard_map/ppermute | solution.py:82
  165.2 2.5 spread.1
  167.8 2.7 convolution_convert_fusion.inner_ref
  170.5 10.2 %project_in.1 = f32[3072,256]{1,0:T(8,128)} custom-call(s32[32]{0:T(128)} %stack.163.order_ref, bf16[2048,256]{1,0:T(8,128)(2,1)} %fusion.28.normed_ref, bf16[256,48]{1,0:T(8,128)(2,1)} %convolution_convert_fusion.inner_ref, bf16[48,3072]{1,0:T(8,128)(2,1)} %get-tuple-element.212.b_ref, bf16[64,5120]{1,0:T(8,128)(2,1)} %copy-done.6, ...), custom_call_target="tpu_custom_call" | custom-call | tf_op jit(solution)/shard_map/project_in/pallas_call | solution.py:310
  187.6 23.8 %collective-permute-done.44.refs_4_ = bf16[512,2048]{1,0:T(8,128)(2,1)} collective-permute-done((bf16[512,2048]{1,0:T(8,128)(2,1)}, bf16[512,2048]{1,0:T(8,128)(2,1)}, u32[]{:S(2)}, u32[]{:S(2)}) %collective-permute-start.44) | collective-permute-done | bytes 2097184 | tf_op jit(solution)/shard_map/ppermute | solution.py:82
  218.4 14.9 %attend.1 = (bf16[2048,256]{1,0:T(8,128)(2,1)}, bf16[8,4,256,1024]{3,2,1,0:T(8,128)(2,1)}, f32[8,1,1024]{2,1,0:T(1,128)}) custom-call(s32[1]{0:T(128)} %bitcast.32.seq_ref, s32[1,1024]{1,0:T(1,128)} %bitcast.183, bf16[2048,256]{1,0:T(8,128)(2,1)} %bitcast.156, bf16[8,128,256]{2,1,0:T(8,128)(2,1)} %copy-done.26, bf16[8,128,256]{2,1,0:T(8,128)(2,1)} %copy-done.28, ...), custom_call_target="tpu_custom_call" | custom-call | tf_op jit(solution)/shard_map/attend/pallas_call | solution.py:765
  233.4 2.1 convolution_convert_fusion.2.inner_ref
  235.4 8.0 %project_out.1 = (f32[256,2048]{1,0:T(8,128)}, bf16[256,2048]{1,0:T(8,128)(2,1)}) custom-call(s32[32]{0:T(128)} %stack.163.order_ref, bf16[2048,256]{1,0:T(8,128)(2,1)} %get-tuple-element.213.mixed_ref.o_ref, bf16[16,256]{1,0:T(8,128)(2,1)} %convolution_convert_fusion.2.inner_ref, bf16[16,2048]{1,0:T(8,128)(2,1)} %get-tuple-element.215.b_ref, ...), custom_call_target="tpu_custom_call" | custom-call | tf_op jit(solution)/shard_map/project_out/pallas_call | solution.py:353
  244.7 4.2 all-to-all-start.3
  249.4 10.2 %collective-permute-done.46.refs_6_ = bf16[512,2048]{1,0:T(8,128)(2,1)} collective-permute-done((bf16[512,2048]{1,0:T(8,128)(2,1)}, bf16[512,2048]{1,0:T(8,128)(2,1)}, u32[]{:S(2)}, u32[]{:S(2)}) %collective-permute-start.46) | collective-permute-done | bytes 2097184 | tf_op jit(solution)/shard_map/ppermute | solution.py:82
  259.6 2.4 slice.191
  263.4 2.3 slice.190
  266.3 14.2 %all-to-all-done.3 = bf16[4,64,2048]{2,1,0:T(8,128)(2,1)} async-done(((bf16[4,64,2048]{2,1,0:T(8,128)(2,1)}), bf16[4,64,2048]{2,1,0:T(8,128)(2,1)}, u32[]{:S(2)}, u32[]{:S(2)}) %all-to-all-start.3) | async-done | bytes 1048608 | tf_op jit(solution)/shard_map/all_to_all | solution.py:1096
  283.1 10.7 %place.2 = (bf16[2048,2048]{1,0:T(8,128)(2,1)}, bf16[2048,2048]{1,0:T(8,128)(2,1)}) custom-call(s32[7]{0:T(128)} %stack.171.sources_ref, bf16[512,2048]{1,0:T(8,128)(2,1)} %pad_maximum_fusion.refs_0_, bf16[512,2048]{1,0:T(8,128)(2,1)} %collective-permute-done.32.refs_1_, bf16[512,2048]{1,0:T(8,128)(2,1)} %collective-permute-done.33.refs_2_, ...), custom_call_target="tpu_custom_call" | custom-call | tf_op jit(solution)/shard_map/place/pallas_call | solution.py:254
  294.4 2.9 finish.2
  297.3 15.8 %lower_back.1 = (bf16[1024,2048]{1,0:T(8,128)(2,1)}, bf16[1024,16]{1,0:T(8,128)(2,1)}) custom-call(bf16[256,2048]{1,0:T(8,128)(2,1)} %multiply_convert_fusion.g0, bf16[256,2048]{1,0:T(8,128)(2,1)} %collective-permute-done.49.g1, bf16[256,2048]{1,0:T(8,128)(2,1)} %collective-permute-done.50.g2, bf16[256,2048]{1,0:T(8,128)(2,1)} %collective-permute-done.51.g3, ...), custom_call_target="tpu_custom_call" | custom-call | tf_op jit(solution)/shard_map/lower_back/pallas_call | solution.py:516
  316.2 5.3 all_tokens.1
  321.5 18.1 %units.2 = (bf16[1024,1024]{1,0:T(8,128)(2,1)}, bf16[1024,1024]{1,0:T(8,128)(2,1)}, bf16[1024,1024]{1,0:T(8,128)(2,1)}, f32[1024,48]{1,0:T(8,128)}) custom-call(bf16[1024,2048]{1,0:T(8,128)(2,1)} %get-tuple-element.219.whole_ref, bf16[1024,32]{1,0:T(8,128)(2,1)} %get-tuple-element.220.low_ref, bf16[2048,2048]{1,0:T(8,128)(2,1)} %get-tuple-element.236.gate_ref.up_ref.w_ref, ...), custom_call_target="tpu_custom_call" | custom-call | tf_op jit(solution)/shard_map/units/pallas_call | solution.py:588
  342.2 14.2 %units_back_first.1.first_ref = bf16[1024,2048]{1,0:T(8,128)(2,1)} custom-call(bf16[1024,1024]{1,0:T(8,128)(2,1)} %get-tuple-element.258.g_ref.dg_ref, bf16[1024,1024]{1,0:T(8,128)(2,1)} %get-tuple-element.259.u_ref.du_ref, bf16[2048,2048]{1,0:T(8,128)(2,1)} %get-tuple-element.236.gate_ref.up_ref.w_ref), custom_call_target="tpu_custom_call" | custom-call | tf_op jit(solution)/shard_map/units_back_first/pallas_call | solution.py:638
  356.4 5.4 units_grads.2
  361.8 2.5 collective-permute-done.57.refs_6_
  368.0 6.1 %place.3.refs_0_ = bf16[2048,2048]{1,0:T(8,128)(2,1)} custom-call(s32[7]{0:T(128)} %stack.171.sources_ref, bf16[256,2048]{1,0:T(8,128)(2,1)} %bitcast.69.refs_0_, bf16[256,2048]{1,0:T(8,128)(2,1)} %collective-permute-done.52.refs_1_, bf16[256,2048]{1,0:T(8,128)(2,1)} %collective-permute-done.53.refs_2_, bf16[256,2048]{1,0:T(8,128)(2,1)} %copy-done.39, ...), custom_call_target="tpu_custom_call" | custom-call | tf_op jit(solution)/shard_map/place/pallas_call | solution.py:254
  374.1 3.9 collective-permute-done.59.refs_2_
  380.0 2.2 finish.3.gate_ref.up_ref.w_ref
  382.2 18.0 %units.3 = (bf16[1024,1024]{1,0:T(8,128)(2,1)}, bf16[1024,1024]{1,0:T(8,128)(2,1)}, bf16[1024,1024]{1,0:T(8,128)(2,1)}, f32[1024,48]{1,0:T(8,128)}) custom-call(bf16[1024,2048]{1,0:T(8,128)(2,1)} %get-tuple-element.219.whole_ref, bf16[1024,32]{1,0:T(8,128)(2,1)} %get-tuple-element.220.low_ref, bf16[2048,2048]{1,0:T(8,128)(2,1)} %finish.3.gate_ref.up_ref.w_ref, ...), custom_call_target="tpu_custom_call" | custom-call | tf_op jit(solution)/shard_map/units/pallas_call | solution.py:588
  400.2 9.7 %units_back.2 = (bf16[2,256,1024]{2,1,0:T(8,128)(2,1)}, bf16[2,256,1024]{2,1,0:T(8,128)(2,1)}) custom-call(bf16[1024,2048]{1,0:T(8,128)(2,1)} %units_back_first.1.first_ref, bf16[1024,1024]{1,0:T(8,128)(2,1)} %get-tuple-element.272.g_ref.dg_ref, bf16[1024,1024]{1,0:T(8,128)(2,1)} %get-tuple-element.273.u_ref.du_ref, ...), custom_call_target="tpu_custom_call" | custom-call | tf_op jit(solution)/shard_map/units_back/pallas_call | solution.py:669
  409.9 2.9 collective-permute-done.60.l1
  414.3 9.8 %units_back.3 = (bf16[2,256,1024]{2,1,0:T(8,128)(2,1)}, bf16[2,256,1024]{2,1,0:T(8,128)(2,1)}) custom-call(bf16[1024,2048]{1,0:T(8,128)(2,1)} %units_back_first.1.first_ref, bf16[1024,1024]{1,0:T(8,128)(2,1)} %get-tuple-element.272.g_ref.dg_ref, bf16[1024,1024]{1,0:T(8,128)(2,1)} %get-tuple-element.273.u_ref.du_ref, ...), custom_call_target="tpu_custom_call" | custom-call | tf_op jit(solution)/shard_map/units_back/pallas_call | solution.py:669
  429.9 17.3 %lower.1 = (bf16[2,256,2048]{2,1,0:T(8,128)(2,1)}, bf16[2,256,2048]{2,1,0:T(8,128)(2,1)}, f32[16,2048]{1,0:T(8,128)}, f32[32,2048]{1,0:T(8,128)}) custom-call(bf16[1024,1024]{1,0:T(8,128)(2,1)} %get-tuple-element.260.act_ref.aa_ref, bf16[1024,1024]{1,0:T(8,128)(2,1)} %get-tuple-element.298.ab_ref.act_ref, bf16[2048,2048]{1,0:T(8,128)(2,1)} %get-tuple-element.245.weight_ref, ...), custom_call_target="tpu_custom_call" | custom-call | tf_op jit(solution)/shard_map/lower/pallas_call | solution.py:714
  447.2 2.6 collective-permute-done.63.r2
  450.6 6.5 %hidden_back.1 = (f32[256,2048]{1,0:T(8,128)}, bf16[256,2048]{1,0:T(8,128)(2,1)}, bf16[256,16]{1,0:T(8,128)(2,1)}) custom-call(bf16[2,256,1024]{2,1,0:T(8,128)(2,1)} %get-tuple-element.284.l0, bf16[2,256,1024]{2,1,0:T(8,128)(2,1)} %copy-done.52, bf16[256,1024]{1,0:T(8,128)(2,1)} %copy-done.63, bf16[2,256,1024]{2,1,0:T(8,128)(2,1)} %get-tuple-element.286.r0, ...), custom_call_target="tpu_custom_call" | custom-call | flops 7000000000 | tf_op jit(solution)/shard_map/hidden_back/pallas_call | solution.py:487
  457.1 4.4 collective-permute-done.64
  464.4 6.7 %project_out_back.1.do_ref = bf16[2048,256]{1,0:T(8,128)(2,1)} custom-call(s32[32]{0:T(128)} %stack.163.order_ref, bf16[256,2048]{1,0:T(8,128)(2,1)} %get-tuple-element.293.grad_ref, bf16[16,2048]{1,0:T(8,128)(2,1)} %get-tuple-element.214.a_ref, bf16[256,16]{1,0:T(8,128)(2,1)} %get-tuple-element.294.inner_ref, bf16[64,5120]{1,0:T(8,128)(2,1)} %copy-done.6, ...), custom_call_target="tpu_custom_call" | custom-call | tf_op jit(solution)/shard_map/project_out_back/pallas_call | solution.py:405
  471.1 12.2 %attend_back.2 = (f32[1024,256]{1,0:T(8,128)}, bf16[2,4,128,256]{3,2,1,0:T(8,128)(2,1)}, bf16[2,4,128,256]{3,2,1,0:T(8,128)(2,1)}) custom-call(bf16[2048,256]{1,0:T(8,128)(2,1)} %bitcast.157, bf16[8,128,256]{2,1,0:T(8,128)(2,1)} %copy-done.26, bf16[8,128,256]{2,1,0:T(8,128)(2,1)} %copy-done.28, bf16[8,128,256]{2,1,0:T(8,128)(2,1)} %copy-done.27, ...), custom_call_target="tpu_custom_call" | custom-call | tf_op jit(solution)/shard_map/attend_back/pallas_call | solution.py:809
  483.4 5.6 units_grads.3
  492.8 12.1 %attend_back.3 = (f32[1024,256]{1,0:T(8,128)}, bf16[2,4,128,256]{3,2,1,0:T(8,128)(2,1)}, bf16[2,4,128,256]{3,2,1,0:T(8,128)(2,1)}) custom-call(bf16[2048,256]{1,0:T(8,128)(2,1)} %bitcast.158, bf16[8,128,256]{2,1,0:T(8,128)(2,1)} %copy-done.26, bf16[8,128,256]{2,1,0:T(8,128)(2,1)} %copy-done.28, bf16[8,128,256]{2,1,0:T(8,128)(2,1)} %copy-done.27, ...), custom_call_target="tpu_custom_call" | custom-call | tf_op jit(solution)/shard_map/attend_back/pallas_call | solution.py:809
  510.0 6.8 %collective-permute-done.69 = bf16[4,128,256]{2,1,0:T(8,128)(2,1)S(1)} collective-permute-done((bf16[4,128,256]{2,1,0:T(8,128)(2,1)S(1)}, bf16[4,128,256]{2,1,0:T(8,128)(2,1)S(1)}, u32[]{:S(2)}, u32[]{:S(2)}) %collective-permute-start.69) | collective-permute-done | bytes 262176 | tf_op jit(solution)/shard_map/ppermute | solution.py:146
  521.5 2.6 pack.1
  528.2 11.3 %project_in_back.1 = bf16[256,2048]{1,0:T(8,128)(2,1)} custom-call(s32[32]{0:T(128)} %stack.163.order_ref, bf16[3072,256]{1,0:T(8,128)(2,1)} %copy-done.2, bf16[48,2048]{1,0:T(8,128)(2,1)} %get-tuple-element.211.a_ref, bf16[48,256]{1,0:T(8,128)(2,1)} %copy-done.58, bf16[256,2048]{1,0:T(8,128)(2,1)} %bitcast.160, f32[1,2048]{1,0:T(1,128)} %bitcast.173, ...), custom_call_target="tpu_custom_call" | custom-call | tf_op jit(solution)/shard_map/project_in_back/pallas_call | solution.py:449
  540.5 3.4 all-to-all-start.4
  543.9 3.5 fusion.9
  547.4 7.7 %all-to-all-done.4.came_ref = bf16[8,16,1376]{2,1,0:T(8,128)(2,1)S(1)} async-done(((bf16[8,16,1376]{2,1,0:T(8,128)(2,1)}), bf16[8,16,1376]{2,1,0:T(8,128)(2,1)S(1)}, u32[]{:S(2)}, u32[]{:S(2)}) %all-to-all-start.4) | async-done | bytes 352288 | tf_op jit(solution)/shard_map/all_to_all | solution.py:1185
  555.9 2.4 sort.1
  (327 shorter events, 108.9 us)
Async XLA Ops:
  4.3 23.9 %collective-permute-start = (bf16[64,5120]{1,0:T(8,128)(2,1)S(1)}, bf16[64,5120]{1,0:T(8,128)(2,1)S(1)}, u32[]{:S(2)}, u32[]{:S(2)}) collective-permute-start(bf16[64,5120]{1,0:T(8,128)(2,1)S(1)} %constant_dynamic-update-slice_fusion.refs_0_), channel_id=1, source_target_pairs={{0,8},{8,16},{16,24},{24,28},{28,20},{20,12},{12,4},{4,0},{1,9},{9... | collective-permute-start | bytes 1966088 | tf_op jit(solution)/shard_map/ppermute | solution.py:81
  7.4 20.8 %collective-permute-start.1 = (bf16[64,5120]{1,0:T(8,128)(2,1)S(1)}, bf16[64,5120]{1,0:T(8,128)(2,1)S(1)}, u32[]{:S(2)}, u32[]{:S(2)}) collective-permute-start(bf16[64,5120]{1,0:T(8,128)(2,1)S(1)} %constant_dynamic-update-slice_fusion.refs_0_), channel_id=1, source_target_pairs={{8,0},{16,8},{24,16},{28,24},{20,28},{12,20},{4,12},{0,4},{9,1},{1... | collective-permute-start | bytes 1966088 | tf_op jit(solution)/shard_map/ppermute | solution.py:82
  7.4 20.8 %collective-permute-start.2 = (bf16[64,5120]{1,0:T(8,128)(2,1)S(1)}, bf16[64,5120]{1,0:T(8,128)(2,1)S(1)}, u32[]{:S(2)}, u32[]{:S(2)}) collective-permute-start(bf16[64,5120]{1,0:T(8,128)(2,1)S(1)} %constant_dynamic-update-slice_fusion.refs_0_), channel_id=1, source_target_pairs={{0,1},{1,0},{2,3},{3,2},{4,5},{5,4},{6,7},{7,6},{8,9},{9,8},{10,11... | collective-permute-start | bytes 1966088 | tf_op jit(solution)/shard_map/ppermute | solution.py:146
  7.4 20.9 %collective-permute-start.3 = (bf16[64,5120]{1,0:T(8,128)(2,1)S(1)}, bf16[64,5120]{1,0:T(8,128)(2,1)S(1)}, u32[]{:S(2)}, u32[]{:S(2)}) collective-permute-start(bf16[64,5120]{1,0:T(8,128)(2,1)S(1)} %constant_dynamic-update-slice_fusion.refs_0_), channel_id=1, source_target_pairs={{0,2},{1,3},{2,0},{3,1},{4,6},{5,7},{6,4},{7,5},{8,10},{9,11},{10,... | collective-permute-start | bytes 1966088 | tf_op jit(solution)/shard_map/ppermute | solution.py:146
  10.6 15.1 %all-to-all-start = ((s32[8,1,128]{2,1,0:T(1,128)}), s32[8,1,128]{2,1,0:T(1,128)S(1)}, u32[]{:S(2)}, u32[]{:S(2)}) async-start(s32[8,1,128]{2,1,0:T(1,128)} %broadcast_in_dim.22), calls=%async_computation | async-start | bytes 8192 | tf_op jit(solution)/shard_map/all_to_all | solution.py:1034
  28.3 15.0 %collective-permute-start.5 = (bf16[64,5120]{1,0:T(8,128)(2,1)S(1)}, bf16[64,5120]{1,0:T(8,128)(2,1)S(1)}, u32[]{:S(2)}, u32[]{:S(2)}) collective-permute-start(bf16[64,5120]{1,0:T(8,128)(2,1)S(1)} %collective-permute-done.1.refs_8_), channel_id=1, source_target_pairs={{8,0},{16,8},{24,16},{28,24},{20,28},{12,20},{4,12},{0,4},{9,1},{1... | collective-permute-start | bytes 1966088 | tf_op jit(solution)/shard_map/ppermute | solution.py:82
  29.8 13.5 %collective-permute-start.8 = (bf16[64,5120]{1,0:T(8,128)(2,1)S(1)}, bf16[64,5120]{1,0:T(8,128)(2,1)S(1)}, u32[]{:S(2)}, u32[]{:S(2)}) collective-permute-start(bf16[64,5120]{1,0:T(8,128)(2,1)S(1)} %collective-permute-done.1.refs_8_), channel_id=1, source_target_pairs={{0,1},{1,0},{2,3},{3,2},{4,5},{5,4},{6,7},{7,6},{8,9},{9,8},{10,11... | collective-permute-start | bytes 1966088 | tf_op jit(solution)/shard_map/ppermute | solution.py:146
  29.8 17.3 %collective-permute-start.4 = (bf16[64,5120]{1,0:T(8,128)(2,1)S(1)}, bf16[64,5120]{1,0:T(8,128)(2,1)}, u32[]{:S(2)}, u32[]{:S(2)}) collective-permute-start(bf16[64,5120]{1,0:T(8,128)(2,1)S(1)} %collective-permute-done.refs_4_), channel_id=1, source_target_pairs={{0,8},{8,16},{16,24},{24,28},{28,20},{20,12},{12,4},{4,0},{1,9},{9... | collective-permute-start | bytes 1966088 | tf_op jit(solution)/shard_map/ppermute | solution.py:81
  30.3 16.7 %collective-permute-start.7 = (bf16[64,5120]{1,0:T(8,128)(2,1)S(1)}, bf16[64,5120]{1,0:T(8,128)(2,1)S(1)}, u32[]{:S(2)}, u32[]{:S(2)}) collective-permute-start(bf16[64,5120]{1,0:T(8,128)(2,1)S(1)} %collective-permute-done.refs_4_), channel_id=1, source_target_pairs={{0,1},{1,0},{2,3},{3,2},{4,5},{5,4},{6,7},{7,6},{8,9},{9,8},{10,11... | collective-permute-start | bytes 1966088 | tf_op jit(solution)/shard_map/ppermute | solution.py:146
  30.6 16.9 %collective-permute-start.9 = (bf16[64,5120]{1,0:T(8,128)(2,1)S(1)}, bf16[64,5120]{1,0:T(8,128)(2,1)S(1)}, u32[]{:S(2)}, u32[]{:S(2)}) collective-permute-start(bf16[64,5120]{1,0:T(8,128)(2,1)S(1)} %collective-permute-done.refs_4_), channel_id=1, source_target_pairs={{0,2},{1,3},{2,0},{3,1},{4,6},{5,7},{6,4},{7,5},{8,10},{9,11},{10,... | collective-permute-start | bytes 1966088 | tf_op jit(solution)/shard_map/ppermute | solution.py:146
  49.2 16.4 %collective-permute-start.11 = (bf16[64,5120]{1,0:T(8,128)(2,1)}, bf16[64,5120]{1,0:T(8,128)(2,1)S(1)}, u32[]{:S(2)}, u32[]{:S(2)}) collective-permute-start(bf16[64,5120]{1,0:T(8,128)(2,1)} %collective-permute-done.4.refs_12_), channel_id=1, source_target_pairs={{0,8},{8,16},{16,24},{24,28},{28,20},{20,12},{12,4},{4,0},{1,9},{9... | collective-permute-start | bytes 1966088 | tf_op jit(solution)/shard_map/ppermute | solution.py:81
  49.8 19.2 %all-to-all-start.1 = ((bf16[4,64,2048]{2,1,0:T(8,128)(2,1)}), bf16[4,64,2048]{2,1,0:T(8,128)(2,1)}, u32[]{:S(2)}, u32[]{:S(2)}) async-start(bf16[4,64,2048]{2,1,0:T(8,128)(2,1)} %get-tuple-element.184), calls=%async_computation.1 | async-start | bytes 2097152 | tf_op jit(solution)/shard_map/all_to_all | solution.py:1042
  54.0 28.6 %collective-permute-start.16 = (bf16[64,5120]{1,0:T(8,128)(2,1)S(1)}, bf16[64,5120]{1,0:T(8,128)(2,1)}, u32[]{:S(2)}, u32[]{:S(2)}) collective-permute-start(bf16[64,5120]{1,0:T(8,128)(2,1)S(1)} %collective-permute-done.1.refs_8_), channel_id=1, source_target_pairs={{0,2},{1,3},{2,0},{3,1},{4,6},{5,7},{6,4},{7,5},{8,10},{9,11},{10,... | collective-permute-start | bytes 1966088 | tf_op jit(solution)/shard_map/ppermute | solution.py:146
  56.0 26.6 %collective-permute-start.14 = (bf16[64,5120]{1,0:T(8,128)(2,1)}, bf16[64,5120]{1,0:T(8,128)(2,1)}, u32[]{:S(2)}, u32[]{:S(2)}) collective-permute-start(bf16[64,5120]{1,0:T(8,128)(2,1)} %collective-permute-done.4.refs_12_), channel_id=1, source_target_pairs={{0,1},{1,0},{2,3},{3,2},{4,5},{5,4},{6,7},{7,6},{8,9},{9,8},{10,11... | collective-permute-start | bytes 1966088 | tf_op jit(solution)/shard_map/ppermute | solution.py:146
  56.0 26.6 %collective-permute-start.12 = (bf16[64,5120]{1,0:T(8,128)(2,1)}, bf16[64,5120]{1,0:T(8,128)(2,1)S(1)}, u32[]{:S(2)}, u32[]{:S(2)}) collective-permute-start(bf16[64,5120]{1,0:T(8,128)(2,1)} %copy-done.11), channel_id=1, source_target_pairs={{8,0},{16,8},{24,16},{28,24},{20,28},{12,20},{4,12},{0,4},{9,1},{1... | collective-permute-start | bytes 1966088 | tf_op jit(solution)/shard_map/ppermute | solution.py:82
  57.5 25.1 %collective-permute-start.15 = (bf16[64,5120]{1,0:T(8,128)(2,1)}, bf16[64,5120]{1,0:T(8,128)(2,1)}, u32[]{:S(2)}, u32[]{:S(2)}) collective-permute-start(bf16[64,5120]{1,0:T(8,128)(2,1)} %copy-done.11), channel_id=1, source_target_pairs={{0,1},{1,0},{2,3},{3,2},{4,5},{5,4},{6,7},{7,6},{8,9},{9,8},{10,11... | collective-permute-start | bytes 1966088 | tf_op jit(solution)/shard_map/ppermute | solution.py:146
  65.6 17.0 %collective-permute-start.13 = (bf16[64,5120]{1,0:T(8,128)(2,1)}, bf16[64,5120]{1,0:T(8,128)(2,1)}, u32[]{:S(2)}, u32[]{:S(2)}) collective-permute-start(bf16[64,5120]{1,0:T(8,128)(2,1)} %copy-done.15), channel_id=1, source_target_pairs={{0,1},{1,0},{2,3},{3,2},{4,5},{5,4},{6,7},{7,6},{8,9},{9,8},{10,11... | collective-permute-start | bytes 1966088 | tf_op jit(solution)/shard_map/ppermute | solution.py:146
  69.0 18.5 %all-to-all-start.2 = ((bf16[8,16,1376]{2,1,0:T(8,128)(2,1)}), bf16[8,16,1376]{2,1,0:T(8,128)(2,1)}, u32[]{:S(2)}, u32[]{:S(2)}) async-start(bf16[8,16,1376]{2,1,0:T(8,128)(2,1)} %pick.1), calls=%async_computation.2 | async-start | bytes 720896 | tf_op jit(solution)/shard_map/all_to_all | solution.py:1044
  82.6 9.5 %collective-permute-start.17 = (bf16[32,5120]{1,0:T(8,128)(2,1)}, bf16[32,5120]{1,0:T(8,128)(2,1)S(1)}, u32[]{:S(2)}, u32[]{:S(2)}) collective-permute-start(bf16[32,5120]{1,0:T(8,128)(2,1)} %slice.181), channel_id=1, source_target_pairs={{0,8},{8,16},{16,24},{24,28},{28,20},{20,12},{12,4},{4,0},{1,9},{9... | collective-permute-start | bytes 983048 | tf_op jit(solution)/shard_map/ppermute | solution.py:86
  83.3 17.9 %collective-permute-start.10 = (bf16[64,5120]{1,0:T(8,128)(2,1)}, bf16[64,5120]{1,0:T(8,128)(2,1)S(1)}, u32[]{:S(2)}, u32[]{:S(2)}) collective-permute-start(bf16[64,5120]{1,0:T(8,128)(2,1)} %collective-permute-done.4.refs_12_), channel_id=1, source_target_pairs={{0,2},{1,3},{2,0},{3,1},{4,6},{5,7},{6,4},{7,5},{8,10},{9,11},{10,... | collective-permute-start | bytes 1966088 | tf_op jit(solution)/shard_map/ppermute | solution.py:146
  83.7 30.0 %collective-permute-start.25 = (bf16[64,5120]{1,0:T(8,128)(2,1)S(1)}, bf16[64,5120]{1,0:T(8,128)(2,1)}, u32[]{:S(2)}, u32[]{:S(2)}) collective-permute-start(bf16[64,5120]{1,0:T(8,128)(2,1)S(1)} %copy-done.12), channel_id=1, source_target_pairs={{0,2},{1,3},{2,0},{3,1},{4,6},{5,7},{6,4},{7,5},{8,10},{9,11},{10,... | collective-permute-start | bytes 1966088 | tf_op jit(solution)/shard_map/ppermute | solution.py:146
  86.1 8.7 %collective-permute-start.18 = (bf16[32,5120]{1,0:T(8,128)(2,1)}, bf16[32,5120]{1,0:T(8,128)(2,1)}, u32[]{:S(2)}, u32[]{:S(2)}) collective-permute-start(bf16[32,5120]{1,0:T(8,128)(2,1)} %slice.182), channel_id=1, source_target_pairs={{8,0},{16,8},{24,16},{28,24},{20,28},{12,20},{4,12},{0,4},{9,1},{1... | collective-permute-start | bytes 983048 | tf_op jit(solution)/shard_map/ppermute | solution.py:87
  87.5 13.7 %collective-permute-start.21 = (bf16[64,5120]{1,0:T(8,128)(2,1)S(1)}, bf16[64,5120]{1,0:T(8,128)(2,1)}, u32[]{:S(2)}, u32[]{:S(2)}) collective-permute-start(bf16[64,5120]{1,0:T(8,128)(2,1)S(1)} %collective-permute-done.11.refs_20_), channel_id=1, source_target_pairs={{0,1},{1,0},{2,3},{3,2},{4,5},{5,4},{6,7},{7,6},{8,9},{9,8},{10,11... | collective-permute-start | bytes 1966088 | tf_op jit(solution)/shard_map/ppermute | solution.py:146
  92.9 8.3 %collective-permute-start.19 = (bf16[64,5120]{1,0:T(8,128)(2,1)}, bf16[64,5120]{1,0:T(8,128)(2,1)S(1)}, u32[]{:S(2)}, u32[]{:S(2)}) collective-permute-start(bf16[64,5120]{1,0:T(8,128)(2,1)} %collective-permute-done.16.refs_10_), channel_id=1, source_target_pairs={{0,1},{1,0},{2,3},{3,2},{4,5},{5,4},{6,7},{7,6},{8,9},{9,8},{10,11... | collective-permute-start | bytes 1966088 | tf_op jit(solution)/shard_map/ppermute | solution.py:146
  101.2 13.8 %collective-permute-start.24 = (bf16[64,5120]{1,0:T(8,128)(2,1)S(1)}, bf16[64,5120]{1,0:T(8,128)(2,1)}, u32[]{:S(2)}, u32[]{:S(2)}) collective-permute-start(bf16[64,5120]{1,0:T(8,128)(2,1)S(1)} %constant_dynamic-update-slice_fusion.4.refs_28_), channel_id=1, source_target_pairs={{0,1},{1,0},{2,3},{3,2},{4,5},{5,4},{6,7},{7,6},{8,9},{9,8},{10,11... | collective-permute-start | bytes 1966088 | tf_op jit(solution)/shard_map/ppermute | solution.py:146
  102.1 13.6 %collective-permute-start.23 = (bf16[64,5120]{1,0:T(8,128)(2,1)S(1)}, bf16[64,5120]{1,0:T(8,128)(2,1)}, u32[]{:S(2)}, u32[]{:S(2)}) collective-permute-start(bf16[64,5120]{1,0:T(8,128)(2,1)S(1)} %collective-permute-done.12.refs_24_), channel_id=1, source_target_pairs={{0,1},{1,0},{2,3},{3,2},{4,5},{5,4},{6,7},{7,6},{8,9},{9,8},{10,11... | collective-permute-start | bytes 1966088 | tf_op jit(solution)/shard_map/ppermute | solution.py:146
  102.1 13.6 %collective-permute-start.22 = (bf16[64,5120]{1,0:T(8,128)(2,1)S(1)}, bf16[64,5120]{1,0:T(8,128)(2,1)}, u32[]{:S(2)}, u32[]{:S(2)}) collective-permute-start(bf16[64,5120]{1,0:T(8,128)(2,1)S(1)} %collective-permute-done.10.refs_14_), channel_id=1, source_target_pairs={{0,1},{1,0},{2,3},{3,2},{4,5},{5,4},{6,7},{7,6},{8,9},{9,8},{10,11... | collective-permute-start | bytes 1966088 | tf_op jit(solution)/shard_map/ppermute | solution.py:146
  106.1 47.9 %collective-permute-start.32 = (bf16[512,2048]{1,0:T(8,128)(2,1)}, bf16[512,2048]{1,0:T(8,128)(2,1)}, u32[]{:S(2)}, u32[]{:S(2)}) collective-permute-start(bf16[512,2048]{1,0:T(8,128)(2,1)} %pad_maximum_fusion.refs_0_), channel_id=1, source_target_pairs={{0,8},{8,16},{16,24},{24,28},{28,20},{20,12},{12,4},{4,0},{1,9},{9... | collective-permute-start | bytes 6291464 | tf_op jit(solution)/shard_map/ppermute | solution.py:81
  113.7 46.3 %collective-permute-start.33 = (bf16[512,2048]{1,0:T(8,128)(2,1)}, bf16[512,2048]{1,0:T(8,128)(2,1)}, u32[]{:S(2)}, u32[]{:S(2)}) collective-permute-start(bf16[512,2048]{1,0:T(8,128)(2,1)} %pad_maximum_fusion.refs_0_), channel_id=1, source_target_pairs={{8,0},{16,8},{24,16},{28,24},{20,28},{12,20},{4,12},{0,4},{9,1},{1... | collective-permute-start | bytes 6291464 | tf_op jit(solution)/shard_map/ppermute | solution.py:82
  115.1 10.1 %collective-permute-start.26 = (bf16[8,16,608]{2,1,0:T(8,128)(2,1)S(1)}, bf16[8,16,608]{2,1,0:T(8,128)(2,1)}, u32[]{:S(2)}, u32[]{:S(2)}) collective-permute-start(bf16[8,16,608]{2,1,0:T(8,128)(2,1)S(1)} %slice.140), channel_id=1, source_target_pairs={{0,2},{1,3},{2,0},{3,1},{4,6},{5,7},{6,4},{7,5},{8,10},{9,11},{10,... | collective-permute-start | bytes 466952 | tf_op jit(solution)/shard_map/ppermute | solution.py:146
  115.7 20.5 %collective-permute-start.29 = (bf16[64,5120]{1,0:T(8,128)(2,1)S(1)}, bf16[64,5120]{1,0:T(8,128)(2,1)S(1)}, u32[]{:S(2)}, u32[]{:S(2)}) collective-permute-start(bf16[64,5120]{1,0:T(8,128)(2,1)S(1)} %collective-permute-done.11.refs_20_), channel_id=1, source_target_pairs={{0,2},{1,3},{2,0},{3,1},{4,6},{5,7},{6,4},{7,5},{8,10},{9,11},{10,... | collective-permute-start | bytes 1966088 | tf_op jit(solution)/shard_map/ppermute | solution.py:146
  125.1 11.1 %collective-permute-start.28 = (bf16[8,16,608]{2,1,0:T(8,128)(2,1)}, bf16[8,16,608]{2,1,0:T(8,128)(2,1)S(1)}, u32[]{:S(2)}, u32[]{:S(2)}) collective-permute-start(bf16[8,16,608]{2,1,0:T(8,128)(2,1)} %collective-permute-done.26.p2), channel_id=1, source_target_pairs={{0,1},{1,0},{2,3},{3,2},{4,5},{5,4},{6,7},{7,6},{8,9},{9,8},{10,11... | collective-permute-start | bytes 466952 | tf_op jit(solution)/shard_map/ppermute | solution.py:146
  125.6 34.3 %collective-permute-start.31 = (bf16[64,5120]{1,0:T(8,128)(2,1)S(1)}, bf16[64,5120]{1,0:T(8,128)(2,1)S(1)}, u32[]{:S(2)}, u32[]{:S(2)}) collective-permute-start(bf16[64,5120]{1,0:T(8,128)(2,1)S(1)} %collective-permute-done.12.refs_24_), channel_id=1, source_target_pairs={{0,2},{1,3},{2,0},{3,1},{4,6},{5,7},{6,4},{7,5},{8,10},{9,11},{10,... | collective-permute-start | bytes 1966088 | tf_op jit(solution)/shard_map/ppermute | solution.py:146
  136.3 23.7 %collective-permute-start.34 = (bf16[64,5120]{1,0:T(8,128)(2,1)S(1)}, bf16[64,5120]{1,0:T(8,128)(2,1)S(1)}, u32[]{:S(2)}, u32[]{:S(2)}) collective-permute-start(bf16[64,5120]{1,0:T(8,128)(2,1)S(1)} %collective-permute-done.29.refs_22_), channel_id=1, source_target_pairs={{0,1},{1,0},{2,3},{3,2},{4,5},{5,4},{6,7},{7,6},{8,9},{9,8},{10,11... | collective-permute-start | bytes 1966088 | tf_op jit(solution)/shard_map/ppermute | solution.py:146
  136.3 25.2 %collective-permute-start.30 = (bf16[64,5120]{1,0:T(8,128)(2,1)S(1)}, bf16[64,5120]{1,0:T(8,128)(2,1)}, u32[]{:S(2)}, u32[]{:S(2)}) collective-permute-start(bf16[64,5120]{1,0:T(8,128)(2,1)S(1)} %constant_dynamic-update-slice_fusion.4.refs_28_), channel_id=1, source_target_pairs={{0,2},{1,3},{2,0},{3,1},{4,6},{5,7},{6,4},{7,5},{8,10},{9,11},{10,... | collective-permute-start | bytes 1966088 | tf_op jit(solution)/shard_map/ppermute | solution.py:146
  163.1 48.3 %collective-permute-start.44 = (bf16[512,2048]{1,0:T(8,128)(2,1)}, bf16[512,2048]{1,0:T(8,128)(2,1)}, u32[]{:S(2)}, u32[]{:S(2)}) collective-permute-start(bf16[512,2048]{1,0:T(8,128)(2,1)} %collective-permute-done.33.refs_2_), channel_id=1, source_target_pairs={{8,0},{16,8},{24,16},{28,24},{20,28},{12,20},{4,12},{0,4},{9,1},{1... | collective-permute-start | bytes 6291464 | tf_op jit(solution)/shard_map/ppermute | solution.py:82
  164.6 47.9 %collective-permute-start.43 = (bf16[512,2048]{1,0:T(8,128)(2,1)}, bf16[512,2048]{1,0:T(8,128)(2,1)}, u32[]{:S(2)}, u32[]{:S(2)}) collective-permute-start(bf16[512,2048]{1,0:T(8,128)(2,1)} %collective-permute-done.32.refs_1_), channel_id=1, source_target_pairs={{0,8},{8,16},{16,24},{24,28},{28,20},{20,12},{12,4},{4,0},{1,9},{9... | collective-permute-start | bytes 6291464 | tf_op jit(solution)/shard_map/ppermute | solution.py:81
  184.4 30.4 %collective-permute-start.38 = (bf16[8,128,256]{2,1,0:T(8,128)(2,1)S(1)}, bf16[8,128,256]{2,1,0:T(8,128)(2,1)S(1)}, u32[]{:S(2)}, u32[]{:S(2)}) collective-permute-start(bf16[8,128,256]{2,1,0:T(8,128)(2,1)S(1)} %pad_maximum_fusion.4.kv0), channel_id=1, source_target_pairs={{0,2},{1,3},{2,0},{3,1},{4,6},{5,7},{6,4},{7,5},{8,10},{9,11},{10,... | collective-permute-start | bytes 1572872 | tf_op jit(solution)/shard_map/ppermute | solution.py:146
  212.5 47.1 %collective-permute-start.46 = (bf16[512,2048]{1,0:T(8,128)(2,1)}, bf16[512,2048]{1,0:T(8,128)(2,1)}, u32[]{:S(2)}, u32[]{:S(2)}) collective-permute-start(bf16[512,2048]{1,0:T(8,128)(2,1)} %collective-permute-done.44.refs_4_), channel_id=1, source_target_pairs={{8,0},{16,8},{24,16},{28,24},{20,28},{12,20},{4,12},{0,4},{9,1},{1... | collective-permute-start | bytes 6291464 | tf_op jit(solution)/shard_map/ppermute | solution.py:82
  214.0 48.0 %collective-permute-start.45 = (bf16[512,2048]{1,0:T(8,128)(2,1)}, bf16[512,2048]{1,0:T(8,128)(2,1)}, u32[]{:S(2)}, u32[]{:S(2)}) collective-permute-start(bf16[512,2048]{1,0:T(8,128)(2,1)} %collective-permute-done.43.refs_3_), channel_id=1, source_target_pairs={{0,8},{8,16},{16,24},{24,28},{28,20},{20,12},{12,4},{4,0},{1,9},{9... | collective-permute-start | bytes 6291464 | tf_op jit(solution)/shard_map/ppermute | solution.py:81
  216.5 32.4 %collective-permute-start.50 = (bf16[256,2048]{1,0:T(8,128)(2,1)}, bf16[256,2048]{1,0:T(8,128)(2,1)}, u32[]{:S(2)}, u32[]{:S(2)}) collective-permute-start(bf16[256,2048]{1,0:T(8,128)(2,1)} %multiply_convert_fusion.g0), channel_id=1, source_target_pairs={{0,2},{1,3},{2,0},{3,1},{4,6},{5,7},{6,4},{7,5},{8,10},{9,11},{10,... | collective-permute-start | bytes 3145736 | tf_op jit(solution)/shard_map/ppermute | solution.py:146
  217.4 63.0 %collective-permute-start.49 = (bf16[256,2048]{1,0:T(8,128)(2,1)}, bf16[256,2048]{1,0:T(8,128)(2,1)}, u32[]{:S(2)}, u32[]{:S(2)}) collective-permute-start(bf16[256,2048]{1,0:T(8,128)(2,1)} %multiply_convert_fusion.g0), channel_id=1, source_target_pairs={{0,1},{1,0},{2,3},{3,2},{4,5},{5,4},{6,7},{7,6},{8,9},{9,8},{10,11... | collective-permute-start | bytes 3145736 | tf_op jit(solution)/shard_map/ppermute | solution.py:146
  243.5 37.6 %collective-permute-start.41 = (bf16[256,2048]{1,0:T(8,128)(2,1)}, bf16[256,2048]{1,0:T(8,128)(2,1)}, u32[]{:S(2)}, u32[]{:S(2)}) collective-permute-start(bf16[256,2048]{1,0:T(8,128)(2,1)} %get-tuple-element.217.n0), channel_id=1, source_target_pairs={{0,2},{1,3},{2,0},{3,1},{4,6},{5,7},{6,4},{7,5},{8,10},{9,11},{10,... | collective-permute-start | bytes 3145736 | tf_op jit(solution)/shard_map/ppermute | solution.py:146
  244.7 35.8 %all-to-all-start.3 = ((bf16[4,64,2048]{2,1,0:T(8,128)(2,1)}), bf16[4,64,2048]{2,1,0:T(8,128)(2,1)}, u32[]{:S(2)}, u32[]{:S(2)}) async-start(bf16[4,64,2048]{2,1,0:T(8,128)(2,1)} %get-tuple-element.250), calls=%async_computation.3 | async-start | bytes 2097152 | tf_op jit(solution)/shard_map/all_to_all | solution.py:1096
  248.9 44.8 %collective-permute-start.51 = (bf16[256,2048]{1,0:T(8,128)(2,1)}, bf16[256,2048]{1,0:T(8,128)(2,1)}, u32[]{:S(2)}, u32[]{:S(2)}) collective-permute-start(bf16[256,2048]{1,0:T(8,128)(2,1)} %collective-permute-done.50.g2), channel_id=1, source_target_pairs={{0,1},{1,0},{2,3},{3,2},{4,5},{5,4},{6,7},{7,6},{8,9},{9,8},{10,11... | collective-permute-start | bytes 3145736 | tf_op jit(solution)/shard_map/ppermute | solution.py:146
  262.0 31.9 %collective-permute-start.48 = (bf16[256,2048]{1,0:T(8,128)(2,1)}, bf16[256,2048]{1,0:T(8,128)(2,1)}, u32[]{:S(2)}, u32[]{:S(2)}) collective-permute-start(bf16[256,2048]{1,0:T(8,128)(2,1)} %slice.191), channel_id=1, source_target_pairs={{8,0},{16,8},{24,16},{28,24},{20,28},{12,20},{4,12},{0,4},{9,1},{1... | collective-permute-start | bytes 3145736 | tf_op jit(solution)/shard_map/ppermute | solution.py:87
  265.7 28.7 %collective-permute-start.47 = (bf16[256,2048]{1,0:T(8,128)(2,1)}, bf16[256,2048]{1,0:T(8,128)(2,1)}, u32[]{:S(2)}, u32[]{:S(2)}) collective-permute-start(bf16[256,2048]{1,0:T(8,128)(2,1)} %slice.190), channel_id=1, source_target_pairs={{0,8},{8,16},{16,24},{24,28},{28,20},{20,12},{12,4},{4,0},{1,9},{9... | collective-permute-start | bytes 3145736 | tf_op jit(solution)/shard_map/ppermute | solution.py:86
  280.5 32.7 %collective-permute-start.52 = (bf16[256,2048]{1,0:T(8,128)(2,1)}, bf16[256,2048]{1,0:T(8,128)(2,1)}, u32[]{:S(2)}, u32[]{:S(2)}) collective-permute-start(bf16[256,2048]{1,0:T(8,128)(2,1)} %bitcast.69.refs_0_), channel_id=1, source_target_pairs={{0,8},{8,16},{16,24},{24,28},{28,20},{20,12},{12,4},{4,0},{1,9},{9... | collective-permute-start | bytes 3145736 | tf_op jit(solution)/shard_map/ppermute | solution.py:81
  281.1 32.0 %collective-permute-start.53 = (bf16[256,2048]{1,0:T(8,128)(2,1)}, bf16[256,2048]{1,0:T(8,128)(2,1)}, u32[]{:S(2)}, u32[]{:S(2)}) collective-permute-start(bf16[256,2048]{1,0:T(8,128)(2,1)} %bitcast.69.refs_0_), channel_id=1, source_target_pairs={{8,0},{16,8},{24,16},{28,24},{20,28},{12,20},{4,12},{0,4},{9,1},{1... | collective-permute-start | bytes 3145736 | tf_op jit(solution)/shard_map/ppermute | solution.py:82
  293.8 21.4 %collective-permute-start.40 = (bf16[256,2048]{1,0:T(8,128)(2,1)S(1)}, bf16[256,2048]{1,0:T(8,128)(2,1)S(1)}, u32[]{:S(2)}, u32[]{:S(2)}) collective-permute-start(bf16[256,2048]{1,0:T(8,128)(2,1)S(1)} %copy-done.40), channel_id=1, source_target_pairs={{0,1},{1,0},{2,3},{3,2},{4,5},{5,4},{6,7},{7,6},{8,9},{9,8},{10,11... | collective-permute-start | bytes 3145736 | tf_op jit(solution)/shard_map/ppermute | solution.py:146
  293.9 21.3 %collective-permute-start.42 = (bf16[256,2048]{1,0:T(8,128)(2,1)}, bf16[256,2048]{1,0:T(8,128)(2,1)}, u32[]{:S(2)}, u32[]{:S(2)}) collective-permute-start(bf16[256,2048]{1,0:T(8,128)(2,1)} %collective-permute-done.41.n2), channel_id=1, source_target_pairs={{0,1},{1,0},{2,3},{3,2},{4,5},{5,4},{6,7},{7,6},{8,9},{9,8},{10,11... | collective-permute-start | bytes 3145736 | tf_op jit(solution)/shard_map/ppermute | solution.py:146
  313.1 26.5 %collective-permute-start.55 = (bf16[256,2048]{1,0:T(8,128)(2,1)}, bf16[256,2048]{1,0:T(8,128)(2,1)S(1)}, u32[]{:S(2)}, u32[]{:S(2)}) collective-permute-start(bf16[256,2048]{1,0:T(8,128)(2,1)} %collective-permute-done.53.refs_2_), channel_id=1, source_target_pairs={{8,0},{16,8},{24,16},{28,24},{20,28},{12,20},{4,12},{0,4},{9,1},{1... | collective-permute-start | bytes 3145736 | tf_op jit(solution)/shard_map/ppermute | solution.py:82
  314.6 25.1 %collective-permute-start.54 = (bf16[256,2048]{1,0:T(8,128)(2,1)}, bf16[256,2048]{1,0:T(8,128)(2,1)S(1)}, u32[]{:S(2)}, u32[]{:S(2)}) collective-permute-start(bf16[256,2048]{1,0:T(8,128)(2,1)} %collective-permute-done.52.refs_1_), channel_id=1, source_target_pairs={{0,8},{8,16},{16,24},{24,28},{28,20},{20,12},{12,4},{4,0},{1,9},{9... | collective-permute-start | bytes 3145736 | tf_op jit(solution)/shard_map/ppermute | solution.py:81
  339.7 24.6 %collective-permute-start.57 = (bf16[256,2048]{1,0:T(8,128)(2,1)S(1)}, bf16[256,2048]{1,0:T(8,128)(2,1)S(1)}, u32[]{:S(2)}, u32[]{:S(2)}) collective-permute-start(bf16[256,2048]{1,0:T(8,128)(2,1)S(1)} %collective-permute-done.55.refs_4_), channel_id=1, source_target_pairs={{8,0},{16,8},{24,16},{28,24},{20,28},{12,20},{4,12},{0,4},{9,1},{1... | collective-permute-start | bytes 3145736 | tf_op jit(solution)/shard_map/ppermute | solution.py:82
  341.1 24.8 %collective-permute-start.56 = (bf16[256,2048]{1,0:T(8,128)(2,1)S(1)}, bf16[256,2048]{1,0:T(8,128)(2,1)S(1)}, u32[]{:S(2)}, u32[]{:S(2)}) collective-permute-start(bf16[256,2048]{1,0:T(8,128)(2,1)S(1)} %collective-permute-done.54.refs_3_), channel_id=1, source_target_pairs={{0,8},{8,16},{16,24},{24,28},{28,20},{20,12},{12,4},{4,0},{1,9},{9... | collective-permute-start | bytes 3145736 | tf_op jit(solution)/shard_map/ppermute | solution.py:81
  365.9 12.2 %collective-permute-start.59 = (bf16[128,2048]{1,0:T(8,128)(2,1)S(1)}, bf16[128,2048]{1,0:T(8,128)(2,1)S(1)}, u32[]{:S(2)}, u32[]{:S(2)}) collective-permute-start(bf16[128,2048]{1,0:T(8,128)(2,1)S(1)} %slice.193), channel_id=1, source_target_pairs={{8,0},{16,8},{24,16},{28,24},{20,28},{12,20},{4,12},{0,4},{9,1},{1... | collective-permute-start | bytes 1572872 | tf_op jit(solution)/shard_map/ppermute | solution.py:87
  367.3 11.9 %collective-permute-start.58 = (bf16[128,2048]{1,0:T(8,128)(2,1)S(1)}, bf16[128,2048]{1,0:T(8,128)(2,1)S(1)}, u32[]{:S(2)}, u32[]{:S(2)}) collective-permute-start(bf16[128,2048]{1,0:T(8,128)(2,1)S(1)} %slice.192), channel_id=1, source_target_pairs={{0,8},{8,16},{16,24},{24,28},{28,20},{20,12},{12,4},{4,0},{1,9},{9... | collective-permute-start | bytes 1572872 | tf_op jit(solution)/shard_map/ppermute | solution.py:86
  424.3 22.8 %collective-permute-start.62 = (bf16[256,1024]{1,0:T(8,128)(2,1)S(1)}, bf16[256,1024]{1,0:T(8,128)(2,1)S(1)}, u32[]{:S(2)}, u32[]{:S(2)}) collective-permute-start(bf16[256,1024]{1,0:T(8,128)(2,1)S(1)} %fusion.11), channel_id=1, source_target_pairs={{0,2},{1,3},{2,0},{3,1},{4,6},{5,7},{6,4},{7,5},{8,10},{9,11},{10,... | collective-permute-start | bytes 1572872 | tf_op jit(solution)/shard_map/ppermute | solution.py:146
  428.7 21.1 %collective-permute-start.63 = (bf16[256,1024]{1,0:T(8,128)(2,1)S(1)}, bf16[256,1024]{1,0:T(8,128)(2,1)S(1)}, u32[]{:S(2)}, u32[]{:S(2)}) collective-permute-start(bf16[256,1024]{1,0:T(8,128)(2,1)S(1)} %fusion.12), channel_id=1, source_target_pairs={{0,2},{1,3},{2,0},{3,1},{4,6},{5,7},{6,4},{7,5},{8,10},{9,11},{10,... | collective-permute-start | bytes 1572872 | tf_op jit(solution)/shard_map/ppermute | solution.py:146
  463.3 25.7 %collective-permute-start.65 = (bf16[256,2048]{1,0:T(8,128)(2,1)}, bf16[256,2048]{1,0:T(8,128)(2,1)}, u32[]{:S(2)}, u32[]{:S(2)}) collective-permute-start(bf16[256,2048]{1,0:T(8,128)(2,1)} %fusion.8), channel_id=1, source_target_pairs={{0,2},{1,3},{2,0},{3,1},{4,6},{5,7},{6,4},{7,5},{8,10},{9,11},{10,... | collective-permute-start | bytes 3145736 | tf_op jit(solution)/shard_map/ppermute | solution.py:146
  491.8 14.6 %collective-permute-start.67 = (bf16[4,128,256]{2,1,0:T(8,128)(2,1)S(1)}, bf16[4,128,256]{2,1,0:T(8,128)(2,1)S(1)}, u32[]{:S(2)}, u32[]{:S(2)}) collective-permute-start(bf16[4,128,256]{2,1,0:T(8,128)(2,1)S(1)} %fusion.15), channel_id=1, source_target_pairs={{0,2},{1,3},{2,0},{3,1},{4,6},{5,7},{6,4},{7,5},{8,10},{9,11},{10,... | collective-permute-start | bytes 786440 | tf_op jit(solution)/shard_map/ppermute | solution.py:146
  508.2 8.6 %collective-permute-start.69 = (bf16[4,128,256]{2,1,0:T(8,128)(2,1)S(1)}, bf16[4,128,256]{2,1,0:T(8,128)(2,1)S(1)}, u32[]{:S(2)}, u32[]{:S(2)}) collective-permute-start(bf16[4,128,256]{2,1,0:T(8,128)(2,1)S(1)} %fusion.16), channel_id=1, source_target_pairs={{0,2},{1,3},{2,0},{3,1},{4,6},{5,7},{6,4},{7,5},{8,10},{9,11},{10,... | collective-permute-start | bytes 786440 | tf_op jit(solution)/shard_map/ppermute | solution.py:146
  527.0 12.5 %collective-permute-start.71 = (bf16[8,16,608]{2,1,0:T(8,128)(2,1)S(1)}, bf16[8,16,608]{2,1,0:T(8,128)(2,1)S(1)}, u32[]{:S(2)}, u32[]{:S(2)}) collective-permute-start(bf16[8,16,608]{2,1,0:T(8,128)(2,1)S(1)} %fusion.19), channel_id=1, source_target_pairs={{0,2},{1,3},{2,0},{3,1},{4,6},{5,7},{6,4},{7,5},{8,10},{9,11},{10,... | collective-permute-start | bytes 466952 | tf_op jit(solution)/shard_map/ppermute | solution.py:146
  540.5 14.6 %all-to-all-start.4 = ((bf16[8,16,1376]{2,1,0:T(8,128)(2,1)}), bf16[8,16,1376]{2,1,0:T(8,128)(2,1)S(1)}, u32[]{:S(2)}, u32[]{:S(2)}) async-start(bf16[8,16,1376]{2,1,0:T(8,128)(2,1)} %pad_maximum_fusion.5), calls=%async_computation.4 | async-start | bytes 720896 | tf_op jit(solution)/shard_map/all_to_all | solution.py:1185
  (79 other events, 821.0 us)

commit v5 on v4

--- a/solution.py
+++ b/solution.py
@@ -83,8 +83,9 @@
             self.pieces += [self.left, self.right]
             return self.left, self.right
         half = self.left.shape[0] // 2
-        top = lax.ppermute(clock(self.left[:half]), "dp", right)
-        bottom = lax.ppermute(clock(self.right[half:]), "dp", left)
+        last_left, last_right = clock((self.left, self.right))
+        top = lax.ppermute(last_left[:half], "dp", right)
+        bottom = lax.ppermute(last_right[half:], "dp", left)
         self.pieces.append((top, bottom))
         return top, bottom
 
@@ -1014,7 +1015,7 @@
                 new = [new]
         elif first_came is not None:
             age += 1
-            if age == 3:
+            if age == 3 and len(first_ring.pieces) == 3:
                 waits += first_came
                 first_came = None
         elif not first_ring.complete():
@@ -1086,14 +1087,14 @@
     query_prep = lambda v: prepare(v, query_gain, cosine, sine)
     key_prep = lambda v: prepare(v, key_gain, cosine, sine)
     keys_values = jnp.concatenate([key_prep(key_lin), value_lin], axis=1).astype(BF16)
-    keys_values = seq_pieces(keys_values)
+    grads = seq_pieces(clock(grad_out))
+    keys_values = seq_pieces(after(keys_values, grads[2]))
     queries = (query_prep(query_lin) * scale).astype(BF16).reshape(n_query, block)
     limit = jnp.minimum(positions, length - 1).astype(jnp.int32)
     limit = jnp.tile(limit, GROUP)[None, :]
-    belt.advance(queries)
-    grads = seq_pieces(after(grad_out, keys_values[2]))
+    belt.advance(queries, keys_values[2])
+    swapped_b = lax.all_to_all(after(slots_b, queries), "seq", 0, 0, tiled=True)
     mixed, raised, inverse = attend(seq, limit, queries, keys_values)
-    swapped_b = lax.all_to_all(after(slots_b, queries), "seq", 0, 0, tiled=True)
     belt.advance(mixed)
 
     inner_out = contract(ao, mixed, 1, 0).astype(BF16)

time: 569 us -> 561 us (0.986)
  waiting for transfers between devices: 173 us -> 160 us
    all_to_all x1, waiting for transfers between devices: 14.2 us -> 0.01 us  [shards(): swapped_b = lax.all_to_all(after(slots_b, queries), 'seq', 0, 0, tiled=True)]
    ppermute x9, waiting for transfers between devices: 53.8 us -> 43.2 us  [step(): self.right = lax.ppermute(clock(self.right), 'dp', left)]
    ppermute x9, waiting for transfers between devices: 31.3 us -> 22.4 us  [step(): self.left = lax.ppermute(clock(self.left), 'dp', right)]
    all_to_all x1, waiting for transfers between devices: 3.39 us -> 10.1 us  [shards(): swapped_a = lax.all_to_all(clock(slots_a), 'seq', 0, 0, tiled=True)]
    ppermute x6, waiting for transfers between devices: 9.7 us -> 15.6 us  [the longest x3 10.7 us: step(): top = lax.ppermute(last_left[:half], 'dp', right)]
    unnamed x140 -> x128, local copies, waits for them, and re-layouts: 15.9 us -> 15.8 us
  transfers between devices with their start and end apart: 77 -> 77, of which waited for: 32 -> 33; matrix products, arithmetic and copies ran while one was open for 9% -> 9% of each run, Pallas kernels for 33% -> 33%
where the time goes in v5:
time: 561 us; the launch traced here: 551 us
  Pallas kernels  235 us (42%)
  waiting for transfers between devices  160 us (29%)
  starting transfers between devices  78.4 us (14%)
  local copies, waits for them, and re-layouts  32.8 us (6%)
  other arithmetic  32.4 us (6%)
  matrix products  8.22 us (1%)
    ppermute x48, waiting for transfers between devices, partner(): return lax.ppermute(operand, 'seq', [(i, i ^ bit) for i in range(size)])  54.9 us
    ppermute x9, waiting for transfers between devices, step(): self.right = lax.ppermute(clock(self.right), 'dp', left)  43.2 us
    pallas_call x2, Pallas kernels, units(): call(units_kernel, 'units', grid=(steps,), in_specs=[fixed(tokens, width)...  36 us
    ppermute x48, starting transfers between devices, partner(): return lax.ppermute(operand, 'seq', [(i, i ^ bit) for i in range(size)])  28.4 us
    pallas_call x2, Pallas kernels, attend_back(): call(attend_back_kernel, 'attend_back', grid=(count,), in_specs=[head_row...  24.3 us
    ppermute x9, waiting for transfers between devices, step(): self.left = lax.ppermute(clock(self.left), 'dp', right)  22.4 us
    pallas_call x2, Pallas kernels, units_back(): call(units_back_kernel, 'units_back', grid=(steps,), in_specs=[pl.BlockSp...  19.5 us
    pallas_call x1, Pallas kernels, lower(): call(lower_kernel, 'lower', grid=(width // step,), in_specs=[fixed(tokens...  17.3 us
  transfers between devices with their start and end apart: 77, of which 33 were waited for; matrix products, arithmetic and copies ran while one was open for 9% of the time, Pallas kernels for 33%

profile of v5, /device:TPU:0, one launch (start us, length us, event | category | flops | bytes accessed | tf_op | source)
XLA Modules:
  0.0 550.5 jit_solution(2823980320604058523)
XLA Ops:
  4.3 3.1 collective-permute-start
  10.6 5.8 %all-to-all-start = ((s32[8,1,128]{2,1,0:T(1,128)}), s32[8,1,128]{2,1,0:T(1,128)S(1)}, u32[]{:S(2)}, u32[]{:S(2)}) async-start(s32[8,1,128]{2,1,0:T(1,128)} %broadcast_in_dim.22), calls=%async_computation | async-start | bytes 8192 | tf_op jit(solution)/shard_map/all_to_all | solution.py:1035
  19.3 3.0 columns.1
  22.3 3.3 all-to-all-done
  32.0 11.2 %collective-permute-done.5.refs_16_ = bf16[64,5120]{1,0:T(8,128)(2,1)S(1)} collective-permute-done((bf16[64,5120]{1,0:T(8,128)(2,1)S(1)}, bf16[64,5120]{1,0:T(8,128)(2,1)S(1)}, u32[]{:S(2)}, u32[]{:S(2)}) %collective-permute-start.5) | collective-permute-done | bytes 655392 | tf_op jit(solution)/shard_map/ppermute | solution.py:82
  46.5 4.2 all-to-all-start.1
  53.1 9.7 %collective-permute-done.16.refs_10_ = bf16[64,5120]{1,0:T(8,128)(2,1)} collective-permute-done((bf16[64,5120]{1,0:T(8,128)(2,1)S(1)}, bf16[64,5120]{1,0:T(8,128)(2,1)}, u32[]{:S(2)}, u32[]{:S(2)}) %collective-permute-start.16) | collective-permute-done | bytes 655392 | tf_op jit(solution)/shard_map/ppermute | solution.py:147
  62.7 10.1 %all-to-all-done.1 = bf16[4,64,2048]{2,1,0:T(8,128)(2,1)} async-done(((bf16[4,64,2048]{2,1,0:T(8,128)(2,1)}), bf16[4,64,2048]{2,1,0:T(8,128)(2,1)}, u32[]{:S(2)}, u32[]{:S(2)}) %all-to-all-start.1) | async-done | bytes 1048608 | tf_op jit(solution)/shard_map/all_to_all | solution.py:1043
  72.8 4.1 all-to-all-start.2
  76.9 3.2 pad_maximum_fusion.refs_0_
  80.3 1.9 collective-permute-start.17
  85.1 3.2 all-to-all-done.2.mine_ref
  94.7 5.4 collective-permute-done.10.refs_14_
  102.2 2.8 bitcast_convert_fusion
  106.5 5.1 collective-permute-done.25.refs_18_
  114.1 2.3 copy.58
  118.0 2.7 multiply_convert_fusion.g0
  124.1 9.1 %collective-permute-done.29.refs_22_ = bf16[64,5120]{1,0:T(8,128)(2,1)S(1)} collective-permute-done((bf16[64,5120]{1,0:T(8,128)(2,1)S(1)}, bf16[64,5120]{1,0:T(8,128)(2,1)S(1)}, u32[]{:S(2)}, u32[]{:S(2)}) %collective-permute-start.29) | collective-permute-done | bytes 655392 | tf_op jit(solution)/shard_map/ppermute | solution.py:147
  134.8 18.0 %collective-permute-done.32.refs_1_ = bf16[512,2048]{1,0:T(8,128)(2,1)} collective-permute-done((bf16[512,2048]{1,0:T(8,128)(2,1)}, bf16[512,2048]{1,0:T(8,128)(2,1)}, u32[]{:S(2)}, u32[]{:S(2)}) %collective-permute-start.32) | collective-permute-done | bytes 2097184 | tf_op jit(solution)/shard_map/ppermute | solution.py:81
  152.8 4.0 collective-permute-done.33.refs_2_
  163.7 2.3 spread.1
  166.0 2.7 convolution_convert_fusion.inner_ref
  168.8 10.2 %project_in.1 = f32[3072,256]{1,0:T(8,128)} custom-call(s32[32]{0:T(128)} %stack.163.order_ref, bf16[2048,256]{1,0:T(8,128)(2,1)} %fusion.28.normed_ref, bf16[256,48]{1,0:T(8,128)(2,1)} %convolution_convert_fusion.inner_ref, bf16[48,3072]{1,0:T(8,128)(2,1)} %get-tuple-element.213.b_ref, bf16[64,5120]{1,0:T(8,128)(2,1)} %copy-done.6, ...), custom_call_target="tpu_custom_call" | custom-call | tf_op jit(solution)/shard_map/project_in/pallas_call | solution.py:311
  183.6 3.7 collective-permute-done.37.g2
  190.9 17.4 %collective-permute-done.45.refs_4_ = bf16[512,2048]{1,0:T(8,128)(2,1)} collective-permute-done((bf16[512,2048]{1,0:T(8,128)(2,1)}, bf16[512,2048]{1,0:T(8,128)(2,1)}, u32[]{:S(2)}, u32[]{:S(2)}) %collective-permute-start.45) | collective-permute-done | bytes 2097184 | tf_op jit(solution)/shard_map/ppermute | solution.py:82
  211.3 4.4 all-to-all-start.3
  219.0 14.9 %attend.1 = (bf16[2048,256]{1,0:T(8,128)(2,1)}, bf16[8,4,256,1024]{3,2,1,0:T(8,128)(2,1)}, f32[8,1,1024]{2,1,0:T(1,128)}) custom-call(s32[1]{0:T(128)} %bitcast.32.seq_ref, s32[1,1024]{1,0:T(1,128)} %bitcast.183, bf16[2048,256]{1,0:T(8,128)(2,1)} %bitcast.156, bf16[8,128,256]{2,1,0:T(8,128)(2,1)} %pad_maximum_fusion.4.kv0, ...), custom_call_target="tpu_custom_call" | custom-call | tf_op jit(solution)/shard_map/attend/pallas_call | solution.py:766
  233.9 2.1 convolution_convert_fusion.2.inner_ref
  236.0 8.0 %project_out.1 = (f32[256,2048]{1,0:T(8,128)}, bf16[256,2048]{1,0:T(8,128)(2,1)}) custom-call(s32[32]{0:T(128)} %stack.163.order_ref, bf16[2048,256]{1,0:T(8,128)(2,1)} %get-tuple-element.216.mixed_ref.o_ref, bf16[16,256]{1,0:T(8,128)(2,1)} %convolution_convert_fusion.2.inner_ref, bf16[16,2048]{1,0:T(8,128)(2,1)} %get-tuple-element.218.b_ref, ...), custom_call_target="tpu_custom_call" | custom-call | tf_op jit(solution)/shard_map/project_out/pallas_call | solution.py:354
  245.8 10.0 %collective-permute-done.47.refs_6_ = bf16[512,2048]{1,0:T(8,128)(2,1)} collective-permute-done((bf16[512,2048]{1,0:T(8,128)(2,1)}, bf16[512,2048]{1,0:T(8,128)(2,1)}, u32[]{:S(2)}, u32[]{:S(2)}) %collective-permute-start.47) | collective-permute-done | bytes 2097184 | tf_op jit(solution)/shard_map/ppermute | solution.py:82
  256.9 2.3 slice.148
  259.9 2.3 slice.149
  266.2 10.7 %place.2 = (bf16[2048,2048]{1,0:T(8,128)(2,1)}, bf16[2048,2048]{1,0:T(8,128)(2,1)}) custom-call(s32[7]{0:T(128)} %stack.171.sources_ref, bf16[512,2048]{1,0:T(8,128)(2,1)} %pad_maximum_fusion.refs_0_, bf16[512,2048]{1,0:T(8,128)(2,1)} %collective-permute-done.32.refs_1_, bf16[512,2048]{1,0:T(8,128)(2,1)} %collective-permute-done.33.refs_2_, ...), custom_call_target="tpu_custom_call" | custom-call | tf_op jit(solution)/shard_map/place/pallas_call | solution.py:255
  277.0 8.6 %collective-permute-done.48.refs_2_ = bf16[256,2048]{1,0:T(8,128)(2,1)} collective-permute-done((bf16[256,2048]{1,0:T(8,128)(2,1)}, bf16[256,2048]{1,0:T(8,128)(2,1)}, u32[]{:S(2)}, u32[]{:S(2)}) %collective-permute-start.48) | collective-permute-done | bytes 1048608 | tf_op jit(solution)/shard_map/ppermute | solution.py:87
  285.6 3.0 collective-permute-done.49.refs_3_
  288.7 2.9 finish.2
  291.6 15.8 %lower_back.1 = (bf16[1024,2048]{1,0:T(8,128)(2,1)}, bf16[1024,16]{1,0:T(8,128)(2,1)}) custom-call(bf16[256,2048]{1,0:T(8,128)(2,1)} %multiply_convert_fusion.g0, bf16[256,2048]{1,0:T(8,128)(2,1)} %collective-permute-done.50.g1, bf16[256,2048]{1,0:T(8,128)(2,1)} %collective-permute-done.37.g2, bf16[256,2048]{1,0:T(8,128)(2,1)} %collective-permute-done.51.g3, ...), custom_call_target="tpu_custom_call" | custom-call | tf_op jit(solution)/shard_map/lower_back/pallas_call | solution.py:517
  310.8 5.3 all_tokens.1
  316.2 18.1 %units.2 = (bf16[1024,1024]{1,0:T(8,128)(2,1)}, bf16[1024,1024]{1,0:T(8,128)(2,1)}, bf16[1024,1024]{1,0:T(8,128)(2,1)}, f32[1024,48]{1,0:T(8,128)}) custom-call(bf16[1024,2048]{1,0:T(8,128)(2,1)} %get-tuple-element.222.whole_ref, bf16[1024,32]{1,0:T(8,128)(2,1)} %get-tuple-element.223.low_ref, bf16[2048,2048]{1,0:T(8,128)(2,1)} %get-tuple-element.239.gate_ref.up_ref.w_ref, ...), custom_call_target="tpu_custom_call" | custom-call | tf_op jit(solution)/shard_map/units/pallas_call | solution.py:589
  336.4 14.2 %units_back_first.1.first_ref = bf16[1024,2048]{1,0:T(8,128)(2,1)} custom-call(bf16[1024,1024]{1,0:T(8,128)(2,1)} %get-tuple-element.260.g_ref.dg_ref, bf16[1024,1024]{1,0:T(8,128)(2,1)} %get-tuple-element.261.u_ref.du_ref, bf16[2048,2048]{1,0:T(8,128)(2,1)} %get-tuple-element.239.gate_ref.up_ref.w_ref), custom_call_target="tpu_custom_call" | custom-call | tf_op jit(solution)/shard_map/units_back_first/pallas_call | solution.py:639
  350.6 5.4 units_grads.2
  356.0 2.9 collective-permute-done.56.refs_5_
  359.4 2.1 collective-permute-start.59
  361.5 6.2 %place.3.refs_0_ = bf16[2048,2048]{1,0:T(8,128)(2,1)} custom-call(s32[7]{0:T(128)} %stack.171.sources_ref, bf16[256,2048]{1,0:T(8,128)(2,1)} %bitcast.69.refs_0_, bf16[256,2048]{1,0:T(8,128)(2,1)} %collective-permute-done.52.refs_1_, bf16[256,2048]{1,0:T(8,128)(2,1)} %collective-permute-done.53.refs_2_, bf16[256,2048]{1,0:T(8,128)(2,1)} %copy-done.33, ...), custom_call_target="tpu_custom_call" | custom-call | tf_op jit(solution)/shard_map/place/pallas_call | solution.py:255
  369.9 2.2 finish.3.gate_ref.up_ref.w_ref
  372.1 18.0 %units.3 = (bf16[1024,1024]{1,0:T(8,128)(2,1)}, bf16[1024,1024]{1,0:T(8,128)(2,1)}, bf16[1024,1024]{1,0:T(8,128)(2,1)}, f32[1024,48]{1,0:T(8,128)}) custom-call(bf16[1024,2048]{1,0:T(8,128)(2,1)} %get-tuple-element.222.whole_ref, bf16[1024,32]{1,0:T(8,128)(2,1)} %get-tuple-element.223.low_ref, bf16[2048,2048]{1,0:T(8,128)(2,1)} %finish.3.gate_ref.up_ref.w_ref, ...), custom_call_target="tpu_custom_call" | custom-call | tf_op jit(solution)/shard_map/units/pallas_call | solution.py:589
  390.1 9.7 %units_back.2 = (bf16[2,256,1024]{2,1,0:T(8,128)(2,1)}, bf16[2,256,1024]{2,1,0:T(8,128)(2,1)}) custom-call(bf16[1024,2048]{1,0:T(8,128)(2,1)} %units_back_first.1.first_ref, bf16[1024,1024]{1,0:T(8,128)(2,1)} %get-tuple-element.274.g_ref.dg_ref, bf16[1024,1024]{1,0:T(8,128)(2,1)} %get-tuple-element.275.u_ref.du_ref, ...), custom_call_target="tpu_custom_call" | custom-call | tf_op jit(solution)/shard_map/units_back/pallas_call | solution.py:670
  399.8 2.9 collective-permute-done.60.l1
  404.3 9.8 %units_back.3 = (bf16[2,256,1024]{2,1,0:T(8,128)(2,1)}, bf16[2,256,1024]{2,1,0:T(8,128)(2,1)}) custom-call(bf16[1024,2048]{1,0:T(8,128)(2,1)} %units_back_first.1.first_ref, bf16[1024,1024]{1,0:T(8,128)(2,1)} %get-tuple-element.274.g_ref.dg_ref, bf16[1024,1024]{1,0:T(8,128)(2,1)} %get-tuple-element.275.u_ref.du_ref, ...), custom_call_target="tpu_custom_call" | custom-call | tf_op jit(solution)/shard_map/units_back/pallas_call | solution.py:670
  420.2 17.3 %lower.1 = (bf16[2,256,2048]{2,1,0:T(8,128)(2,1)}, bf16[2,256,2048]{2,1,0:T(8,128)(2,1)}, f32[16,2048]{1,0:T(8,128)}, f32[32,2048]{1,0:T(8,128)}) custom-call(bf16[1024,1024]{1,0:T(8,128)(2,1)} %get-tuple-element.262.act_ref.aa_ref, bf16[1024,1024]{1,0:T(8,128)(2,1)} %get-tuple-element.300.ab_ref.act_ref, bf16[2048,2048]{1,0:T(8,128)(2,1)} %get-tuple-element.247.weight_ref, ...), custom_call_target="tpu_custom_call" | custom-call | tf_op jit(solution)/shard_map/lower/pallas_call | solution.py:715
  437.6 2.2 collective-permute-done.63.r2
  440.5 6.5 %hidden_back.1 = (f32[256,2048]{1,0:T(8,128)}, bf16[256,2048]{1,0:T(8,128)(2,1)}, bf16[256,16]{1,0:T(8,128)(2,1)}) custom-call(bf16[2,256,1024]{2,1,0:T(8,128)(2,1)} %get-tuple-element.286.l0, bf16[2,256,1024]{2,1,0:T(8,128)(2,1)} %copy-done.46, bf16[256,1024]{1,0:T(8,128)(2,1)} %copy-done.57, bf16[2,256,1024]{2,1,0:T(8,128)(2,1)} %get-tuple-element.288.r0, ...), custom_call_target="tpu_custom_call" | custom-call | flops 7000000000 | tf_op jit(solution)/shard_map/hidden_back/pallas_call | solution.py:488
  447.1 4.4 collective-permute-done.64
  454.7 6.7 %project_out_back.1.do_ref = bf16[2048,256]{1,0:T(8,128)(2,1)} custom-call(s32[32]{0:T(128)} %stack.163.order_ref, bf16[256,2048]{1,0:T(8,128)(2,1)} %get-tuple-element.295.grad_ref, bf16[16,2048]{1,0:T(8,128)(2,1)} %get-tuple-element.217.a_ref, bf16[256,16]{1,0:T(8,128)(2,1)} %get-tuple-element.296.inner_ref, bf16[64,5120]{1,0:T(8,128)(2,1)} %copy-done.6, ...), custom_call_target="tpu_custom_call" | custom-call | tf_op jit(solution)/shard_map/project_out_back/pallas_call | solution.py:406
  461.4 12.2 %attend_back.2 = (f32[1024,256]{1,0:T(8,128)}, bf16[2,4,128,256]{3,2,1,0:T(8,128)(2,1)}, bf16[2,4,128,256]{3,2,1,0:T(8,128)(2,1)}) custom-call(bf16[2048,256]{1,0:T(8,128)(2,1)} %bitcast.157, bf16[8,128,256]{2,1,0:T(8,128)(2,1)} %pad_maximum_fusion.4.kv0, bf16[8,128,256]{2,1,0:T(8,128)(2,1)} %collective-permute-done.38.kv1, ...), custom_call_target="tpu_custom_call" | custom-call | tf_op jit(solution)/shard_map/attend_back/pallas_call | solution.py:810
  473.7 5.6 %units_grads.3 = (f32[16,1024]{1,0:T(8,128)}, f32[16,1024]{1,0:T(8,128)}, f32[16,1024]{1,0:T(8,128)}) custom-call(bf16[1024,32]{1,0:T(8,128)(2,1)} %get-tuple-element.223.low_ref, bf16[1024,16]{1,0:T(8,128)(2,1)} %get-tuple-element.258.d_down_ref, bf16[1024,1024]{1,0:T(8,128)(2,1)} %get-tuple-element.300.ab_ref.act_ref, ...), custom_call_target="tpu_custom_call" | custom-call | tf_op jit(solution)/shard_map/units_grads/pallas_call | solution.py:619
  483.1 12.1 %attend_back.3 = (f32[1024,256]{1,0:T(8,128)}, bf16[2,4,128,256]{3,2,1,0:T(8,128)(2,1)}, bf16[2,4,128,256]{3,2,1,0:T(8,128)(2,1)}) custom-call(bf16[2048,256]{1,0:T(8,128)(2,1)} %bitcast.158, bf16[8,128,256]{2,1,0:T(8,128)(2,1)} %pad_maximum_fusion.4.kv0, bf16[8,128,256]{2,1,0:T(8,128)(2,1)} %collective-permute-done.38.kv1, ...), custom_call_target="tpu_custom_call" | custom-call | tf_op jit(solution)/shard_map/attend_back/pallas_call | solution.py:810
  500.3 6.7 %collective-permute-done.69 = bf16[4,128,256]{2,1,0:T(8,128)(2,1)S(1)} collective-permute-done((bf16[4,128,256]{2,1,0:T(8,128)(2,1)S(1)}, bf16[4,128,256]{2,1,0:T(8,128)(2,1)S(1)}, u32[]{:S(2)}, u32[]{:S(2)}) %collective-permute-start.69) | collective-permute-done | bytes 262176 | tf_op jit(solution)/shard_map/ppermute | solution.py:147
  511.8 2.6 pack.1
  518.5 11.3 %project_in_back.1 = bf16[256,2048]{1,0:T(8,128)(2,1)} custom-call(s32[32]{0:T(128)} %stack.163.order_ref, bf16[3072,256]{1,0:T(8,128)(2,1)} %copy-done.2, bf16[48,2048]{1,0:T(8,128)(2,1)} %get-tuple-element.212.a_ref, bf16[48,256]{1,0:T(8,128)(2,1)} %copy-done.52, bf16[256,2048]{1,0:T(8,128)(2,1)} %bitcast.160, f32[1,2048]{1,0:T(1,128)} %bitcast.173, ...), custom_call_target="tpu_custom_call" | custom-call | tf_op jit(solution)/shard_map/project_in_back/pallas_call | solution.py:450
  530.8 5.4 all-to-all-start.4
  536.2 3.5 fusion.9
  539.7 7.5 %all-to-all-done.4.came_ref = bf16[8,16,1376]{2,1,0:T(8,128)(2,1)S(1)} async-done(((bf16[8,16,1376]{2,1,0:T(8,128)(2,1)}), bf16[8,16,1376]{2,1,0:T(8,128)(2,1)S(1)}, u32[]{:S(2)}, u32[]{:S(2)}) %all-to-all-start.4) | async-done | bytes 352288 | tf_op jit(solution)/shard_map/all_to_all | solution.py:1186
  547.9 2.4 sort.1
  (315 shorter events, 110.4 us)
Async XLA Ops:
  4.3 23.8 %collective-permute-start = (bf16[64,5120]{1,0:T(8,128)(2,1)S(1)}, bf16[64,5120]{1,0:T(8,128)(2,1)S(1)}, u32[]{:S(2)}, u32[]{:S(2)}) collective-permute-start(bf16[64,5120]{1,0:T(8,128)(2,1)S(1)} %constant_dynamic-update-slice_fusion.refs_0_), channel_id=1, source_target_pairs={{0,8},{8,16},{16,24},{24,28},{28,20},{20,12},{12,4},{4,0},{1,9},{9... | collective-permute-start | bytes 1966088 | tf_op jit(solution)/shard_map/ppermute | solution.py:81
  7.4 20.8 %collective-permute-start.1 = (bf16[64,5120]{1,0:T(8,128)(2,1)S(1)}, bf16[64,5120]{1,0:T(8,128)(2,1)S(1)}, u32[]{:S(2)}, u32[]{:S(2)}) collective-permute-start(bf16[64,5120]{1,0:T(8,128)(2,1)S(1)} %constant_dynamic-update-slice_fusion.refs_0_), channel_id=1, source_target_pairs={{8,0},{16,8},{24,16},{28,24},{20,28},{12,20},{4,12},{0,4},{9,1},{1... | collective-permute-start | bytes 1966088 | tf_op jit(solution)/shard_map/ppermute | solution.py:82
  7.4 20.8 %collective-permute-start.2 = (bf16[64,5120]{1,0:T(8,128)(2,1)S(1)}, bf16[64,5120]{1,0:T(8,128)(2,1)S(1)}, u32[]{:S(2)}, u32[]{:S(2)}) collective-permute-start(bf16[64,5120]{1,0:T(8,128)(2,1)S(1)} %constant_dynamic-update-slice_fusion.refs_0_), channel_id=1, source_target_pairs={{0,1},{1,0},{2,3},{3,2},{4,5},{5,4},{6,7},{7,6},{8,9},{9,8},{10,11... | collective-permute-start | bytes 1966088 | tf_op jit(solution)/shard_map/ppermute | solution.py:147
  7.4 20.8 %collective-permute-start.3 = (bf16[64,5120]{1,0:T(8,128)(2,1)S(1)}, bf16[64,5120]{1,0:T(8,128)(2,1)S(1)}, u32[]{:S(2)}, u32[]{:S(2)}) collective-permute-start(bf16[64,5120]{1,0:T(8,128)(2,1)S(1)} %constant_dynamic-update-slice_fusion.refs_0_), channel_id=1, source_target_pairs={{0,2},{1,3},{2,0},{3,1},{4,6},{5,7},{6,4},{7,5},{8,10},{9,11},{10,... | collective-permute-start | bytes 1966088 | tf_op jit(solution)/shard_map/ppermute | solution.py:147
  10.6 15.1 %all-to-all-start = ((s32[8,1,128]{2,1,0:T(1,128)}), s32[8,1,128]{2,1,0:T(1,128)S(1)}, u32[]{:S(2)}, u32[]{:S(2)}) async-start(s32[8,1,128]{2,1,0:T(1,128)} %broadcast_in_dim.22), calls=%async_computation | async-start | bytes 8192 | tf_op jit(solution)/shard_map/all_to_all | solution.py:1035
  28.2 15.0 %collective-permute-start.5 = (bf16[64,5120]{1,0:T(8,128)(2,1)S(1)}, bf16[64,5120]{1,0:T(8,128)(2,1)S(1)}, u32[]{:S(2)}, u32[]{:S(2)}) collective-permute-start(bf16[64,5120]{1,0:T(8,128)(2,1)S(1)} %collective-permute-done.1.refs_8_), channel_id=1, source_target_pairs={{8,0},{16,8},{24,16},{28,24},{20,28},{12,20},{4,12},{0,4},{9,1},{1... | collective-permute-start | bytes 1966088 | tf_op jit(solution)/shard_map/ppermute | solution.py:82
  29.7 13.5 %collective-permute-start.8 = (bf16[64,5120]{1,0:T(8,128)(2,1)S(1)}, bf16[64,5120]{1,0:T(8,128)(2,1)S(1)}, u32[]{:S(2)}, u32[]{:S(2)}) collective-permute-start(bf16[64,5120]{1,0:T(8,128)(2,1)S(1)} %collective-permute-done.1.refs_8_), channel_id=1, source_target_pairs={{0,1},{1,0},{2,3},{3,2},{4,5},{5,4},{6,7},{7,6},{8,9},{9,8},{10,11... | collective-permute-start | bytes 1966088 | tf_op jit(solution)/shard_map/ppermute | solution.py:147
  29.7 21.0 %collective-permute-start.4 = (bf16[64,5120]{1,0:T(8,128)(2,1)S(1)}, bf16[64,5120]{1,0:T(8,128)(2,1)}, u32[]{:S(2)}, u32[]{:S(2)}) collective-permute-start(bf16[64,5120]{1,0:T(8,128)(2,1)S(1)} %collective-permute-done.refs_4_), channel_id=1, source_target_pairs={{0,8},{8,16},{16,24},{24,28},{28,20},{20,12},{12,4},{4,0},{1,9},{9... | collective-permute-start | bytes 1966088 | tf_op jit(solution)/shard_map/ppermute | solution.py:81
  30.3 20.5 %collective-permute-start.7 = (bf16[64,5120]{1,0:T(8,128)(2,1)S(1)}, bf16[64,5120]{1,0:T(8,128)(2,1)}, u32[]{:S(2)}, u32[]{:S(2)}) collective-permute-start(bf16[64,5120]{1,0:T(8,128)(2,1)S(1)} %collective-permute-done.refs_4_), channel_id=1, source_target_pairs={{0,1},{1,0},{2,3},{3,2},{4,5},{5,4},{6,7},{7,6},{8,9},{9,8},{10,11... | collective-permute-start | bytes 1966088 | tf_op jit(solution)/shard_map/ppermute | solution.py:147
  30.5 20.2 %collective-permute-start.9 = (bf16[64,5120]{1,0:T(8,128)(2,1)S(1)}, bf16[64,5120]{1,0:T(8,128)(2,1)}, u32[]{:S(2)}, u32[]{:S(2)}) collective-permute-start(bf16[64,5120]{1,0:T(8,128)(2,1)S(1)} %collective-permute-done.refs_4_), channel_id=1, source_target_pairs={{0,2},{1,3},{2,0},{3,1},{4,6},{5,7},{6,4},{7,5},{8,10},{9,11},{10,... | collective-permute-start | bytes 1966088 | tf_op jit(solution)/shard_map/ppermute | solution.py:147
  45.0 17.8 %collective-permute-start.16 = (bf16[64,5120]{1,0:T(8,128)(2,1)S(1)}, bf16[64,5120]{1,0:T(8,128)(2,1)}, u32[]{:S(2)}, u32[]{:S(2)}) collective-permute-start(bf16[64,5120]{1,0:T(8,128)(2,1)S(1)} %collective-permute-done.1.refs_8_), channel_id=1, source_target_pairs={{0,2},{1,3},{2,0},{3,1},{4,6},{5,7},{6,4},{7,5},{8,10},{9,11},{10,... | collective-permute-start | bytes 1966088 | tf_op jit(solution)/shard_map/ppermute | solution.py:147
  46.5 26.3 %all-to-all-start.1 = ((bf16[4,64,2048]{2,1,0:T(8,128)(2,1)}), bf16[4,64,2048]{2,1,0:T(8,128)(2,1)}, u32[]{:S(2)}, u32[]{:S(2)}) async-start(bf16[4,64,2048]{2,1,0:T(8,128)(2,1)} %get-tuple-element.185), calls=%async_computation.1 | async-start | bytes 2097152 | tf_op jit(solution)/shard_map/all_to_all | solution.py:1043
  50.8 29.4 %collective-permute-start.11 = (bf16[64,5120]{1,0:T(8,128)(2,1)}, bf16[64,5120]{1,0:T(8,128)(2,1)S(1)}, u32[]{:S(2)}, u32[]{:S(2)}) collective-permute-start(bf16[64,5120]{1,0:T(8,128)(2,1)} %collective-permute-done.4.refs_12_), channel_id=1, source_target_pairs={{0,8},{8,16},{16,24},{24,28},{28,20},{20,12},{12,4},{4,0},{1,9},{9... | collective-permute-start | bytes 1966088 | tf_op jit(solution)/shard_map/ppermute | solution.py:81
  51.4 28.8 %collective-permute-start.14 = (bf16[64,5120]{1,0:T(8,128)(2,1)}, bf16[64,5120]{1,0:T(8,128)(2,1)}, u32[]{:S(2)}, u32[]{:S(2)}) collective-permute-start(bf16[64,5120]{1,0:T(8,128)(2,1)} %collective-permute-done.4.refs_12_), channel_id=1, source_target_pairs={{0,1},{1,0},{2,3},{3,2},{4,5},{5,4},{6,7},{7,6},{8,9},{9,8},{10,11... | collective-permute-start | bytes 1966088 | tf_op jit(solution)/shard_map/ppermute | solution.py:147
  51.6 28.6 %collective-permute-start.12 = (bf16[64,5120]{1,0:T(8,128)(2,1)}, bf16[64,5120]{1,0:T(8,128)(2,1)S(1)}, u32[]{:S(2)}, u32[]{:S(2)}) collective-permute-start(bf16[64,5120]{1,0:T(8,128)(2,1)} %copy-done.11), channel_id=1, source_target_pairs={{8,0},{16,8},{24,16},{28,24},{20,28},{12,20},{4,12},{0,4},{9,1},{1... | collective-permute-start | bytes 1966088 | tf_op jit(solution)/shard_map/ppermute | solution.py:82
  53.0 27.2 %collective-permute-start.15 = (bf16[64,5120]{1,0:T(8,128)(2,1)}, bf16[64,5120]{1,0:T(8,128)(2,1)}, u32[]{:S(2)}, u32[]{:S(2)}) collective-permute-start(bf16[64,5120]{1,0:T(8,128)(2,1)} %copy-done.11), channel_id=1, source_target_pairs={{0,1},{1,0},{2,3},{3,2},{4,5},{5,4},{6,7},{7,6},{8,9},{9,8},{10,11... | collective-permute-start | bytes 1966088 | tf_op jit(solution)/shard_map/ppermute | solution.py:147
  62.7 17.5 %collective-permute-start.13 = (bf16[64,5120]{1,0:T(8,128)(2,1)}, bf16[64,5120]{1,0:T(8,128)(2,1)}, u32[]{:S(2)}, u32[]{:S(2)}) collective-permute-start(bf16[64,5120]{1,0:T(8,128)(2,1)} %collective-permute-done.9.refs_6_), channel_id=1, source_target_pairs={{0,1},{1,0},{2,3},{3,2},{4,5},{5,4},{6,7},{7,6},{8,9},{9,8},{10,11... | collective-permute-start | bytes 1966088 | tf_op jit(solution)/shard_map/ppermute | solution.py:147
  72.8 15.6 %all-to-all-start.2 = ((bf16[8,16,1376]{2,1,0:T(8,128)(2,1)}), bf16[8,16,1376]{2,1,0:T(8,128)(2,1)}, u32[]{:S(2)}, u32[]{:S(2)}) async-start(bf16[8,16,1376]{2,1,0:T(8,128)(2,1)} %pick.1), calls=%async_computation.2 | async-start | bytes 720896 | tf_op jit(solution)/shard_map/all_to_all | solution.py:1045
  80.3 10.5 %collective-permute-start.17 = (bf16[32,5120]{1,0:T(8,128)(2,1)S(1)}, bf16[32,5120]{1,0:T(8,128)(2,1)S(1)}, u32[]{:S(2)}, u32[]{:S(2)}) collective-permute-start(bf16[32,5120]{1,0:T(8,128)(2,1)S(1)} %slice.138), channel_id=1, source_target_pairs={{0,8},{8,16},{16,24},{24,28},{28,20},{20,12},{12,4},{4,0},{1,9},{9... | collective-permute-start | bytes 983048 | tf_op jit(solution)/shard_map/ppermute | solution.py:87
  82.2 17.9 %collective-permute-start.10 = (bf16[64,5120]{1,0:T(8,128)(2,1)}, bf16[64,5120]{1,0:T(8,128)(2,1)S(1)}, u32[]{:S(2)}, u32[]{:S(2)}) collective-permute-start(bf16[64,5120]{1,0:T(8,128)(2,1)} %collective-permute-done.4.refs_12_), channel_id=1, source_target_pairs={{0,2},{1,3},{2,0},{3,1},{4,6},{5,7},{6,4},{7,5},{8,10},{9,11},{10,... | collective-permute-start | bytes 1966088 | tf_op jit(solution)/shard_map/ppermute | solution.py:147
  83.7 27.9 %collective-permute-start.25 = (bf16[64,5120]{1,0:T(8,128)(2,1)S(1)}, bf16[64,5120]{1,0:T(8,128)(2,1)}, u32[]{:S(2)}, u32[]{:S(2)}) collective-permute-start(bf16[64,5120]{1,0:T(8,128)(2,1)S(1)} %copy-done.12), channel_id=1, source_target_pairs={{0,2},{1,3},{2,0},{3,1},{4,6},{5,7},{6,4},{7,5},{8,10},{9,11},{10,... | collective-permute-start | bytes 1966088 | tf_op jit(solution)/shard_map/ppermute | solution.py:147
  85.0 8.7 %collective-permute-start.18 = (bf16[32,5120]{1,0:T(8,128)(2,1)}, bf16[32,5120]{1,0:T(8,128)(2,1)}, u32[]{:S(2)}, u32[]{:S(2)}) collective-permute-start(bf16[32,5120]{1,0:T(8,128)(2,1)} %slice.139), channel_id=1, source_target_pairs={{8,0},{16,8},{24,16},{28,24},{20,28},{12,20},{4,12},{0,4},{9,1},{1... | collective-permute-start | bytes 983048 | tf_op jit(solution)/shard_map/ppermute | solution.py:88
  85.1 15.0 %collective-permute-start.21 = (bf16[64,5120]{1,0:T(8,128)(2,1)S(1)}, bf16[64,5120]{1,0:T(8,128)(2,1)}, u32[]{:S(2)}, u32[]{:S(2)}) collective-permute-start(bf16[64,5120]{1,0:T(8,128)(2,1)S(1)} %collective-permute-done.11.refs_20_), channel_id=1, source_target_pairs={{0,1},{1,0},{2,3},{3,2},{4,5},{5,4},{6,7},{7,6},{8,9},{9,8},{10,11... | collective-permute-start | bytes 1966088 | tf_op jit(solution)/shard_map/ppermute | solution.py:147
  91.5 8.6 %collective-permute-start.19 = (bf16[64,5120]{1,0:T(8,128)(2,1)}, bf16[64,5120]{1,0:T(8,128)(2,1)S(1)}, u32[]{:S(2)}, u32[]{:S(2)}) collective-permute-start(bf16[64,5120]{1,0:T(8,128)(2,1)} %collective-permute-done.16.refs_10_), channel_id=1, source_target_pairs={{0,1},{1,0},{2,3},{3,2},{4,5},{5,4},{6,7},{7,6},{8,9},{9,8},{10,11... | collective-permute-start | bytes 1966088 | tf_op jit(solution)/shard_map/ppermute | solution.py:147
  100.1 11.9 %collective-permute-start.24 = (bf16[64,5120]{1,0:T(8,128)(2,1)S(1)}, bf16[64,5120]{1,0:T(8,128)(2,1)}, u32[]{:S(2)}, u32[]{:S(2)}) collective-permute-start(bf16[64,5120]{1,0:T(8,128)(2,1)S(1)} %constant_dynamic-update-slice_fusion.4.refs_28_), channel_id=1, source_target_pairs={{0,1},{1,0},{2,3},{3,2},{4,5},{5,4},{6,7},{7,6},{8,9},{9,8},{10,11... | collective-permute-start | bytes 1966088 | tf_op jit(solution)/shard_map/ppermute | solution.py:147
  101.0 12.5 %collective-permute-start.23 = (bf16[64,5120]{1,0:T(8,128)(2,1)S(1)}, bf16[64,5120]{1,0:T(8,128)(2,1)}, u32[]{:S(2)}, u32[]{:S(2)}) collective-permute-start(bf16[64,5120]{1,0:T(8,128)(2,1)S(1)} %collective-permute-done.12.refs_24_), channel_id=1, source_target_pairs={{0,1},{1,0},{2,3},{3,2},{4,5},{5,4},{6,7},{7,6},{8,9},{9,8},{10,11... | collective-permute-start | bytes 1966088 | tf_op jit(solution)/shard_map/ppermute | solution.py:147
  101.0 12.5 %collective-permute-start.22 = (bf16[64,5120]{1,0:T(8,128)(2,1)S(1)}, bf16[64,5120]{1,0:T(8,128)(2,1)}, u32[]{:S(2)}, u32[]{:S(2)}) collective-permute-start(bf16[64,5120]{1,0:T(8,128)(2,1)S(1)} %collective-permute-done.10.refs_14_), channel_id=1, source_target_pairs={{0,1},{1,0},{2,3},{3,2},{4,5},{5,4},{6,7},{7,6},{8,9},{9,8},{10,11... | collective-permute-start | bytes 1966088 | tf_op jit(solution)/shard_map/ppermute | solution.py:147
  105.0 47.9 %collective-permute-start.32 = (bf16[512,2048]{1,0:T(8,128)(2,1)}, bf16[512,2048]{1,0:T(8,128)(2,1)}, u32[]{:S(2)}, u32[]{:S(2)}) collective-permute-start(bf16[512,2048]{1,0:T(8,128)(2,1)} %pad_maximum_fusion.refs_0_), channel_id=1, source_target_pairs={{0,8},{8,16},{16,24},{24,28},{28,20},{20,12},{12,4},{4,0},{1,9},{9... | collective-permute-start | bytes 6291464 | tf_op jit(solution)/shard_map/ppermute | solution.py:81
  111.6 45.3 %collective-permute-start.33 = (bf16[512,2048]{1,0:T(8,128)(2,1)}, bf16[512,2048]{1,0:T(8,128)(2,1)}, u32[]{:S(2)}, u32[]{:S(2)}) collective-permute-start(bf16[512,2048]{1,0:T(8,128)(2,1)} %pad_maximum_fusion.refs_0_), channel_id=1, source_target_pairs={{8,0},{16,8},{24,16},{28,24},{20,28},{12,20},{4,12},{0,4},{9,1},{1... | collective-permute-start | bytes 6291464 | tf_op jit(solution)/shard_map/ppermute | solution.py:82
  112.0 10.1 %collective-permute-start.26 = (bf16[8,16,608]{2,1,0:T(8,128)(2,1)S(1)}, bf16[8,16,608]{2,1,0:T(8,128)(2,1)}, u32[]{:S(2)}, u32[]{:S(2)}) collective-permute-start(bf16[8,16,608]{2,1,0:T(8,128)(2,1)S(1)} %slice.140), channel_id=1, source_target_pairs={{0,2},{1,3},{2,0},{3,1},{4,6},{5,7},{6,4},{7,5},{8,10},{9,11},{10,... | collective-permute-start | bytes 466952 | tf_op jit(solution)/shard_map/ppermute | solution.py:147
  113.5 19.7 %collective-permute-start.29 = (bf16[64,5120]{1,0:T(8,128)(2,1)S(1)}, bf16[64,5120]{1,0:T(8,128)(2,1)S(1)}, u32[]{:S(2)}, u32[]{:S(2)}) collective-permute-start(bf16[64,5120]{1,0:T(8,128)(2,1)S(1)} %collective-permute-done.11.refs_20_), channel_id=1, source_target_pairs={{0,2},{1,3},{2,0},{3,1},{4,6},{5,7},{6,4},{7,5},{8,10},{9,11},{10,... | collective-permute-start | bytes 1966088 | tf_op jit(solution)/shard_map/ppermute | solution.py:147
  122.1 11.1 %collective-permute-start.28 = (bf16[8,16,608]{2,1,0:T(8,128)(2,1)}, bf16[8,16,608]{2,1,0:T(8,128)(2,1)S(1)}, u32[]{:S(2)}, u32[]{:S(2)}) collective-permute-start(bf16[8,16,608]{2,1,0:T(8,128)(2,1)} %collective-permute-done.26.p2), channel_id=1, source_target_pairs={{0,1},{1,0},{2,3},{3,2},{4,5},{5,4},{6,7},{7,6},{8,9},{9,8},{10,11... | collective-permute-start | bytes 466952 | tf_op jit(solution)/shard_map/ppermute | solution.py:147
  122.6 34.3 %collective-permute-start.31 = (bf16[64,5120]{1,0:T(8,128)(2,1)S(1)}, bf16[64,5120]{1,0:T(8,128)(2,1)S(1)}, u32[]{:S(2)}, u32[]{:S(2)}) collective-permute-start(bf16[64,5120]{1,0:T(8,128)(2,1)S(1)} %collective-permute-done.12.refs_24_), channel_id=1, source_target_pairs={{0,2},{1,3},{2,0},{3,1},{4,6},{5,7},{6,4},{7,5},{8,10},{9,11},{10,... | collective-permute-start | bytes 1966088 | tf_op jit(solution)/shard_map/ppermute | solution.py:147
  133.2 23.7 %collective-permute-start.34 = (bf16[64,5120]{1,0:T(8,128)(2,1)S(1)}, bf16[64,5120]{1,0:T(8,128)(2,1)S(1)}, u32[]{:S(2)}, u32[]{:S(2)}) collective-permute-start(bf16[64,5120]{1,0:T(8,128)(2,1)S(1)} %collective-permute-done.29.refs_22_), channel_id=1, source_target_pairs={{0,1},{1,0},{2,3},{3,2},{4,5},{5,4},{6,7},{7,6},{8,9},{9,8},{10,11... | collective-permute-start | bytes 1966088 | tf_op jit(solution)/shard_map/ppermute | solution.py:147
  133.3 24.5 %collective-permute-start.30 = (bf16[64,5120]{1,0:T(8,128)(2,1)S(1)}, bf16[64,5120]{1,0:T(8,128)(2,1)}, u32[]{:S(2)}, u32[]{:S(2)}) collective-permute-start(bf16[64,5120]{1,0:T(8,128)(2,1)S(1)} %constant_dynamic-update-slice_fusion.4.refs_28_), channel_id=1, source_target_pairs={{0,2},{1,3},{2,0},{3,1},{4,6},{5,7},{6,4},{7,5},{8,10},{9,11},{10,... | collective-permute-start | bytes 1966088 | tf_op jit(solution)/shard_map/ppermute | solution.py:147
  160.1 48.3 %collective-permute-start.45 = (bf16[512,2048]{1,0:T(8,128)(2,1)}, bf16[512,2048]{1,0:T(8,128)(2,1)}, u32[]{:S(2)}, u32[]{:S(2)}) collective-permute-start(bf16[512,2048]{1,0:T(8,128)(2,1)} %collective-permute-done.33.refs_2_), channel_id=1, source_target_pairs={{8,0},{16,8},{24,16},{28,24},{20,28},{12,20},{4,12},{0,4},{9,1},{1... | collective-permute-start | bytes 6291464 | tf_op jit(solution)/shard_map/ppermute | solution.py:82
  160.8 47.9 %collective-permute-start.44 = (bf16[512,2048]{1,0:T(8,128)(2,1)}, bf16[512,2048]{1,0:T(8,128)(2,1)}, u32[]{:S(2)}, u32[]{:S(2)}) collective-permute-start(bf16[512,2048]{1,0:T(8,128)(2,1)} %collective-permute-done.32.refs_1_), channel_id=1, source_target_pairs={{0,8},{8,16},{16,24},{24,28},{28,20},{20,12},{12,4},{4,0},{1,9},{9... | collective-permute-start | bytes 6291464 | tf_op jit(solution)/shard_map/ppermute | solution.py:81
  162.2 25.2 %collective-permute-start.37 = (bf16[256,2048]{1,0:T(8,128)(2,1)}, bf16[256,2048]{1,0:T(8,128)(2,1)}, u32[]{:S(2)}, u32[]{:S(2)}) collective-permute-start(bf16[256,2048]{1,0:T(8,128)(2,1)} %multiply_convert_fusion.g0), channel_id=1, source_target_pairs={{0,2},{1,3},{2,0},{3,1},{4,6},{5,7},{6,4},{7,5},{8,10},{9,11},{10,... | collective-permute-start | bytes 3145736 | tf_op jit(solution)/shard_map/ppermute | solution.py:147
  187.4 21.4 %collective-permute-start.39 = (bf16[8,128,256]{2,1,0:T(8,128)(2,1)}, bf16[8,128,256]{2,1,0:T(8,128)(2,1)}, u32[]{:S(2)}, u32[]{:S(2)}) collective-permute-start(bf16[8,128,256]{2,1,0:T(8,128)(2,1)} %pad_maximum_fusion.4.kv0), channel_id=1, source_target_pairs={{0,2},{1,3},{2,0},{3,1},{4,6},{5,7},{6,4},{7,5},{8,10},{9,11},{10,... | collective-permute-start | bytes 1572872 | tf_op jit(solution)/shard_map/ppermute | solution.py:147
  208.8 47.1 %collective-permute-start.47 = (bf16[512,2048]{1,0:T(8,128)(2,1)}, bf16[512,2048]{1,0:T(8,128)(2,1)}, u32[]{:S(2)}, u32[]{:S(2)}) collective-permute-start(bf16[512,2048]{1,0:T(8,128)(2,1)} %collective-permute-done.45.refs_4_), channel_id=1, source_target_pairs={{8,0},{16,8},{24,16},{28,24},{20,28},{12,20},{4,12},{0,4},{9,1},{1... | collective-permute-start | bytes 6291464 | tf_op jit(solution)/shard_map/ppermute | solution.py:82
  210.1 46.8 %collective-permute-start.46 = (bf16[512,2048]{1,0:T(8,128)(2,1)}, bf16[512,2048]{1,0:T(8,128)(2,1)}, u32[]{:S(2)}, u32[]{:S(2)}) collective-permute-start(bf16[512,2048]{1,0:T(8,128)(2,1)} %collective-permute-done.44.refs_3_), channel_id=1, source_target_pairs={{0,8},{8,16},{16,24},{24,28},{28,20},{20,12},{12,4},{4,0},{1,9},{9... | collective-permute-start | bytes 6291464 | tf_op jit(solution)/shard_map/ppermute | solution.py:81
  210.8 52.8 %collective-permute-start.50 = (bf16[256,2048]{1,0:T(8,128)(2,1)}, bf16[256,2048]{1,0:T(8,128)(2,1)}, u32[]{:S(2)}, u32[]{:S(2)}) collective-permute-start(bf16[256,2048]{1,0:T(8,128)(2,1)} %multiply_convert_fusion.g0), channel_id=1, source_target_pairs={{0,1},{1,0},{2,3},{3,2},{4,5},{5,4},{6,7},{7,6},{8,9},{9,8},{10,11... | collective-permute-start | bytes 3145736 | tf_op jit(solution)/shard_map/ppermute | solution.py:147
  211.3 53.0 %collective-permute-start.51 = (bf16[256,2048]{1,0:T(8,128)(2,1)}, bf16[256,2048]{1,0:T(8,128)(2,1)}, u32[]{:S(2)}, u32[]{:S(2)}) collective-permute-start(bf16[256,2048]{1,0:T(8,128)(2,1)} %collective-permute-done.37.g2), channel_id=1, source_target_pairs={{0,1},{1,0},{2,3},{3,2},{4,5},{5,4},{6,7},{7,6},{8,9},{9,8},{10,11... | collective-permute-start | bytes 3145736 | tf_op jit(solution)/shard_map/ppermute | solution.py:147
  211.3 52.3 %all-to-all-start.3 = ((bf16[4,64,2048]{2,1,0:T(8,128)(2,1)}), bf16[4,64,2048]{2,1,0:T(8,128)(2,1)}, u32[]{:S(2)}, u32[]{:S(2)}) async-start(bf16[4,64,2048]{2,1,0:T(8,128)(2,1)} %get-tuple-element.252), calls=%async_computation.3 | async-start | bytes 2097152 | tf_op jit(solution)/shard_map/all_to_all | solution.py:1096
  244.0 32.9 %collective-permute-start.42 = (bf16[256,2048]{1,0:T(8,128)(2,1)}, bf16[256,2048]{1,0:T(8,128)(2,1)}, u32[]{:S(2)}, u32[]{:S(2)}) collective-permute-start(bf16[256,2048]{1,0:T(8,128)(2,1)} %get-tuple-element.220.n0), channel_id=1, source_target_pairs={{0,2},{1,3},{2,0},{3,1},{4,6},{5,7},{6,4},{7,5},{8,10},{9,11},{10,... | collective-permute-start | bytes 3145736 | tf_op jit(solution)/shard_map/ppermute | solution.py:147
  259.2 26.4 %collective-permute-start.48 = (bf16[256,2048]{1,0:T(8,128)(2,1)}, bf16[256,2048]{1,0:T(8,128)(2,1)}, u32[]{:S(2)}, u32[]{:S(2)}) collective-permute-start(bf16[256,2048]{1,0:T(8,128)(2,1)} %slice.148), channel_id=1, source_target_pairs={{0,8},{8,16},{16,24},{24,28},{28,20},{20,12},{12,4},{4,0},{1,9},{9... | collective-permute-start | bytes 3145736 | tf_op jit(solution)/shard_map/ppermute | solution.py:87
  262.3 26.4 %collective-permute-start.49 = (bf16[256,2048]{1,0:T(8,128)(2,1)}, bf16[256,2048]{1,0:T(8,128)(2,1)}, u32[]{:S(2)}, u32[]{:S(2)}) collective-permute-start(bf16[256,2048]{1,0:T(8,128)(2,1)} %slice.149), channel_id=1, source_target_pairs={{8,0},{16,8},{24,16},{28,24},{20,28},{12,20},{4,12},{0,4},{9,1},{1... | collective-permute-start | bytes 3145736 | tf_op jit(solution)/shard_map/ppermute | solution.py:88
  263.6 43.8 %collective-permute-start.52 = (bf16[256,2048]{1,0:T(8,128)(2,1)}, bf16[256,2048]{1,0:T(8,128)(2,1)}, u32[]{:S(2)}, u32[]{:S(2)}) collective-permute-start(bf16[256,2048]{1,0:T(8,128)(2,1)} %bitcast.69.refs_0_), channel_id=1, source_target_pairs={{0,8},{8,16},{16,24},{24,28},{28,20},{20,12},{12,4},{4,0},{1,9},{9... | collective-permute-start | bytes 3145736 | tf_op jit(solution)/shard_map/ppermute | solution.py:81
  264.3 43.6 %collective-permute-start.53 = (bf16[256,2048]{1,0:T(8,128)(2,1)}, bf16[256,2048]{1,0:T(8,128)(2,1)}, u32[]{:S(2)}, u32[]{:S(2)}) collective-permute-start(bf16[256,2048]{1,0:T(8,128)(2,1)} %bitcast.69.refs_0_), channel_id=1, source_target_pairs={{8,0},{16,8},{24,16},{28,24},{20,28},{12,20},{4,12},{0,4},{9,1},{1... | collective-permute-start | bytes 3145736 | tf_op jit(solution)/shard_map/ppermute | solution.py:82
  276.9 32.9 %collective-permute-start.41 = (bf16[256,2048]{1,0:T(8,128)(2,1)S(1)}, bf16[256,2048]{1,0:T(8,128)(2,1)S(1)}, u32[]{:S(2)}, u32[]{:S(2)}) collective-permute-start(bf16[256,2048]{1,0:T(8,128)(2,1)S(1)} %copy-done.34), channel_id=1, source_target_pairs={{0,1},{1,0},{2,3},{3,2},{4,5},{5,4},{6,7},{7,6},{8,9},{9,8},{10,11... | collective-permute-start | bytes 3145736 | tf_op jit(solution)/shard_map/ppermute | solution.py:147
  285.6 24.3 %collective-permute-start.43 = (bf16[256,2048]{1,0:T(8,128)(2,1)}, bf16[256,2048]{1,0:T(8,128)(2,1)}, u32[]{:S(2)}, u32[]{:S(2)}) collective-permute-start(bf16[256,2048]{1,0:T(8,128)(2,1)} %collective-permute-done.42.n2), channel_id=1, source_target_pairs={{0,1},{1,0},{2,3},{3,2},{4,5},{5,4},{6,7},{7,6},{8,9},{9,8},{10,11... | collective-permute-start | bytes 3145736 | tf_op jit(solution)/shard_map/ppermute | solution.py:147
  307.9 26.4 %collective-permute-start.55 = (bf16[256,2048]{1,0:T(8,128)(2,1)}, bf16[256,2048]{1,0:T(8,128)(2,1)S(1)}, u32[]{:S(2)}, u32[]{:S(2)}) collective-permute-start(bf16[256,2048]{1,0:T(8,128)(2,1)} %collective-permute-done.53.refs_2_), channel_id=1, source_target_pairs={{8,0},{16,8},{24,16},{28,24},{20,28},{12,20},{4,12},{0,4},{9,1},{1... | collective-permute-start | bytes 3145736 | tf_op jit(solution)/shard_map/ppermute | solution.py:82
  309.2 25.1 %collective-permute-start.54 = (bf16[256,2048]{1,0:T(8,128)(2,1)}, bf16[256,2048]{1,0:T(8,128)(2,1)S(1)}, u32[]{:S(2)}, u32[]{:S(2)}) collective-permute-start(bf16[256,2048]{1,0:T(8,128)(2,1)} %collective-permute-done.52.refs_1_), channel_id=1, source_target_pairs={{0,8},{8,16},{16,24},{24,28},{28,20},{20,12},{12,4},{4,0},{1,9},{9... | collective-permute-start | bytes 3145736 | tf_op jit(solution)/shard_map/ppermute | solution.py:81
  334.3 21.7 %collective-permute-start.57 = (bf16[256,2048]{1,0:T(8,128)(2,1)S(1)}, bf16[256,2048]{1,0:T(8,128)(2,1)S(1)}, u32[]{:S(2)}, u32[]{:S(2)}) collective-permute-start(bf16[256,2048]{1,0:T(8,128)(2,1)S(1)} %collective-permute-done.55.refs_4_), channel_id=1, source_target_pairs={{8,0},{16,8},{24,16},{28,24},{20,28},{12,20},{4,12},{0,4},{9,1},{1... | collective-permute-start | bytes 3145736 | tf_op jit(solution)/shard_map/ppermute | solution.py:82
  335.7 23.2 %collective-permute-start.56 = (bf16[256,2048]{1,0:T(8,128)(2,1)S(1)}, bf16[256,2048]{1,0:T(8,128)(2,1)S(1)}, u32[]{:S(2)}, u32[]{:S(2)}) collective-permute-start(bf16[256,2048]{1,0:T(8,128)(2,1)S(1)} %collective-permute-done.54.refs_3_), channel_id=1, source_target_pairs={{0,8},{8,16},{16,24},{24,28},{28,20},{20,12},{12,4},{4,0},{1,9},{9... | collective-permute-start | bytes 3145736 | tf_op jit(solution)/shard_map/ppermute | solution.py:81
  358.9 9.4 %collective-permute-start.58 = (bf16[128,2048]{1,0:T(8,128)(2,1)S(1)}, bf16[128,2048]{1,0:T(8,128)(2,1)S(1)}, u32[]{:S(2)}, u32[]{:S(2)}) collective-permute-start(bf16[128,2048]{1,0:T(8,128)(2,1)S(1)} %slice.150), channel_id=1, source_target_pairs={{0,8},{8,16},{16,24},{24,28},{28,20},{20,12},{12,4},{4,0},{1,9},{9... | collective-permute-start | bytes 1572872 | tf_op jit(solution)/shard_map/ppermute | solution.py:87
  359.4 9.6 %collective-permute-start.59 = (bf16[128,2048]{1,0:T(8,128)(2,1)S(1)}, bf16[128,2048]{1,0:T(8,128)(2,1)S(1)}, u32[]{:S(2)}, u32[]{:S(2)}) collective-permute-start(bf16[128,2048]{1,0:T(8,128)(2,1)S(1)} %slice.151), channel_id=1, source_target_pairs={{8,0},{16,8},{24,16},{28,24},{20,28},{12,20},{4,12},{0,4},{9,1},{1... | collective-permute-start | bytes 1572872 | tf_op jit(solution)/shard_map/ppermute | solution.py:88
  414.3 23.2 %collective-permute-start.62 = (bf16[256,1024]{1,0:T(8,128)(2,1)S(1)}, bf16[256,1024]{1,0:T(8,128)(2,1)S(1)}, u32[]{:S(2)}, u32[]{:S(2)}) collective-permute-start(bf16[256,1024]{1,0:T(8,128)(2,1)S(1)} %fusion.11), channel_id=1, source_target_pairs={{0,2},{1,3},{2,0},{3,1},{4,6},{5,7},{6,4},{7,5},{8,10},{9,11},{10,... | collective-permute-start | bytes 1572872 | tf_op jit(solution)/shard_map/ppermute | solution.py:147
  418.6 21.1 %collective-permute-start.63 = (bf16[256,1024]{1,0:T(8,128)(2,1)S(1)}, bf16[256,1024]{1,0:T(8,128)(2,1)S(1)}, u32[]{:S(2)}, u32[]{:S(2)}) collective-permute-start(bf16[256,1024]{1,0:T(8,128)(2,1)S(1)} %fusion.12), channel_id=1, source_target_pairs={{0,2},{1,3},{2,0},{3,1},{4,6},{5,7},{6,4},{7,5},{8,10},{9,11},{10,... | collective-permute-start | bytes 1572872 | tf_op jit(solution)/shard_map/ppermute | solution.py:147
  453.2 26.1 %collective-permute-start.65 = (bf16[256,2048]{1,0:T(8,128)(2,1)}, bf16[256,2048]{1,0:T(8,128)(2,1)}, u32[]{:S(2)}, u32[]{:S(2)}) collective-permute-start(bf16[256,2048]{1,0:T(8,128)(2,1)} %fusion.8), channel_id=1, source_target_pairs={{0,2},{1,3},{2,0},{3,1},{4,6},{5,7},{6,4},{7,5},{8,10},{9,11},{10,... | collective-permute-start | bytes 3145736 | tf_op jit(solution)/shard_map/ppermute | solution.py:147
  482.1 14.6 %collective-permute-start.67 = (bf16[4,128,256]{2,1,0:T(8,128)(2,1)S(1)}, bf16[4,128,256]{2,1,0:T(8,128)(2,1)S(1)}, u32[]{:S(2)}, u32[]{:S(2)}) collective-permute-start(bf16[4,128,256]{2,1,0:T(8,128)(2,1)S(1)} %fusion.15), channel_id=1, source_target_pairs={{0,2},{1,3},{2,0},{3,1},{4,6},{5,7},{6,4},{7,5},{8,10},{9,11},{10,... | collective-permute-start | bytes 786440 | tf_op jit(solution)/shard_map/ppermute | solution.py:147
  498.4 8.6 %collective-permute-start.69 = (bf16[4,128,256]{2,1,0:T(8,128)(2,1)S(1)}, bf16[4,128,256]{2,1,0:T(8,128)(2,1)S(1)}, u32[]{:S(2)}, u32[]{:S(2)}) collective-permute-start(bf16[4,128,256]{2,1,0:T(8,128)(2,1)S(1)} %fusion.16), channel_id=1, source_target_pairs={{0,2},{1,3},{2,0},{3,1},{4,6},{5,7},{6,4},{7,5},{8,10},{9,11},{10,... | collective-permute-start | bytes 786440 | tf_op jit(solution)/shard_map/ppermute | solution.py:147
  517.3 12.5 %collective-permute-start.71 = (bf16[8,16,608]{2,1,0:T(8,128)(2,1)S(1)}, bf16[8,16,608]{2,1,0:T(8,128)(2,1)S(1)}, u32[]{:S(2)}, u32[]{:S(2)}) collective-permute-start(bf16[8,16,608]{2,1,0:T(8,128)(2,1)S(1)} %fusion.19), channel_id=1, source_target_pairs={{0,2},{1,3},{2,0},{3,1},{4,6},{5,7},{6,4},{7,5},{8,10},{9,11},{10,... | collective-permute-start | bytes 466952 | tf_op jit(solution)/shard_map/ppermute | solution.py:147
  530.8 16.4 %all-to-all-start.4 = ((bf16[8,16,1376]{2,1,0:T(8,128)(2,1)}), bf16[8,16,1376]{2,1,0:T(8,128)(2,1)S(1)}, u32[]{:S(2)}, u32[]{:S(2)}) async-start(bf16[8,16,1376]{2,1,0:T(8,128)(2,1)} %pad_maximum_fusion.5), calls=%async_computation.4 | async-start | bytes 720896 | tf_op jit(solution)/shard_map/all_to_all | solution.py:1186
  (73 other events, 749.8 us)

commit v6 on v5

--- a/solution.py
+++ b/solution.py
@@ -152,9 +152,9 @@
     return [own, partner(own, 1), across, partner(across, 1)]
 
 
-def seq_shares(keep, give):
+def seq_shares(keep, give, wait=()):
     arrived = partner(give, 1)
-    sent = (keep[1].astype(F32) + arrived[1].astype(F32)).astype(BF16)
+    sent = (after(keep, wait)[1].astype(F32) + arrived[1].astype(F32)).astype(BF16)
     return (keep, arrived, partner(sent, 2)), sent
 
 
@@ -485,10 +485,18 @@
 
 def hidden_back(left, right, hidden, cot, valid, gain, bo):
     block, width = hidden.shape
+    rows = block // 4
+    share = pl.BlockSpec((1, rows, width // 2), lambda i: (0, i, 0))
+    across = pl.BlockSpec((rows, width // 2), lambda i: (i, 0))
+    whole = pl.BlockSpec((rows, width), lambda i: (i, 0))
     return call(
         hidden_back_kernel,
         "hidden_back",
         flops=7e9,
+        grid=(4,),
+        in_specs=[share, share, across] * 2
+        + [whole, whole, pl.BlockSpec((rows, 1), lambda i: (i, 0)), fixed(1, width), fixed(*bo.shape)],
+        out_specs=[whole, whole, pl.BlockSpec((rows, RANK), lambda i: (i, 0))],
         out_shape=[shape((block, width), F32), shape((block, width), BF16), shape((block, RANK), BF16)],
     )(*left, *right, hidden, cot, valid, gain, bo)
 
@@ -1143,8 +1151,7 @@
     )
     d_query, keep, give = back(0, d_mixed)
     gbg_b, gbu_b, gad_b = units_grads(low_n2, d_down, after(act_b, d_query), dg_b, du_b)
-    give, gbg_b = after((give, gbg_b), lowered[2])
-    first_kv, sent = seq_shares(keep, give)
+    first_kv, sent = seq_shares(keep, give, (gbg_b, lowered[2]))
     other_query, keep, give = back(1, after(d_mixed, sent))
     other_kv, sent = seq_shares(keep, give)
 
@@ -1181,7 +1188,7 @@
     keep, give, whole = pack(seq, partial, n_dp, whole)
     (keep, arrived, across), _ = seq_shares(keep, give)
     summed = total((keep, arrived, across)).astype(BF16)
-    summed = after(jnp.concatenate([summed, whole], axis=2), grad_tokens)
+    summed = after(jnp.concatenate([summed, whole], axis=2), output)
     sizes = [each] * 9 + [thin] * 2 + [local] * 3
     came = lax.all_to_all(summed, "dp", 0, 0, tiled=True)
     gao, gbo, gag, gau, gbd, gaq, gak, gav, gbq, gbk, gbv, gbg, gbu, gad = sort(ids, came, sizes)

time: 561 us -> 558 us (level)
  waiting for transfers between devices: 160 us -> 154 us
    all_to_all x1, waiting for transfers between devices: 7.48 us -> 0.01 us  [shards(): came = lax.all_to_all(summed, 'dp', 0, 0, tiled=True)]
    unnamed x128 -> x130, local copies, waits for them, and re-layouts: 15.8 us -> 17.5 us
  transfers between devices with their start and end apart: 77 -> 77, of which waited for: 33 -> 33; matrix products, arithmetic and copies ran while one was open for 9% -> 10% of each run, Pallas kernels for 33% -> 34%
where the time goes in v6:
time: 558 us; the launch traced here: 547 us
  Pallas kernels  235 us (42%)
  waiting for transfers between devices  154 us (28%)
  starting transfers between devices  78.4 us (14%)
  local copies, waits for them, and re-layouts  34.5 us (6%)
  other arithmetic  33.4 us (6%)
  matrix products  8.22 us (1%)
    ppermute x48, waiting for transfers between devices, partner(): return lax.ppermute(operand, 'seq', [(i, i ^ bit) for i in range(size)])  56.3 us
    ppermute x9, waiting for transfers between devices, step(): self.right = lax.ppermute(clock(self.right), 'dp', left)  43.3 us
    pallas_call x2, Pallas kernels, units(): call(units_kernel, 'units', grid=(steps,), in_specs=[fixed(tokens, width)...  36.1 us
    ppermute x48, starting transfers between devices, partner(): return lax.ppermute(operand, 'seq', [(i, i ^ bit) for i in range(size)])  28.7 us
    pallas_call x2, Pallas kernels, attend_back(): call(attend_back_kernel, 'attend_back', grid=(count,), in_specs=[head_row...  24.2 us
    ppermute x9, waiting for transfers between devices, step(): self.left = lax.ppermute(clock(self.left), 'dp', right)  22.4 us
    pallas_call x2, Pallas kernels, units_back(): call(units_back_kernel, 'units_back', grid=(steps,), in_specs=[pl.BlockSp...  19.5 us
    unnamed x130, local copies, waits for them, and re-layouts  17.5 us
  transfers between devices with their start and end apart: 77, of which 33 were waited for; matrix products, arithmetic and copies ran while one was open for 10% of the time, Pallas kernels for 34%

profile of v6, /device:TPU:0, one launch (start us, length us, event | category | flops | bytes accessed | tf_op | source)
XLA Modules:
  0.0 547.2 jit_solution(9204516807728625993)
XLA Ops:
  4.3 3.1 collective-permute-start
  7.4 1.9 collective-permute-start.3
  10.6 5.8 %all-to-all-start = ((s32[8,1,128]{2,1,0:T(1,128)}), s32[8,1,128]{2,1,0:T(1,128)S(1)}, u32[]{:S(2)}, u32[]{:S(2)}) async-start(s32[8,1,128]{2,1,0:T(1,128)} %broadcast_in_dim.22), calls=%async_computation | async-start | bytes 8192 | tf_op jit(solution)/shard_map/all_to_all | solution.py:1043
  19.3 3.0 columns.1
  22.3 3.3 all-to-all-done
  32.1 11.2 %collective-permute-done.5.refs_16_ = bf16[64,5120]{1,0:T(8,128)(2,1)S(1)} collective-permute-done((bf16[64,5120]{1,0:T(8,128)(2,1)S(1)}, bf16[64,5120]{1,0:T(8,128)(2,1)S(1)}, u32[]{:S(2)}, u32[]{:S(2)}) %collective-permute-start.5) | collective-permute-done | bytes 655392 | tf_op jit(solution)/shard_map/ppermute | solution.py:82
  46.5 4.2 all-to-all-start.1
  53.2 9.7 %collective-permute-done.16.refs_10_ = bf16[64,5120]{1,0:T(8,128)(2,1)} collective-permute-done((bf16[64,5120]{1,0:T(8,128)(2,1)S(1)}, bf16[64,5120]{1,0:T(8,128)(2,1)}, u32[]{:S(2)}, u32[]{:S(2)}) %collective-permute-start.16) | collective-permute-done | bytes 655392 | tf_op jit(solution)/shard_map/ppermute | solution.py:147
  62.8 10.1 %all-to-all-done.1 = bf16[4,64,2048]{2,1,0:T(8,128)(2,1)} async-done(((bf16[4,64,2048]{2,1,0:T(8,128)(2,1)}), bf16[4,64,2048]{2,1,0:T(8,128)(2,1)}, u32[]{:S(2)}, u32[]{:S(2)}) %all-to-all-start.1) | async-done | bytes 1048608 | tf_op jit(solution)/shard_map/all_to_all | solution.py:1051
  72.9 4.1 all-to-all-start.2
  77.0 3.2 pad_maximum_fusion.refs_0_
  80.3 1.9 collective-permute-start.17
  85.2 3.3 all-to-all-done.2.mine_ref
  94.8 5.4 collective-permute-done.10.refs_14_
  102.3 2.8 bitcast_convert_fusion
  106.5 5.1 collective-permute-done.25.refs_18_
  114.2 2.3 copy.58
  118.1 2.7 multiply_convert_fusion.g0
  124.2 9.1 %collective-permute-done.29.refs_22_ = bf16[64,5120]{1,0:T(8,128)(2,1)S(1)} collective-permute-done((bf16[64,5120]{1,0:T(8,128)(2,1)S(1)}, bf16[64,5120]{1,0:T(8,128)(2,1)S(1)}, u32[]{:S(2)}, u32[]{:S(2)}) %collective-permute-start.29) | collective-permute-done | bytes 655392 | tf_op jit(solution)/shard_map/ppermute | solution.py:147
  134.9 18.0 %collective-permute-done.32.refs_1_ = bf16[512,2048]{1,0:T(8,128)(2,1)} collective-permute-done((bf16[512,2048]{1,0:T(8,128)(2,1)}, bf16[512,2048]{1,0:T(8,128)(2,1)}, u32[]{:S(2)}, u32[]{:S(2)}) %collective-permute-start.32) | collective-permute-done | bytes 2097184 | tf_op jit(solution)/shard_map/ppermute | solution.py:81
  152.9 4.1 collective-permute-done.33.refs_2_
  163.8 2.3 spread.1
  166.1 2.7 convolution_convert_fusion.inner_ref
  168.8 10.2 %project_in.1 = f32[3072,256]{1,0:T(8,128)} custom-call(s32[32]{0:T(128)} %stack.163.order_ref, bf16[2048,256]{1,0:T(8,128)(2,1)} %fusion.27.normed_ref, bf16[256,48]{1,0:T(8,128)(2,1)} %convolution_convert_fusion.inner_ref, bf16[48,3072]{1,0:T(8,128)(2,1)} %get-tuple-element.212.b_ref, bf16[64,5120]{1,0:T(8,128)(2,1)} %copy-done.6, ...), custom_call_target="tpu_custom_call" | custom-call | tf_op jit(solution)/shard_map/project_in/pallas_call | solution.py:311
  183.7 3.7 collective-permute-done.37.g2
  191.0 17.4 %collective-permute-done.45.refs_4_ = bf16[512,2048]{1,0:T(8,128)(2,1)} collective-permute-done((bf16[512,2048]{1,0:T(8,128)(2,1)}, bf16[512,2048]{1,0:T(8,128)(2,1)}, u32[]{:S(2)}, u32[]{:S(2)}) %collective-permute-start.45) | collective-permute-done | bytes 2097184 | tf_op jit(solution)/shard_map/ppermute | solution.py:82
  211.4 4.4 all-to-all-start.3
  219.1 14.9 %attend.1 = (bf16[2048,256]{1,0:T(8,128)(2,1)}, bf16[8,4,256,1024]{3,2,1,0:T(8,128)(2,1)}, f32[8,1,1024]{2,1,0:T(1,128)}) custom-call(s32[1]{0:T(128)} %bitcast.32.seq_ref, s32[1,1024]{1,0:T(1,128)} %bitcast.181, bf16[2048,256]{1,0:T(8,128)(2,1)} %bitcast.153, bf16[8,128,256]{2,1,0:T(8,128)(2,1)} %pad_maximum_fusion.4.kv0, ...), custom_call_target="tpu_custom_call" | custom-call | tf_op jit(solution)/shard_map/attend/pallas_call | solution.py:774
  234.0 2.1 convolution_convert_fusion.2.inner_ref
  236.1 8.0 %project_out.1 = (f32[256,2048]{1,0:T(8,128)}, bf16[256,2048]{1,0:T(8,128)(2,1)}) custom-call(s32[32]{0:T(128)} %stack.163.order_ref, bf16[2048,256]{1,0:T(8,128)(2,1)} %get-tuple-element.215.mixed_ref.o_ref, bf16[16,256]{1,0:T(8,128)(2,1)} %convolution_convert_fusion.2.inner_ref, bf16[16,2048]{1,0:T(8,128)(2,1)} %get-tuple-element.217.b_ref, ...), custom_call_target="tpu_custom_call" | custom-call | tf_op jit(solution)/shard_map/project_out/pallas_call | solution.py:354
  245.9 10.0 %collective-permute-done.47.refs_6_ = bf16[512,2048]{1,0:T(8,128)(2,1)} collective-permute-done((bf16[512,2048]{1,0:T(8,128)(2,1)}, bf16[512,2048]{1,0:T(8,128)(2,1)}, u32[]{:S(2)}, u32[]{:S(2)}) %collective-permute-start.47) | collective-permute-done | bytes 2097184 | tf_op jit(solution)/shard_map/ppermute | solution.py:82
  257.0 2.3 slice.148
  260.0 2.3 slice.149
  266.3 10.7 %place.2 = (bf16[2048,2048]{1,0:T(8,128)(2,1)}, bf16[2048,2048]{1,0:T(8,128)(2,1)}) custom-call(s32[7]{0:T(128)} %stack.171.sources_ref, bf16[512,2048]{1,0:T(8,128)(2,1)} %pad_maximum_fusion.refs_0_, bf16[512,2048]{1,0:T(8,128)(2,1)} %collective-permute-done.32.refs_1_, bf16[512,2048]{1,0:T(8,128)(2,1)} %collective-permute-done.33.refs_2_, ...), custom_call_target="tpu_custom_call" | custom-call | tf_op jit(solution)/shard_map/place/pallas_call | solution.py:255
  277.1 8.6 %collective-permute-done.48.refs_2_ = bf16[256,2048]{1,0:T(8,128)(2,1)} collective-permute-done((bf16[256,2048]{1,0:T(8,128)(2,1)}, bf16[256,2048]{1,0:T(8,128)(2,1)}, u32[]{:S(2)}, u32[]{:S(2)}) %collective-permute-start.48) | collective-permute-done | bytes 1048608 | tf_op jit(solution)/shard_map/ppermute | solution.py:87
  285.7 3.0 collective-permute-done.49.refs_3_
  288.8 2.9 finish.2
  291.7 15.8 %lower_back.1 = (bf16[1024,2048]{1,0:T(8,128)(2,1)}, bf16[1024,16]{1,0:T(8,128)(2,1)}) custom-call(bf16[256,2048]{1,0:T(8,128)(2,1)} %multiply_convert_fusion.g0, bf16[256,2048]{1,0:T(8,128)(2,1)} %collective-permute-done.50.g1, bf16[256,2048]{1,0:T(8,128)(2,1)} %collective-permute-done.37.g2, bf16[256,2048]{1,0:T(8,128)(2,1)} %collective-permute-done.51.g3, ...), custom_call_target="tpu_custom_call" | custom-call | tf_op jit(solution)/shard_map/lower_back/pallas_call | solution.py:525
  311.0 5.3 all_tokens.1
  316.3 18.1 %units.2 = (bf16[1024,1024]{1,0:T(8,128)(2,1)}, bf16[1024,1024]{1,0:T(8,128)(2,1)}, bf16[1024,1024]{1,0:T(8,128)(2,1)}, f32[1024,48]{1,0:T(8,128)}) custom-call(bf16[1024,2048]{1,0:T(8,128)(2,1)} %get-tuple-element.221.whole_ref, bf16[1024,32]{1,0:T(8,128)(2,1)} %get-tuple-element.222.low_ref, bf16[2048,2048]{1,0:T(8,128)(2,1)} %get-tuple-element.238.gate_ref.up_ref.w_ref, ...), custom_call_target="tpu_custom_call" | custom-call | tf_op jit(solution)/shard_map/units/pallas_call | solution.py:597
  336.6 14.2 %units_back_first.1.first_ref = bf16[1024,2048]{1,0:T(8,128)(2,1)} custom-call(bf16[1024,1024]{1,0:T(8,128)(2,1)} %get-tuple-element.259.g_ref.dg_ref, bf16[1024,1024]{1,0:T(8,128)(2,1)} %get-tuple-element.260.u_ref.du_ref, bf16[2048,2048]{1,0:T(8,128)(2,1)} %get-tuple-element.238.gate_ref.up_ref.w_ref), custom_call_target="tpu_custom_call" | custom-call | tf_op jit(solution)/shard_map/units_back_first/pallas_call | solution.py:647
  350.8 5.4 units_grads.2
  356.2 2.9 collective-permute-done.56.refs_5_
  359.6 1.9 collective-permute-start.59
  361.5 6.1 %place.3.refs_0_ = bf16[2048,2048]{1,0:T(8,128)(2,1)} custom-call(s32[7]{0:T(128)} %stack.171.sources_ref, bf16[256,2048]{1,0:T(8,128)(2,1)} %bitcast.69.refs_0_, bf16[256,2048]{1,0:T(8,128)(2,1)} %collective-permute-done.52.refs_1_, bf16[256,2048]{1,0:T(8,128)(2,1)} %collective-permute-done.53.refs_2_, bf16[256,2048]{1,0:T(8,128)(2,1)} %copy-done.34, ...), custom_call_target="tpu_custom_call" | custom-call | tf_op jit(solution)/shard_map/place/pallas_call | solution.py:255
  370.2 2.2 finish.3.gate_ref.up_ref.w_ref
  372.4 18.0 %units.3 = (bf16[1024,1024]{1,0:T(8,128)(2,1)}, bf16[1024,1024]{1,0:T(8,128)(2,1)}, bf16[1024,1024]{1,0:T(8,128)(2,1)}, f32[1024,48]{1,0:T(8,128)}) custom-call(bf16[1024,2048]{1,0:T(8,128)(2,1)} %get-tuple-element.221.whole_ref, bf16[1024,32]{1,0:T(8,128)(2,1)} %get-tuple-element.222.low_ref, bf16[2048,2048]{1,0:T(8,128)(2,1)} %finish.3.gate_ref.up_ref.w_ref, ...), custom_call_target="tpu_custom_call" | custom-call | tf_op jit(solution)/shard_map/units/pallas_call | solution.py:597
  390.3 9.7 %units_back.2 = (bf16[2,256,1024]{2,1,0:T(8,128)(2,1)}, bf16[2,256,1024]{2,1,0:T(8,128)(2,1)}) custom-call(bf16[1024,2048]{1,0:T(8,128)(2,1)} %units_back_first.1.first_ref, bf16[1024,1024]{1,0:T(8,128)(2,1)} %get-tuple-element.273.g_ref.dg_ref, bf16[1024,1024]{1,0:T(8,128)(2,1)} %get-tuple-element.274.u_ref.du_ref, ...), custom_call_target="tpu_custom_call" | custom-call | tf_op jit(solution)/shard_map/units_back/pallas_call | solution.py:678
  400.0 2.9 collective-permute-done.60.l1
  404.5 9.8 %units_back.3 = (bf16[2,256,1024]{2,1,0:T(8,128)(2,1)}, bf16[2,256,1024]{2,1,0:T(8,128)(2,1)}) custom-call(bf16[1024,2048]{1,0:T(8,128)(2,1)} %units_back_first.1.first_ref, bf16[1024,1024]{1,0:T(8,128)(2,1)} %get-tuple-element.273.g_ref.dg_ref, bf16[1024,1024]{1,0:T(8,128)(2,1)} %get-tuple-element.274.u_ref.du_ref, ...), custom_call_target="tpu_custom_call" | custom-call | tf_op jit(solution)/shard_map/units_back/pallas_call | solution.py:678
  420.4 17.3 %lower.1 = (bf16[2,256,2048]{2,1,0:T(8,128)(2,1)}, bf16[2,256,2048]{2,1,0:T(8,128)(2,1)}, f32[16,2048]{1,0:T(8,128)}, f32[32,2048]{1,0:T(8,128)}) custom-call(bf16[1024,1024]{1,0:T(8,128)(2,1)} %get-tuple-element.261.act_ref.aa_ref, bf16[1024,1024]{1,0:T(8,128)(2,1)} %get-tuple-element.298.ab_ref.act_ref, bf16[2048,2048]{1,0:T(8,128)(2,1)} %get-tuple-element.246.weight_ref, ...), custom_call_target="tpu_custom_call" | custom-call | tf_op jit(solution)/shard_map/lower/pallas_call | solution.py:723
  437.7 2.2 collective-permute-done.63.r2
  440.8 6.1 %hidden_back.1 = (f32[256,2048]{1,0:T(8,128)}, bf16[256,2048]{1,0:T(8,128)(2,1)}, bf16[256,16]{1,0:T(8,128)(2,1)}) custom-call(bf16[2,256,1024]{2,1,0:T(8,128)(2,1)} %get-tuple-element.285.l0, bf16[2,256,1024]{2,1,0:T(8,128)(2,1)} %copy-done.47, bf16[256,1024]{1,0:T(8,128)(2,1)} %copy-done.59, bf16[2,256,1024]{2,1,0:T(8,128)(2,1)} %get-tuple-element.287.r0, ...), custom_call_target="tpu_custom_call" | custom-call | flops 7000000000 | tf_op jit(solution)/shard_map/hidden_back/pallas_call | solution.py:492
  447.0 4.1 collective-permute-done.64
  455.4 6.8 %project_out_back.1.do_ref = bf16[2048,256]{1,0:T(8,128)(2,1)} custom-call(s32[32]{0:T(128)} %stack.163.order_ref, bf16[256,2048]{1,0:T(8,128)(2,1)} %get-tuple-element.294.grad_ref, bf16[16,2048]{1,0:T(8,128)(2,1)} %get-tuple-element.216.a_ref, bf16[256,16]{1,0:T(8,128)(2,1)} %get-tuple-element.295.inner_ref, bf16[64,5120]{1,0:T(8,128)(2,1)} %copy-done.6, ...), custom_call_target="tpu_custom_call" | custom-call | tf_op jit(solution)/shard_map/project_out_back/pallas_call | solution.py:406
  462.3 12.2 %attend_back.2 = (f32[1024,256]{1,0:T(8,128)}, bf16[2,4,128,256]{3,2,1,0:T(8,128)(2,1)}, bf16[2,4,128,256]{3,2,1,0:T(8,128)(2,1)}) custom-call(bf16[2048,256]{1,0:T(8,128)(2,1)} %bitcast.154, bf16[8,128,256]{2,1,0:T(8,128)(2,1)} %pad_maximum_fusion.4.kv0, bf16[8,128,256]{2,1,0:T(8,128)(2,1)} %collective-permute-done.38.kv1, ...), custom_call_target="tpu_custom_call" | custom-call | tf_op jit(solution)/shard_map/attend_back/pallas_call | solution.py:818
  477.2 5.6 %units_grads.3 = (f32[16,1024]{1,0:T(8,128)}, f32[16,1024]{1,0:T(8,128)}, f32[16,1024]{1,0:T(8,128)}) custom-call(bf16[1024,32]{1,0:T(8,128)(2,1)} %get-tuple-element.222.low_ref, bf16[1024,16]{1,0:T(8,128)(2,1)} %get-tuple-element.257.d_down_ref, bf16[1024,1024]{1,0:T(8,128)(2,1)} %get-tuple-element.298.ab_ref.act_ref, ...), custom_call_target="tpu_custom_call" | custom-call | tf_op jit(solution)/shard_map/units_grads/pallas_call | solution.py:627
  484.5 12.0 %attend_back.3 = (f32[1024,256]{1,0:T(8,128)}, bf16[2,4,128,256]{3,2,1,0:T(8,128)(2,1)}, bf16[2,4,128,256]{3,2,1,0:T(8,128)(2,1)}) custom-call(bf16[2048,256]{1,0:T(8,128)(2,1)} %bitcast.155, bf16[8,128,256]{2,1,0:T(8,128)(2,1)} %pad_maximum_fusion.4.kv0, bf16[8,128,256]{2,1,0:T(8,128)(2,1)} %collective-permute-done.38.kv1, ...), custom_call_target="tpu_custom_call" | custom-call | tf_op jit(solution)/shard_map/attend_back/pallas_call | solution.py:818
  503.0 6.4 %collective-permute-done.69 = bf16[4,128,256]{2,1,0:T(8,128)(2,1)S(1)} collective-permute-done((bf16[4,128,256]{2,1,0:T(8,128)(2,1)S(1)}, bf16[4,128,256]{2,1,0:T(8,128)(2,1)S(1)}, u32[]{:S(2)}, u32[]{:S(2)}) %collective-permute-start.69) | collective-permute-done | bytes 262176 | tf_op jit(solution)/shard_map/ppermute | solution.py:147
  514.1 2.8 pack.1
  521.4 2.9 fusion.7
  527.1 5.3 all-to-all-start.4
  532.4 11.2 %project_in_back.1 = bf16[256,2048]{1,0:T(8,128)(2,1)} custom-call(s32[32]{0:T(128)} %stack.163.order_ref, bf16[3072,256]{1,0:T(8,128)(2,1)} %copy-done.2, bf16[48,2048]{1,0:T(8,128)(2,1)} %get-tuple-element.211.a_ref, bf16[48,256]{1,0:T(8,128)(2,1)} %copy-done.53, bf16[256,2048]{1,0:T(8,128)(2,1)} %bitcast.157, f32[1,2048]{1,0:T(1,128)} %bitcast.171, ...), custom_call_target="tpu_custom_call" | custom-call | tf_op jit(solution)/shard_map/project_in_back/pallas_call | solution.py:450
  544.4 2.4 sort.1
  (317 shorter events, 114.0 us)
Async XLA Ops:
  4.3 23.9 %collective-permute-start = (bf16[64,5120]{1,0:T(8,128)(2,1)S(1)}, bf16[64,5120]{1,0:T(8,128)(2,1)S(1)}, u32[]{:S(2)}, u32[]{:S(2)}) collective-permute-start(bf16[64,5120]{1,0:T(8,128)(2,1)S(1)} %constant_dynamic-update-slice_fusion.refs_0_), channel_id=1, source_target_pairs={{0,8},{8,16},{16,24},{24,28},{28,20},{20,12},{12,4},{4,0},{1,9},{9... | collective-permute-start | bytes 1966088 | tf_op jit(solution)/shard_map/ppermute | solution.py:81
  7.4 20.9 %collective-permute-start.1 = (bf16[64,5120]{1,0:T(8,128)(2,1)S(1)}, bf16[64,5120]{1,0:T(8,128)(2,1)S(1)}, u32[]{:S(2)}, u32[]{:S(2)}) collective-permute-start(bf16[64,5120]{1,0:T(8,128)(2,1)S(1)} %constant_dynamic-update-slice_fusion.refs_0_), channel_id=1, source_target_pairs={{8,0},{16,8},{24,16},{28,24},{20,28},{12,20},{4,12},{0,4},{9,1},{1... | collective-permute-start | bytes 1966088 | tf_op jit(solution)/shard_map/ppermute | solution.py:82
  7.4 20.9 %collective-permute-start.2 = (bf16[64,5120]{1,0:T(8,128)(2,1)S(1)}, bf16[64,5120]{1,0:T(8,128)(2,1)S(1)}, u32[]{:S(2)}, u32[]{:S(2)}) collective-permute-start(bf16[64,5120]{1,0:T(8,128)(2,1)S(1)} %constant_dynamic-update-slice_fusion.refs_0_), channel_id=1, source_target_pairs={{0,1},{1,0},{2,3},{3,2},{4,5},{5,4},{6,7},{7,6},{8,9},{9,8},{10,11... | collective-permute-start | bytes 1966088 | tf_op jit(solution)/shard_map/ppermute | solution.py:147
  7.4 20.9 %collective-permute-start.3 = (bf16[64,5120]{1,0:T(8,128)(2,1)S(1)}, bf16[64,5120]{1,0:T(8,128)(2,1)S(1)}, u32[]{:S(2)}, u32[]{:S(2)}) collective-permute-start(bf16[64,5120]{1,0:T(8,128)(2,1)S(1)} %constant_dynamic-update-slice_fusion.refs_0_), channel_id=1, source_target_pairs={{0,2},{1,3},{2,0},{3,1},{4,6},{5,7},{6,4},{7,5},{8,10},{9,11},{10,... | collective-permute-start | bytes 1966088 | tf_op jit(solution)/shard_map/ppermute | solution.py:147
  10.6 15.1 %all-to-all-start = ((s32[8,1,128]{2,1,0:T(1,128)}), s32[8,1,128]{2,1,0:T(1,128)S(1)}, u32[]{:S(2)}, u32[]{:S(2)}) async-start(s32[8,1,128]{2,1,0:T(1,128)} %broadcast_in_dim.22), calls=%async_computation | async-start | bytes 8192 | tf_op jit(solution)/shard_map/all_to_all | solution.py:1043
  28.3 15.0 %collective-permute-start.5 = (bf16[64,5120]{1,0:T(8,128)(2,1)S(1)}, bf16[64,5120]{1,0:T(8,128)(2,1)S(1)}, u32[]{:S(2)}, u32[]{:S(2)}) collective-permute-start(bf16[64,5120]{1,0:T(8,128)(2,1)S(1)} %collective-permute-done.1.refs_8_), channel_id=1, source_target_pairs={{8,0},{16,8},{24,16},{28,24},{20,28},{12,20},{4,12},{0,4},{9,1},{1... | collective-permute-start | bytes 1966088 | tf_op jit(solution)/shard_map/ppermute | solution.py:82
  29.8 13.5 %collective-permute-start.8 = (bf16[64,5120]{1,0:T(8,128)(2,1)S(1)}, bf16[64,5120]{1,0:T(8,128)(2,1)S(1)}, u32[]{:S(2)}, u32[]{:S(2)}) collective-permute-start(bf16[64,5120]{1,0:T(8,128)(2,1)S(1)} %collective-permute-done.1.refs_8_), channel_id=1, source_target_pairs={{0,1},{1,0},{2,3},{3,2},{4,5},{5,4},{6,7},{7,6},{8,9},{9,8},{10,11... | collective-permute-start | bytes 1966088 | tf_op jit(solution)/shard_map/ppermute | solution.py:147
  29.8 21.0 %collective-permute-start.4 = (bf16[64,5120]{1,0:T(8,128)(2,1)S(1)}, bf16[64,5120]{1,0:T(8,128)(2,1)}, u32[]{:S(2)}, u32[]{:S(2)}) collective-permute-start(bf16[64,5120]{1,0:T(8,128)(2,1)S(1)} %collective-permute-done.refs_4_), channel_id=1, source_target_pairs={{0,8},{8,16},{16,24},{24,28},{28,20},{20,12},{12,4},{4,0},{1,9},{9... | collective-permute-start | bytes 1966088 | tf_op jit(solution)/shard_map/ppermute | solution.py:81
  30.4 20.5 %collective-permute-start.7 = (bf16[64,5120]{1,0:T(8,128)(2,1)S(1)}, bf16[64,5120]{1,0:T(8,128)(2,1)}, u32[]{:S(2)}, u32[]{:S(2)}) collective-permute-start(bf16[64,5120]{1,0:T(8,128)(2,1)S(1)} %collective-permute-done.refs_4_), channel_id=1, source_target_pairs={{0,1},{1,0},{2,3},{3,2},{4,5},{5,4},{6,7},{7,6},{8,9},{9,8},{10,11... | collective-permute-start | bytes 1966088 | tf_op jit(solution)/shard_map/ppermute | solution.py:147
  30.6 20.2 %collective-permute-start.9 = (bf16[64,5120]{1,0:T(8,128)(2,1)S(1)}, bf16[64,5120]{1,0:T(8,128)(2,1)}, u32[]{:S(2)}, u32[]{:S(2)}) collective-permute-start(bf16[64,5120]{1,0:T(8,128)(2,1)S(1)} %collective-permute-done.refs_4_), channel_id=1, source_target_pairs={{0,2},{1,3},{2,0},{3,1},{4,6},{5,7},{6,4},{7,5},{8,10},{9,11},{10,... | collective-permute-start | bytes 1966088 | tf_op jit(solution)/shard_map/ppermute | solution.py:147
  45.1 17.8 %collective-permute-start.16 = (bf16[64,5120]{1,0:T(8,128)(2,1)S(1)}, bf16[64,5120]{1,0:T(8,128)(2,1)}, u32[]{:S(2)}, u32[]{:S(2)}) collective-permute-start(bf16[64,5120]{1,0:T(8,128)(2,1)S(1)} %collective-permute-done.1.refs_8_), channel_id=1, source_target_pairs={{0,2},{1,3},{2,0},{3,1},{4,6},{5,7},{6,4},{7,5},{8,10},{9,11},{10,... | collective-permute-start | bytes 1966088 | tf_op jit(solution)/shard_map/ppermute | solution.py:147
  46.5 26.3 %all-to-all-start.1 = ((bf16[4,64,2048]{2,1,0:T(8,128)(2,1)}), bf16[4,64,2048]{2,1,0:T(8,128)(2,1)}, u32[]{:S(2)}, u32[]{:S(2)}) async-start(bf16[4,64,2048]{2,1,0:T(8,128)(2,1)} %get-tuple-element.184), calls=%async_computation.1 | async-start | bytes 2097152 | tf_op jit(solution)/shard_map/all_to_all | solution.py:1051
  50.8 29.4 %collective-permute-start.11 = (bf16[64,5120]{1,0:T(8,128)(2,1)}, bf16[64,5120]{1,0:T(8,128)(2,1)S(1)}, u32[]{:S(2)}, u32[]{:S(2)}) collective-permute-start(bf16[64,5120]{1,0:T(8,128)(2,1)} %collective-permute-done.4.refs_12_), channel_id=1, source_target_pairs={{0,8},{8,16},{16,24},{24,28},{28,20},{20,12},{12,4},{4,0},{1,9},{9... | collective-permute-start | bytes 1966088 | tf_op jit(solution)/shard_map/ppermute | solution.py:81
  51.5 28.8 %collective-permute-start.14 = (bf16[64,5120]{1,0:T(8,128)(2,1)}, bf16[64,5120]{1,0:T(8,128)(2,1)}, u32[]{:S(2)}, u32[]{:S(2)}) collective-permute-start(bf16[64,5120]{1,0:T(8,128)(2,1)} %collective-permute-done.4.refs_12_), channel_id=1, source_target_pairs={{0,1},{1,0},{2,3},{3,2},{4,5},{5,4},{6,7},{7,6},{8,9},{9,8},{10,11... | collective-permute-start | bytes 1966088 | tf_op jit(solution)/shard_map/ppermute | solution.py:147
  51.6 28.6 %collective-permute-start.12 = (bf16[64,5120]{1,0:T(8,128)(2,1)}, bf16[64,5120]{1,0:T(8,128)(2,1)S(1)}, u32[]{:S(2)}, u32[]{:S(2)}) collective-permute-start(bf16[64,5120]{1,0:T(8,128)(2,1)} %copy-done.11), channel_id=1, source_target_pairs={{8,0},{16,8},{24,16},{28,24},{20,28},{12,20},{4,12},{0,4},{9,1},{1... | collective-permute-start | bytes 1966088 | tf_op jit(solution)/shard_map/ppermute | solution.py:82
  53.1 27.2 %collective-permute-start.15 = (bf16[64,5120]{1,0:T(8,128)(2,1)}, bf16[64,5120]{1,0:T(8,128)(2,1)}, u32[]{:S(2)}, u32[]{:S(2)}) collective-permute-start(bf16[64,5120]{1,0:T(8,128)(2,1)} %copy-done.11), channel_id=1, source_target_pairs={{0,1},{1,0},{2,3},{3,2},{4,5},{5,4},{6,7},{7,6},{8,9},{9,8},{10,11... | collective-permute-start | bytes 1966088 | tf_op jit(solution)/shard_map/ppermute | solution.py:147
  62.8 17.5 %collective-permute-start.13 = (bf16[64,5120]{1,0:T(8,128)(2,1)}, bf16[64,5120]{1,0:T(8,128)(2,1)}, u32[]{:S(2)}, u32[]{:S(2)}) collective-permute-start(bf16[64,5120]{1,0:T(8,128)(2,1)} %collective-permute-done.9.refs_6_), channel_id=1, source_target_pairs={{0,1},{1,0},{2,3},{3,2},{4,5},{5,4},{6,7},{7,6},{8,9},{9,8},{10,11... | collective-permute-start | bytes 1966088 | tf_op jit(solution)/shard_map/ppermute | solution.py:147
  72.9 15.6 %all-to-all-start.2 = ((bf16[8,16,1376]{2,1,0:T(8,128)(2,1)}), bf16[8,16,1376]{2,1,0:T(8,128)(2,1)}, u32[]{:S(2)}, u32[]{:S(2)}) async-start(bf16[8,16,1376]{2,1,0:T(8,128)(2,1)} %pick.1), calls=%async_computation.2 | async-start | bytes 720896 | tf_op jit(solution)/shard_map/all_to_all | solution.py:1053
  80.3 10.6 %collective-permute-start.17 = (bf16[32,5120]{1,0:T(8,128)(2,1)S(1)}, bf16[32,5120]{1,0:T(8,128)(2,1)S(1)}, u32[]{:S(2)}, u32[]{:S(2)}) collective-permute-start(bf16[32,5120]{1,0:T(8,128)(2,1)S(1)} %slice.138), channel_id=1, source_target_pairs={{0,8},{8,16},{16,24},{24,28},{28,20},{20,12},{12,4},{4,0},{1,9},{9... | collective-permute-start | bytes 983048 | tf_op jit(solution)/shard_map/ppermute | solution.py:87
  82.3 17.9 %collective-permute-start.10 = (bf16[64,5120]{1,0:T(8,128)(2,1)}, bf16[64,5120]{1,0:T(8,128)(2,1)S(1)}, u32[]{:S(2)}, u32[]{:S(2)}) collective-permute-start(bf16[64,5120]{1,0:T(8,128)(2,1)} %collective-permute-done.4.refs_12_), channel_id=1, source_target_pairs={{0,2},{1,3},{2,0},{3,1},{4,6},{5,7},{6,4},{7,5},{8,10},{9,11},{10,... | collective-permute-start | bytes 1966088 | tf_op jit(solution)/shard_map/ppermute | solution.py:147
  83.8 27.9 %collective-permute-start.25 = (bf16[64,5120]{1,0:T(8,128)(2,1)S(1)}, bf16[64,5120]{1,0:T(8,128)(2,1)}, u32[]{:S(2)}, u32[]{:S(2)}) collective-permute-start(bf16[64,5120]{1,0:T(8,128)(2,1)S(1)} %copy-done.12), channel_id=1, source_target_pairs={{0,2},{1,3},{2,0},{3,1},{4,6},{5,7},{6,4},{7,5},{8,10},{9,11},{10,... | collective-permute-start | bytes 1966088 | tf_op jit(solution)/shard_map/ppermute | solution.py:147
  85.1 8.7 %collective-permute-start.18 = (bf16[32,5120]{1,0:T(8,128)(2,1)}, bf16[32,5120]{1,0:T(8,128)(2,1)}, u32[]{:S(2)}, u32[]{:S(2)}) collective-permute-start(bf16[32,5120]{1,0:T(8,128)(2,1)} %slice.139), channel_id=1, source_target_pairs={{8,0},{16,8},{24,16},{28,24},{20,28},{12,20},{4,12},{0,4},{9,1},{1... | collective-permute-start | bytes 983048 | tf_op jit(solution)/shard_map/ppermute | solution.py:88
  85.2 15.0 %collective-permute-start.21 = (bf16[64,5120]{1,0:T(8,128)(2,1)S(1)}, bf16[64,5120]{1,0:T(8,128)(2,1)}, u32[]{:S(2)}, u32[]{:S(2)}) collective-permute-start(bf16[64,5120]{1,0:T(8,128)(2,1)S(1)} %collective-permute-done.11.refs_20_), channel_id=1, source_target_pairs={{0,1},{1,0},{2,3},{3,2},{4,5},{5,4},{6,7},{7,6},{8,9},{9,8},{10,11... | collective-permute-start | bytes 1966088 | tf_op jit(solution)/shard_map/ppermute | solution.py:147
  91.6 8.6 %collective-permute-start.19 = (bf16[64,5120]{1,0:T(8,128)(2,1)}, bf16[64,5120]{1,0:T(8,128)(2,1)S(1)}, u32[]{:S(2)}, u32[]{:S(2)}) collective-permute-start(bf16[64,5120]{1,0:T(8,128)(2,1)} %collective-permute-done.16.refs_10_), channel_id=1, source_target_pairs={{0,1},{1,0},{2,3},{3,2},{4,5},{5,4},{6,7},{7,6},{8,9},{9,8},{10,11... | collective-permute-start | bytes 1966088 | tf_op jit(solution)/shard_map/ppermute | solution.py:147
  100.2 11.9 %collective-permute-start.24 = (bf16[64,5120]{1,0:T(8,128)(2,1)S(1)}, bf16[64,5120]{1,0:T(8,128)(2,1)}, u32[]{:S(2)}, u32[]{:S(2)}) collective-permute-start(bf16[64,5120]{1,0:T(8,128)(2,1)S(1)} %constant_dynamic-update-slice_fusion.4.refs_28_), channel_id=1, source_target_pairs={{0,1},{1,0},{2,3},{3,2},{4,5},{5,4},{6,7},{7,6},{8,9},{9,8},{10,11... | collective-permute-start | bytes 1966088 | tf_op jit(solution)/shard_map/ppermute | solution.py:147
  101.1 12.5 %collective-permute-start.23 = (bf16[64,5120]{1,0:T(8,128)(2,1)S(1)}, bf16[64,5120]{1,0:T(8,128)(2,1)}, u32[]{:S(2)}, u32[]{:S(2)}) collective-permute-start(bf16[64,5120]{1,0:T(8,128)(2,1)S(1)} %collective-permute-done.12.refs_24_), channel_id=1, source_target_pairs={{0,1},{1,0},{2,3},{3,2},{4,5},{5,4},{6,7},{7,6},{8,9},{9,8},{10,11... | collective-permute-start | bytes 1966088 | tf_op jit(solution)/shard_map/ppermute | solution.py:147
  101.1 12.5 %collective-permute-start.22 = (bf16[64,5120]{1,0:T(8,128)(2,1)S(1)}, bf16[64,5120]{1,0:T(8,128)(2,1)}, u32[]{:S(2)}, u32[]{:S(2)}) collective-permute-start(bf16[64,5120]{1,0:T(8,128)(2,1)S(1)} %collective-permute-done.10.refs_14_), channel_id=1, source_target_pairs={{0,1},{1,0},{2,3},{3,2},{4,5},{5,4},{6,7},{7,6},{8,9},{9,8},{10,11... | collective-permute-start | bytes 1966088 | tf_op jit(solution)/shard_map/ppermute | solution.py:147
  105.1 47.9 %collective-permute-start.32 = (bf16[512,2048]{1,0:T(8,128)(2,1)}, bf16[512,2048]{1,0:T(8,128)(2,1)}, u32[]{:S(2)}, u32[]{:S(2)}) collective-permute-start(bf16[512,2048]{1,0:T(8,128)(2,1)} %pad_maximum_fusion.refs_0_), channel_id=1, source_target_pairs={{0,8},{8,16},{16,24},{24,28},{28,20},{20,12},{12,4},{4,0},{1,9},{9... | collective-permute-start | bytes 6291464 | tf_op jit(solution)/shard_map/ppermute | solution.py:81
  111.7 45.3 %collective-permute-start.33 = (bf16[512,2048]{1,0:T(8,128)(2,1)}, bf16[512,2048]{1,0:T(8,128)(2,1)}, u32[]{:S(2)}, u32[]{:S(2)}) collective-permute-start(bf16[512,2048]{1,0:T(8,128)(2,1)} %pad_maximum_fusion.refs_0_), channel_id=1, source_target_pairs={{8,0},{16,8},{24,16},{28,24},{20,28},{12,20},{4,12},{0,4},{9,1},{1... | collective-permute-start | bytes 6291464 | tf_op jit(solution)/shard_map/ppermute | solution.py:82
  112.1 10.1 %collective-permute-start.26 = (bf16[8,16,608]{2,1,0:T(8,128)(2,1)S(1)}, bf16[8,16,608]{2,1,0:T(8,128)(2,1)}, u32[]{:S(2)}, u32[]{:S(2)}) collective-permute-start(bf16[8,16,608]{2,1,0:T(8,128)(2,1)S(1)} %slice.140), channel_id=1, source_target_pairs={{0,2},{1,3},{2,0},{3,1},{4,6},{5,7},{6,4},{7,5},{8,10},{9,11},{10,... | collective-permute-start | bytes 466952 | tf_op jit(solution)/shard_map/ppermute | solution.py:147
  113.6 19.7 %collective-permute-start.29 = (bf16[64,5120]{1,0:T(8,128)(2,1)S(1)}, bf16[64,5120]{1,0:T(8,128)(2,1)S(1)}, u32[]{:S(2)}, u32[]{:S(2)}) collective-permute-start(bf16[64,5120]{1,0:T(8,128)(2,1)S(1)} %collective-permute-done.11.refs_20_), channel_id=1, source_target_pairs={{0,2},{1,3},{2,0},{3,1},{4,6},{5,7},{6,4},{7,5},{8,10},{9,11},{10,... | collective-permute-start | bytes 1966088 | tf_op jit(solution)/shard_map/ppermute | solution.py:147
  122.2 11.1 %collective-permute-start.28 = (bf16[8,16,608]{2,1,0:T(8,128)(2,1)}, bf16[8,16,608]{2,1,0:T(8,128)(2,1)S(1)}, u32[]{:S(2)}, u32[]{:S(2)}) collective-permute-start(bf16[8,16,608]{2,1,0:T(8,128)(2,1)} %collective-permute-done.26.p2), channel_id=1, source_target_pairs={{0,1},{1,0},{2,3},{3,2},{4,5},{5,4},{6,7},{7,6},{8,9},{9,8},{10,11... | collective-permute-start | bytes 466952 | tf_op jit(solution)/shard_map/ppermute | solution.py:147
  122.7 34.3 %collective-permute-start.31 = (bf16[64,5120]{1,0:T(8,128)(2,1)S(1)}, bf16[64,5120]{1,0:T(8,128)(2,1)S(1)}, u32[]{:S(2)}, u32[]{:S(2)}) collective-permute-start(bf16[64,5120]{1,0:T(8,128)(2,1)S(1)} %collective-permute-done.12.refs_24_), channel_id=1, source_target_pairs={{0,2},{1,3},{2,0},{3,1},{4,6},{5,7},{6,4},{7,5},{8,10},{9,11},{10,... | collective-permute-start | bytes 1966088 | tf_op jit(solution)/shard_map/ppermute | solution.py:147
  133.3 23.7 %collective-permute-start.34 = (bf16[64,5120]{1,0:T(8,128)(2,1)S(1)}, bf16[64,5120]{1,0:T(8,128)(2,1)S(1)}, u32[]{:S(2)}, u32[]{:S(2)}) collective-permute-start(bf16[64,5120]{1,0:T(8,128)(2,1)S(1)} %collective-permute-done.29.refs_22_), channel_id=1, source_target_pairs={{0,1},{1,0},{2,3},{3,2},{4,5},{5,4},{6,7},{7,6},{8,9},{9,8},{10,11... | collective-permute-start | bytes 1966088 | tf_op jit(solution)/shard_map/ppermute | solution.py:147
  133.4 24.5 %collective-permute-start.30 = (bf16[64,5120]{1,0:T(8,128)(2,1)S(1)}, bf16[64,5120]{1,0:T(8,128)(2,1)}, u32[]{:S(2)}, u32[]{:S(2)}) collective-permute-start(bf16[64,5120]{1,0:T(8,128)(2,1)S(1)} %constant_dynamic-update-slice_fusion.4.refs_28_), channel_id=1, source_target_pairs={{0,2},{1,3},{2,0},{3,1},{4,6},{5,7},{6,4},{7,5},{8,10},{9,11},{10,... | collective-permute-start | bytes 1966088 | tf_op jit(solution)/shard_map/ppermute | solution.py:147
  160.2 48.3 %collective-permute-start.45 = (bf16[512,2048]{1,0:T(8,128)(2,1)}, bf16[512,2048]{1,0:T(8,128)(2,1)}, u32[]{:S(2)}, u32[]{:S(2)}) collective-permute-start(bf16[512,2048]{1,0:T(8,128)(2,1)} %collective-permute-done.33.refs_2_), channel_id=1, source_target_pairs={{8,0},{16,8},{24,16},{28,24},{20,28},{12,20},{4,12},{0,4},{9,1},{1... | collective-permute-start | bytes 6291464 | tf_op jit(solution)/shard_map/ppermute | solution.py:82
  160.9 47.9 %collective-permute-start.44 = (bf16[512,2048]{1,0:T(8,128)(2,1)}, bf16[512,2048]{1,0:T(8,128)(2,1)}, u32[]{:S(2)}, u32[]{:S(2)}) collective-permute-start(bf16[512,2048]{1,0:T(8,128)(2,1)} %collective-permute-done.32.refs_1_), channel_id=1, source_target_pairs={{0,8},{8,16},{16,24},{24,28},{28,20},{20,12},{12,4},{4,0},{1,9},{9... | collective-permute-start | bytes 6291464 | tf_op jit(solution)/shard_map/ppermute | solution.py:81
  162.3 25.2 %collective-permute-start.37 = (bf16[256,2048]{1,0:T(8,128)(2,1)}, bf16[256,2048]{1,0:T(8,128)(2,1)}, u32[]{:S(2)}, u32[]{:S(2)}) collective-permute-start(bf16[256,2048]{1,0:T(8,128)(2,1)} %multiply_convert_fusion.g0), channel_id=1, source_target_pairs={{0,2},{1,3},{2,0},{3,1},{4,6},{5,7},{6,4},{7,5},{8,10},{9,11},{10,... | collective-permute-start | bytes 3145736 | tf_op jit(solution)/shard_map/ppermute | solution.py:147
  187.5 21.4 %collective-permute-start.39 = (bf16[8,128,256]{2,1,0:T(8,128)(2,1)}, bf16[8,128,256]{2,1,0:T(8,128)(2,1)}, u32[]{:S(2)}, u32[]{:S(2)}) collective-permute-start(bf16[8,128,256]{2,1,0:T(8,128)(2,1)} %pad_maximum_fusion.4.kv0), channel_id=1, source_target_pairs={{0,2},{1,3},{2,0},{3,1},{4,6},{5,7},{6,4},{7,5},{8,10},{9,11},{10,... | collective-permute-start | bytes 1572872 | tf_op jit(solution)/shard_map/ppermute | solution.py:147
  208.9 47.1 %collective-permute-start.47 = (bf16[512,2048]{1,0:T(8,128)(2,1)}, bf16[512,2048]{1,0:T(8,128)(2,1)}, u32[]{:S(2)}, u32[]{:S(2)}) collective-permute-start(bf16[512,2048]{1,0:T(8,128)(2,1)} %collective-permute-done.45.refs_4_), channel_id=1, source_target_pairs={{8,0},{16,8},{24,16},{28,24},{20,28},{12,20},{4,12},{0,4},{9,1},{1... | collective-permute-start | bytes 6291464 | tf_op jit(solution)/shard_map/ppermute | solution.py:82
  210.2 46.8 %collective-permute-start.46 = (bf16[512,2048]{1,0:T(8,128)(2,1)}, bf16[512,2048]{1,0:T(8,128)(2,1)}, u32[]{:S(2)}, u32[]{:S(2)}) collective-permute-start(bf16[512,2048]{1,0:T(8,128)(2,1)} %collective-permute-done.44.refs_3_), channel_id=1, source_target_pairs={{0,8},{8,16},{16,24},{24,28},{28,20},{20,12},{12,4},{4,0},{1,9},{9... | collective-permute-start | bytes 6291464 | tf_op jit(solution)/shard_map/ppermute | solution.py:81
  210.9 52.8 %collective-permute-start.50 = (bf16[256,2048]{1,0:T(8,128)(2,1)}, bf16[256,2048]{1,0:T(8,128)(2,1)}, u32[]{:S(2)}, u32[]{:S(2)}) collective-permute-start(bf16[256,2048]{1,0:T(8,128)(2,1)} %multiply_convert_fusion.g0), channel_id=1, source_target_pairs={{0,1},{1,0},{2,3},{3,2},{4,5},{5,4},{6,7},{7,6},{8,9},{9,8},{10,11... | collective-permute-start | bytes 3145736 | tf_op jit(solution)/shard_map/ppermute | solution.py:147
  211.4 53.0 %collective-permute-start.51 = (bf16[256,2048]{1,0:T(8,128)(2,1)}, bf16[256,2048]{1,0:T(8,128)(2,1)}, u32[]{:S(2)}, u32[]{:S(2)}) collective-permute-start(bf16[256,2048]{1,0:T(8,128)(2,1)} %collective-permute-done.37.g2), channel_id=1, source_target_pairs={{0,1},{1,0},{2,3},{3,2},{4,5},{5,4},{6,7},{7,6},{8,9},{9,8},{10,11... | collective-permute-start | bytes 3145736 | tf_op jit(solution)/shard_map/ppermute | solution.py:147
  211.4 52.3 %all-to-all-start.3 = ((bf16[4,64,2048]{2,1,0:T(8,128)(2,1)}), bf16[4,64,2048]{2,1,0:T(8,128)(2,1)}, u32[]{:S(2)}, u32[]{:S(2)}) async-start(bf16[4,64,2048]{2,1,0:T(8,128)(2,1)} %get-tuple-element.251), calls=%async_computation.3 | async-start | bytes 2097152 | tf_op jit(solution)/shard_map/all_to_all | solution.py:1104
  244.2 32.9 %collective-permute-start.42 = (bf16[256,2048]{1,0:T(8,128)(2,1)}, bf16[256,2048]{1,0:T(8,128)(2,1)}, u32[]{:S(2)}, u32[]{:S(2)}) collective-permute-start(bf16[256,2048]{1,0:T(8,128)(2,1)} %get-tuple-element.219.n0), channel_id=1, source_target_pairs={{0,2},{1,3},{2,0},{3,1},{4,6},{5,7},{6,4},{7,5},{8,10},{9,11},{10,... | collective-permute-start | bytes 3145736 | tf_op jit(solution)/shard_map/ppermute | solution.py:147
  259.3 26.4 %collective-permute-start.48 = (bf16[256,2048]{1,0:T(8,128)(2,1)}, bf16[256,2048]{1,0:T(8,128)(2,1)}, u32[]{:S(2)}, u32[]{:S(2)}) collective-permute-start(bf16[256,2048]{1,0:T(8,128)(2,1)} %slice.148), channel_id=1, source_target_pairs={{0,8},{8,16},{16,24},{24,28},{28,20},{20,12},{12,4},{4,0},{1,9},{9... | collective-permute-start | bytes 3145736 | tf_op jit(solution)/shard_map/ppermute | solution.py:87
  262.3 26.4 %collective-permute-start.49 = (bf16[256,2048]{1,0:T(8,128)(2,1)}, bf16[256,2048]{1,0:T(8,128)(2,1)}, u32[]{:S(2)}, u32[]{:S(2)}) collective-permute-start(bf16[256,2048]{1,0:T(8,128)(2,1)} %slice.149), channel_id=1, source_target_pairs={{8,0},{16,8},{24,16},{28,24},{20,28},{12,20},{4,12},{0,4},{9,1},{1... | collective-permute-start | bytes 3145736 | tf_op jit(solution)/shard_map/ppermute | solution.py:88
  263.7 43.8 %collective-permute-start.52 = (bf16[256,2048]{1,0:T(8,128)(2,1)}, bf16[256,2048]{1,0:T(8,128)(2,1)}, u32[]{:S(2)}, u32[]{:S(2)}) collective-permute-start(bf16[256,2048]{1,0:T(8,128)(2,1)} %bitcast.69.refs_0_), channel_id=1, source_target_pairs={{0,8},{8,16},{16,24},{24,28},{28,20},{20,12},{12,4},{4,0},{1,9},{9... | collective-permute-start | bytes 3145736 | tf_op jit(solution)/shard_map/ppermute | solution.py:81
  264.4 43.6 %collective-permute-start.53 = (bf16[256,2048]{1,0:T(8,128)(2,1)}, bf16[256,2048]{1,0:T(8,128)(2,1)}, u32[]{:S(2)}, u32[]{:S(2)}) collective-permute-start(bf16[256,2048]{1,0:T(8,128)(2,1)} %bitcast.69.refs_0_), channel_id=1, source_target_pairs={{8,0},{16,8},{24,16},{28,24},{20,28},{12,20},{4,12},{0,4},{9,1},{1... | collective-permute-start | bytes 3145736 | tf_op jit(solution)/shard_map/ppermute | solution.py:82
  277.0 32.9 %collective-permute-start.41 = (bf16[256,2048]{1,0:T(8,128)(2,1)S(1)}, bf16[256,2048]{1,0:T(8,128)(2,1)S(1)}, u32[]{:S(2)}, u32[]{:S(2)}) collective-permute-start(bf16[256,2048]{1,0:T(8,128)(2,1)S(1)} %copy-done.35), channel_id=1, source_target_pairs={{0,1},{1,0},{2,3},{3,2},{4,5},{5,4},{6,7},{7,6},{8,9},{9,8},{10,11... | collective-permute-start | bytes 3145736 | tf_op jit(solution)/shard_map/ppermute | solution.py:147
  285.7 24.3 %collective-permute-start.43 = (bf16[256,2048]{1,0:T(8,128)(2,1)}, bf16[256,2048]{1,0:T(8,128)(2,1)}, u32[]{:S(2)}, u32[]{:S(2)}) collective-permute-start(bf16[256,2048]{1,0:T(8,128)(2,1)} %collective-permute-done.42.n2), channel_id=1, source_target_pairs={{0,1},{1,0},{2,3},{3,2},{4,5},{5,4},{6,7},{7,6},{8,9},{9,8},{10,11... | collective-permute-start | bytes 3145736 | tf_op jit(solution)/shard_map/ppermute | solution.py:147
  307.9 26.5 %collective-permute-start.55 = (bf16[256,2048]{1,0:T(8,128)(2,1)}, bf16[256,2048]{1,0:T(8,128)(2,1)S(1)}, u32[]{:S(2)}, u32[]{:S(2)}) collective-permute-start(bf16[256,2048]{1,0:T(8,128)(2,1)} %collective-permute-done.53.refs_2_), channel_id=1, source_target_pairs={{8,0},{16,8},{24,16},{28,24},{20,28},{12,20},{4,12},{0,4},{9,1},{1... | collective-permute-start | bytes 3145736 | tf_op jit(solution)/shard_map/ppermute | solution.py:82
  309.3 25.2 %collective-permute-start.54 = (bf16[256,2048]{1,0:T(8,128)(2,1)}, bf16[256,2048]{1,0:T(8,128)(2,1)S(1)}, u32[]{:S(2)}, u32[]{:S(2)}) collective-permute-start(bf16[256,2048]{1,0:T(8,128)(2,1)} %collective-permute-done.52.refs_1_), channel_id=1, source_target_pairs={{0,8},{8,16},{16,24},{24,28},{28,20},{20,12},{12,4},{4,0},{1,9},{9... | collective-permute-start | bytes 3145736 | tf_op jit(solution)/shard_map/ppermute | solution.py:81
  334.5 21.7 %collective-permute-start.57 = (bf16[256,2048]{1,0:T(8,128)(2,1)S(1)}, bf16[256,2048]{1,0:T(8,128)(2,1)S(1)}, u32[]{:S(2)}, u32[]{:S(2)}) collective-permute-start(bf16[256,2048]{1,0:T(8,128)(2,1)S(1)} %collective-permute-done.55.refs_4_), channel_id=1, source_target_pairs={{8,0},{16,8},{24,16},{28,24},{20,28},{12,20},{4,12},{0,4},{9,1},{1... | collective-permute-start | bytes 3145736 | tf_op jit(solution)/shard_map/ppermute | solution.py:82
  335.9 23.2 %collective-permute-start.56 = (bf16[256,2048]{1,0:T(8,128)(2,1)S(1)}, bf16[256,2048]{1,0:T(8,128)(2,1)S(1)}, u32[]{:S(2)}, u32[]{:S(2)}) collective-permute-start(bf16[256,2048]{1,0:T(8,128)(2,1)S(1)} %collective-permute-done.54.refs_3_), channel_id=1, source_target_pairs={{0,8},{8,16},{16,24},{24,28},{28,20},{20,12},{12,4},{4,0},{1,9},{9... | collective-permute-start | bytes 3145736 | tf_op jit(solution)/shard_map/ppermute | solution.py:81
  359.2 9.4 %collective-permute-start.58 = (bf16[128,2048]{1,0:T(8,128)(2,1)S(1)}, bf16[128,2048]{1,0:T(8,128)(2,1)S(1)}, u32[]{:S(2)}, u32[]{:S(2)}) collective-permute-start(bf16[128,2048]{1,0:T(8,128)(2,1)S(1)} %slice.150), channel_id=1, source_target_pairs={{0,8},{8,16},{16,24},{24,28},{28,20},{20,12},{12,4},{4,0},{1,9},{9... | collective-permute-start | bytes 1572872 | tf_op jit(solution)/shard_map/ppermute | solution.py:87
  359.6 9.4 %collective-permute-start.59 = (bf16[128,2048]{1,0:T(8,128)(2,1)S(1)}, bf16[128,2048]{1,0:T(8,128)(2,1)S(1)}, u32[]{:S(2)}, u32[]{:S(2)}) collective-permute-start(bf16[128,2048]{1,0:T(8,128)(2,1)S(1)} %slice.151), channel_id=1, source_target_pairs={{8,0},{16,8},{24,16},{28,24},{20,28},{12,20},{4,12},{0,4},{9,1},{1... | collective-permute-start | bytes 1572872 | tf_op jit(solution)/shard_map/ppermute | solution.py:88
  414.5 23.2 %collective-permute-start.62 = (bf16[256,1024]{1,0:T(8,128)(2,1)S(1)}, bf16[256,1024]{1,0:T(8,128)(2,1)S(1)}, u32[]{:S(2)}, u32[]{:S(2)}) collective-permute-start(bf16[256,1024]{1,0:T(8,128)(2,1)S(1)} %fusion.10), channel_id=1, source_target_pairs={{0,2},{1,3},{2,0},{3,1},{4,6},{5,7},{6,4},{7,5},{8,10},{9,11},{10,... | collective-permute-start | bytes 1572872 | tf_op jit(solution)/shard_map/ppermute | solution.py:147
  418.9 21.1 %collective-permute-start.63 = (bf16[256,1024]{1,0:T(8,128)(2,1)S(1)}, bf16[256,1024]{1,0:T(8,128)(2,1)S(1)}, u32[]{:S(2)}, u32[]{:S(2)}) collective-permute-start(bf16[256,1024]{1,0:T(8,128)(2,1)S(1)} %fusion.11), channel_id=1, source_target_pairs={{0,2},{1,3},{2,0},{3,1},{4,6},{5,7},{6,4},{7,5},{8,10},{9,11},{10,... | collective-permute-start | bytes 1572872 | tf_op jit(solution)/shard_map/ppermute | solution.py:147
  453.9 28.9 %collective-permute-start.65 = (bf16[256,2048]{1,0:T(8,128)(2,1)}, bf16[256,2048]{1,0:T(8,128)(2,1)}, u32[]{:S(2)}, u32[]{:S(2)}) collective-permute-start(bf16[256,2048]{1,0:T(8,128)(2,1)} %fusion.8), channel_id=1, source_target_pairs={{0,2},{1,3},{2,0},{3,1},{4,6},{5,7},{6,4},{7,5},{8,10},{9,11},{10,... | collective-permute-start | bytes 3145736 | tf_op jit(solution)/shard_map/ppermute | solution.py:147
  474.5 8.4 %collective-permute-start.66 = (bf16[2,4,128,256]{3,2,1,0:T(8,128)(2,1)}, bf16[2,4,128,256]{3,2,1,0:T(8,128)(2,1)}, u32[]{:S(2)}, u32[]{:S(2)}) collective-permute-start(bf16[2,4,128,256]{3,2,1,0:T(8,128)(2,1)} %get-tuple-element.301), channel_id=1, source_target_pairs={{0,1},{1,0},{2,3},{3,2},{4,5},{5,4},{6,7},{7,6},{8,9},{9,8},{10,11... | collective-permute-start | bytes 1572872 | tf_op jit(solution)/shard_map/ppermute | solution.py:147
  483.9 14.3 %collective-permute-start.67 = (bf16[4,128,256]{2,1,0:T(8,128)(2,1)S(1)}, bf16[4,128,256]{2,1,0:T(8,128)(2,1)S(1)}, u32[]{:S(2)}, u32[]{:S(2)}) collective-permute-start(bf16[4,128,256]{2,1,0:T(8,128)(2,1)S(1)} %fusion.14), channel_id=1, source_target_pairs={{0,2},{1,3},{2,0},{3,1},{4,6},{5,7},{6,4},{7,5},{8,10},{9,11},{10,... | collective-permute-start | bytes 786440 | tf_op jit(solution)/shard_map/ppermute | solution.py:147
  500.8 8.6 %collective-permute-start.69 = (bf16[4,128,256]{2,1,0:T(8,128)(2,1)S(1)}, bf16[4,128,256]{2,1,0:T(8,128)(2,1)S(1)}, u32[]{:S(2)}, u32[]{:S(2)}) collective-permute-start(bf16[4,128,256]{2,1,0:T(8,128)(2,1)S(1)} %fusion.15), channel_id=1, source_target_pairs={{0,2},{1,3},{2,0},{3,1},{4,6},{5,7},{6,4},{7,5},{8,10},{9,11},{10,... | collective-permute-start | bytes 786440 | tf_op jit(solution)/shard_map/ppermute | solution.py:147
  527.1 16.5 %all-to-all-start.4 = ((bf16[8,16,1376]{2,1,0:T(8,128)(2,1)}), bf16[8,16,1376]{2,1,0:T(8,128)(2,1)S(1)}, u32[]{:S(2)}, u32[]{:S(2)}) async-start(bf16[8,16,1376]{2,1,0:T(8,128)(2,1)} %pad_maximum_fusion.5), calls=%async_computation.4 | async-start | bytes 720896 | tf_op jit(solution)/shard_map/all_to_all | solution.py:1193
  (74 other events, 783.4 us)

commit v7 on v6

--- a/solution.py
+++ b/solution.py
@@ -520,7 +520,7 @@
 def lower_back(grads, weight, bd, ad):
     block, width = grads[0].shape
     units = weight.shape[0]
-    step = 256
+    step = 512
     tokens = 4 * block
     return call(
         lower_back_kernel,
@@ -643,7 +643,7 @@
 def units_back_first(d_gate, d_up, both):
     tokens, half = d_gate.shape
     width = both.shape[0]
-    step = 256
+    step = 512
     return call(
         units_back_first_kernel,
         "units_back_first",
@@ -716,7 +716,7 @@
 def lower(act_a, act_b, weight, inners, bd, grads, whole):
     block, width = grads[0].shape
     tokens, half = act_a.shape
-    step = 256
+    step = 512
     tile = pl.BlockSpec((block, step), lambda n: (0, n))
     thin = pl.BlockSpec((RANK, step), lambda n: (0, n))
     out = pl.BlockSpec((2, block, step), lambda n: (0, 0, n))

time: 558 us -> 557 us (level)
  starting transfers between devices: 78.4 us -> 86.2 us
    all_to_all x1, starting transfers between devices: 4.41 us -> 13.7 us  [shards(): swapped_b = lax.all_to_all(after(slots_b, queries), 'seq', 0, 0, tiled=True)]
    ppermute x9, waiting for transfers between devices: 43.3 us -> 36.1 us  [step(): self.right = lax.ppermute(clock(self.right), 'dp', left)]
  transfers between devices with their start and end apart: 77 -> 77, of which waited for: 33 -> 35; matrix products, arithmetic and copies ran while one was open for 10% -> 10% of each run, Pallas kernels for 34% -> 33%
where the time goes in v7:
time: 557 us; the launch traced here: 547 us
  Pallas kernels  233 us (42%)
  waiting for transfers between devices  149 us (27%)
  starting transfers between devices  86.2 us (15%)
  local copies, waits for them, and re-layouts  34.2 us (6%)
  other arithmetic  33.4 us (6%)
  matrix products  8.22 us (1%)
    ppermute x48, waiting for transfers between devices, partner(): return lax.ppermute(operand, 'seq', [(i, i ^ bit) for i in range(size)])  60.9 us
    pallas_call x2, Pallas kernels, units(): call(units_kernel, 'units', grid=(steps,), in_specs=[fixed(tokens, width)...  36.1 us
    ppermute x9, waiting for transfers between devices, step(): self.right = lax.ppermute(clock(self.right), 'dp', left)  36.1 us
    ppermute x48, starting transfers between devices, partner(): return lax.ppermute(operand, 'seq', [(i, i ^ bit) for i in range(size)])  27.1 us
    pallas_call x2, Pallas kernels, attend_back(): call(attend_back_kernel, 'attend_back', grid=(count,), in_specs=[head_row...  24.4 us
    ppermute x9, waiting for transfers between devices, step(): self.left = lax.ppermute(clock(self.left), 'dp', right)  20.9 us
    pallas_call x2, Pallas kernels, units_back(): call(units_back_kernel, 'units_back', grid=(steps,), in_specs=[pl.BlockSp...  19.5 us
    unnamed x130, local copies, waits for them, and re-layouts  17.2 us
  transfers between devices with their start and end apart: 77, of which 35 were waited for; matrix products, arithmetic and copies ran while one was open for 10% of the time, Pallas kernels for 33%

profile of v7, /device:TPU:0, one launch (start us, length us, event | category | flops | bytes accessed | tf_op | source)
XLA Modules:
  0.0 547.2 jit_solution(9090571962268946510)
XLA Ops:
  4.3 3.1 collective-permute-start
  7.4 1.9 collective-permute-start.3
  10.6 5.8 %all-to-all-start = ((s32[8,1,128]{2,1,0:T(1,128)}), s32[8,1,128]{2,1,0:T(1,128)S(1)}, u32[]{:S(2)}, u32[]{:S(2)}) async-start(s32[8,1,128]{2,1,0:T(1,128)} %broadcast_in_dim.22), calls=%async_computation | async-start | bytes 8192 | tf_op jit(solution)/shard_map/all_to_all | solution.py:1043
  19.3 3.0 columns.1
  22.3 3.3 all-to-all-done
  26.3 1.9 pick.1
  32.1 11.2 %collective-permute-done.5.refs_16_ = bf16[64,5120]{1,0:T(8,128)(2,1)S(1)} collective-permute-done((bf16[64,5120]{1,0:T(8,128)(2,1)S(1)}, bf16[64,5120]{1,0:T(8,128)(2,1)S(1)}, u32[]{:S(2)}, u32[]{:S(2)}) %collective-permute-start.5) | collective-permute-done | bytes 655392 | tf_op jit(solution)/shard_map/ppermute | solution.py:82
  46.5 4.2 all-to-all-start.1
  53.2 9.7 %collective-permute-done.16.refs_10_ = bf16[64,5120]{1,0:T(8,128)(2,1)} collective-permute-done((bf16[64,5120]{1,0:T(8,128)(2,1)S(1)}, bf16[64,5120]{1,0:T(8,128)(2,1)}, u32[]{:S(2)}, u32[]{:S(2)}) %collective-permute-start.16) | collective-permute-done | bytes 655392 | tf_op jit(solution)/shard_map/ppermute | solution.py:147
  62.8 10.1 %all-to-all-done.1 = bf16[4,64,2048]{2,1,0:T(8,128)(2,1)} async-done(((bf16[4,64,2048]{2,1,0:T(8,128)(2,1)}), bf16[4,64,2048]{2,1,0:T(8,128)(2,1)}, u32[]{:S(2)}, u32[]{:S(2)}) %all-to-all-start.1) | async-done | bytes 1048608 | tf_op jit(solution)/shard_map/all_to_all | solution.py:1051
  72.9 4.1 all-to-all-start.2
  77.0 3.2 pad_maximum_fusion.refs_0_
  80.3 1.9 collective-permute-start.17
  85.2 3.3 all-to-all-done.2.mine_ref
  94.8 5.4 collective-permute-done.10.refs_14_
  102.3 2.8 bitcast_convert_fusion
  106.5 5.1 collective-permute-done.25.refs_18_
  114.2 2.3 copy.58
  118.1 2.7 multiply_convert_fusion.g0
  124.2 9.1 %collective-permute-done.29.refs_22_ = bf16[64,5120]{1,0:T(8,128)(2,1)S(1)} collective-permute-done((bf16[64,5120]{1,0:T(8,128)(2,1)S(1)}, bf16[64,5120]{1,0:T(8,128)(2,1)S(1)}, u32[]{:S(2)}, u32[]{:S(2)}) %collective-permute-start.29) | collective-permute-done | bytes 655392 | tf_op jit(solution)/shard_map/ppermute | solution.py:147
  134.9 18.0 %collective-permute-done.32.refs_1_ = bf16[512,2048]{1,0:T(8,128)(2,1)} collective-permute-done((bf16[512,2048]{1,0:T(8,128)(2,1)}, bf16[512,2048]{1,0:T(8,128)(2,1)}, u32[]{:S(2)}, u32[]{:S(2)}) %collective-permute-start.32) | collective-permute-done | bytes 2097184 | tf_op jit(solution)/shard_map/ppermute | solution.py:81
  152.9 4.1 collective-permute-done.33.refs_2_
  163.8 2.3 spread.1
  166.1 2.7 convolution_convert_fusion.inner_ref
  168.8 10.2 %project_in.1 = f32[3072,256]{1,0:T(8,128)} custom-call(s32[32]{0:T(128)} %stack.163.order_ref, bf16[2048,256]{1,0:T(8,128)(2,1)} %fusion.27.normed_ref, bf16[256,48]{1,0:T(8,128)(2,1)} %convolution_convert_fusion.inner_ref, bf16[48,3072]{1,0:T(8,128)(2,1)} %get-tuple-element.212.b_ref, bf16[64,5120]{1,0:T(8,128)(2,1)} %copy-done.6, ...), custom_call_target="tpu_custom_call" | custom-call | tf_op jit(solution)/shard_map/project_in/pallas_call | solution.py:311
  183.7 3.7 collective-permute-done.37.g2
  191.0 17.4 %collective-permute-done.45.refs_4_ = bf16[512,2048]{1,0:T(8,128)(2,1)} collective-permute-done((bf16[512,2048]{1,0:T(8,128)(2,1)}, bf16[512,2048]{1,0:T(8,128)(2,1)}, u32[]{:S(2)}, u32[]{:S(2)}) %collective-permute-start.45) | collective-permute-done | bytes 2097184 | tf_op jit(solution)/shard_map/ppermute | solution.py:82
  211.4 13.7 %all-to-all-start.3 = ((bf16[4,64,2048]{2,1,0:T(8,128)(2,1)}), bf16[4,64,2048]{2,1,0:T(8,128)(2,1)}, u32[]{:S(2)}, u32[]{:S(2)}) async-start(bf16[4,64,2048]{2,1,0:T(8,128)(2,1)} %get-tuple-element.251), calls=%async_computation.3 | async-start | bytes 2097152 | tf_op jit(solution)/shard_map/all_to_all | solution.py:1104
  228.4 14.9 %attend.1 = (bf16[2048,256]{1,0:T(8,128)(2,1)}, bf16[8,4,256,1024]{3,2,1,0:T(8,128)(2,1)}, f32[8,1,1024]{2,1,0:T(1,128)}) custom-call(s32[1]{0:T(128)} %bitcast.32.seq_ref, s32[1,1024]{1,0:T(1,128)} %bitcast.181, bf16[2048,256]{1,0:T(8,128)(2,1)} %bitcast.153, bf16[8,128,256]{2,1,0:T(8,128)(2,1)} %pad_maximum_fusion.4.kv0, ...), custom_call_target="tpu_custom_call" | custom-call | tf_op jit(solution)/shard_map/attend/pallas_call | solution.py:774
  243.4 2.1 convolution_convert_fusion.2.inner_ref
  245.4 8.0 %project_out.1 = (f32[256,2048]{1,0:T(8,128)}, bf16[256,2048]{1,0:T(8,128)(2,1)}) custom-call(s32[32]{0:T(128)} %stack.163.order_ref, bf16[2048,256]{1,0:T(8,128)(2,1)} %get-tuple-element.215.mixed_ref.o_ref, bf16[16,256]{1,0:T(8,128)(2,1)} %convolution_convert_fusion.2.inner_ref, bf16[16,2048]{1,0:T(8,128)(2,1)} %get-tuple-element.217.b_ref, ...), custom_call_target="tpu_custom_call" | custom-call | tf_op jit(solution)/shard_map/project_out/pallas_call | solution.py:354
  257.0 2.3 slice.148
  260.0 2.3 slice.149
  266.3 10.7 %place.2 = (bf16[2048,2048]{1,0:T(8,128)(2,1)}, bf16[2048,2048]{1,0:T(8,128)(2,1)}) custom-call(s32[7]{0:T(128)} %stack.171.sources_ref, bf16[512,2048]{1,0:T(8,128)(2,1)} %pad_maximum_fusion.refs_0_, bf16[512,2048]{1,0:T(8,128)(2,1)} %collective-permute-done.32.refs_1_, bf16[512,2048]{1,0:T(8,128)(2,1)} %collective-permute-done.33.refs_2_, ...), custom_call_target="tpu_custom_call" | custom-call | tf_op jit(solution)/shard_map/place/pallas_call | solution.py:255
  277.0 2.2 collective-permute-done.42.n2
  279.2 6.5 %collective-permute-done.48.refs_2_ = bf16[256,2048]{1,0:T(8,128)(2,1)} collective-permute-done((bf16[256,2048]{1,0:T(8,128)(2,1)}, bf16[256,2048]{1,0:T(8,128)(2,1)}, u32[]{:S(2)}, u32[]{:S(2)}) %collective-permute-start.48) | collective-permute-done | bytes 1048608 | tf_op jit(solution)/shard_map/ppermute | solution.py:87
  285.7 3.0 collective-permute-done.49.refs_3_
  288.8 2.9 finish.2
  291.7 15.5 %lower_back.1 = (bf16[1024,2048]{1,0:T(8,128)(2,1)}, bf16[1024,16]{1,0:T(8,128)(2,1)}) custom-call(bf16[256,2048]{1,0:T(8,128)(2,1)} %multiply_convert_fusion.g0, bf16[256,2048]{1,0:T(8,128)(2,1)} %collective-permute-done.50.g1, bf16[256,2048]{1,0:T(8,128)(2,1)} %collective-permute-done.37.g2, bf16[256,2048]{1,0:T(8,128)(2,1)} %collective-permute-done.51.g3, ...), custom_call_target="tpu_custom_call" | custom-call | tf_op jit(solution)/shard_map/lower_back/pallas_call | solution.py:525
  311.6 5.3 all_tokens.1
  316.9 18.1 %units.2 = (bf16[1024,1024]{1,0:T(8,128)(2,1)}, bf16[1024,1024]{1,0:T(8,128)(2,1)}, bf16[1024,1024]{1,0:T(8,128)(2,1)}, f32[1024,48]{1,0:T(8,128)}) custom-call(bf16[1024,2048]{1,0:T(8,128)(2,1)} %get-tuple-element.221.whole_ref, bf16[1024,32]{1,0:T(8,128)(2,1)} %get-tuple-element.222.low_ref, bf16[2048,2048]{1,0:T(8,128)(2,1)} %get-tuple-element.238.gate_ref.up_ref.w_ref, ...), custom_call_target="tpu_custom_call" | custom-call | tf_op jit(solution)/shard_map/units/pallas_call | solution.py:597
  337.2 13.4 %units_back_first.1.first_ref = bf16[1024,2048]{1,0:T(8,128)(2,1)} custom-call(bf16[1024,1024]{1,0:T(8,128)(2,1)} %get-tuple-element.259.g_ref.dg_ref, bf16[1024,1024]{1,0:T(8,128)(2,1)} %get-tuple-element.260.u_ref.du_ref, bf16[2048,2048]{1,0:T(8,128)(2,1)} %get-tuple-element.238.gate_ref.up_ref.w_ref), custom_call_target="tpu_custom_call" | custom-call | tf_op jit(solution)/shard_map/units_back_first/pallas_call | solution.py:647
  350.5 5.4 units_grads.2
  361.3 6.1 %place.3.refs_0_ = bf16[2048,2048]{1,0:T(8,128)(2,1)} custom-call(s32[7]{0:T(128)} %stack.171.sources_ref, bf16[256,2048]{1,0:T(8,128)(2,1)} %bitcast.69.refs_0_, bf16[256,2048]{1,0:T(8,128)(2,1)} %collective-permute-done.52.refs_1_, bf16[256,2048]{1,0:T(8,128)(2,1)} %collective-permute-done.53.refs_2_, bf16[256,2048]{1,0:T(8,128)(2,1)} %copy-done.34, ...), custom_call_target="tpu_custom_call" | custom-call | tf_op jit(solution)/shard_map/place/pallas_call | solution.py:255
  370.8 2.2 finish.3.gate_ref.up_ref.w_ref
  373.0 18.0 %units.3 = (bf16[1024,1024]{1,0:T(8,128)(2,1)}, bf16[1024,1024]{1,0:T(8,128)(2,1)}, bf16[1024,1024]{1,0:T(8,128)(2,1)}, f32[1024,48]{1,0:T(8,128)}) custom-call(bf16[1024,2048]{1,0:T(8,128)(2,1)} %get-tuple-element.221.whole_ref, bf16[1024,32]{1,0:T(8,128)(2,1)} %get-tuple-element.222.low_ref, bf16[2048,2048]{1,0:T(8,128)(2,1)} %finish.3.gate_ref.up_ref.w_ref, ...), custom_call_target="tpu_custom_call" | custom-call | tf_op jit(solution)/shard_map/units/pallas_call | solution.py:597
  391.0 9.7 %units_back.2 = (bf16[2,256,1024]{2,1,0:T(8,128)(2,1)}, bf16[2,256,1024]{2,1,0:T(8,128)(2,1)}) custom-call(bf16[1024,2048]{1,0:T(8,128)(2,1)} %units_back_first.1.first_ref, bf16[1024,1024]{1,0:T(8,128)(2,1)} %get-tuple-element.273.g_ref.dg_ref, bf16[1024,1024]{1,0:T(8,128)(2,1)} %get-tuple-element.274.u_ref.du_ref, ...), custom_call_target="tpu_custom_call" | custom-call | tf_op jit(solution)/shard_map/units_back/pallas_call | solution.py:678
  400.7 2.9 collective-permute-done.60.l1
  405.1 9.8 %units_back.3 = (bf16[2,256,1024]{2,1,0:T(8,128)(2,1)}, bf16[2,256,1024]{2,1,0:T(8,128)(2,1)}) custom-call(bf16[1024,2048]{1,0:T(8,128)(2,1)} %units_back_first.1.first_ref, bf16[1024,1024]{1,0:T(8,128)(2,1)} %get-tuple-element.273.g_ref.dg_ref, bf16[1024,1024]{1,0:T(8,128)(2,1)} %get-tuple-element.274.u_ref.du_ref, ...), custom_call_target="tpu_custom_call" | custom-call | tf_op jit(solution)/shard_map/units_back/pallas_call | solution.py:678
  420.7 16.2 %lower.1 = (bf16[2,256,2048]{2,1,0:T(8,128)(2,1)}, bf16[2,256,2048]{2,1,0:T(8,128)(2,1)}, f32[16,2048]{1,0:T(8,128)}, f32[32,2048]{1,0:T(8,128)}) custom-call(bf16[1024,1024]{1,0:T(8,128)(2,1)} %get-tuple-element.261.act_ref.aa_ref, bf16[1024,1024]{1,0:T(8,128)(2,1)} %get-tuple-element.298.ab_ref.act_ref, bf16[2048,2048]{1,0:T(8,128)(2,1)} %get-tuple-element.246.weight_ref, ...), custom_call_target="tpu_custom_call" | custom-call | tf_op jit(solution)/shard_map/lower/pallas_call | solution.py:723
  436.9 3.7 collective-permute-done.63.r2
  441.4 6.1 %hidden_back.1 = (f32[256,2048]{1,0:T(8,128)}, bf16[256,2048]{1,0:T(8,128)(2,1)}, bf16[256,16]{1,0:T(8,128)(2,1)}) custom-call(bf16[2,256,1024]{2,1,0:T(8,128)(2,1)} %get-tuple-element.285.l0, bf16[2,256,1024]{2,1,0:T(8,128)(2,1)} %copy-done.47, bf16[256,1024]{1,0:T(8,128)(2,1)} %copy-done.59, bf16[2,256,1024]{2,1,0:T(8,128)(2,1)} %get-tuple-element.287.r0, ...), custom_call_target="tpu_custom_call" | custom-call | flops 7000000000 | tf_op jit(solution)/shard_map/hidden_back/pallas_call | solution.py:492
  447.6 4.1 collective-permute-done.64
  455.7 6.8 %project_out_back.1.do_ref = bf16[2048,256]{1,0:T(8,128)(2,1)} custom-call(s32[32]{0:T(128)} %stack.163.order_ref, bf16[256,2048]{1,0:T(8,128)(2,1)} %get-tuple-element.294.grad_ref, bf16[16,2048]{1,0:T(8,128)(2,1)} %get-tuple-element.216.a_ref, bf16[256,16]{1,0:T(8,128)(2,1)} %get-tuple-element.295.inner_ref, bf16[64,5120]{1,0:T(8,128)(2,1)} %copy-done.6, ...), custom_call_target="tpu_custom_call" | custom-call | tf_op jit(solution)/shard_map/project_out_back/pallas_call | solution.py:406
  462.6 12.3 %attend_back.2 = (f32[1024,256]{1,0:T(8,128)}, bf16[2,4,128,256]{3,2,1,0:T(8,128)(2,1)}, bf16[2,4,128,256]{3,2,1,0:T(8,128)(2,1)}) custom-call(bf16[2048,256]{1,0:T(8,128)(2,1)} %bitcast.154, bf16[8,128,256]{2,1,0:T(8,128)(2,1)} %pad_maximum_fusion.4.kv0, bf16[8,128,256]{2,1,0:T(8,128)(2,1)} %collective-permute-done.38.kv1, ...), custom_call_target="tpu_custom_call" | custom-call | tf_op jit(solution)/shard_map/attend_back/pallas_call | solution.py:818
  477.7 5.4 units_grads.3
  485.1 12.0 %attend_back.3 = (f32[1024,256]{1,0:T(8,128)}, bf16[2,4,128,256]{3,2,1,0:T(8,128)(2,1)}, bf16[2,4,128,256]{3,2,1,0:T(8,128)(2,1)}) custom-call(bf16[2048,256]{1,0:T(8,128)(2,1)} %bitcast.155, bf16[8,128,256]{2,1,0:T(8,128)(2,1)} %pad_maximum_fusion.4.kv0, bf16[8,128,256]{2,1,0:T(8,128)(2,1)} %collective-permute-done.38.kv1, ...), custom_call_target="tpu_custom_call" | custom-call | tf_op jit(solution)/shard_map/attend_back/pallas_call | solution.py:818
  503.2 6.7 %collective-permute-done.69 = bf16[4,128,256]{2,1,0:T(8,128)(2,1)S(1)} collective-permute-done((bf16[4,128,256]{2,1,0:T(8,128)(2,1)S(1)}, bf16[4,128,256]{2,1,0:T(8,128)(2,1)S(1)}, u32[]{:S(2)}, u32[]{:S(2)}) %collective-permute-start.69) | collective-permute-done | bytes 262176 | tf_op jit(solution)/shard_map/ppermute | solution.py:147
  514.8 2.8 pack.1
  521.6 2.9 fusion.7
  524.5 2.2 collective-permute-done.71
  527.7 5.0 all-to-all-start.4
  532.7 11.2 %project_in_back.1 = bf16[256,2048]{1,0:T(8,128)(2,1)} custom-call(s32[32]{0:T(128)} %stack.163.order_ref, bf16[3072,256]{1,0:T(8,128)(2,1)} %copy-done.2, bf16[48,2048]{1,0:T(8,128)(2,1)} %get-tuple-element.211.a_ref, bf16[48,256]{1,0:T(8,128)(2,1)} %copy-done.53, bf16[256,2048]{1,0:T(8,128)(2,1)} %bitcast.157, f32[1,2048]{1,0:T(1,128)} %bitcast.171, ...), custom_call_target="tpu_custom_call" | custom-call | tf_op jit(solution)/shard_map/project_in_back/pallas_call | solution.py:450
  544.7 2.4 sort.1
  (317 shorter events, 116.4 us)
Async XLA Ops:
  4.3 23.9 %collective-permute-start = (bf16[64,5120]{1,0:T(8,128)(2,1)S(1)}, bf16[64,5120]{1,0:T(8,128)(2,1)S(1)}, u32[]{:S(2)}, u32[]{:S(2)}) collective-permute-start(bf16[64,5120]{1,0:T(8,128)(2,1)S(1)} %constant_dynamic-update-slice_fusion.refs_0_), channel_id=1, source_target_pairs={{0,8},{8,16},{16,24},{24,28},{28,20},{20,12},{12,4},{4,0},{1,9},{9... | collective-permute-start | bytes 1966088 | tf_op jit(solution)/shard_map/ppermute | solution.py:81
  7.4 20.8 %collective-permute-start.1 = (bf16[64,5120]{1,0:T(8,128)(2,1)S(1)}, bf16[64,5120]{1,0:T(8,128)(2,1)S(1)}, u32[]{:S(2)}, u32[]{:S(2)}) collective-permute-start(bf16[64,5120]{1,0:T(8,128)(2,1)S(1)} %constant_dynamic-update-slice_fusion.refs_0_), channel_id=1, source_target_pairs={{8,0},{16,8},{24,16},{28,24},{20,28},{12,20},{4,12},{0,4},{9,1},{1... | collective-permute-start | bytes 1966088 | tf_op jit(solution)/shard_map/ppermute | solution.py:82
  7.4 20.9 %collective-permute-start.2 = (bf16[64,5120]{1,0:T(8,128)(2,1)S(1)}, bf16[64,5120]{1,0:T(8,128)(2,1)S(1)}, u32[]{:S(2)}, u32[]{:S(2)}) collective-permute-start(bf16[64,5120]{1,0:T(8,128)(2,1)S(1)} %constant_dynamic-update-slice_fusion.refs_0_), channel_id=1, source_target_pairs={{0,1},{1,0},{2,3},{3,2},{4,5},{5,4},{6,7},{7,6},{8,9},{9,8},{10,11... | collective-permute-start | bytes 1966088 | tf_op jit(solution)/shard_map/ppermute | solution.py:147
  7.4 20.9 %collective-permute-start.3 = (bf16[64,5120]{1,0:T(8,128)(2,1)S(1)}, bf16[64,5120]{1,0:T(8,128)(2,1)S(1)}, u32[]{:S(2)}, u32[]{:S(2)}) collective-permute-start(bf16[64,5120]{1,0:T(8,128)(2,1)S(1)} %constant_dynamic-update-slice_fusion.refs_0_), channel_id=1, source_target_pairs={{0,2},{1,3},{2,0},{3,1},{4,6},{5,7},{6,4},{7,5},{8,10},{9,11},{10,... | collective-permute-start | bytes 1966088 | tf_op jit(solution)/shard_map/ppermute | solution.py:147
  10.6 15.1 %all-to-all-start = ((s32[8,1,128]{2,1,0:T(1,128)}), s32[8,1,128]{2,1,0:T(1,128)S(1)}, u32[]{:S(2)}, u32[]{:S(2)}) async-start(s32[8,1,128]{2,1,0:T(1,128)} %broadcast_in_dim.22), calls=%async_computation | async-start | bytes 8192 | tf_op jit(solution)/shard_map/all_to_all | solution.py:1043
  28.3 15.0 %collective-permute-start.5 = (bf16[64,5120]{1,0:T(8,128)(2,1)S(1)}, bf16[64,5120]{1,0:T(8,128)(2,1)S(1)}, u32[]{:S(2)}, u32[]{:S(2)}) collective-permute-start(bf16[64,5120]{1,0:T(8,128)(2,1)S(1)} %collective-permute-done.1.refs_8_), channel_id=1, source_target_pairs={{8,0},{16,8},{24,16},{28,24},{20,28},{12,20},{4,12},{0,4},{9,1},{1... | collective-permute-start | bytes 1966088 | tf_op jit(solution)/shard_map/ppermute | solution.py:82
  29.8 13.5 %collective-permute-start.8 = (bf16[64,5120]{1,0:T(8,128)(2,1)S(1)}, bf16[64,5120]{1,0:T(8,128)(2,1)S(1)}, u32[]{:S(2)}, u32[]{:S(2)}) collective-permute-start(bf16[64,5120]{1,0:T(8,128)(2,1)S(1)} %collective-permute-done.1.refs_8_), channel_id=1, source_target_pairs={{0,1},{1,0},{2,3},{3,2},{4,5},{5,4},{6,7},{7,6},{8,9},{9,8},{10,11... | collective-permute-start | bytes 1966088 | tf_op jit(solution)/shard_map/ppermute | solution.py:147
  29.8 21.0 %collective-permute-start.4 = (bf16[64,5120]{1,0:T(8,128)(2,1)S(1)}, bf16[64,5120]{1,0:T(8,128)(2,1)}, u32[]{:S(2)}, u32[]{:S(2)}) collective-permute-start(bf16[64,5120]{1,0:T(8,128)(2,1)S(1)} %collective-permute-done.refs_4_), channel_id=1, source_target_pairs={{0,8},{8,16},{16,24},{24,28},{28,20},{20,12},{12,4},{4,0},{1,9},{9... | collective-permute-start | bytes 1966088 | tf_op jit(solution)/shard_map/ppermute | solution.py:81
  30.4 20.5 %collective-permute-start.7 = (bf16[64,5120]{1,0:T(8,128)(2,1)S(1)}, bf16[64,5120]{1,0:T(8,128)(2,1)}, u32[]{:S(2)}, u32[]{:S(2)}) collective-permute-start(bf16[64,5120]{1,0:T(8,128)(2,1)S(1)} %collective-permute-done.refs_4_), channel_id=1, source_target_pairs={{0,1},{1,0},{2,3},{3,2},{4,5},{5,4},{6,7},{7,6},{8,9},{9,8},{10,11... | collective-permute-start | bytes 1966088 | tf_op jit(solution)/shard_map/ppermute | solution.py:147
  30.6 20.2 %collective-permute-start.9 = (bf16[64,5120]{1,0:T(8,128)(2,1)S(1)}, bf16[64,5120]{1,0:T(8,128)(2,1)}, u32[]{:S(2)}, u32[]{:S(2)}) collective-permute-start(bf16[64,5120]{1,0:T(8,128)(2,1)S(1)} %collective-permute-done.refs_4_), channel_id=1, source_target_pairs={{0,2},{1,3},{2,0},{3,1},{4,6},{5,7},{6,4},{7,5},{8,10},{9,11},{10,... | collective-permute-start | bytes 1966088 | tf_op jit(solution)/shard_map/ppermute | solution.py:147
  45.1 17.8 %collective-permute-start.16 = (bf16[64,5120]{1,0:T(8,128)(2,1)S(1)}, bf16[64,5120]{1,0:T(8,128)(2,1)}, u32[]{:S(2)}, u32[]{:S(2)}) collective-permute-start(bf16[64,5120]{1,0:T(8,128)(2,1)S(1)} %collective-permute-done.1.refs_8_), channel_id=1, source_target_pairs={{0,2},{1,3},{2,0},{3,1},{4,6},{5,7},{6,4},{7,5},{8,10},{9,11},{10,... | collective-permute-start | bytes 1966088 | tf_op jit(solution)/shard_map/ppermute | solution.py:147
  46.5 26.3 %all-to-all-start.1 = ((bf16[4,64,2048]{2,1,0:T(8,128)(2,1)}), bf16[4,64,2048]{2,1,0:T(8,128)(2,1)}, u32[]{:S(2)}, u32[]{:S(2)}) async-start(bf16[4,64,2048]{2,1,0:T(8,128)(2,1)} %get-tuple-element.184), calls=%async_computation.1 | async-start | bytes 2097152 | tf_op jit(solution)/shard_map/all_to_all | solution.py:1051
  50.8 29.4 %collective-permute-start.11 = (bf16[64,5120]{1,0:T(8,128)(2,1)}, bf16[64,5120]{1,0:T(8,128)(2,1)S(1)}, u32[]{:S(2)}, u32[]{:S(2)}) collective-permute-start(bf16[64,5120]{1,0:T(8,128)(2,1)} %collective-permute-done.4.refs_12_), channel_id=1, source_target_pairs={{0,8},{8,16},{16,24},{24,28},{28,20},{20,12},{12,4},{4,0},{1,9},{9... | collective-permute-start | bytes 1966088 | tf_op jit(solution)/shard_map/ppermute | solution.py:81
  51.5 28.8 %collective-permute-start.14 = (bf16[64,5120]{1,0:T(8,128)(2,1)}, bf16[64,5120]{1,0:T(8,128)(2,1)}, u32[]{:S(2)}, u32[]{:S(2)}) collective-permute-start(bf16[64,5120]{1,0:T(8,128)(2,1)} %collective-permute-done.4.refs_12_), channel_id=1, source_target_pairs={{0,1},{1,0},{2,3},{3,2},{4,5},{5,4},{6,7},{7,6},{8,9},{9,8},{10,11... | collective-permute-start | bytes 1966088 | tf_op jit(solution)/shard_map/ppermute | solution.py:147
  51.6 28.6 %collective-permute-start.12 = (bf16[64,5120]{1,0:T(8,128)(2,1)}, bf16[64,5120]{1,0:T(8,128)(2,1)S(1)}, u32[]{:S(2)}, u32[]{:S(2)}) collective-permute-start(bf16[64,5120]{1,0:T(8,128)(2,1)} %copy-done.11), channel_id=1, source_target_pairs={{8,0},{16,8},{24,16},{28,24},{20,28},{12,20},{4,12},{0,4},{9,1},{1... | collective-permute-start | bytes 1966088 | tf_op jit(solution)/shard_map/ppermute | solution.py:82
  53.1 27.2 %collective-permute-start.15 = (bf16[64,5120]{1,0:T(8,128)(2,1)}, bf16[64,5120]{1,0:T(8,128)(2,1)}, u32[]{:S(2)}, u32[]{:S(2)}) collective-permute-start(bf16[64,5120]{1,0:T(8,128)(2,1)} %copy-done.11), channel_id=1, source_target_pairs={{0,1},{1,0},{2,3},{3,2},{4,5},{5,4},{6,7},{7,6},{8,9},{9,8},{10,11... | collective-permute-start | bytes 1966088 | tf_op jit(solution)/shard_map/ppermute | solution.py:147
  62.8 17.5 %collective-permute-start.13 = (bf16[64,5120]{1,0:T(8,128)(2,1)}, bf16[64,5120]{1,0:T(8,128)(2,1)}, u32[]{:S(2)}, u32[]{:S(2)}) collective-permute-start(bf16[64,5120]{1,0:T(8,128)(2,1)} %collective-permute-done.9.refs_6_), channel_id=1, source_target_pairs={{0,1},{1,0},{2,3},{3,2},{4,5},{5,4},{6,7},{7,6},{8,9},{9,8},{10,11... | collective-permute-start | bytes 1966088 | tf_op jit(solution)/shard_map/ppermute | solution.py:147
  72.9 15.6 %all-to-all-start.2 = ((bf16[8,16,1376]{2,1,0:T(8,128)(2,1)}), bf16[8,16,1376]{2,1,0:T(8,128)(2,1)}, u32[]{:S(2)}, u32[]{:S(2)}) async-start(bf16[8,16,1376]{2,1,0:T(8,128)(2,1)} %pick.1), calls=%async_computation.2 | async-start | bytes 720896 | tf_op jit(solution)/shard_map/all_to_all | solution.py:1053
  80.3 10.6 %collective-permute-start.17 = (bf16[32,5120]{1,0:T(8,128)(2,1)S(1)}, bf16[32,5120]{1,0:T(8,128)(2,1)S(1)}, u32[]{:S(2)}, u32[]{:S(2)}) collective-permute-start(bf16[32,5120]{1,0:T(8,128)(2,1)S(1)} %slice.138), channel_id=1, source_target_pairs={{0,8},{8,16},{16,24},{24,28},{28,20},{20,12},{12,4},{4,0},{1,9},{9... | collective-permute-start | bytes 983048 | tf_op jit(solution)/shard_map/ppermute | solution.py:87
  82.3 17.9 %collective-permute-start.10 = (bf16[64,5120]{1,0:T(8,128)(2,1)}, bf16[64,5120]{1,0:T(8,128)(2,1)S(1)}, u32[]{:S(2)}, u32[]{:S(2)}) collective-permute-start(bf16[64,5120]{1,0:T(8,128)(2,1)} %collective-permute-done.4.refs_12_), channel_id=1, source_target_pairs={{0,2},{1,3},{2,0},{3,1},{4,6},{5,7},{6,4},{7,5},{8,10},{9,11},{10,... | collective-permute-start | bytes 1966088 | tf_op jit(solution)/shard_map/ppermute | solution.py:147
  83.8 27.9 %collective-permute-start.25 = (bf16[64,5120]{1,0:T(8,128)(2,1)S(1)}, bf16[64,5120]{1,0:T(8,128)(2,1)}, u32[]{:S(2)}, u32[]{:S(2)}) collective-permute-start(bf16[64,5120]{1,0:T(8,128)(2,1)S(1)} %copy-done.12), channel_id=1, source_target_pairs={{0,2},{1,3},{2,0},{3,1},{4,6},{5,7},{6,4},{7,5},{8,10},{9,11},{10,... | collective-permute-start | bytes 1966088 | tf_op jit(solution)/shard_map/ppermute | solution.py:147
  85.1 8.7 %collective-permute-start.18 = (bf16[32,5120]{1,0:T(8,128)(2,1)}, bf16[32,5120]{1,0:T(8,128)(2,1)}, u32[]{:S(2)}, u32[]{:S(2)}) collective-permute-start(bf16[32,5120]{1,0:T(8,128)(2,1)} %slice.139), channel_id=1, source_target_pairs={{8,0},{16,8},{24,16},{28,24},{20,28},{12,20},{4,12},{0,4},{9,1},{1... | collective-permute-start | bytes 983048 | tf_op jit(solution)/shard_map/ppermute | solution.py:88
  85.2 15.0 %collective-permute-start.21 = (bf16[64,5120]{1,0:T(8,128)(2,1)S(1)}, bf16[64,5120]{1,0:T(8,128)(2,1)}, u32[]{:S(2)}, u32[]{:S(2)}) collective-permute-start(bf16[64,5120]{1,0:T(8,128)(2,1)S(1)} %collective-permute-done.11.refs_20_), channel_id=1, source_target_pairs={{0,1},{1,0},{2,3},{3,2},{4,5},{5,4},{6,7},{7,6},{8,9},{9,8},{10,11... | collective-permute-start | bytes 1966088 | tf_op jit(solution)/shard_map/ppermute | solution.py:147
  91.6 8.6 %collective-permute-start.19 = (bf16[64,5120]{1,0:T(8,128)(2,1)}, bf16[64,5120]{1,0:T(8,128)(2,1)S(1)}, u32[]{:S(2)}, u32[]{:S(2)}) collective-permute-start(bf16[64,5120]{1,0:T(8,128)(2,1)} %collective-permute-done.16.refs_10_), channel_id=1, source_target_pairs={{0,1},{1,0},{2,3},{3,2},{4,5},{5,4},{6,7},{7,6},{8,9},{9,8},{10,11... | collective-permute-start | bytes 1966088 | tf_op jit(solution)/shard_map/ppermute | solution.py:147
  100.2 11.9 %collective-permute-start.24 = (bf16[64,5120]{1,0:T(8,128)(2,1)S(1)}, bf16[64,5120]{1,0:T(8,128)(2,1)}, u32[]{:S(2)}, u32[]{:S(2)}) collective-permute-start(bf16[64,5120]{1,0:T(8,128)(2,1)S(1)} %constant_dynamic-update-slice_fusion.4.refs_28_), channel_id=1, source_target_pairs={{0,1},{1,0},{2,3},{3,2},{4,5},{5,4},{6,7},{7,6},{8,9},{9,8},{10,11... | collective-permute-start | bytes 1966088 | tf_op jit(solution)/shard_map/ppermute | solution.py:147
  101.1 12.5 %collective-permute-start.23 = (bf16[64,5120]{1,0:T(8,128)(2,1)S(1)}, bf16[64,5120]{1,0:T(8,128)(2,1)}, u32[]{:S(2)}, u32[]{:S(2)}) collective-permute-start(bf16[64,5120]{1,0:T(8,128)(2,1)S(1)} %collective-permute-done.12.refs_24_), channel_id=1, source_target_pairs={{0,1},{1,0},{2,3},{3,2},{4,5},{5,4},{6,7},{7,6},{8,9},{9,8},{10,11... | collective-permute-start | bytes 1966088 | tf_op jit(solution)/shard_map/ppermute | solution.py:147
  101.1 12.5 %collective-permute-start.22 = (bf16[64,5120]{1,0:T(8,128)(2,1)S(1)}, bf16[64,5120]{1,0:T(8,128)(2,1)}, u32[]{:S(2)}, u32[]{:S(2)}) collective-permute-start(bf16[64,5120]{1,0:T(8,128)(2,1)S(1)} %collective-permute-done.10.refs_14_), channel_id=1, source_target_pairs={{0,1},{1,0},{2,3},{3,2},{4,5},{5,4},{6,7},{7,6},{8,9},{9,8},{10,11... | collective-permute-start | bytes 1966088 | tf_op jit(solution)/shard_map/ppermute | solution.py:147
  105.1 47.9 %collective-permute-start.32 = (bf16[512,2048]{1,0:T(8,128)(2,1)}, bf16[512,2048]{1,0:T(8,128)(2,1)}, u32[]{:S(2)}, u32[]{:S(2)}) collective-permute-start(bf16[512,2048]{1,0:T(8,128)(2,1)} %pad_maximum_fusion.refs_0_), channel_id=1, source_target_pairs={{0,8},{8,16},{16,24},{24,28},{28,20},{20,12},{12,4},{4,0},{1,9},{9... | collective-permute-start | bytes 6291464 | tf_op jit(solution)/shard_map/ppermute | solution.py:81
  111.7 45.3 %collective-permute-start.33 = (bf16[512,2048]{1,0:T(8,128)(2,1)}, bf16[512,2048]{1,0:T(8,128)(2,1)}, u32[]{:S(2)}, u32[]{:S(2)}) collective-permute-start(bf16[512,2048]{1,0:T(8,128)(2,1)} %pad_maximum_fusion.refs_0_), channel_id=1, source_target_pairs={{8,0},{16,8},{24,16},{28,24},{20,28},{12,20},{4,12},{0,4},{9,1},{1... | collective-permute-start | bytes 6291464 | tf_op jit(solution)/shard_map/ppermute | solution.py:82
  112.1 10.1 %collective-permute-start.26 = (bf16[8,16,608]{2,1,0:T(8,128)(2,1)S(1)}, bf16[8,16,608]{2,1,0:T(8,128)(2,1)}, u32[]{:S(2)}, u32[]{:S(2)}) collective-permute-start(bf16[8,16,608]{2,1,0:T(8,128)(2,1)S(1)} %slice.140), channel_id=1, source_target_pairs={{0,2},{1,3},{2,0},{3,1},{4,6},{5,7},{6,4},{7,5},{8,10},{9,11},{10,... | collective-permute-start | bytes 466952 | tf_op jit(solution)/shard_map/ppermute | solution.py:147
  113.6 19.7 %collective-permute-start.29 = (bf16[64,5120]{1,0:T(8,128)(2,1)S(1)}, bf16[64,5120]{1,0:T(8,128)(2,1)S(1)}, u32[]{:S(2)}, u32[]{:S(2)}) collective-permute-start(bf16[64,5120]{1,0:T(8,128)(2,1)S(1)} %collective-permute-done.11.refs_20_), channel_id=1, source_target_pairs={{0,2},{1,3},{2,0},{3,1},{4,6},{5,7},{6,4},{7,5},{8,10},{9,11},{10,... | collective-permute-start | bytes 1966088 | tf_op jit(solution)/shard_map/ppermute | solution.py:147
  122.2 11.1 %collective-permute-start.28 = (bf16[8,16,608]{2,1,0:T(8,128)(2,1)}, bf16[8,16,608]{2,1,0:T(8,128)(2,1)S(1)}, u32[]{:S(2)}, u32[]{:S(2)}) collective-permute-start(bf16[8,16,608]{2,1,0:T(8,128)(2,1)} %collective-permute-done.26.p2), channel_id=1, source_target_pairs={{0,1},{1,0},{2,3},{3,2},{4,5},{5,4},{6,7},{7,6},{8,9},{9,8},{10,11... | collective-permute-start | bytes 466952 | tf_op jit(solution)/shard_map/ppermute | solution.py:147
  122.7 34.3 %collective-permute-start.31 = (bf16[64,5120]{1,0:T(8,128)(2,1)S(1)}, bf16[64,5120]{1,0:T(8,128)(2,1)S(1)}, u32[]{:S(2)}, u32[]{:S(2)}) collective-permute-start(bf16[64,5120]{1,0:T(8,128)(2,1)S(1)} %collective-permute-done.12.refs_24_), channel_id=1, source_target_pairs={{0,2},{1,3},{2,0},{3,1},{4,6},{5,7},{6,4},{7,5},{8,10},{9,11},{10,... | collective-permute-start | bytes 1966088 | tf_op jit(solution)/shard_map/ppermute | solution.py:147
  133.3 23.7 %collective-permute-start.34 = (bf16[64,5120]{1,0:T(8,128)(2,1)S(1)}, bf16[64,5120]{1,0:T(8,128)(2,1)S(1)}, u32[]{:S(2)}, u32[]{:S(2)}) collective-permute-start(bf16[64,5120]{1,0:T(8,128)(2,1)S(1)} %collective-permute-done.29.refs_22_), channel_id=1, source_target_pairs={{0,1},{1,0},{2,3},{3,2},{4,5},{5,4},{6,7},{7,6},{8,9},{9,8},{10,11... | collective-permute-start | bytes 1966088 | tf_op jit(solution)/shard_map/ppermute | solution.py:147
  133.4 24.5 %collective-permute-start.30 = (bf16[64,5120]{1,0:T(8,128)(2,1)S(1)}, bf16[64,5120]{1,0:T(8,128)(2,1)}, u32[]{:S(2)}, u32[]{:S(2)}) collective-permute-start(bf16[64,5120]{1,0:T(8,128)(2,1)S(1)} %constant_dynamic-update-slice_fusion.4.refs_28_), channel_id=1, source_target_pairs={{0,2},{1,3},{2,0},{3,1},{4,6},{5,7},{6,4},{7,5},{8,10},{9,11},{10,... | collective-permute-start | bytes 1966088 | tf_op jit(solution)/shard_map/ppermute | solution.py:147
  160.2 48.3 %collective-permute-start.45 = (bf16[512,2048]{1,0:T(8,128)(2,1)}, bf16[512,2048]{1,0:T(8,128)(2,1)}, u32[]{:S(2)}, u32[]{:S(2)}) collective-permute-start(bf16[512,2048]{1,0:T(8,128)(2,1)} %collective-permute-done.33.refs_2_), channel_id=1, source_target_pairs={{8,0},{16,8},{24,16},{28,24},{20,28},{12,20},{4,12},{0,4},{9,1},{1... | collective-permute-start | bytes 6291464 | tf_op jit(solution)/shard_map/ppermute | solution.py:82
  160.9 47.9 %collective-permute-start.44 = (bf16[512,2048]{1,0:T(8,128)(2,1)}, bf16[512,2048]{1,0:T(8,128)(2,1)}, u32[]{:S(2)}, u32[]{:S(2)}) collective-permute-start(bf16[512,2048]{1,0:T(8,128)(2,1)} %collective-permute-done.32.refs_1_), channel_id=1, source_target_pairs={{0,8},{8,16},{16,24},{24,28},{28,20},{20,12},{12,4},{4,0},{1,9},{9... | collective-permute-start | bytes 6291464 | tf_op jit(solution)/shard_map/ppermute | solution.py:81
  162.3 25.2 %collective-permute-start.37 = (bf16[256,2048]{1,0:T(8,128)(2,1)}, bf16[256,2048]{1,0:T(8,128)(2,1)}, u32[]{:S(2)}, u32[]{:S(2)}) collective-permute-start(bf16[256,2048]{1,0:T(8,128)(2,1)} %multiply_convert_fusion.g0), channel_id=1, source_target_pairs={{0,2},{1,3},{2,0},{3,1},{4,6},{5,7},{6,4},{7,5},{8,10},{9,11},{10,... | collective-permute-start | bytes 3145736 | tf_op jit(solution)/shard_map/ppermute | solution.py:147
  187.5 21.4 %collective-permute-start.39 = (bf16[8,128,256]{2,1,0:T(8,128)(2,1)}, bf16[8,128,256]{2,1,0:T(8,128)(2,1)}, u32[]{:S(2)}, u32[]{:S(2)}) collective-permute-start(bf16[8,128,256]{2,1,0:T(8,128)(2,1)} %pad_maximum_fusion.4.kv0), channel_id=1, source_target_pairs={{0,2},{1,3},{2,0},{3,1},{4,6},{5,7},{6,4},{7,5},{8,10},{9,11},{10,... | collective-permute-start | bytes 1572872 | tf_op jit(solution)/shard_map/ppermute | solution.py:147
  208.9 47.1 %collective-permute-start.47 = (bf16[512,2048]{1,0:T(8,128)(2,1)}, bf16[512,2048]{1,0:T(8,128)(2,1)}, u32[]{:S(2)}, u32[]{:S(2)}) collective-permute-start(bf16[512,2048]{1,0:T(8,128)(2,1)} %collective-permute-done.45.refs_4_), channel_id=1, source_target_pairs={{8,0},{16,8},{24,16},{28,24},{20,28},{12,20},{4,12},{0,4},{9,1},{1... | collective-permute-start | bytes 6291464 | tf_op jit(solution)/shard_map/ppermute | solution.py:82
  210.2 46.8 %collective-permute-start.46 = (bf16[512,2048]{1,0:T(8,128)(2,1)}, bf16[512,2048]{1,0:T(8,128)(2,1)}, u32[]{:S(2)}, u32[]{:S(2)}) collective-permute-start(bf16[512,2048]{1,0:T(8,128)(2,1)} %collective-permute-done.44.refs_3_), channel_id=1, source_target_pairs={{0,8},{8,16},{16,24},{24,28},{28,20},{20,12},{12,4},{4,0},{1,9},{9... | collective-permute-start | bytes 6291464 | tf_op jit(solution)/shard_map/ppermute | solution.py:81
  210.9 14.3 %collective-permute-start.38 = (bf16[8,128,256]{2,1,0:T(8,128)(2,1)}, bf16[8,128,256]{2,1,0:T(8,128)(2,1)}, u32[]{:S(2)}, u32[]{:S(2)}) collective-permute-start(bf16[8,128,256]{2,1,0:T(8,128)(2,1)} %pad_maximum_fusion.4.kv0), channel_id=1, source_target_pairs={{0,1},{1,0},{2,3},{3,2},{4,5},{5,4},{6,7},{7,6},{8,9},{9,8},{10,11... | collective-permute-start | bytes 1572872 | tf_op jit(solution)/shard_map/ppermute | solution.py:147
  210.9 52.8 %collective-permute-start.50 = (bf16[256,2048]{1,0:T(8,128)(2,1)}, bf16[256,2048]{1,0:T(8,128)(2,1)}, u32[]{:S(2)}, u32[]{:S(2)}) collective-permute-start(bf16[256,2048]{1,0:T(8,128)(2,1)} %multiply_convert_fusion.g0), channel_id=1, source_target_pairs={{0,1},{1,0},{2,3},{3,2},{4,5},{5,4},{6,7},{7,6},{8,9},{9,8},{10,11... | collective-permute-start | bytes 3145736 | tf_op jit(solution)/shard_map/ppermute | solution.py:147
  211.4 53.0 %collective-permute-start.51 = (bf16[256,2048]{1,0:T(8,128)(2,1)}, bf16[256,2048]{1,0:T(8,128)(2,1)}, u32[]{:S(2)}, u32[]{:S(2)}) collective-permute-start(bf16[256,2048]{1,0:T(8,128)(2,1)} %collective-permute-done.37.g2), channel_id=1, source_target_pairs={{0,1},{1,0},{2,3},{3,2},{4,5},{5,4},{6,7},{7,6},{8,9},{9,8},{10,11... | collective-permute-start | bytes 3145736 | tf_op jit(solution)/shard_map/ppermute | solution.py:147
  211.4 52.3 %all-to-all-start.3 = ((bf16[4,64,2048]{2,1,0:T(8,128)(2,1)}), bf16[4,64,2048]{2,1,0:T(8,128)(2,1)}, u32[]{:S(2)}, u32[]{:S(2)}) async-start(bf16[4,64,2048]{2,1,0:T(8,128)(2,1)} %get-tuple-element.251), calls=%async_computation.3 | async-start | bytes 2097152 | tf_op jit(solution)/shard_map/all_to_all | solution.py:1104
  253.5 25.7 %collective-permute-start.42 = (bf16[256,2048]{1,0:T(8,128)(2,1)}, bf16[256,2048]{1,0:T(8,128)(2,1)}, u32[]{:S(2)}, u32[]{:S(2)}) collective-permute-start(bf16[256,2048]{1,0:T(8,128)(2,1)} %get-tuple-element.219.n0), channel_id=1, source_target_pairs={{0,2},{1,3},{2,0},{3,1},{4,6},{5,7},{6,4},{7,5},{8,10},{9,11},{10,... | collective-permute-start | bytes 3145736 | tf_op jit(solution)/shard_map/ppermute | solution.py:147
  259.3 26.4 %collective-permute-start.48 = (bf16[256,2048]{1,0:T(8,128)(2,1)}, bf16[256,2048]{1,0:T(8,128)(2,1)}, u32[]{:S(2)}, u32[]{:S(2)}) collective-permute-start(bf16[256,2048]{1,0:T(8,128)(2,1)} %slice.148), channel_id=1, source_target_pairs={{0,8},{8,16},{16,24},{24,28},{28,20},{20,12},{12,4},{4,0},{1,9},{9... | collective-permute-start | bytes 3145736 | tf_op jit(solution)/shard_map/ppermute | solution.py:87
  262.3 26.4 %collective-permute-start.49 = (bf16[256,2048]{1,0:T(8,128)(2,1)}, bf16[256,2048]{1,0:T(8,128)(2,1)}, u32[]{:S(2)}, u32[]{:S(2)}) collective-permute-start(bf16[256,2048]{1,0:T(8,128)(2,1)} %slice.149), channel_id=1, source_target_pairs={{8,0},{16,8},{24,16},{28,24},{20,28},{12,20},{4,12},{0,4},{9,1},{1... | collective-permute-start | bytes 3145736 | tf_op jit(solution)/shard_map/ppermute | solution.py:88
  263.7 43.5 %collective-permute-start.52 = (bf16[256,2048]{1,0:T(8,128)(2,1)}, bf16[256,2048]{1,0:T(8,128)(2,1)}, u32[]{:S(2)}, u32[]{:S(2)}) collective-permute-start(bf16[256,2048]{1,0:T(8,128)(2,1)} %bitcast.69.refs_0_), channel_id=1, source_target_pairs={{0,8},{8,16},{16,24},{24,28},{28,20},{20,12},{12,4},{4,0},{1,9},{9... | collective-permute-start | bytes 3145736 | tf_op jit(solution)/shard_map/ppermute | solution.py:81
  264.4 44.1 %collective-permute-start.53 = (bf16[256,2048]{1,0:T(8,128)(2,1)}, bf16[256,2048]{1,0:T(8,128)(2,1)}, u32[]{:S(2)}, u32[]{:S(2)}) collective-permute-start(bf16[256,2048]{1,0:T(8,128)(2,1)} %bitcast.69.refs_0_), channel_id=1, source_target_pairs={{8,0},{16,8},{24,16},{28,24},{20,28},{12,20},{4,12},{0,4},{9,1},{1... | collective-permute-start | bytes 3145736 | tf_op jit(solution)/shard_map/ppermute | solution.py:82
  279.2 31.4 %collective-permute-start.41 = (bf16[256,2048]{1,0:T(8,128)(2,1)S(1)}, bf16[256,2048]{1,0:T(8,128)(2,1)S(1)}, u32[]{:S(2)}, u32[]{:S(2)}) collective-permute-start(bf16[256,2048]{1,0:T(8,128)(2,1)S(1)} %copy-done.35), channel_id=1, source_target_pairs={{0,1},{1,0},{2,3},{3,2},{4,5},{5,4},{6,7},{7,6},{8,9},{9,8},{10,11... | collective-permute-start | bytes 3145736 | tf_op jit(solution)/shard_map/ppermute | solution.py:147
  285.7 24.8 %collective-permute-start.43 = (bf16[256,2048]{1,0:T(8,128)(2,1)}, bf16[256,2048]{1,0:T(8,128)(2,1)}, u32[]{:S(2)}, u32[]{:S(2)}) collective-permute-start(bf16[256,2048]{1,0:T(8,128)(2,1)} %collective-permute-done.42.n2), channel_id=1, source_target_pairs={{0,1},{1,0},{2,3},{3,2},{4,5},{5,4},{6,7},{7,6},{8,9},{9,8},{10,11... | collective-permute-start | bytes 3145736 | tf_op jit(solution)/shard_map/ppermute | solution.py:147
  308.5 26.5 %collective-permute-start.55 = (bf16[256,2048]{1,0:T(8,128)(2,1)}, bf16[256,2048]{1,0:T(8,128)(2,1)S(1)}, u32[]{:S(2)}, u32[]{:S(2)}) collective-permute-start(bf16[256,2048]{1,0:T(8,128)(2,1)} %collective-permute-done.53.refs_2_), channel_id=1, source_target_pairs={{8,0},{16,8},{24,16},{28,24},{20,28},{12,20},{4,12},{0,4},{9,1},{1... | collective-permute-start | bytes 3145736 | tf_op jit(solution)/shard_map/ppermute | solution.py:82
  309.3 25.7 %collective-permute-start.54 = (bf16[256,2048]{1,0:T(8,128)(2,1)}, bf16[256,2048]{1,0:T(8,128)(2,1)S(1)}, u32[]{:S(2)}, u32[]{:S(2)}) collective-permute-start(bf16[256,2048]{1,0:T(8,128)(2,1)} %collective-permute-done.52.refs_1_), channel_id=1, source_target_pairs={{0,8},{8,16},{16,24},{24,28},{28,20},{20,12},{12,4},{4,0},{1,9},{9... | collective-permute-start | bytes 3145736 | tf_op jit(solution)/shard_map/ppermute | solution.py:81
  335.1 22.0 %collective-permute-start.57 = (bf16[256,2048]{1,0:T(8,128)(2,1)S(1)}, bf16[256,2048]{1,0:T(8,128)(2,1)S(1)}, u32[]{:S(2)}, u32[]{:S(2)}) collective-permute-start(bf16[256,2048]{1,0:T(8,128)(2,1)S(1)} %collective-permute-done.55.refs_4_), channel_id=1, source_target_pairs={{8,0},{16,8},{24,16},{28,24},{20,28},{12,20},{4,12},{0,4},{9,1},{1... | collective-permute-start | bytes 3145736 | tf_op jit(solution)/shard_map/ppermute | solution.py:82
  336.0 22.5 %collective-permute-start.56 = (bf16[256,2048]{1,0:T(8,128)(2,1)S(1)}, bf16[256,2048]{1,0:T(8,128)(2,1)S(1)}, u32[]{:S(2)}, u32[]{:S(2)}) collective-permute-start(bf16[256,2048]{1,0:T(8,128)(2,1)S(1)} %collective-permute-done.54.refs_3_), channel_id=1, source_target_pairs={{0,8},{8,16},{16,24},{24,28},{28,20},{20,12},{12,4},{4,0},{1,9},{9... | collective-permute-start | bytes 3145736 | tf_op jit(solution)/shard_map/ppermute | solution.py:81
  358.5 9.8 %collective-permute-start.58 = (bf16[128,2048]{1,0:T(8,128)(2,1)S(1)}, bf16[128,2048]{1,0:T(8,128)(2,1)S(1)}, u32[]{:S(2)}, u32[]{:S(2)}) collective-permute-start(bf16[128,2048]{1,0:T(8,128)(2,1)S(1)} %slice.150), channel_id=1, source_target_pairs={{0,8},{8,16},{16,24},{24,28},{28,20},{20,12},{12,4},{4,0},{1,9},{9... | collective-permute-start | bytes 1572872 | tf_op jit(solution)/shard_map/ppermute | solution.py:87
  360.3 9.6 %collective-permute-start.59 = (bf16[128,2048]{1,0:T(8,128)(2,1)S(1)}, bf16[128,2048]{1,0:T(8,128)(2,1)S(1)}, u32[]{:S(2)}, u32[]{:S(2)}) collective-permute-start(bf16[128,2048]{1,0:T(8,128)(2,1)S(1)} %slice.151), channel_id=1, source_target_pairs={{8,0},{16,8},{24,16},{28,24},{20,28},{12,20},{4,12},{0,4},{9,1},{1... | collective-permute-start | bytes 1572872 | tf_op jit(solution)/shard_map/ppermute | solution.py:88
  415.1 21.7 %collective-permute-start.62 = (bf16[256,1024]{1,0:T(8,128)(2,1)S(1)}, bf16[256,1024]{1,0:T(8,128)(2,1)S(1)}, u32[]{:S(2)}, u32[]{:S(2)}) collective-permute-start(bf16[256,1024]{1,0:T(8,128)(2,1)S(1)} %fusion.10), channel_id=1, source_target_pairs={{0,2},{1,3},{2,0},{3,1},{4,6},{5,7},{6,4},{7,5},{8,10},{9,11},{10,... | collective-permute-start | bytes 1572872 | tf_op jit(solution)/shard_map/ppermute | solution.py:147
  419.5 21.1 %collective-permute-start.63 = (bf16[256,1024]{1,0:T(8,128)(2,1)S(1)}, bf16[256,1024]{1,0:T(8,128)(2,1)S(1)}, u32[]{:S(2)}, u32[]{:S(2)}) collective-permute-start(bf16[256,1024]{1,0:T(8,128)(2,1)S(1)} %fusion.11), channel_id=1, source_target_pairs={{0,2},{1,3},{2,0},{3,1},{4,6},{5,7},{6,4},{7,5},{8,10},{9,11},{10,... | collective-permute-start | bytes 1572872 | tf_op jit(solution)/shard_map/ppermute | solution.py:147
  454.5 28.6 %collective-permute-start.65 = (bf16[256,2048]{1,0:T(8,128)(2,1)}, bf16[256,2048]{1,0:T(8,128)(2,1)}, u32[]{:S(2)}, u32[]{:S(2)}) collective-permute-start(bf16[256,2048]{1,0:T(8,128)(2,1)} %fusion.8), channel_id=1, source_target_pairs={{0,2},{1,3},{2,0},{3,1},{4,6},{5,7},{6,4},{7,5},{8,10},{9,11},{10,... | collective-permute-start | bytes 3145736 | tf_op jit(solution)/shard_map/ppermute | solution.py:147
  484.2 14.6 %collective-permute-start.67 = (bf16[4,128,256]{2,1,0:T(8,128)(2,1)S(1)}, bf16[4,128,256]{2,1,0:T(8,128)(2,1)S(1)}, u32[]{:S(2)}, u32[]{:S(2)}) collective-permute-start(bf16[4,128,256]{2,1,0:T(8,128)(2,1)S(1)} %fusion.14), channel_id=1, source_target_pairs={{0,2},{1,3},{2,0},{3,1},{4,6},{5,7},{6,4},{7,5},{8,10},{9,11},{10,... | collective-permute-start | bytes 786440 | tf_op jit(solution)/shard_map/ppermute | solution.py:147
  501.4 8.6 %collective-permute-start.69 = (bf16[4,128,256]{2,1,0:T(8,128)(2,1)S(1)}, bf16[4,128,256]{2,1,0:T(8,128)(2,1)S(1)}, u32[]{:S(2)}, u32[]{:S(2)}) collective-permute-start(bf16[4,128,256]{2,1,0:T(8,128)(2,1)S(1)} %fusion.15), channel_id=1, source_target_pairs={{0,2},{1,3},{2,0},{3,1},{4,6},{5,7},{6,4},{7,5},{8,10},{9,11},{10,... | collective-permute-start | bytes 786440 | tf_op jit(solution)/shard_map/ppermute | solution.py:147
  527.7 16.2 %all-to-all-start.4 = ((bf16[8,16,1376]{2,1,0:T(8,128)(2,1)}), bf16[8,16,1376]{2,1,0:T(8,128)(2,1)S(1)}, u32[]{:S(2)}, u32[]{:S(2)}) async-start(bf16[8,16,1376]{2,1,0:T(8,128)(2,1)} %pad_maximum_fusion.5), calls=%async_computation.4 | async-start | bytes 720896 | tf_op jit(solution)/shard_map/all_to_all | solution.py:1193
  (74 other events, 787.8 us)
